TPU v7x, 32 devices: a whole 2x2x4 slice. The times are simulated.
32 devices in a mesh: batch: 8 (over z, x), proto: 4 (over y, core).
Axes of the slice: x: 2, y: 2, z: 4, core: 2. Of those that a mesh axis runs over, the one named last changes fastest.
Arguments:
- embeddings: bfloat16 [2048, 256], P('batch'), may hold values from -64 to 64
- prototypes: bfloat16 [65536, 256], P('proto'), may hold values from -1 to 1
- row_cot: float32 [2048], P('batch'), may hold values from -6 to 6
- col_cot: float32 [65536], P('proto'), may hold values from -6 to 6
Outputs:
- embed_grad: float32 [2048, 256], P('batch')
- proto_grad: float32 [65536, 256], P(('proto', 'batch'))
All inputs are finite; a program needn't handle non-finite values.
Results may differ from a plain program's by a relative error of at most 0.0033.
Values may be sent and summed in bfloat16 or wider, within the bound.
No kernel may reach another device: no remote copies, remote signals or barrier semaphores. Data moves between devices by JAX's collectives and lax.ppermute only.
A program may use at most 128 MiB of HBM per device.

v0:
```python
import functools
import math

import jax
import jax.numpy as jnp
from jax import lax
from jax.experimental import pallas as pl
from jax.experimental.pallas import tpu as pltpu
from jax.sharding import PartitionSpec as P

score_scale = 4.0
to_base2 = score_scale * math.log2(math.e)
lanes = 128
sublanes = 8
both = ("batch", "proto")
f32 = jnp.float32
bf16 = jnp.bfloat16
whole = pl.BlockSpec(memory_space=pltpu.VMEM)
anywhere = pl.BlockSpec(memory_space=pl.ANY)
in_smem = pl.BlockSpec(memory_space=pltpu.SMEM)
kept_products = ((0, 0), (0, 1), (1, 0))


def grant(megabytes):
    return pltpu.CompilerParams(vmem_limit_bytes=megabytes * 1024 * 1024)


beside_plan = grant(26)

dot_nt = functools.partial(
    lax.dot_general,
    dimension_numbers=(((1,), (1,)), ((), ())),
    preferred_element_type=f32,
)
dot_nn = functools.partial(jnp.dot, preferred_element_type=f32)


def tree(join, items):
    items = list(items)
    while len(items) > 1:
        items = [join(*items[k : k + 2]) if k + 1 < len(items) else items[k] for k in range(0, len(items), 2)]
    return items[0]


def add(a, b):
    return a + b


def partners(x, axis, stride=1, size=None):
    total = lax.axis_size(axis)
    return [x] + [
        lax.ppermute(x, axis, [(i, i ^ (d * stride)) for i in range(total)]) for d in range(1, size or total)
    ]


def total_pieces(x):
    pieces = partners(x, "proto")
    total, stride = lax.axis_size("batch"), 1
    while stride < total:
        size = min(4, total // stride) if stride > 1 else 2
        pieces = partners(tree(add, pieces), "batch", stride, size)
        stride *= size
    return pieces


def swap_copies(copies, axis):
    return lax.all_to_all(copies, axis, split_axis=0, concat_axis=0, tiled=True)


def share(x, axis):
    return swap_copies(jnp.broadcast_to(x[None], (lax.axis_size(axis),) + x.shape), axis)


def diagonal():
    shape = (lanes, lanes)
    return lax.broadcasted_iota(jnp.int32, shape, 0) == lax.broadcasted_iota(jnp.int32, shape, 1)


def lanes_to_rows(vector, target):
    eye = diagonal()
    for k in range(vector.shape[1] // lanes):
        piece = vector[:, k * lanes : (k + 1) * lanes]
        column = jnp.sum(jnp.where(eye, piece, 0.0), axis=1, keepdims=True)
        target[k * lanes : (k + 1) * lanes, :] = jnp.broadcast_to(column, (lanes, lanes))


def rows_to_lanes(source, target):
    eye = diagonal()
    for k in range(source.shape[0] // lanes):
        piece = source[k * lanes : (k + 1) * lanes, :]
        target[:, k * lanes : (k + 1) * lanes] = jnp.sum(
            jnp.where(eye, piece, 0.0), axis=0, keepdims=True
        )


def lane_total(value, join):
    return jnp.broadcast_to(join(value, axis=1, keepdims=True), value.shape)


def chunks(width, size=lanes):
    return [slice(k * size, (k + 1) * size) for k in range(width // size)]


def tiles(count, height, body, carry=0):
    height = min(height, count)

    def tile(index, carry):
        base = pl.multiple_of(index * height, height)
        return body([pl.ds(base + g * sublanes, sublanes) for g in range(height // sublanes)], carry)

    return lax.fori_loop(0, count // height, tile, carry)


def sum_rows(ref):
    return tree(add, [ref[d] for d in range(ref.shape[0])])


def weighted(e_ref, weight_ref, part_ref):
    count, rows = e_ref.shape

    def body(ats, carry):
        sums = [None] * len(ats)
        for c in chunks(rows):
            weight = weight_ref[:, c]
            for g, at in enumerate(ats):
                term = e_ref[at, c] * weight
                sums[g] = term if sums[g] is None else sums[g] + term
        for g, at in enumerate(ats):
            part_ref[at, :] = sums[g]
        return carry

    tiles(count, 8 * sublanes, body)


def accumulate(e_ref, column_ref, acc_ref):
    count, rows = e_ref.shape

    def body(ats, acc):
        for at in ats:
            column = column_ref[at, :]
            acc = [total + e_ref[at, c] * column for total, c in zip(acc, chunks(rows))]
        return tuple(acc)

    zero = jnp.zeros((sublanes, lanes), f32)
    acc = tiles(count, max(sublanes, (1 << 17) // rows), body, (zero,) * (rows // lanes))
    for total, c in zip(acc, chunks(rows)):
        acc_ref[:, c] = total


def split(value):
    high = value.astype(bf16).astype(f32)
    return high, value - high


def stack_lanes(values):
    which = lax.broadcasted_iota(jnp.int32, values[0].shape, 1)
    result = jnp.zeros(values[0].shape, f32)
    for k, value in enumerate(values):
        result = jnp.where(which == k, value, result)
    return result.astype(bf16)


def stack_sublanes(values, width):
    height = -(-len(values) // (2 * sublanes)) * 2 * sublanes
    pieces = []
    for start in range(0, height, sublanes):
        which = lax.broadcasted_iota(jnp.int32, (sublanes, width), 0)
        result = jnp.zeros((sublanes, width), f32)
        for k, value in enumerate(values[start : start + sublanes]):
            result = jnp.where(which == k, value, result)
        pieces.append(result)
    return jnp.concatenate(pieces, axis=0).astype(bf16)


def left_factors(products, single):
    values = []
    for value in products:
        parts = split(value)
        values += [parts[a] for a, _ in kept_products]
    return values + list(split(single))


def right_factors(products, single):
    values = []
    for value in products:
        parts = split(value)
        values += [parts[b] for _, b in kept_products]
    return values + [single] * 2


def row_lse_kernel(e_ref, p_ref, copies_ref, s_ref, top_ref, mass_ref, lse_ref):
    step = pl.program_id(0)
    _, rows, width = s_ref.shape
    low = -1e30

    @pl.when(step == 0)
    def _():
        top_ref[...] = jnp.full_like(top_ref, low)
        s_ref[...] = jnp.full_like(s_ref, low)
        mass_ref[...] = jnp.zeros_like(mass_ref)

    def scores(k):
        top = top_ref[k]
        for at in chunks(width, 2 * lanes):
            t = dot_nt(e_ref[...], p_ref[k * width + at.start : k * width + at.stop, :]) * to_base2
            s_ref[k, :, at] = t
            top = jnp.maximum(top, jnp.maximum(t[:, :lanes], t[:, lanes:]))
        mass_ref[k] = mass_ref[k] * jnp.exp2(top_ref[k] - top)
        top_ref[k] = top

    def masses(k):
        for g in range(rows // sublanes):
            at = slice(g * sublanes, (g + 1) * sublanes)
            top = top_ref[k, at, :]
            mass = mass_ref[k, at, :]
            for c in chunks(width):
                mass = mass + jnp.exp2(s_ref[k, at, c] - top)
            mass_ref[k, at, :] = mass

    scores(0)
    masses(1)
    scores(1)
    masses(0)

    @pl.when(step == pl.num_programs(0) - 1)
    def _():
        masses(1)
        top = jnp.maximum(top_ref[0], top_ref[1])
        mass = mass_ref[0] * jnp.exp2(top_ref[0] - top) + mass_ref[1] * jnp.exp2(top_ref[1] - top)
        peak = lane_total(top, jnp.max)
        mass = lane_total(mass * jnp.exp2(top - peak), jnp.sum)
        top_ref[0] = peak + jnp.log2(mass)
        rows_to_lanes(top_ref.at[0], lse_ref)
        for d in range(copies_ref.shape[0]):
            copies_ref[d] = lse_ref[...]


def row_lse(embeddings, prototypes, copies):
    rows, depth = embeddings.shape
    count = prototypes.shape[0]
    width = min(2048, count)
    return pl.pallas_call(
        row_lse_kernel,
        grid=(count // width,),
        in_specs=[
            pl.BlockSpec((rows, depth), lambda s: (0, 0)),
            pl.BlockSpec((width, depth), lambda s: (s, 0)),
        ],
        out_specs=pl.BlockSpec((copies, 1, rows), lambda s: (0, 0, 0)),
        out_shape=jax.ShapeDtypeStruct((copies, 1, rows), f32),
        scratch_shapes=[
            pltpu.VMEM((2, rows, width // 2), f32),
            pltpu.VMEM((2, rows, lanes), f32),
            pltpu.VMEM((2, rows, lanes), f32),
            pltpu.VMEM((1, rows), f32),
        ],
        compiler_params=beside_plan,
        cost_estimate=pl.CostEstimate(
            flops=2 * rows * count * depth, bytes_accessed=count * depth * 2, transcendentals=rows * count
        ),
        name="row_lse",
    )(embeddings, pltpu.with_memory_space_constraint(prototypes, pltpu.HBM))


def col_softmax_kernel(
    proto,
    me_ref,
    lse_ref,
    mine_ref,
    other_ref,
    p_ref,
    cot_ref,
    e_ref,
    copies_ref,
    col_lse_ref,
    f_ref,
    all_ref,
    a_ref,
    h_ref,
    cot_tall_ref,
    t_ref,
    acc_ref,
    part_ref,
    sem,
):
    count, rows = e_ref.shape
    members, half, _ = mine_ref.shape
    held = 2 * half
    moves = []
    for ref, which in ((mine_ref, me_ref[1]), (other_ref, 1 - me_ref[1])):
        for d in range(members):
            start = pl.multiple_of(d * held + which * half, half)
            moves.append(pltpu.make_async_copy(ref.at[d], all_ref.at[pl.ds(start, half), :], sem.at[len(moves)]))
    for move in moves:
        move.start()
    for d in range(members):
        pieces = [lse_ref[d * proto + k] for k in range(proto)]
        top = tree(jnp.maximum, pieces)
        mass = tree(add, [jnp.exp2(piece - top) for piece in pieces])
        f_ref[:, d * held : (d + 1) * held] = -math.log2(rows) - (top + jnp.log2(mass))
    lanes_to_rows(cot_ref[...], cot_tall_ref)
    for move in moves:
        move.wait()

    height = t_ref.shape[1]
    blocks = count // height

    def scores(block, slot):
        p = p_ref[pl.ds(pl.multiple_of(block * height, height), height), :]
        part = None
        for c in chunks(rows, 2 * lanes):
            t = dot_nt(p, all_ref[c, :]) * to_base2 + f_ref[:, c]
            t_ref[slot, :, c] = t
            here = jnp.maximum(t[:, :lanes], t[:, lanes:])
            part = here if part is None else jnp.maximum(part, here)
        a_ref[pl.ds(pl.multiple_of(block * height, height), height), :] = lane_total(part, jnp.max)

    def exponent(block, slot):
        for g in range(height // sublanes):
            at = pl.ds(pl.multiple_of(block * height, height) + g * sublanes, sublanes)
            inner = slice(g * sublanes, (g + 1) * sublanes)
            top = a_ref[at, :]
            mass = jnp.zeros((sublanes, lanes), f32)
            for c in chunks(rows):
                e = jnp.exp2(t_ref[slot, inner, c] - top)
                e_ref[at, c] = e
                mass = mass + e
            part_ref[at, :] = mass

    if blocks == 1:
        scores(0, 0)
        exponent(0, 0)
    else:
        scores(0, 0)

        def pair(index, carry):
            scores(2 * index + 1, 1)
            exponent(2 * index, 0)
            scores(jnp.minimum(2 * index + 2, blocks - 1), 0)
            exponent(2 * index + 1, 1)
            return carry

        lax.fori_loop(0, blocks // 2, pair, 0)
    top = a_ref[...]
    h_ref[...] = jnp.exp2(top + math.log2(rows))
    mass = lane_total(part_ref[...], jnp.sum)
    part_ref[...] = top + jnp.log2(mass)
    a_ref[...] = 1.0 / mass
    rows_to_lanes(part_ref, col_lse_ref)
    accumulate(e_ref, a_ref, acc_ref)
    rho = jnp.sum(acc_ref[...], axis=0, keepdims=True)
    copies_ref[...] = rho


def col_softmax(me, lse, mine, other, prototypes, col_cot):
    members, half, depth = mine.shape
    rows = 2 * members * half
    count = prototypes.shape[0]
    devices = lse.shape[0]
    height = min(count, 2 * lanes) if rows <= 4096 else lanes
    return pl.pallas_call(
        functools.partial(col_softmax_kernel, devices // members),
        in_specs=[in_smem, whole, anywhere, anywhere, whole, whole],
        out_specs=[whole] * 8,
        out_shape=[
            jax.ShapeDtypeStruct((count, rows), f32),
            jax.ShapeDtypeStruct((1, rows), f32),
            jax.ShapeDtypeStruct((1, count), f32),
            jax.ShapeDtypeStruct((1, rows), f32),
            jax.ShapeDtypeStruct((rows, depth), bf16),
            jax.ShapeDtypeStruct((count, lanes), f32),
            jax.ShapeDtypeStruct((count, lanes), f32),
            jax.ShapeDtypeStruct((count, lanes), f32),
        ],
        scratch_shapes=[
            pltpu.VMEM((2, height, rows), f32),
            pltpu.VMEM((sublanes, rows), f32),
            pltpu.VMEM((count, lanes), f32),
            pltpu.SemaphoreType.DMA((2 * members,)),
        ],
        compiler_params=beside_plan,
        cost_estimate=pl.CostEstimate(
            flops=2 * rows * count * depth, bytes_accessed=count * rows * 4, transcendentals=rows * count
        ),
        name="col_softmax",
    )(me, lse, mine, other, prototypes, col_cot)


def second_pair_kernel(pieces, me_ref, *refs):
    rho_refs = refs[:pieces]
    row_cot_ref, cot_ref, a_ref, e_ref, out_ref, r_ref, ratio_ref, z_ref, weight_ref, acc_ref, part_ref = refs[pieces:]
    held = row_cot_ref.shape[1]
    r_ref[...] = 1.0 / tree(add, [ref[...] for ref in rho_refs])
    weight_ref[...] = jnp.broadcast_to(r_ref[...], weight_ref.shape)
    weighted(e_ref, weight_ref, part_ref)
    z_ref[...] = cot_ref[...] / lane_total(part_ref[...], jnp.sum)
    accumulate(e_ref, z_ref, acc_ref)
    part_ref[...] = z_ref[...] / a_ref[...]
    rows_to_lanes(part_ref, ratio_ref)
    out_ref[...] = -r_ref[...] * jnp.sum(acc_ref[...], axis=0, keepdims=True)
    mine = pl.ds(pl.multiple_of(me_ref[0] * held, held), held)
    out_ref[:, mine] += jnp.where(me_ref[2] == 0, row_cot_ref[...], 0.0)


def second_pair(me, rho_pieces, row_cot, cot, a, e):
    count, rows = e.shape
    return pl.pallas_call(
        functools.partial(second_pair_kernel, len(rho_pieces)),
        in_specs=[in_smem] + [whole] * (len(rho_pieces) + 4),
        out_specs=[whole] * 4,
        out_shape=[
            jax.ShapeDtypeStruct((1, rows), f32),
            jax.ShapeDtypeStruct((1, rows), f32),
            jax.ShapeDtypeStruct((1, count), f32),
            jax.ShapeDtypeStruct((count, lanes), f32),
        ],
        scratch_shapes=[
            pltpu.VMEM((sublanes, rows), f32),
            pltpu.VMEM((sublanes, rows), f32),
            pltpu.VMEM((count, lanes), f32),
        ],
        compiler_params=beside_plan,
        cost_estimate=pl.CostEstimate(
            flops=4 * rows * count, bytes_accessed=count * rows * 4, transcendentals=0
        ),
        name="second_pair",
    )(me, *rho_pieces, row_cot, cot, a, e)


def first_pair_kernel(bar_ref, r_ref, a_ref, e_ref, out_ref, v_ref, y_ref, ay_ref, weight_ref, acc_ref, part_ref):
    v_ref[...] = r_ref[...] * sum_rows(bar_ref)
    weight_ref[...] = jnp.broadcast_to(v_ref[...], weight_ref.shape)
    weighted(e_ref, weight_ref, part_ref)
    part_ref[...] = lane_total(part_ref[...], jnp.sum) * a_ref[...]
    ay_ref[...] = part_ref[...] * a_ref[...]
    accumulate(e_ref, ay_ref, acc_ref)
    rows_to_lanes(part_ref, y_ref)
    out_ref[...] = jnp.sum(acc_ref[...], axis=0, keepdims=True)


def first_pair(bar, r, a, e):
    count, rows = e.shape
    return pl.pallas_call(
        first_pair_kernel,
        in_specs=[whole] * 4,
        out_specs=[whole] * 4,
        out_shape=[
            jax.ShapeDtypeStruct((1, rows), f32),
            jax.ShapeDtypeStruct((1, rows), f32),
            jax.ShapeDtypeStruct((1, count), f32),
            jax.ShapeDtypeStruct((count, lanes), f32),
        ],
        scratch_shapes=[
            pltpu.VMEM((sublanes, rows), f32),
            pltpu.VMEM((sublanes, rows), f32),
            pltpu.VMEM((count, lanes), f32),
        ],
        compiler_params=beside_plan,
        cost_estimate=pl.CostEstimate(
            flops=4 * rows * count, bytes_accessed=count * rows * 4, transcendentals=0
        ),
        name="first_pair",
    )(bar, r, a, e)


def embed_kernel(
    total, me_ref, last_ref, f_ref, r_ref, v_ref, e_ref, p_ref, out_ref, left_ref, right_ref, tall_ref, b_ref
):
    step = pl.program_id(0)
    rows, width = b_ref.shape

    @pl.when(step == 0)
    def _():
        out_ref[...] = jnp.zeros_like(out_ref)
        right_ref[...] = jnp.zeros_like(right_ref)
        mine = pl.ds(pl.multiple_of(me_ref[0] * rows, rows), rows)
        x = tree(add, [last_ref[d, :, mine] for d in range(last_ref.shape[0])])
        for k, value in enumerate((f_ref[:, mine], r_ref[:, mine], v_ref[:, mine], x)):
            lanes_to_rows(value, tall_ref.at[k])
        r, v, x = (tall_ref[k] for k in (1, 2, 3))
        one = jnp.ones_like(r)
        left_ref[...] = stack_lanes(left_factors([-r, -x, one], -v))

    y, lse, a = (last_ref[step, :, total + k * width : total + (k + 1) * width] for k in range(3))
    w = jnp.exp2(lse + math.log2(total))
    rows_of = stack_sublanes(right_factors([a, w, y], jnp.ones_like(a)), width)
    right_ref[0 : rows_of.shape[0], :] = rows_of
    e = e_ref[...]
    left = left_ref[...]
    f = tall_ref[0]
    sub = min(2 * lanes, width)
    group = min(4 * sub, width)
    for c in chunks(width, sub):
        s = dot_nt(e, p_ref[c, :])
        bracket = dot_nn(left, right_ref[:, c])
        t = s * to_base2 - lse[:, c]
        plan = jnp.concatenate([jnp.exp2(t[:, at] + f) for at in chunks(sub)], axis=1)
        b_ref[:, c] = (plan * bracket).astype(bf16)
        if c.stop % group == 0:
            done = slice(c.stop - group, c.stop)
            out_ref[...] += score_scale * dot_nn(b_ref[:, done], p_ref[done, :])


def embed_part(me, last, f, r, v, embeddings, prototypes):
    rows, depth = embeddings.shape
    members = last.shape[0]
    total = f.shape[1]
    count = prototypes.shape[0]
    width = count // members
    full = lambda shape: pl.BlockSpec(shape, lambda s, me: (0,) * len(shape))
    return pl.pallas_call(
        functools.partial(embed_kernel, total),
        grid_spec=pltpu.PrefetchScalarGridSpec(
            num_scalar_prefetch=1,
            grid=(members,),
            in_specs=[
                full(last.shape),
                full(f.shape),
                full(f.shape),
                full(f.shape),
                full((rows, depth)),
                pl.BlockSpec((width, depth), lambda s, me: (s, 0)),
            ],
            out_specs=full((rows, depth)),
            scratch_shapes=[
                pltpu.VMEM((rows, lanes), bf16),
                pltpu.VMEM((lanes, width), bf16),
                pltpu.VMEM((4, rows, lanes), f32),
                pltpu.VMEM((rows, width), bf16),
            ],
        ),
        out_shape=jax.ShapeDtypeStruct((rows, depth), f32),
        compiler_params=beside_plan,
        cost_estimate=pl.CostEstimate(
            flops=4 * rows * count * depth, bytes_accessed=count * depth * 2, transcendentals=rows * count
        ),
        name="embed_part",
    )(me, last, f, r, v, embeddings, pltpu.with_memory_space_constraint(prototypes, pltpu.HBM))


def proto_kernel(last_ref, r_ref, v_ref, a_ref, h_ref, z_ref, ay_ref, all_ref, e_ref, out_ref, right_ref, b_ref):
    count, rows = e_ref.shape
    height = b_ref.shape[1]
    x = tree(add, [last_ref[d, :, 0:rows] for d in range(last_ref.shape[0])])
    right_ref[...] = jnp.zeros_like(right_ref)
    rows_of = stack_sublanes(right_factors([-r_ref[...], -v_ref[...], -x], jnp.ones_like(x)), rows)
    right_ref[0 : rows_of.shape[0], :] = rows_of

    blocks = count // height

    def bracket(block, slot):
        at = pl.ds(pl.multiple_of(block * height, height), height)
        left = stack_lanes(left_factors([z_ref[at, :], a_ref[at, :], h_ref[at, :]], ay_ref[at, :]))
        for c in chunks(rows, 2 * lanes):
            b_ref[slot, :, c] = (e_ref[at, c] * dot_nn(left, right_ref[:, c])).astype(bf16)

    def product(block, slot):
        at = pl.ds(pl.multiple_of(block * height, height), height)
        out_ref[at, :] = score_scale * dot_nn(b_ref[slot], all_ref[...])

    bracket(0, 0)
    if blocks == 1:
        product(0, 0)
    else:

        def pair(index, carry):
            bracket(2 * index + 1, 1)
            product(2 * index, 0)
            bracket(jnp.minimum(2 * index + 2, blocks - 1), 0)
            product(2 * index + 1, 1)
            return carry

        lax.fori_loop(0, blocks // 2, pair, 0)


def proto_part(last, r, v, a, h, z, ay, all_rows, e):
    count, rows = e.shape
    depth = all_rows.shape[1]
    height = min(count, 2 * lanes)
    return pl.pallas_call(
        proto_kernel,
        in_specs=[whole] * 9,
        out_specs=whole,
        out_shape=jax.ShapeDtypeStruct((count, depth), f32),
        scratch_shapes=[pltpu.VMEM((lanes, rows), bf16), pltpu.VMEM((2, height, rows), bf16)],
        compiler_params=beside_plan,
        cost_estimate=pl.CostEstimate(
            flops=2 * rows * count * depth, bytes_accessed=count * rows * 4, transcendentals=0
        ),
        name="proto_part",
    )(last, r, v, a, h, z, ay, all_rows, e)


def shards(embeddings, prototypes, row_cot, col_cot):
    batch, proto = lax.axis_size("batch"), lax.axis_size("proto")
    held = embeddings.shape[0]
    count = prototypes.shape[0] // batch
    member, holder = lax.axis_index("batch"), lax.axis_index("proto")
    me = jnp.stack([member, holder % 2, holder]).astype(jnp.int32)
    own = lax.dynamic_slice_in_dim(prototypes, member * count, count, axis=0)
    own_cot = lax.dynamic_slice_in_dim(col_cot, member * count, count, axis=0)[None, :]

    half = lax.dynamic_slice_in_dim(embeddings, (holder % 2) * (held // 2), held // 2, axis=0)
    copies = jnp.broadcast_to(half[None], (batch,) + half.shape)
    copies, me, own, own_cot, row_cot, embeddings = lax.optimization_barrier(
        (copies, me, own, own_cot, row_cot, embeddings)
    )
    mine = swap_copies(copies, "batch")
    lse = row_lse(embeddings, prototypes, batch * proto)
    mine, lse = lax.optimization_barrier((mine, lse))
    other = lax.ppermute(mine, "proto", [(i, i ^ 1) for i in range(proto)])
    lse = swap_copies(lse, both)
    e, rho, col_lse, f, all_rows, a, h, cot = col_softmax(me, lse, mine, other, own, own_cot)
    bar, r, ratio, z = second_pair(me, total_pieces(rho), row_cot[None, :], cot, a, e)
    bar = share(tree(add, partners(bar, "proto")), "batch")
    x, v, y, ay = first_pair(bar, r, a, e)
    x = tree(add, partners(x, "proto"))
    last = share(jnp.concatenate([x, y, col_lse, ratio], axis=1), "batch")
    embed = embed_part(me, last, f, r, v, embeddings, prototypes)
    embed_grad = tree(add, partners(embed, "proto"))
    proto_grad = proto_part(last, r, v, a, h, z, ay, all_rows, e)
    return (embed_grad, proto_grad)


def solution(mesh):
    in_specs = (P("batch", None), P("proto", None), P("batch"), P("proto"))
    out_specs = (P("batch", None), P(("proto", "batch"), None))
    return jax.shard_map(shards, mesh=mesh, in_specs=in_specs, out_specs=out_specs, check_vma=False)
```

profile of v0, /device:TPU:0, one launch (start us, length us, event | category | flops | bytes accessed | tf_op | source)
XLA Modules:
  0.0 140.6 jit_solution(14662962251561384959)
XLA Ops:
  0.6 0.7 dynamic_slice.11
  1.4 1.3 constant_dynamic-slice_fusion.p_ref
  2.7 0.8 constant_dynamic-slice_fusion.1
  3.6 0.8 broadcast_in_dim.28
  4.4 7.3 %all-to-all-start = ((bf16[8,128,256]{2,1,0:T(8,128)(2,1)}), bf16[8,128,256]{2,1,0:T(8,128)(2,1)S(1)}, u32[]{:S(2)}, u32[]{:S(2)}) async-start(bf16[8,128,256]{2,1,0:T(8,128)(2,1)} %broadcast_in_dim.28), calls=%async_computation | async-start | bytes 1048576 | tf_op jit(solution)/shard_map/all_to_all | solution.py:67
  11.7 0.9 copy-done.13
  12.6 9.1 %row_lse.1 = f32[32,1,256]{2,1,0:T(1,128)S(1)} custom-call(bf16[256,256]{1,0:T(8,128)(2,1)S(1)} %copy-done.13, bf16[16384,256]{1,0:T(8,128)(2,1)} %p_ref.3), custom_call_target="tpu_custom_call" | custom-call | flops 2147483648 | bytes 8388608 | tf_op jit(solution)/shard_map/row_lse/pallas_call | solution.py:242
  21.7 4.5 %all-to-all-done.mine_ref = bf16[8,128,256]{2,1,0:T(8,128)(2,1)S(1)} async-done(((bf16[8,128,256]{2,1,0:T(8,128)(2,1)}), bf16[8,128,256]{2,1,0:T(8,128)(2,1)S(1)}, u32[]{:S(2)}, u32[]{:S(2)}) %all-to-all-start) | async-done | bytes 524320 | tf_op jit(solution)/shard_map/all_to_all | solution.py:67
  26.2 10.8 %all_to_all.20.lse_ref = f32[32,1,256]{2,1,0:T(1,128)S(1)} all-to-all(f32[32,1,256]{2,1,0:T(1,128)S(1)} %row_lse.1), channel_id=1, replica_groups=mesh['batch'=8,'proto'=4] {'batch','proto'}, dimensions={0} | all-to-all | bytes 65536 | tf_op jit(solution)/shard_map/all_to_all | solution.py:67
  37.0 10.6 %col_softmax.1 = (f32[2048,2048]{1,0:T(8,128)S(1)}, f32[1,2048]{1,0:T(1,128)S(1)}, f32[1,2048]{1,0:T(1,128)S(1)}, f32[1,2048]{1,0:T(1,128)S(1)}, bf16[2048,256]{...) custom-call(s32[3]{0:T(128)S(1)} %pad_add_fusion.me_ref, ...), custom_call_target="tpu_custom_call" | custom-call | flops 2147483648 | bytes 16777216 | tf_op jit(solution)/shard_map/col_softmax/pallas_call | solution.py:361
  47.7 5.7 %copy-done = f32[2048,2048]{1,0:T(8,128)} copy-done((f32[2048,2048]{1,0:T(8,128)}, f32[2048,2048]{1,0:T(8,128)S(1)}, u32[]{:S(2)}) %copy-start) | copy-done | bytes 16777240
  53.4 1.0 copy-done.5
  54.4 1.0 copy-done.7
  55.3 1.0 copy-done.9
  56.3 0.2 collective-permute-start.3
  56.5 1.6 %collective-permute-start.2 = (f32[1,2048]{1,0:T(1,128)S(1)}, f32[1,2048]{1,0:T(1,128)S(1)}, u32[]{:S(2)}, u32[]{:S(2)}) collective-permute-start(f32[1,2048]{1,0:T(1,128)S(1)} %get-tuple-element.33), channel_id=1, source_target_pairs={{0,2},{1,3},{2,0},{3,1},{4,6},{5,7},{6,4},{7,5},{8,10},{9,11},{10,... | collective-permute-start | bytes 24584 | tf_op jit(solution)/shard_map/ppermute | solution.py:52
  58.1 0.1 collective-permute-start.1
  58.2 1.2 collective-permute-done.3
  59.4 0.8 collective-permute-done.2
  60.2 0.7 collective-permute-start.4
  60.9 3.0 %collective-permute-done.4 = f32[1,2048]{1,0:T(1,128)S(1)} collective-permute-done((f32[1,2048]{1,0:T(1,128)S(1)}, f32[1,2048]{1,0:T(1,128)S(1)}, u32[]{:S(2)}, u32[]{:S(2)}) %collective-permute-start.4) | collective-permute-done | bytes 8224 | tf_op jit(solution)/shard_map/ppermute | solution.py:52
  63.9 0.7 collective-permute-start.7
  64.6 1.5 %collective-permute-start.6 = (f32[1,2048]{1,0:T(1,128)S(1)}, f32[1,2048]{1,0:T(1,128)S(1)}, u32[]{:S(2)}, u32[]{:S(2)}) collective-permute-start(f32[1,2048]{1,0:T(1,128)S(1)} %add.57.refs_0_), channel_id=1, source_target_pairs={{0,16},{4,20},{8,24},{12,28},{16,0},{20,4},{24,8},{28,12},{1,17},{... | collective-permute-start | bytes 24584 | tf_op jit(solution)/shard_map/ppermute | solution.py:52
  66.1 2.3 %collective-permute-start.5 = (f32[1,2048]{1,0:T(1,128)S(1)}, f32[1,2048]{1,0:T(1,128)S(1)}, u32[]{:S(2)}, u32[]{:S(2)}) collective-permute-start(f32[1,2048]{1,0:T(1,128)S(1)} %add.57.refs_0_), channel_id=1, source_target_pairs={{0,8},{4,12},{8,0},{12,4},{16,24},{20,28},{24,16},{28,20},{1,9},{5... | collective-permute-start | bytes 24584 | tf_op jit(solution)/shard_map/ppermute | solution.py:52
  68.4 1.1 collective-permute-done.7.refs_3_
  69.5 0.6 collective-permute-done.5.refs_1_
  70.0 5.8 %copy-done.1 = f32[2048,2048]{1,0:T(8,128)S(1)} copy-done((f32[2048,2048]{1,0:T(8,128)S(1)}, f32[2048,2048]{1,0:T(8,128)}, u32[]{:S(2)}) %copy-start.1) | copy-done | bytes 16777240
  75.8 1.2 copy-done.6
  77.0 4.1 %second_pair.1 = (f32[1,2048]{1,0:T(1,128)S(1)}, f32[1,2048]{1,0:T(1,128)S(1)}, f32[1,2048]{1,0:T(1,128)S(1)}, f32[2048,128]{1,0:T(8,128)S(1)}) custom-call(s32[3]{0:T(128)S(1)} %pad_add_fusion.me_ref, f32[1,2048]{1,0:T(1,128)S(1)} %add.57.refs_0_, f32[1,2048]{1,0:T(1,128)S(1)} %collective-permute-done.5.refs_1_, ...), custom_call_target="tpu_custom_call" | custom-call | flops 16777216 | bytes 16777216 | tf_op jit(solution)/shard_map/second_pair/pallas_call | solution.py:407
  81.1 1.0 copy-done.11
  82.1 1.6 %collective-permute-start.9 = (f32[1,2048]{1,0:T(1,128)S(1)}, f32[1,2048]{1,0:T(1,128)S(1)}, u32[]{:S(2)}, u32[]{:S(2)}) collective-permute-start(f32[1,2048]{1,0:T(1,128)S(1)} %get-tuple-element.38), channel_id=1, source_target_pairs={{0,2},{1,3},{2,0},{3,1},{4,6},{5,7},{6,4},{7,5},{8,10},{9,11},{10,... | collective-permute-start | bytes 24584 | tf_op jit(solution)/shard_map/ppermute | solution.py:52
  83.7 0.3 collective-permute-start.8
  83.9 1.2 collective-permute-done.10
  85.1 0.6 collective-permute-done.9
  85.8 10.4 %all_to_all.21.bar_ref = f32[8,1,2048]{2,1,0:T(1,128)S(1)} all-to-all(f32[8,1,2048]{2,1,0:T(1,128)S(1)} %broadcast_in_dim.32), channel_id=1, replica_groups=mesh['batch'=8,'proto'=4] {'batch'}, dimensions={0} | all-to-all | bytes 131072 | tf_op jit(solution)/shard_map/all_to_all | solution.py:67
  96.3 3.3 %first_pair.1 = (f32[1,2048]{1,0:T(1,128)S(1)}, f32[1,2048]{1,0:T(1,128)S(1)}, f32[1,2048]{1,0:T(1,128)S(1)}, f32[2048,128]{1,0:T(8,128)S(1)}) custom-call(f32[8,1,2048]{2,1,0:T(1,128)S(1)} %all_to_all.21.bar_ref, f32[1,2048]{1,0:T(1,128)S(1)} %get-tuple-element.39.r_ref, f32[2048,128]{1,0:T(8,128)S(1)} %get-tuple-element.36.refs_6_.a_ref, ...), custom_call_target="tpu_custom_call" | custom-call | flops 16777216 | bytes 16777216 | tf_op jit(solution)/shard_map/first_pair/pallas_call | solution.py:443
  99.6 1.5 %collective-permute-start.12 = (f32[1,2048]{1,0:T(1,128)S(1)}, f32[1,2048]{1,0:T(1,128)S(1)}, u32[]{:S(2)}, u32[]{:S(2)}) collective-permute-start(f32[1,2048]{1,0:T(1,128)S(1)} %get-tuple-element.40), channel_id=1, source_target_pairs={{0,2},{1,3},{2,0},{3,1},{4,6},{5,7},{6,4},{7,5},{8,10},{9,11},{10,... | collective-permute-start | bytes 24584 | tf_op jit(solution)/shard_map/ppermute | solution.py:52
  101.1 0.3 collective-permute-start.11
  101.5 1.3 collective-permute-done.13
  102.7 0.6 collective-permute-done.12
  103.4 0.1 broadcast_in_dim.34
  103.6 12.4 %all_to_all.22.last_ref = f32[8,1,8192]{2,1,0:T(1,128)S(1)} all-to-all(f32[8,1,8192]{2,1,0:T(1,128)S(1)} %broadcast_in_dim.34), channel_id=1, replica_groups=mesh['batch'=8,'proto'=4] {'batch'}, dimensions={0} | all-to-all | bytes 524288 | tf_op jit(solution)/shard_map/all_to_all | solution.py:67
  116.0 11.3 %embed_part.1 = f32[256,256]{1,0:T(8,128)S(1)} custom-call(s32[3]{0:T(128)S(1)} %pad_add_fusion.me_ref, f32[8,1,8192]{2,1,0:T(1,128)S(1)} %all_to_all.22.last_ref, f32[1,2048]{1,0:T(1,128)S(1)} %get-tuple-element.44.f_ref, f32[1,2048]{1,0:T(1,128)S(1)} %get-tuple-element.39.r_ref, f32[1,2048]{1,0:T(1,128)S(1)} %get-tuple-element.45.v_ref, ...), custom_call_target="tpu_custom_call" | custom-call | flops 4294967296 | bytes 8388608 | tf_op jit(solution)/shard_map/embed_part/pallas_call | solution.py:511
  127.3 0.6 collective-permute-start.15
  128.0 1.2 collective-permute-start.14
  129.2 7.4 %proto_part.1 = f32[2048,256]{1,0:T(8,128)} custom-call(f32[8,1,8192]{2,1,0:T(1,128)S(1)} %all_to_all.22.last_ref, f32[1,2048]{1,0:T(1,128)S(1)} %get-tuple-element.39.r_ref, f32[1,2048]{1,0:T(1,128)S(1)} %get-tuple-element.45.v_ref, f32[2048,128]{1,0:T(8,128)S(1)} %copy-done.4, f32[2048,128]{1,0:T(8,128)S(1)} %copy-done.10, f32[2048,128]{1,0:T(8,128)S(1)} %copy-done.12, ...), custom_call_target="tpu_custom_call" | custom-call | flops 2147483648 | bytes 16777216 | tf_op jit(solution)/shard_map/proto_part/pallas_call | solution.py:580
  136.6 3.3 %collective-permute-done.15 = f32[256,256]{1,0:T(8,128)S(1)} collective-permute-done((f32[256,256]{1,0:T(8,128)S(1)}, f32[256,256]{1,0:T(8,128)S(1)}, u32[]{:S(2)}, u32[]{:S(2)}) %collective-permute-start.15) | collective-permute-done | bytes 262176 | tf_op jit(solution)/shard_map/ppermute | solution.py:52
  139.8 0.8 add_add_fusion
  (42 shorter events, 0.4 us)
Async XLA Ops:
  4.4 21.7 %all-to-all-start = ((bf16[8,128,256]{2,1,0:T(8,128)(2,1)}), bf16[8,128,256]{2,1,0:T(8,128)(2,1)S(1)}, u32[]{:S(2)}, u32[]{:S(2)}) async-start(bf16[8,128,256]{2,1,0:T(8,128)(2,1)} %broadcast_in_dim.28), calls=%async_computation | async-start | bytes 1048576 | tf_op jit(solution)/shard_map/all_to_all | solution.py:67
  11.7 0.9 copy-start.13
  12.6 57.5 %copy-start.15 = (f32[256]{0:T(256)S(1)}, f32[256]{0:T(256)}, u32[]{:S(2)}) copy-start(f32[256]{0:T(256)} %param.6) | copy-start | bytes 3076
  26.1 10.8 %collective-permute-start = (bf16[8,128,256]{2,1,0:T(8,128)(2,1)S(1)}, bf16[8,128,256]{2,1,0:T(8,128)(2,1)S(1)}, u32[]{:S(2)}, u32[]{:S(2)}) collective-permute-start(bf16[8,128,256]{2,1,0:T(8,128)(2,1)S(1)} %all-to-all-done.mine_ref), channel_id=1, source_target_pairs={{0,1},{1,0},{2,3},{3,2},{4,5},{5,4},{6,7},{7,6},{8,9},{9,8},{10,11... | collective-permute-start | bytes 1572872 | tf_op jit(solution)/shard_map/ppermute | solution.py:611
  47.6 5.8 %copy-start = (f32[2048,2048]{1,0:T(8,128)}, f32[2048,2048]{1,0:T(8,128)S(1)}, u32[]{:S(2)}) copy-start(f32[2048,2048]{1,0:T(8,128)S(1)} %get-tuple-element.37.refs_7_.e_ref) | copy-start | bytes 50331652
  53.4 1.0 copy-start.5
  54.4 1.0 copy-start.7
  55.3 1.0 copy-start.9
  56.3 39.9 %copy-start.3 = (f32[2048,128]{1,0:T(8,128)}, f32[2048,128]{1,0:T(8,128)S(1)}, u32[]{:S(2)}) copy-start(f32[2048,128]{1,0:T(8,128)S(1)} %get-tuple-element.36.refs_6_.a_ref) | copy-start | bytes 3145732
  56.3 3.1 %collective-permute-start.3 = (f32[1,2048]{1,0:T(1,128)S(1)}, f32[1,2048]{1,0:T(1,128)S(1)}, u32[]{:S(2)}, u32[]{:S(2)}) collective-permute-start(f32[1,2048]{1,0:T(1,128)S(1)} %get-tuple-element.33), channel_id=1, source_target_pairs={{0,3},{1,2},{2,1},{3,0},{4,7},{5,6},{6,5},{7,4},{8,11},{9,10},{10,... | collective-permute-start | bytes 24584 | tf_op jit(solution)/shard_map/ppermute | solution.py:52
  56.5 3.7 %collective-permute-start.2 = (f32[1,2048]{1,0:T(1,128)S(1)}, f32[1,2048]{1,0:T(1,128)S(1)}, u32[]{:S(2)}, u32[]{:S(2)}) collective-permute-start(f32[1,2048]{1,0:T(1,128)S(1)} %get-tuple-element.33), channel_id=1, source_target_pairs={{0,2},{1,3},{2,0},{3,1},{4,6},{5,7},{6,4},{7,5},{8,10},{9,11},{10,... | collective-permute-start | bytes 24584 | tf_op jit(solution)/shard_map/ppermute | solution.py:52
  58.1 2.1 %collective-permute-start.1 = (f32[1,2048]{1,0:T(1,128)S(1)}, f32[1,2048]{1,0:T(1,128)S(1)}, u32[]{:S(2)}, u32[]{:S(2)}) collective-permute-start(f32[1,2048]{1,0:T(1,128)S(1)} %get-tuple-element.33), channel_id=1, source_target_pairs={{0,1},{1,0},{2,3},{3,2},{4,5},{5,4},{6,7},{7,6},{8,9},{9,8},{10,11... | collective-permute-start | bytes 24584 | tf_op jit(solution)/shard_map/ppermute | solution.py:52
  60.2 3.7 %collective-permute-start.4 = (f32[1,2048]{1,0:T(1,128)S(1)}, f32[1,2048]{1,0:T(1,128)S(1)}, u32[]{:S(2)}, u32[]{:S(2)}) collective-permute-start(f32[1,2048]{1,0:T(1,128)S(1)} %add_add_fusion.3), channel_id=1, source_target_pairs={{0,4},{4,0},{8,12},{12,8},{16,20},{20,16},{24,28},{28,24},{1,5},{5... | collective-permute-start | bytes 24584 | tf_op jit(solution)/shard_map/ppermute | solution.py:52
  63.9 5.5 %collective-permute-start.7 = (f32[1,2048]{1,0:T(1,128)S(1)}, f32[1,2048]{1,0:T(1,128)S(1)}, u32[]{:S(2)}, u32[]{:S(2)}) collective-permute-start(f32[1,2048]{1,0:T(1,128)S(1)} %add.57.refs_0_), channel_id=1, source_target_pairs={{0,24},{4,28},{8,16},{12,20},{16,8},{20,12},{24,0},{28,4},{1,25},{... | collective-permute-start | bytes 24584 | tf_op jit(solution)/shard_map/ppermute | solution.py:52
  64.6 4.8 %collective-permute-start.6 = (f32[1,2048]{1,0:T(1,128)S(1)}, f32[1,2048]{1,0:T(1,128)S(1)}, u32[]{:S(2)}, u32[]{:S(2)}) collective-permute-start(f32[1,2048]{1,0:T(1,128)S(1)} %add.57.refs_0_), channel_id=1, source_target_pairs={{0,16},{4,20},{8,24},{12,28},{16,0},{20,4},{24,8},{28,12},{1,17},{... | collective-permute-start | bytes 24584 | tf_op jit(solution)/shard_map/ppermute | solution.py:52
  66.1 3.9 %collective-permute-start.5 = (f32[1,2048]{1,0:T(1,128)S(1)}, f32[1,2048]{1,0:T(1,128)S(1)}, u32[]{:S(2)}, u32[]{:S(2)}) collective-permute-start(f32[1,2048]{1,0:T(1,128)S(1)} %add.57.refs_0_), channel_id=1, source_target_pairs={{0,8},{4,12},{8,0},{12,4},{16,24},{20,28},{24,16},{28,20},{1,9},{5... | collective-permute-start | bytes 24584 | tf_op jit(solution)/shard_map/ppermute | solution.py:52
  70.0 5.8 %copy-start.1 = (f32[2048,2048]{1,0:T(8,128)S(1)}, f32[2048,2048]{1,0:T(8,128)}, u32[]{:S(2)}) copy-start(f32[2048,2048]{1,0:T(8,128)} %copy-done) | copy-start | bytes 50331652
  75.8 1.2 copy-start.6
  77.0 19.2 %copy-start.2 = (f32[2048,2048]{1,0:T(8,128)S(1)}, f32[2048,2048]{1,0:T(8,128)}, u32[]{:S(2)}) copy-start(f32[2048,2048]{1,0:T(8,128)} %copy-done) | copy-start | bytes 50331652
  81.1 1.0 copy-start.11
  82.1 3.1 %collective-permute-start.10 = (f32[1,2048]{1,0:T(1,128)S(1)}, f32[1,2048]{1,0:T(1,128)S(1)}, u32[]{:S(2)}, u32[]{:S(2)}) collective-permute-start(f32[1,2048]{1,0:T(1,128)S(1)} %get-tuple-element.38), channel_id=1, source_target_pairs={{0,3},{1,2},{2,1},{3,0},{4,7},{5,6},{6,5},{7,4},{8,11},{9,10},{10,... | collective-permute-start | bytes 24584 | tf_op jit(solution)/shard_map/ppermute | solution.py:52
  82.1 3.7 %collective-permute-start.9 = (f32[1,2048]{1,0:T(1,128)S(1)}, f32[1,2048]{1,0:T(1,128)S(1)}, u32[]{:S(2)}, u32[]{:S(2)}) collective-permute-start(f32[1,2048]{1,0:T(1,128)S(1)} %get-tuple-element.38), channel_id=1, source_target_pairs={{0,2},{1,3},{2,0},{3,1},{4,6},{5,7},{6,4},{7,5},{8,10},{9,11},{10,... | collective-permute-start | bytes 24584 | tf_op jit(solution)/shard_map/ppermute | solution.py:52
  83.7 2.1 %collective-permute-start.8 = (f32[1,2048]{1,0:T(1,128)S(1)}, f32[1,2048]{1,0:T(1,128)S(1)}, u32[]{:S(2)}, u32[]{:S(2)}) collective-permute-start(f32[1,2048]{1,0:T(1,128)S(1)} %get-tuple-element.38), channel_id=1, source_target_pairs={{0,1},{1,0},{2,3},{3,2},{4,5},{5,4},{6,7},{7,6},{8,9},{9,8},{10,11... | collective-permute-start | bytes 24584 | tf_op jit(solution)/shard_map/ppermute | solution.py:52
  96.2 19.7 %copy-start.14 = (bf16[256,256]{1,0:T(8,128)(2,1)S(1)}, bf16[256,256]{1,0:T(8,128)(2,1)}, u32[]{:S(2)}) copy-start(bf16[256,256]{1,0:T(8,128)(2,1)} %e_ref.1) | copy-start | bytes 393220
  99.5 3.2 %collective-permute-start.13 = (f32[1,2048]{1,0:T(1,128)S(1)}, f32[1,2048]{1,0:T(1,128)S(1)}, u32[]{:S(2)}, u32[]{:S(2)}) collective-permute-start(f32[1,2048]{1,0:T(1,128)S(1)} %get-tuple-element.40), channel_id=1, source_target_pairs={{0,3},{1,2},{2,1},{3,0},{4,7},{5,6},{6,5},{7,4},{8,11},{9,10},{10,... | collective-permute-start | bytes 24584 | tf_op jit(solution)/shard_map/ppermute | solution.py:52
  99.6 3.7 %collective-permute-start.12 = (f32[1,2048]{1,0:T(1,128)S(1)}, f32[1,2048]{1,0:T(1,128)S(1)}, u32[]{:S(2)}, u32[]{:S(2)}) collective-permute-start(f32[1,2048]{1,0:T(1,128)S(1)} %get-tuple-element.40), channel_id=1, source_target_pairs={{0,2},{1,3},{2,0},{3,1},{4,6},{5,7},{6,4},{7,5},{8,10},{9,11},{10,... | collective-permute-start | bytes 24584 | tf_op jit(solution)/shard_map/ppermute | solution.py:52
  101.1 2.2 %collective-permute-start.11 = (f32[1,2048]{1,0:T(1,128)S(1)}, f32[1,2048]{1,0:T(1,128)S(1)}, u32[]{:S(2)}, u32[]{:S(2)}) collective-permute-start(f32[1,2048]{1,0:T(1,128)S(1)} %get-tuple-element.40), channel_id=1, source_target_pairs={{0,1},{1,0},{2,3},{3,2},{4,5},{5,4},{6,7},{7,6},{8,9},{9,8},{10,11... | collective-permute-start | bytes 24584 | tf_op jit(solution)/shard_map/ppermute | solution.py:52
  103.3 25.8 %copy-start.4 = (f32[2048,128]{1,0:T(8,128)S(1)}, f32[2048,128]{1,0:T(8,128)}, u32[]{:S(2)}) copy-start(f32[2048,128]{1,0:T(8,128)} %copy-done.3) | copy-start | bytes 3145732
  103.4 25.8 %copy-start.8 = (bf16[2048,256]{1,0:T(8,128)(2,1)S(1)}, bf16[2048,256]{1,0:T(8,128)(2,1)}, u32[]{:S(2)}) copy-start(bf16[2048,256]{1,0:T(8,128)(2,1)} %copy-done.7) | copy-start | bytes 3145732
  103.4 25.8 %copy-start.10 = (f32[2048,128]{1,0:T(8,128)S(1)}, f32[2048,128]{1,0:T(8,128)}, u32[]{:S(2)}) copy-start(f32[2048,128]{1,0:T(8,128)} %copy-done.9) | copy-start | bytes 3145732
  103.4 25.8 %copy-start.12 = (f32[2048,128]{1,0:T(8,128)S(1)}, f32[2048,128]{1,0:T(8,128)}, u32[]{:S(2)}) copy-start(f32[2048,128]{1,0:T(8,128)} %copy-done.11) | copy-start | bytes 3145732
  127.2 9.3 %collective-permute-start.16 = (f32[256,256]{1,0:T(8,128)S(1)}, f32[256,256]{1,0:T(8,128)S(1)}, u32[]{:S(2)}, u32[]{:S(2)}) collective-permute-start(f32[256,256]{1,0:T(8,128)S(1)} %embed_part.1), channel_id=1, source_target_pairs={{0,3},{1,2},{2,1},{3,0},{4,7},{5,6},{6,5},{7,4},{8,11},{9,10},{10,... | collective-permute-start | bytes 786440 | tf_op jit(solution)/shard_map/ppermute | solution.py:52
  127.3 12.5 %collective-permute-start.15 = (f32[256,256]{1,0:T(8,128)S(1)}, f32[256,256]{1,0:T(8,128)S(1)}, u32[]{:S(2)}, u32[]{:S(2)}) collective-permute-start(f32[256,256]{1,0:T(8,128)S(1)} %embed_part.1), channel_id=1, source_target_pairs={{0,2},{1,3},{2,0},{3,1},{4,6},{5,7},{6,4},{7,5},{8,10},{9,11},{10,... | collective-permute-start | bytes 786440 | tf_op jit(solution)/shard_map/ppermute | solution.py:52
  128.0 11.9 %collective-permute-start.14 = (f32[256,256]{1,0:T(8,128)S(1)}, f32[256,256]{1,0:T(8,128)S(1)}, u32[]{:S(2)}, u32[]{:S(2)}) collective-permute-start(f32[256,256]{1,0:T(8,128)S(1)} %embed_part.1), channel_id=1, source_target_pairs={{0,1},{1,0},{2,3},{3,2},{4,5},{5,4},{6,7},{7,6},{8,9},{9,8},{10,11... | collective-permute-start | bytes 786440 | tf_op jit(solution)/shard_map/ppermute | solution.py:52
where the time goes:
time: 142 us; the launch traced here: 141 us
  Pallas kernels  45.7 us (32%)
  blocking collectives  33.7 us (24%)
  local copies, waits for them, and re-layouts  21.4 us (15%)
  starting transfers between devices  20 us (14%)
  waiting for transfers between devices  18.1 us (13%)
    all_to_all x3, blocking collectives, swap_copies(): return lax.all_to_all(copies, axis, split_axis=0, concat_axis=0, tiled=True)  33.7 us
    unnamed x32, local copies, waits for them, and re-layouts  17.5 us
    ppermute x16, waiting for transfers between devices, partners(): lax.ppermute(x, axis, [(i, i ^ d * stride) for i in range(total)])  13.6 us
    ppermute x16, starting transfers between devices, partners(): lax.ppermute(x, axis, [(i, i ^ d * stride) for i in range(total)])  12.7 us
    pallas_call x1, Pallas kernels, embed_part(): pl.pallas_call(functools.partial(embed_kernel, total), grid_spec=pltpu.Pr...  11.3 us
    pallas_call x1, Pallas kernels, col_softmax(): pl.pallas_call(functools.partial(col_softmax_kernel, devices // members),...  10.6 us
    pallas_call x1, Pallas kernels, row_lse(): pl.pallas_call(row_lse_kernel, grid=(count // width,), in_specs=[pl.Block...  9.11 us
    pallas_call x1, Pallas kernels, proto_part(): pl.pallas_call(proto_kernel, in_specs=[whole] * 9, out_specs=whole, out_s...  7.37 us
  transfers between devices with their start and end apart: 18, of which 11 were waited for; matrix products, arithmetic and copies ran while one was open for 0% of the time, Pallas kernels for 12%

commit v1 on v0

--- a/solution.py
+++ b/solution.py
@@ -21,6 +21,18 @@
 kept_products = ((0, 0), (0, 1), (1, 0))
 
 
+def held(shape, dtype=f32):
+    return pltpu.VMEM(shape, dtype)
+
+
+def in_vmem(x):
+    return pltpu.with_memory_space_constraint(x, pltpu.VMEM)
+
+
+def in_hbm(x):
+    return pltpu.with_memory_space_constraint(x, pltpu.HBM)
+
+
 def grant(megabytes):
     return pltpu.CompilerParams(vmem_limit_bytes=megabytes * 1024 * 1024)
 
@@ -188,51 +200,34 @@
     return values + [single] * 2
 
 
-def row_lse_kernel(e_ref, p_ref, copies_ref, s_ref, top_ref, mass_ref, lse_ref):
+def row_lse_kernel(e_ref, p_ref, copies_ref, turned_ref, top_ref, mass_ref):
     step = pl.program_id(0)
-    _, rows, width = s_ref.shape
-    low = -1e30
+    width = p_ref.shape[0]
+    _, rows = top_ref.shape
 
     @pl.when(step == 0)
     def _():
-        top_ref[...] = jnp.full_like(top_ref, low)
-        s_ref[...] = jnp.full_like(s_ref, low)
+        turned_ref[...] = e_ref[...].T
+        top_ref[...] = jnp.full_like(top_ref, -1e30)
         mass_ref[...] = jnp.zeros_like(mass_ref)
 
-    def scores(k):
-        top = top_ref[k]
-        for at in chunks(width, 2 * lanes):
-            t = dot_nt(e_ref[...], p_ref[k * width + at.start : k * width + at.stop, :]) * to_base2
-            s_ref[k, :, at] = t
-            top = jnp.maximum(top, jnp.maximum(t[:, :lanes], t[:, lanes:]))
-        mass_ref[k] = mass_ref[k] * jnp.exp2(top_ref[k] - top)
-        top_ref[k] = top
-
-    def masses(k):
-        for g in range(rows // sublanes):
-            at = slice(g * sublanes, (g + 1) * sublanes)
-            top = top_ref[k, at, :]
-            mass = mass_ref[k, at, :]
-            for c in chunks(width):
-                mass = mass + jnp.exp2(s_ref[k, at, c] - top)
-            mass_ref[k, at, :] = mass
-
-    scores(0)
-    masses(1)
-    scores(1)
-    masses(0)
+    top, mass = top_ref[...], mass_ref[...]
+    for at in chunks(width, 2 * lanes):
+        t = dot_nn(p_ref[at, :], turned_ref[...]) * to_base2
+        t = t.reshape(t.shape[0] // sublanes, sublanes, rows)
+        new = jnp.maximum(top, jnp.max(t, axis=0))
+        mass = mass * jnp.exp2(top - new) + jnp.sum(jnp.exp2(t - new[None]), axis=0)
+        top = new
+    top_ref[...] = top
+    mass_ref[...] = mass
 
     @pl.when(step == pl.num_programs(0) - 1)
     def _():
-        masses(1)
-        top = jnp.maximum(top_ref[0], top_ref[1])
-        mass = mass_ref[0] * jnp.exp2(top_ref[0] - top) + mass_ref[1] * jnp.exp2(top_ref[1] - top)
-        peak = lane_total(top, jnp.max)
-        mass = lane_total(mass * jnp.exp2(top - peak), jnp.sum)
-        top_ref[0] = peak + jnp.log2(mass)
-        rows_to_lanes(top_ref.at[0], lse_ref)
+        peak = jnp.max(top, axis=0, keepdims=True)
+        total = jnp.sum(mass * jnp.exp2(top - peak), axis=0, keepdims=True)
+        lse = peak + jnp.log2(total)
         for d in range(copies_ref.shape[0]):
-            copies_ref[d] = lse_ref[...]
+            copies_ref[d] = lse
 
 
 def row_lse(embeddings, prototypes, copies):
@@ -249,17 +244,16 @@
         out_specs=pl.BlockSpec((copies, 1, rows), lambda s: (0, 0, 0)),
         out_shape=jax.ShapeDtypeStruct((copies, 1, rows), f32),
         scratch_shapes=[
-            pltpu.VMEM((2, rows, width // 2), f32),
-            pltpu.VMEM((2, rows, lanes), f32),
-            pltpu.VMEM((2, rows, lanes), f32),
-            pltpu.VMEM((1, rows), f32),
+            pltpu.VMEM((depth, rows), bf16),
+            pltpu.VMEM((sublanes, rows), f32),
+            pltpu.VMEM((sublanes, rows), f32),
         ],
         compiler_params=beside_plan,
         cost_estimate=pl.CostEstimate(
             flops=2 * rows * count * depth, bytes_accessed=count * depth * 2, transcendentals=rows * count
         ),
         name="row_lse",
-    )(embeddings, pltpu.with_memory_space_constraint(prototypes, pltpu.HBM))
+    )(embeddings, in_hbm(prototypes))
 
 
 def col_softmax_kernel(
@@ -278,6 +272,7 @@
     a_ref,
     h_ref,
     cot_tall_ref,
+    turned_ref,
     t_ref,
     acc_ref,
     part_ref,
@@ -301,6 +296,9 @@
     lanes_to_rows(cot_ref[...], cot_tall_ref)
     for move in moves:
         move.wait()
+    for d in range(members):
+        at = slice(d * held, (d + 1) * held)
+        turned_ref[:, at] = all_ref[at, :].T
 
     height = t_ref.shape[1]
     blocks = count // height
@@ -309,7 +307,7 @@
         p = p_ref[pl.ds(pl.multiple_of(block * height, height), height), :]
         part = None
         for c in chunks(rows, 2 * lanes):
-            t = dot_nt(p, all_ref[c, :]) * to_base2 + f_ref[:, c]
+            t = dot_nn(p, turned_ref[:, c]) * to_base2 + f_ref[:, c]
             t_ref[slot, :, c] = t
             here = jnp.maximum(t[:, :lanes], t[:, lanes:])
             part = here if part is None else jnp.maximum(part, here)
@@ -363,33 +361,34 @@
         in_specs=[in_smem, whole, anywhere, anywhere, whole, whole],
         out_specs=[whole] * 8,
         out_shape=[
-            jax.ShapeDtypeStruct((count, rows), f32),
+            held((count, rows)),
             jax.ShapeDtypeStruct((1, rows), f32),
             jax.ShapeDtypeStruct((1, count), f32),
             jax.ShapeDtypeStruct((1, rows), f32),
-            jax.ShapeDtypeStruct((rows, depth), bf16),
-            jax.ShapeDtypeStruct((count, lanes), f32),
-            jax.ShapeDtypeStruct((count, lanes), f32),
-            jax.ShapeDtypeStruct((count, lanes), f32),
+            held((rows, depth), bf16),
+            held((count, lanes)),
+            held((count, lanes)),
+            held((count, lanes)),
         ],
         scratch_shapes=[
+            pltpu.VMEM((depth, rows), bf16),
             pltpu.VMEM((2, height, rows), f32),
             pltpu.VMEM((sublanes, rows), f32),
             pltpu.VMEM((count, lanes), f32),
             pltpu.SemaphoreType.DMA((2 * members,)),
         ],
-        compiler_params=beside_plan,
+        compiler_params=beside_plan if rows <= 4096 else grant(36),
         cost_estimate=pl.CostEstimate(
             flops=2 * rows * count * depth, bytes_accessed=count * rows * 4, transcendentals=rows * count
         ),
         name="col_softmax",
-    )(me, lse, mine, other, prototypes, col_cot)
+    )(me, lse, in_hbm(mine), in_hbm(other), prototypes, col_cot)
 
 
 def second_pair_kernel(pieces, me_ref, *refs):
     rho_refs = refs[:pieces]
     row_cot_ref, cot_ref, a_ref, e_ref, out_ref, r_ref, ratio_ref, z_ref, weight_ref, acc_ref, part_ref = refs[pieces:]
-    held = row_cot_ref.shape[1]
+    own = row_cot_ref.shape[1]
     r_ref[...] = 1.0 / tree(add, [ref[...] for ref in rho_refs])
     weight_ref[...] = jnp.broadcast_to(r_ref[...], weight_ref.shape)
     weighted(e_ref, weight_ref, part_ref)
@@ -398,7 +397,7 @@
     part_ref[...] = z_ref[...] / a_ref[...]
     rows_to_lanes(part_ref, ratio_ref)
     out_ref[...] = -r_ref[...] * jnp.sum(acc_ref[...], axis=0, keepdims=True)
-    mine = pl.ds(pl.multiple_of(me_ref[0] * held, held), held)
+    mine = pl.ds(pl.multiple_of(me_ref[0] * own, own), own)
     out_ref[:, mine] += jnp.where(me_ref[2] == 0, row_cot_ref[...], 0.0)
 
 
@@ -412,7 +411,7 @@
             jax.ShapeDtypeStruct((1, rows), f32),
             jax.ShapeDtypeStruct((1, rows), f32),
             jax.ShapeDtypeStruct((1, count), f32),
-            jax.ShapeDtypeStruct((count, lanes), f32),
+            held((count, lanes)),
         ],
         scratch_shapes=[
             pltpu.VMEM((sublanes, rows), f32),
@@ -424,7 +423,7 @@
             flops=4 * rows * count, bytes_accessed=count * rows * 4, transcendentals=0
         ),
         name="second_pair",
-    )(me, *rho_pieces, row_cot, cot, a, e)
+    )(me, *rho_pieces, row_cot, in_vmem(cot), in_vmem(a), in_vmem(e))
 
 
 def first_pair_kernel(bar_ref, r_ref, a_ref, e_ref, out_ref, v_ref, y_ref, ay_ref, weight_ref, acc_ref, part_ref):
@@ -448,7 +447,7 @@
             jax.ShapeDtypeStruct((1, rows), f32),
             jax.ShapeDtypeStruct((1, rows), f32),
             jax.ShapeDtypeStruct((1, count), f32),
-            jax.ShapeDtypeStruct((count, lanes), f32),
+            held((count, lanes)),
         ],
         scratch_shapes=[
             pltpu.VMEM((sublanes, rows), f32),
@@ -460,7 +459,7 @@
             flops=4 * rows * count, bytes_accessed=count * rows * 4, transcendentals=0
         ),
         name="first_pair",
-    )(bar, r, a, e)
+    )(bar, r, in_vmem(a), in_vmem(e))
 
 
 def embed_kernel(
@@ -535,7 +534,7 @@
             flops=4 * rows * count * depth, bytes_accessed=count * depth * 2, transcendentals=rows * count
         ),
         name="embed_part",
-    )(me, last, f, r, v, embeddings, pltpu.with_memory_space_constraint(prototypes, pltpu.HBM))
+    )(me, last, f, r, v, embeddings, in_hbm(prototypes))
 
 
 def proto_kernel(last_ref, r_ref, v_ref, a_ref, h_ref, z_ref, ay_ref, all_ref, e_ref, out_ref, right_ref, b_ref):
@@ -588,7 +587,7 @@
             flops=2 * rows * count * depth, bytes_accessed=count * rows * 4, transcendentals=0
         ),
         name="proto_part",
-    )(last, r, v, a, h, z, ay, all_rows, e)
+    )(last, r, v, *map(in_vmem, (a, h, z, ay, all_rows, e)))
 
 
 def shards(embeddings, prototypes, row_cot, col_cot):
@@ -597,17 +596,15 @@
     count = prototypes.shape[0] // batch
     member, holder = lax.axis_index("batch"), lax.axis_index("proto")
     me = jnp.stack([member, holder % 2, holder]).astype(jnp.int32)
-    own = lax.dynamic_slice_in_dim(prototypes, member * count, count, axis=0)
-    own_cot = lax.dynamic_slice_in_dim(col_cot, member * count, count, axis=0)[None, :]
 
     half = lax.dynamic_slice_in_dim(embeddings, (holder % 2) * (held // 2), held // 2, axis=0)
     copies = jnp.broadcast_to(half[None], (batch,) + half.shape)
-    copies, me, own, own_cot, row_cot, embeddings = lax.optimization_barrier(
-        (copies, me, own, own_cot, row_cot, embeddings)
-    )
+    copies, late_prototypes, late_cot = lax.optimization_barrier((copies, prototypes, col_cot))
+    own = lax.dynamic_slice_in_dim(late_prototypes, member * count, count, axis=0)
+    own_cot = lax.dynamic_slice_in_dim(late_cot, member * count, count, axis=0)[None, :]
     mine = swap_copies(copies, "batch")
     lse = row_lse(embeddings, prototypes, batch * proto)
-    mine, lse = lax.optimization_barrier((mine, lse))
+    mine, lse, own, own_cot, me = lax.optimization_barrier((mine, lse, own, own_cot, me))
     other = lax.ppermute(mine, "proto", [(i, i ^ 1) for i in range(proto)])
     lse = swap_copies(lse, both)
     e, rho, col_lse, f, all_rows, a, h, cot = col_softmax(me, lse, mine, other, own, own_cot)

time: 142 us -> 125 us (0.88)
  local copies, waits for them, and re-layouts: 21.4 us -> 7.78 us
  waiting for transfers between devices: 18.1 us -> 15.5 us
    unnamed x32 -> x12, local copies, waits for them, and re-layouts: 17.5 us -> 2.95 us
    all_to_all x1, waiting for transfers between devices: 4.46 us -> 1.67 us  [swap_copies(): return lax.all_to_all(copies, axis, split_axis=0, concat_axis=0, tiled=True)]
  transfers between devices with their start and end apart: 18 -> 18, of which waited for: 11 -> 11; matrix products, arithmetic and copies ran while one was open for 0% -> 2% of each run, Pallas kernels for 12% -> 13%
where the time goes in v1:
time: 125 us; the launch traced here: 124 us
  Pallas kernels  44.9 us (36%)
  blocking collectives  34.1 us (27%)
  starting transfers between devices  20.1 us (16%)
  waiting for transfers between devices  15.5 us (12%)
  local copies, waits for them, and re-layouts  7.78 us (6%)
    all_to_all x3, blocking collectives, swap_copies(): return lax.all_to_all(copies, axis, split_axis=0, concat_axis=0, tiled=True)  34.1 us
    ppermute x16, waiting for transfers between devices, partners(): lax.ppermute(x, axis, [(i, i ^ d * stride) for i in range(total)])  13.8 us
    ppermute x16, starting transfers between devices, partners(): lax.ppermute(x, axis, [(i, i ^ d * stride) for i in range(total)])  12.9 us
    pallas_call x1, Pallas kernels, embed_part(): pl.pallas_call(functools.partial(embed_kernel, total), grid_spec=pltpu.Pr...  11.2 us
    pallas_call x1, Pallas kernels, col_softmax(): pl.pallas_call(functools.partial(col_softmax_kernel, devices // members),...  10.4 us
    pallas_call x1, Pallas kernels, row_lse(): pl.pallas_call(row_lse_kernel, grid=(count // width,), in_specs=[pl.Block...  8.86 us
    all_to_all x1, starting transfers between devices, swap_copies(): return lax.all_to_all(copies, axis, split_axis=0, concat_axis=0, tiled=True)  7.25 us
    pallas_call x1, Pallas kernels, proto_part(): pl.pallas_call(proto_kernel, in_specs=[whole] * 9, out_specs=whole, out_s...  7.17 us
  transfers between devices with their start and end apart: 18, of which 11 were waited for; matrix products, arithmetic and copies ran while one was open for 2% of the time, Pallas kernels for 13%

profile of v1, /device:TPU:0, one launch (start us, length us, event | category | flops | bytes accessed | tf_op | source)
XLA Modules:
  0.0 124.1 jit_solution(13438095832872814866)
XLA Ops:
  0.6 0.8 constant_dynamic-slice_fusion.1
  1.5 0.8 broadcast_in_dim.28
  2.3 7.3 %all-to-all-start = ((bf16[8,128,256]{2,1,0:T(8,128)(2,1)}), bf16[8,128,256]{2,1,0:T(8,128)(2,1)S(1)}, u32[]{:S(2)}, u32[]{:S(2)}) async-start(bf16[8,128,256]{2,1,0:T(8,128)(2,1)} %broadcast_in_dim.28), calls=%async_computation | async-start | bytes 1048576 | tf_op jit(solution)/shard_map/all_to_all | solution.py:79
  9.6 0.7 dynamic_slice.11
  10.3 0.1 pad_add_fusion.me_ref
  10.4 0.9 copy-done.1
  11.3 8.9 %row_lse.1 = f32[32,1,256]{2,1,0:T(1,128)S(1)} custom-call(bf16[256,256]{1,0:T(8,128)(2,1)S(1)} %copy-done.1, bf16[16384,256]{1,0:T(8,128)(2,1)} %p_ref.3), custom_call_target="tpu_custom_call" | custom-call | flops 2147483648 | bytes 8388608 | tf_op jit(solution)/shard_map/row_lse/pallas_call | solution.py:237
  20.1 2.3 %constant_dynamic-slice_fusion.p_ref = bf16[2048,256]{1,0:T(8,128)(2,1)} fusion(bf16[16384,256]{1,0:T(8,128)(2,1)} %p_ref.3, s32[]{:T(128)S(6)} %select_n.18), kind=kLoop, calls=%fused_computation.6 | loop fusion | bytes 2097156 | tf_op jit(solution)/shard_map/dynamic_slice | solution.py:603
  22.4 1.7 %all-to-all-done.mine_ref = bf16[8,128,256]{2,1,0:T(8,128)(2,1)S(1)} async-done(((bf16[8,128,256]{2,1,0:T(8,128)(2,1)}), bf16[8,128,256]{2,1,0:T(8,128)(2,1)S(1)}, u32[]{:S(2)}, u32[]{:S(2)}) %all-to-all-start) | async-done | bytes 524320 | tf_op jit(solution)/shard_map/all_to_all | solution.py:79
  24.1 0.0 collective-permute-start
  24.1 11.5 %all_to_all.20.lse_ref = f32[32,1,256]{2,1,0:T(1,128)S(1)} all-to-all(f32[32,1,256]{2,1,0:T(1,128)S(1)} %row_lse.1), channel_id=1, replica_groups=mesh['batch'=8,'proto'=4] {'batch','proto'}, dimensions={0} | all-to-all | bytes 65536 | tf_op jit(solution)/shard_map/all_to_all | solution.py:79
  35.6 0.8 copy-done.5
  36.4 1.2 copy-done
  37.7 10.4 %col_softmax.1 = (f32[2048,2048]{1,0:T(8,128)S(1)}, f32[1,2048]{1,0:T(1,128)S(1)}, f32[1,2048]{1,0:T(1,128)S(1)}, f32[1,2048]{1,0:T(1,128)S(1)}, bf16[2048,256]{...) custom-call(s32[3]{0:T(128)S(1)} %pad_add_fusion.me_ref, ...), custom_call_target="tpu_custom_call" | custom-call | flops 2147483648 | bytes 16777216 | tf_op jit(solution)/shard_map/col_softmax/pallas_call | solution.py:359
  48.1 0.3 collective-permute-start.3
  48.4 1.5 %collective-permute-start.2 = (f32[1,2048]{1,0:T(1,128)S(1)}, f32[1,2048]{1,0:T(1,128)S(1)}, u32[]{:S(2)}, u32[]{:S(2)}) collective-permute-start(f32[1,2048]{1,0:T(1,128)S(1)} %get-tuple-element.34), channel_id=1, source_target_pairs={{0,2},{1,3},{2,0},{3,1},{4,6},{5,7},{6,4},{7,5},{8,10},{9,11},{10,... | collective-permute-start | bytes 24584 | tf_op jit(solution)/shard_map/ppermute | solution.py:64
  49.9 0.1 collective-permute-start.1
  50.1 1.2 collective-permute-done.3
  51.2 0.8 collective-permute-done.2
  52.1 0.7 collective-permute-start.4
  52.8 3.0 %collective-permute-done.4 = f32[1,2048]{1,0:T(1,128)S(1)} collective-permute-done((f32[1,2048]{1,0:T(1,128)S(1)}, f32[1,2048]{1,0:T(1,128)S(1)}, u32[]{:S(2)}, u32[]{:S(2)}) %collective-permute-start.4) | collective-permute-done | bytes 8224 | tf_op jit(solution)/shard_map/ppermute | solution.py:64
  55.8 0.7 collective-permute-start.7
  56.5 1.4 %collective-permute-start.6 = (f32[1,2048]{1,0:T(1,128)S(1)}, f32[1,2048]{1,0:T(1,128)S(1)}, u32[]{:S(2)}, u32[]{:S(2)}) collective-permute-start(f32[1,2048]{1,0:T(1,128)S(1)} %add.57.refs_0_), channel_id=1, source_target_pairs={{0,16},{4,20},{8,24},{12,28},{16,0},{20,4},{24,8},{28,12},{1,17},{... | collective-permute-start | bytes 24584 | tf_op jit(solution)/shard_map/ppermute | solution.py:64
  57.9 2.3 %collective-permute-start.5 = (f32[1,2048]{1,0:T(1,128)S(1)}, f32[1,2048]{1,0:T(1,128)S(1)}, u32[]{:S(2)}, u32[]{:S(2)}) collective-permute-start(f32[1,2048]{1,0:T(1,128)S(1)} %add.57.refs_0_), channel_id=1, source_target_pairs={{0,8},{4,12},{8,0},{12,4},{16,24},{20,28},{24,16},{28,20},{1,9},{5... | collective-permute-start | bytes 24584 | tf_op jit(solution)/shard_map/ppermute | solution.py:64
  60.3 1.1 collective-permute-done.7.refs_3_
  61.3 0.6 collective-permute-done.5.refs_1_
  61.9 4.0 %second_pair.1 = (f32[1,2048]{1,0:T(1,128)S(1)}, f32[1,2048]{1,0:T(1,128)S(1)}, f32[1,2048]{1,0:T(1,128)S(1)}, f32[2048,128]{1,0:T(8,128)S(1)}) custom-call(s32[3]{0:T(128)S(1)} %pad_add_fusion.me_ref, f32[1,2048]{1,0:T(1,128)S(1)} %add.57.refs_0_, f32[1,2048]{1,0:T(1,128)S(1)} %collective-permute-done.5.refs_1_, ...), custom_call_target="tpu_custom_call" | custom-call | flops 16777216 | bytes 16777216 | tf_op jit(solution)/shard_map/second_pair/pallas_call | solution.py:406
  65.9 0.1 collective-permute-start.10
  66.0 1.6 %collective-permute-start.9 = (f32[1,2048]{1,0:T(1,128)S(1)}, f32[1,2048]{1,0:T(1,128)S(1)}, u32[]{:S(2)}, u32[]{:S(2)}) collective-permute-start(f32[1,2048]{1,0:T(1,128)S(1)} %get-tuple-element.38), channel_id=1, source_target_pairs={{0,2},{1,3},{2,0},{3,1},{4,6},{5,7},{6,4},{7,5},{8,10},{9,11},{10,... | collective-permute-start | bytes 24584 | tf_op jit(solution)/shard_map/ppermute | solution.py:64
  67.6 0.3 collective-permute-start.8
  67.8 1.2 collective-permute-done.10
  69.1 0.6 collective-permute-done.9
  69.8 10.4 %all_to_all.21.bar_ref = f32[8,1,2048]{2,1,0:T(1,128)S(1)} all-to-all(f32[8,1,2048]{2,1,0:T(1,128)S(1)} %broadcast_in_dim.32), channel_id=1, replica_groups=mesh['batch'=8,'proto'=4] {'batch'}, dimensions={0} | all-to-all | bytes 131072 | tf_op jit(solution)/shard_map/all_to_all | solution.py:79
  80.2 3.3 %first_pair.1 = (f32[1,2048]{1,0:T(1,128)S(1)}, f32[1,2048]{1,0:T(1,128)S(1)}, f32[1,2048]{1,0:T(1,128)S(1)}, f32[2048,128]{1,0:T(8,128)S(1)}) custom-call(f32[8,1,2048]{2,1,0:T(1,128)S(1)} %all_to_all.21.bar_ref, f32[1,2048]{1,0:T(1,128)S(1)} %get-tuple-element.39.r_ref, f32[2048,128]{1,0:T(8,128)S(1)} %get-tuple-element.36.refs_6_.a_ref, ...), custom_call_target="tpu_custom_call" | custom-call | flops 16777216 | bytes 16777216 | tf_op jit(solution)/shard_map/first_pair/pallas_call | solution.py:442
  83.4 0.1 collective-permute-start.13
  83.5 1.5 %collective-permute-start.12 = (f32[1,2048]{1,0:T(1,128)S(1)}, f32[1,2048]{1,0:T(1,128)S(1)}, u32[]{:S(2)}, u32[]{:S(2)}) collective-permute-start(f32[1,2048]{1,0:T(1,128)S(1)} %get-tuple-element.40), channel_id=1, source_target_pairs={{0,2},{1,3},{2,0},{3,1},{4,6},{5,7},{6,4},{7,5},{8,10},{9,11},{10,... | collective-permute-start | bytes 24584 | tf_op jit(solution)/shard_map/ppermute | solution.py:64
  85.1 0.3 collective-permute-start.11
  85.4 1.3 %collective-permute-done.13 = f32[1,2048]{1,0:T(1,128)S(1)} collective-permute-done((f32[1,2048]{1,0:T(1,128)S(1)}, f32[1,2048]{1,0:T(1,128)S(1)}, u32[]{:S(2)}, u32[]{:S(2)}) %collective-permute-start.13) | collective-permute-done | bytes 8224 | tf_op jit(solution)/shard_map/ppermute | solution.py:64
  86.6 0.6 collective-permute-done.12
  87.3 0.1 broadcast_in_dim.34
  87.4 12.1 %all_to_all.22.last_ref = f32[8,1,8192]{2,1,0:T(1,128)S(1)} all-to-all(f32[8,1,8192]{2,1,0:T(1,128)S(1)} %broadcast_in_dim.34), channel_id=1, replica_groups=mesh['batch'=8,'proto'=4] {'batch'}, dimensions={0} | all-to-all | bytes 524288 | tf_op jit(solution)/shard_map/all_to_all | solution.py:79
  99.6 11.2 %embed_part.1 = f32[256,256]{1,0:T(8,128)S(1)} custom-call(s32[3]{0:T(128)S(1)} %pad_add_fusion.me_ref, f32[8,1,8192]{2,1,0:T(1,128)S(1)} %all_to_all.22.last_ref, f32[1,2048]{1,0:T(1,128)S(1)} %get-tuple-element.44.f_ref, f32[1,2048]{1,0:T(1,128)S(1)} %get-tuple-element.39.r_ref, f32[1,2048]{1,0:T(1,128)S(1)} %get-tuple-element.45.v_ref, ...), custom_call_target="tpu_custom_call" | custom-call | flops 4294967296 | bytes 8388608 | tf_op jit(solution)/shard_map/embed_part/pallas_call | solution.py:510
  110.8 0.1 collective-permute-start.16
  110.9 0.6 collective-permute-start.15
  111.5 1.2 collective-permute-start.14
  112.7 7.2 %proto_part.1 = f32[2048,256]{1,0:T(8,128)} custom-call(f32[8,1,8192]{2,1,0:T(1,128)S(1)} %all_to_all.22.last_ref, f32[1,2048]{1,0:T(1,128)S(1)} %get-tuple-element.39.r_ref, f32[1,2048]{1,0:T(1,128)S(1)} %get-tuple-element.45.v_ref, f32[2048,128]{1,0:T(8,128)S(1)} %get-tuple-element.36.refs_6_.a_ref, f32[2048,128]{1,0:T(8,128)S(1)} %get-tuple-element.46.h_ref, ...), custom_call_target="tpu_custom_call" | custom-call | flops 2147483648 | bytes 16777216 | tf_op jit(solution)/shard_map/proto_part/pallas_call | solution.py:579
  119.9 3.5 %collective-permute-done.15 = f32[256,256]{1,0:T(8,128)S(1)} collective-permute-done((f32[256,256]{1,0:T(8,128)S(1)}, f32[256,256]{1,0:T(8,128)S(1)}, u32[]{:S(2)}, u32[]{:S(2)}) %collective-permute-start.15) | collective-permute-done | bytes 262176 | tf_op jit(solution)/shard_map/ppermute | solution.py:64
  123.4 0.8 add_add_fusion
  (22 shorter events, 0.2 us)
Async XLA Ops:
  2.3 21.7 %all-to-all-start = ((bf16[8,128,256]{2,1,0:T(8,128)(2,1)}), bf16[8,128,256]{2,1,0:T(8,128)(2,1)S(1)}, u32[]{:S(2)}, u32[]{:S(2)}) async-start(bf16[8,128,256]{2,1,0:T(8,128)(2,1)} %broadcast_in_dim.28), calls=%async_computation | async-start | bytes 1048576 | tf_op jit(solution)/shard_map/all_to_all | solution.py:79
  10.4 0.9 copy-start.1
  11.3 50.6 %copy-start.3 = (f32[256]{0:T(256)S(1)}, f32[256]{0:T(256)}, u32[]{:S(2)}) copy-start(f32[256]{0:T(256)} %param.6) | copy-start | bytes 3076
  24.1 11.5 %copy-start.4 = (bf16[8,128,256]{2,1,0:T(8,128)(2,1)}, bf16[8,128,256]{2,1,0:T(8,128)(2,1)S(1)}, u32[]{:S(2)}) copy-start(bf16[8,128,256]{2,1,0:T(8,128)(2,1)S(1)} %all-to-all-done.mine_ref) | copy-start | bytes 1572868
  24.1 11.5 %collective-permute-start = (bf16[8,128,256]{2,1,0:T(8,128)(2,1)S(1)}, bf16[8,128,256]{2,1,0:T(8,128)(2,1)S(1)}, u32[]{:S(2)}, u32[]{:S(2)}) collective-permute-start(bf16[8,128,256]{2,1,0:T(8,128)(2,1)S(1)} %all-to-all-done.mine_ref), channel_id=1, source_target_pairs={{0,1},{1,0},{2,3},{3,2},{4,5},{5,4},{6,7},{7,6},{8,9},{9,8},{10,11... | collective-permute-start | bytes 1572872 | tf_op jit(solution)/shard_map/ppermute | solution.py:608
  35.6 0.8 copy-start.5
  36.4 1.2 copy-start
  48.1 3.1 %collective-permute-start.3 = (f32[1,2048]{1,0:T(1,128)S(1)}, f32[1,2048]{1,0:T(1,128)S(1)}, u32[]{:S(2)}, u32[]{:S(2)}) collective-permute-start(f32[1,2048]{1,0:T(1,128)S(1)} %get-tuple-element.34), channel_id=1, source_target_pairs={{0,3},{1,2},{2,1},{3,0},{4,7},{5,6},{6,5},{7,4},{8,11},{9,10},{10,... | collective-permute-start | bytes 24584 | tf_op jit(solution)/shard_map/ppermute | solution.py:64
  48.4 3.7 %collective-permute-start.2 = (f32[1,2048]{1,0:T(1,128)S(1)}, f32[1,2048]{1,0:T(1,128)S(1)}, u32[]{:S(2)}, u32[]{:S(2)}) collective-permute-start(f32[1,2048]{1,0:T(1,128)S(1)} %get-tuple-element.34), channel_id=1, source_target_pairs={{0,2},{1,3},{2,0},{3,1},{4,6},{5,7},{6,4},{7,5},{8,10},{9,11},{10,... | collective-permute-start | bytes 24584 | tf_op jit(solution)/shard_map/ppermute | solution.py:64
  49.9 2.1 %collective-permute-start.1 = (f32[1,2048]{1,0:T(1,128)S(1)}, f32[1,2048]{1,0:T(1,128)S(1)}, u32[]{:S(2)}, u32[]{:S(2)}) collective-permute-start(f32[1,2048]{1,0:T(1,128)S(1)} %get-tuple-element.34), channel_id=1, source_target_pairs={{0,1},{1,0},{2,3},{3,2},{4,5},{5,4},{6,7},{7,6},{8,9},{9,8},{10,11... | collective-permute-start | bytes 24584 | tf_op jit(solution)/shard_map/ppermute | solution.py:64
  52.1 3.7 %collective-permute-start.4 = (f32[1,2048]{1,0:T(1,128)S(1)}, f32[1,2048]{1,0:T(1,128)S(1)}, u32[]{:S(2)}, u32[]{:S(2)}) collective-permute-start(f32[1,2048]{1,0:T(1,128)S(1)} %add_add_fusion.3), channel_id=1, source_target_pairs={{0,4},{4,0},{8,12},{12,8},{16,20},{20,16},{24,28},{28,24},{1,5},{5... | collective-permute-start | bytes 24584 | tf_op jit(solution)/shard_map/ppermute | solution.py:64
  55.8 5.5 %collective-permute-start.7 = (f32[1,2048]{1,0:T(1,128)S(1)}, f32[1,2048]{1,0:T(1,128)S(1)}, u32[]{:S(2)}, u32[]{:S(2)}) collective-permute-start(f32[1,2048]{1,0:T(1,128)S(1)} %add.57.refs_0_), channel_id=1, source_target_pairs={{0,24},{4,28},{8,16},{12,20},{16,8},{20,12},{24,0},{28,4},{1,25},{... | collective-permute-start | bytes 24584 | tf_op jit(solution)/shard_map/ppermute | solution.py:64
  56.5 4.8 %collective-permute-start.6 = (f32[1,2048]{1,0:T(1,128)S(1)}, f32[1,2048]{1,0:T(1,128)S(1)}, u32[]{:S(2)}, u32[]{:S(2)}) collective-permute-start(f32[1,2048]{1,0:T(1,128)S(1)} %add.57.refs_0_), channel_id=1, source_target_pairs={{0,16},{4,20},{8,24},{12,28},{16,0},{20,4},{24,8},{28,12},{1,17},{... | collective-permute-start | bytes 24584 | tf_op jit(solution)/shard_map/ppermute | solution.py:64
  57.9 4.0 %collective-permute-start.5 = (f32[1,2048]{1,0:T(1,128)S(1)}, f32[1,2048]{1,0:T(1,128)S(1)}, u32[]{:S(2)}, u32[]{:S(2)}) collective-permute-start(f32[1,2048]{1,0:T(1,128)S(1)} %add.57.refs_0_), channel_id=1, source_target_pairs={{0,8},{4,12},{8,0},{12,4},{16,24},{20,28},{24,16},{28,20},{1,9},{5... | collective-permute-start | bytes 24584 | tf_op jit(solution)/shard_map/ppermute | solution.py:64
  65.9 3.1 %collective-permute-start.10 = (f32[1,2048]{1,0:T(1,128)S(1)}, f32[1,2048]{1,0:T(1,128)S(1)}, u32[]{:S(2)}, u32[]{:S(2)}) collective-permute-start(f32[1,2048]{1,0:T(1,128)S(1)} %get-tuple-element.38), channel_id=1, source_target_pairs={{0,3},{1,2},{2,1},{3,0},{4,7},{5,6},{6,5},{7,4},{8,11},{9,10},{10,... | collective-permute-start | bytes 24584 | tf_op jit(solution)/shard_map/ppermute | solution.py:64
  66.0 3.7 %collective-permute-start.9 = (f32[1,2048]{1,0:T(1,128)S(1)}, f32[1,2048]{1,0:T(1,128)S(1)}, u32[]{:S(2)}, u32[]{:S(2)}) collective-permute-start(f32[1,2048]{1,0:T(1,128)S(1)} %get-tuple-element.38), channel_id=1, source_target_pairs={{0,2},{1,3},{2,0},{3,1},{4,6},{5,7},{6,4},{7,5},{8,10},{9,11},{10,... | collective-permute-start | bytes 24584 | tf_op jit(solution)/shard_map/ppermute | solution.py:64
  67.6 2.1 %collective-permute-start.8 = (f32[1,2048]{1,0:T(1,128)S(1)}, f32[1,2048]{1,0:T(1,128)S(1)}, u32[]{:S(2)}, u32[]{:S(2)}) collective-permute-start(f32[1,2048]{1,0:T(1,128)S(1)} %get-tuple-element.38), channel_id=1, source_target_pairs={{0,1},{1,0},{2,3},{3,2},{4,5},{5,4},{6,7},{7,6},{8,9},{9,8},{10,11... | collective-permute-start | bytes 24584 | tf_op jit(solution)/shard_map/ppermute | solution.py:64
  80.2 19.4 %copy-start.2 = (bf16[256,256]{1,0:T(8,128)(2,1)S(1)}, bf16[256,256]{1,0:T(8,128)(2,1)}, u32[]{:S(2)}) copy-start(bf16[256,256]{1,0:T(8,128)(2,1)} %e_ref.3) | copy-start | bytes 393220
  83.4 3.2 %collective-permute-start.13 = (f32[1,2048]{1,0:T(1,128)S(1)}, f32[1,2048]{1,0:T(1,128)S(1)}, u32[]{:S(2)}, u32[]{:S(2)}) collective-permute-start(f32[1,2048]{1,0:T(1,128)S(1)} %get-tuple-element.40), channel_id=1, source_target_pairs={{0,3},{1,2},{2,1},{3,0},{4,7},{5,6},{6,5},{7,4},{8,11},{9,10},{10,... | collective-permute-start | bytes 24584 | tf_op jit(solution)/shard_map/ppermute | solution.py:64
  83.5 3.7 %collective-permute-start.12 = (f32[1,2048]{1,0:T(1,128)S(1)}, f32[1,2048]{1,0:T(1,128)S(1)}, u32[]{:S(2)}, u32[]{:S(2)}) collective-permute-start(f32[1,2048]{1,0:T(1,128)S(1)} %get-tuple-element.40), channel_id=1, source_target_pairs={{0,2},{1,3},{2,0},{3,1},{4,6},{5,7},{6,4},{7,5},{8,10},{9,11},{10,... | collective-permute-start | bytes 24584 | tf_op jit(solution)/shard_map/ppermute | solution.py:64
  85.1 2.2 %collective-permute-start.11 = (f32[1,2048]{1,0:T(1,128)S(1)}, f32[1,2048]{1,0:T(1,128)S(1)}, u32[]{:S(2)}, u32[]{:S(2)}) collective-permute-start(f32[1,2048]{1,0:T(1,128)S(1)} %get-tuple-element.40), channel_id=1, source_target_pairs={{0,1},{1,0},{2,3},{3,2},{4,5},{5,4},{6,7},{7,6},{8,9},{9,8},{10,11... | collective-permute-start | bytes 24584 | tf_op jit(solution)/shard_map/ppermute | solution.py:64
  110.8 9.1 %collective-permute-start.16 = (f32[256,256]{1,0:T(8,128)S(1)}, f32[256,256]{1,0:T(8,128)S(1)}, u32[]{:S(2)}, u32[]{:S(2)}) collective-permute-start(f32[256,256]{1,0:T(8,128)S(1)} %embed_part.1), channel_id=1, source_target_pairs={{0,3},{1,2},{2,1},{3,0},{4,7},{5,6},{6,5},{7,4},{8,11},{9,10},{10,... | collective-permute-start | bytes 786440 | tf_op jit(solution)/shard_map/ppermute | solution.py:64
  110.9 12.5 %collective-permute-start.15 = (f32[256,256]{1,0:T(8,128)S(1)}, f32[256,256]{1,0:T(8,128)S(1)}, u32[]{:S(2)}, u32[]{:S(2)}) collective-permute-start(f32[256,256]{1,0:T(8,128)S(1)} %embed_part.1), channel_id=1, source_target_pairs={{0,2},{1,3},{2,0},{3,1},{4,6},{5,7},{6,4},{7,5},{8,10},{9,11},{10,... | collective-permute-start | bytes 786440 | tf_op jit(solution)/shard_map/ppermute | solution.py:64
  111.5 11.9 %collective-permute-start.14 = (f32[256,256]{1,0:T(8,128)S(1)}, f32[256,256]{1,0:T(8,128)S(1)}, u32[]{:S(2)}, u32[]{:S(2)}) collective-permute-start(f32[256,256]{1,0:T(8,128)S(1)} %embed_part.1), channel_id=1, source_target_pairs={{0,1},{1,0},{2,3},{3,2},{4,5},{5,4},{6,7},{7,6},{8,9},{9,8},{10,11... | collective-permute-start | bytes 786440 | tf_op jit(solution)/shard_map/ppermute | solution.py:64

commit v2 on v1

--- a/solution.py
+++ b/solution.py
@@ -21,12 +21,16 @@
 kept_products = ((0, 0), (0, 1), (1, 0))
 
 
-def held(shape, dtype=f32):
-    return pltpu.VMEM(shape, dtype)
-
-
-def in_vmem(x):
-    return pltpu.with_memory_space_constraint(x, pltpu.VMEM)
+def held(shape, dtype=f32, small=True):
+    return pltpu.VMEM(shape, dtype) if small else jax.ShapeDtypeStruct(shape, dtype)
+
+
+def in_vmem(x, small=True):
+    return pltpu.with_memory_space_constraint(x, pltpu.VMEM) if small else x
+
+
+def few(rows):
+    return rows <= 4096
 
 
 def in_hbm(x):
@@ -200,6 +204,25 @@
     return values + [single] * 2
 
 
+def half_copies_kernel(me_ref, e_ref, copies_ref):
+    copies, half, _ = copies_ref.shape
+    value = e_ref[pl.ds(pl.multiple_of(me_ref[1] * half, half), half), :]
+    for d in range(copies):
+        copies_ref[d] = value
+
+
+def half_copies(me, embeddings, copies):
+    rows, depth = embeddings.shape
+    return pl.pallas_call(
+        half_copies_kernel,
+        in_specs=[in_smem, whole],
+        out_specs=whole,
+        out_shape=jax.ShapeDtypeStruct((copies, rows // 2, depth), bf16),
+        compiler_params=beside_plan,
+        name="half_copies",
+    )(me, embeddings)
+
+
 def row_lse_kernel(e_ref, p_ref, copies_ref, turned_ref, top_ref, mass_ref):
     step = pl.program_id(0)
     width = p_ref.shape[0]
@@ -212,7 +235,7 @@
         mass_ref[...] = jnp.zeros_like(mass_ref)
 
     top, mass = top_ref[...], mass_ref[...]
-    for at in chunks(width, 2 * lanes):
+    for at in chunks(width, width // 2):
         t = dot_nn(p_ref[at, :], turned_ref[...]) * to_base2
         t = t.reshape(t.shape[0] // sublanes, sublanes, rows)
         new = jnp.maximum(top, jnp.max(t, axis=0))
@@ -262,8 +285,8 @@
     lse_ref,
     mine_ref,
     other_ref,
-    p_ref,
-    cot_ref,
+    p_all_ref,
+    cot_all_ref,
     e_ref,
     copies_ref,
     col_lse_ref,
@@ -272,6 +295,8 @@
     a_ref,
     h_ref,
     cot_tall_ref,
+    p_ref,
+    cot_ref,
     turned_ref,
     t_ref,
     acc_ref,
@@ -286,6 +311,9 @@
         for d in range(members):
             start = pl.multiple_of(d * held + which * half, half)
             moves.append(pltpu.make_async_copy(ref.at[d], all_ref.at[pl.ds(start, half), :], sem.at[len(moves)]))
+    own = pl.ds(pl.multiple_of(me_ref[0] * count, count), count)
+    moves.append(pltpu.make_async_copy(p_all_ref.at[own, :], p_ref, sem.at[len(moves)]))
+    moves.append(pltpu.make_async_copy(cot_all_ref.at[:, own], cot_ref, sem.at[len(moves)]))
     for move in moves:
         move.start()
     for d in range(members):
@@ -293,9 +321,9 @@
         top = tree(jnp.maximum, pieces)
         mass = tree(add, [jnp.exp2(piece - top) for piece in pieces])
         f_ref[:, d * held : (d + 1) * held] = -math.log2(rows) - (top + jnp.log2(mass))
-    lanes_to_rows(cot_ref[...], cot_tall_ref)
     for move in moves:
         move.wait()
+    lanes_to_rows(cot_ref[...], cot_tall_ref)
     for d in range(members):
         at = slice(d * held, (d + 1) * held)
         turned_ref[:, at] = all_ref[at, :].T
@@ -353,36 +381,39 @@
 def col_softmax(me, lse, mine, other, prototypes, col_cot):
     members, half, depth = mine.shape
     rows = 2 * members * half
-    count = prototypes.shape[0]
+    count = prototypes.shape[0] // members
     devices = lse.shape[0]
-    height = min(count, 2 * lanes) if rows <= 4096 else lanes
+    height = min(count, 4 * lanes) if few(rows) else lanes
+    halves = whole if few(rows) else anywhere
     return pl.pallas_call(
         functools.partial(col_softmax_kernel, devices // members),
-        in_specs=[in_smem, whole, anywhere, anywhere, whole, whole],
+        in_specs=[in_smem, whole, halves, halves, anywhere, anywhere],
         out_specs=[whole] * 8,
         out_shape=[
             held((count, rows)),
             jax.ShapeDtypeStruct((1, rows), f32),
             jax.ShapeDtypeStruct((1, count), f32),
             jax.ShapeDtypeStruct((1, rows), f32),
-            held((rows, depth), bf16),
+            held((rows, depth), bf16, few(rows)),
             held((count, lanes)),
             held((count, lanes)),
             held((count, lanes)),
         ],
         scratch_shapes=[
+            pltpu.VMEM((count, depth), bf16),
+            pltpu.VMEM((1, count), f32),
             pltpu.VMEM((depth, rows), bf16),
             pltpu.VMEM((2, height, rows), f32),
             pltpu.VMEM((sublanes, rows), f32),
             pltpu.VMEM((count, lanes), f32),
-            pltpu.SemaphoreType.DMA((2 * members,)),
-        ],
-        compiler_params=beside_plan if rows <= 4096 else grant(36),
+            pltpu.SemaphoreType.DMA((2 * members + 2,)),
+        ],
+        compiler_params=beside_plan if few(rows) else grant(36),
         cost_estimate=pl.CostEstimate(
             flops=2 * rows * count * depth, bytes_accessed=count * rows * 4, transcendentals=rows * count
         ),
         name="col_softmax",
-    )(me, lse, in_hbm(mine), in_hbm(other), prototypes, col_cot)
+    )(me, lse, in_vmem(mine, few(rows)), in_vmem(other, few(rows)), in_hbm(prototypes), in_hbm(col_cot))
 
 
 def second_pair_kernel(pieces, me_ref, *refs):
@@ -575,7 +606,7 @@
 def proto_part(last, r, v, a, h, z, ay, all_rows, e):
     count, rows = e.shape
     depth = all_rows.shape[1]
-    height = min(count, 2 * lanes)
+    height = min(count, 4 * lanes)
     return pl.pallas_call(
         proto_kernel,
         in_specs=[whole] * 9,
@@ -587,27 +618,20 @@
             flops=2 * rows * count * depth, bytes_accessed=count * rows * 4, transcendentals=0
         ),
         name="proto_part",
-    )(last, r, v, *map(in_vmem, (a, h, z, ay, all_rows, e)))
+    )(last, r, v, *map(in_vmem, (a, h, z, ay)), in_vmem(all_rows, few(rows)), in_vmem(e))
 
 
 def shards(embeddings, prototypes, row_cot, col_cot):
     batch, proto = lax.axis_size("batch"), lax.axis_size("proto")
-    held = embeddings.shape[0]
-    count = prototypes.shape[0] // batch
     member, holder = lax.axis_index("batch"), lax.axis_index("proto")
     me = jnp.stack([member, holder % 2, holder]).astype(jnp.int32)
 
-    half = lax.dynamic_slice_in_dim(embeddings, (holder % 2) * (held // 2), held // 2, axis=0)
-    copies = jnp.broadcast_to(half[None], (batch,) + half.shape)
-    copies, late_prototypes, late_cot = lax.optimization_barrier((copies, prototypes, col_cot))
-    own = lax.dynamic_slice_in_dim(late_prototypes, member * count, count, axis=0)
-    own_cot = lax.dynamic_slice_in_dim(late_cot, member * count, count, axis=0)[None, :]
-    mine = swap_copies(copies, "batch")
+    mine = swap_copies(half_copies(me, embeddings, batch), "batch")
     lse = row_lse(embeddings, prototypes, batch * proto)
-    mine, lse, own, own_cot, me = lax.optimization_barrier((mine, lse, own, own_cot, me))
+    mine, lse = lax.optimization_barrier((mine, lse))
     other = lax.ppermute(mine, "proto", [(i, i ^ 1) for i in range(proto)])
     lse = swap_copies(lse, both)
-    e, rho, col_lse, f, all_rows, a, h, cot = col_softmax(me, lse, mine, other, own, own_cot)
+    e, rho, col_lse, f, all_rows, a, h, cot = col_softmax(me, lse, mine, other, prototypes, col_cot[None, :])
     bar, r, ratio, z = second_pair(me, total_pieces(rho), row_cot[None, :], cot, a, e)
     bar = share(tree(add, partners(bar, "proto")), "batch")
     x, v, y, ay = first_pair(bar, r, a, e)

time: 125 us -> 124 us (level)
  local copies, waits for them, and re-layouts: 7.78 us -> 1.99 us
  Pallas kernels: 44.9 us -> 47.7 us
  waiting for transfers between devices: 15.5 us -> 18.1 us
    dynamic_slice x3 -> x0, local copies, waits for them, and re-layouts: 3.82 us -> none  [the longest x1 2.27 us: shards(): lax.dynamic_slice_in_dim(late_prototypes, member * count, count, axis=0)]
    all_to_all x1, waiting for transfers between devices: 1.67 us -> 4.24 us  [swap_copies(): return lax.all_to_all(copies, axis, split_axis=0, concat_axis=0, tiled=True)]
    pallas_call x0 -> x1, Pallas kernels: none -> 1.37 us  [half_copies(): pl.pallas_call(half_copies_kernel, in_specs=[in_smem, whole], out_specs=w...]
    unnamed x12 -> x8, local copies, waits for them, and re-layouts: 2.95 us -> 1.81 us
  transfers between devices with their start and end apart: 18 -> 18, of which waited for: 11 -> 11; matrix products, arithmetic and copies ran while one was open for 2% -> 0% of each run, Pallas kernels for 13% -> 13%
where the time goes in v2:
time: 124 us; the launch traced here: 123 us
  Pallas kernels  47.7 us (38%)
  blocking collectives  33.4 us (27%)
  starting transfers between devices  20.1 us (16%)
  waiting for transfers between devices  18.1 us (15%)
  local copies, waits for them, and re-layouts  1.99 us (2%)
    all_to_all x3, blocking collectives, swap_copies(): return lax.all_to_all(copies, axis, split_axis=0, concat_axis=0, tiled=True)  33.4 us
    ppermute x16, waiting for transfers between devices, partners(): lax.ppermute(x, axis, [(i, i ^ d * stride) for i in range(total)])  13.9 us
    ppermute x16, starting transfers between devices, partners(): lax.ppermute(x, axis, [(i, i ^ d * stride) for i in range(total)])  12.8 us
    pallas_call x1, Pallas kernels, col_softmax(): pl.pallas_call(functools.partial(col_softmax_kernel, devices // members),...  11.3 us
    pallas_call x1, Pallas kernels, embed_part(): pl.pallas_call(functools.partial(embed_kernel, total), grid_spec=pltpu.Pr...  11.2 us
    pallas_call x1, Pallas kernels, row_lse(): pl.pallas_call(row_lse_kernel, grid=(count // width,), in_specs=[pl.Block...  9.34 us
    all_to_all x1, starting transfers between devices, swap_copies(): return lax.all_to_all(copies, axis, split_axis=0, concat_axis=0, tiled=True)  7.25 us
    pallas_call x1, Pallas kernels, proto_part(): pl.pallas_call(proto_kernel, in_specs=[whole] * 9, out_specs=whole, out_s...  7.21 us
  transfers between devices with their start and end apart: 18, of which 11 were waited for; matrix products, arithmetic and copies ran while one was open for 0% of the time, Pallas kernels for 13%

profile of v2, /device:TPU:0, one launch (start us, length us, event | category | flops | bytes accessed | tf_op | source)
XLA Modules:
  0.0 123.0 jit_solution(11005757729572184352)
XLA Ops:
  0.6 0.1 pad_add_fusion.me_ref
  0.7 0.9 copy-done
  1.6 1.4 %half_copies.1 = bf16[8,128,256]{2,1,0:T(8,128)(2,1)} custom-call(s32[3]{0:T(128)S(1)} %pad_add_fusion.me_ref, bf16[256,256]{1,0:T(8,128)(2,1)S(1)} %copy-done), custom_call_target="tpu_custom_call" | custom-call | tf_op jit(solution)/shard_map/half_copies/pallas_call | solution.py:216
  3.0 7.3 %all-to-all-start = ((bf16[8,128,256]{2,1,0:T(8,128)(2,1)}), bf16[8,128,256]{2,1,0:T(8,128)(2,1)S(1)}, u32[]{:S(2)}, u32[]{:S(2)}) async-start(bf16[8,128,256]{2,1,0:T(8,128)(2,1)} %half_copies.1), calls=%async_computation | async-start | bytes 1048576 | tf_op jit(solution)/shard_map/all_to_all | solution.py:83
  10.3 0.9 copy-done.1
  11.2 9.3 %row_lse.1 = f32[32,1,256]{2,1,0:T(1,128)S(1)} custom-call(bf16[256,256]{1,0:T(8,128)(2,1)S(1)} %copy-done.1, bf16[16384,256]{1,0:T(8,128)(2,1)} %p_ref.3), custom_call_target="tpu_custom_call" | custom-call | flops 2147483648 | bytes 8388608 | tf_op jit(solution)/shard_map/row_lse/pallas_call | solution.py:260
  20.5 4.2 %all-to-all-done.mine_ref = bf16[8,128,256]{2,1,0:T(8,128)(2,1)S(1)} async-done(((bf16[8,128,256]{2,1,0:T(8,128)(2,1)}), bf16[8,128,256]{2,1,0:T(8,128)(2,1)S(1)}, u32[]{:S(2)}, u32[]{:S(2)}) %all-to-all-start) | async-done | bytes 524320 | tf_op jit(solution)/shard_map/all_to_all | solution.py:83
  24.7 0.0 collective-permute-start
  24.7 10.8 %all_to_all.20.lse_ref = f32[32,1,256]{2,1,0:T(1,128)S(1)} all-to-all(f32[32,1,256]{2,1,0:T(1,128)S(1)} %row_lse.1), channel_id=1, replica_groups=mesh['batch'=8,'proto'=4] {'batch','proto'}, dimensions={0} | all-to-all | bytes 65536 | tf_op jit(solution)/shard_map/all_to_all | solution.py:83
  35.6 0.0 collective-permute-done.other_ref
  35.6 11.3 %col_softmax.1 = (f32[2048,2048]{1,0:T(8,128)S(1)}, f32[1,2048]{1,0:T(1,128)S(1)}, f32[1,2048]{1,0:T(1,128)S(1)}, f32[1,2048]{1,0:T(1,128)S(1)}, bf16[2048,256]{...) custom-call(s32[3]{0:T(128)S(1)} %pad_add_fusion.me_ref, ...), custom_call_target="tpu_custom_call" | custom-call | flops 2147483648 | bytes 16777216 | tf_op jit(solution)/shard_map/col_softmax/pallas_call | solution.py:388
  46.9 0.3 collective-permute-start.3
  47.2 1.6 %collective-permute-start.2 = (f32[1,2048]{1,0:T(1,128)S(1)}, f32[1,2048]{1,0:T(1,128)S(1)}, u32[]{:S(2)}, u32[]{:S(2)}) collective-permute-start(f32[1,2048]{1,0:T(1,128)S(1)} %get-tuple-element.22), channel_id=1, source_target_pairs={{0,2},{1,3},{2,0},{3,1},{4,6},{5,7},{6,4},{7,5},{8,10},{9,11},{10,... | collective-permute-start | bytes 24584 | tf_op jit(solution)/shard_map/ppermute | solution.py:68
  48.8 0.1 collective-permute-start.1
  48.9 1.2 collective-permute-done.3
  50.1 0.8 collective-permute-done.2
  50.9 0.0 collective-permute-done.1
  50.9 0.7 collective-permute-start.4
  51.6 3.1 %collective-permute-done.4 = f32[1,2048]{1,0:T(1,128)S(1)} collective-permute-done((f32[1,2048]{1,0:T(1,128)S(1)}, f32[1,2048]{1,0:T(1,128)S(1)}, u32[]{:S(2)}, u32[]{:S(2)}) %collective-permute-start.4) | collective-permute-done | bytes 8224 | tf_op jit(solution)/shard_map/ppermute | solution.py:68
  54.6 0.7 collective-permute-start.7
  55.3 1.4 %collective-permute-start.6 = (f32[1,2048]{1,0:T(1,128)S(1)}, f32[1,2048]{1,0:T(1,128)S(1)}, u32[]{:S(2)}, u32[]{:S(2)}) collective-permute-start(f32[1,2048]{1,0:T(1,128)S(1)} %add.47.refs_0_), channel_id=1, source_target_pairs={{0,16},{4,20},{8,24},{12,28},{16,0},{20,4},{24,8},{28,12},{1,17},{... | collective-permute-start | bytes 24584 | tf_op jit(solution)/shard_map/ppermute | solution.py:68
  56.8 2.3 %collective-permute-start.5 = (f32[1,2048]{1,0:T(1,128)S(1)}, f32[1,2048]{1,0:T(1,128)S(1)}, u32[]{:S(2)}, u32[]{:S(2)}) collective-permute-start(f32[1,2048]{1,0:T(1,128)S(1)} %add.47.refs_0_), channel_id=1, source_target_pairs={{0,8},{4,12},{8,0},{12,4},{16,24},{20,28},{24,16},{28,20},{1,9},{5... | collective-permute-start | bytes 24584 | tf_op jit(solution)/shard_map/ppermute | solution.py:68
  59.1 1.1 collective-permute-done.7.refs_3_
  60.2 0.0 collective-permute-done.6.refs_2_
  60.2 0.6 collective-permute-done.5.refs_1_
  60.7 4.0 %second_pair.1 = (f32[1,2048]{1,0:T(1,128)S(1)}, f32[1,2048]{1,0:T(1,128)S(1)}, f32[1,2048]{1,0:T(1,128)S(1)}, f32[2048,128]{1,0:T(8,128)S(1)}) custom-call(s32[3]{0:T(128)S(1)} %pad_add_fusion.me_ref, f32[1,2048]{1,0:T(1,128)S(1)} %add.47.refs_0_, f32[1,2048]{1,0:T(1,128)S(1)} %collective-permute-done.5.refs_1_, ...), custom_call_target="tpu_custom_call" | custom-call | flops 16777216 | bytes 16777216 | tf_op jit(solution)/shard_map/second_pair/pallas_call | solution.py:437
  64.7 0.1 collective-permute-start.10
  64.8 1.6 %collective-permute-start.9 = (f32[1,2048]{1,0:T(1,128)S(1)}, f32[1,2048]{1,0:T(1,128)S(1)}, u32[]{:S(2)}, u32[]{:S(2)}) collective-permute-start(f32[1,2048]{1,0:T(1,128)S(1)} %get-tuple-element.26), channel_id=1, source_target_pairs={{0,2},{1,3},{2,0},{3,1},{4,6},{5,7},{6,4},{7,5},{8,10},{9,11},{10,... | collective-permute-start | bytes 24584 | tf_op jit(solution)/shard_map/ppermute | solution.py:68
  66.4 0.2 collective-permute-start.8
  66.7 1.2 collective-permute-done.10
  67.9 0.7 collective-permute-done.9
  68.6 10.4 %all_to_all.21.bar_ref = f32[8,1,2048]{2,1,0:T(1,128)S(1)} all-to-all(f32[8,1,2048]{2,1,0:T(1,128)S(1)} %broadcast_in_dim.25), channel_id=1, replica_groups=mesh['batch'=8,'proto'=4] {'batch'}, dimensions={0} | all-to-all | bytes 131072 | tf_op jit(solution)/shard_map/all_to_all | solution.py:83
  79.0 3.3 %first_pair.1 = (f32[1,2048]{1,0:T(1,128)S(1)}, f32[1,2048]{1,0:T(1,128)S(1)}, f32[1,2048]{1,0:T(1,128)S(1)}, f32[2048,128]{1,0:T(8,128)S(1)}) custom-call(f32[8,1,2048]{2,1,0:T(1,128)S(1)} %all_to_all.21.bar_ref, f32[1,2048]{1,0:T(1,128)S(1)} %get-tuple-element.27.r_ref, f32[2048,128]{1,0:T(8,128)S(1)} %get-tuple-element.24.refs_6_.a_ref, ...), custom_call_target="tpu_custom_call" | custom-call | flops 16777216 | bytes 16777216 | tf_op jit(solution)/shard_map/first_pair/pallas_call | solution.py:473
  82.2 0.1 collective-permute-start.13
  82.3 1.6 %collective-permute-start.12 = (f32[1,2048]{1,0:T(1,128)S(1)}, f32[1,2048]{1,0:T(1,128)S(1)}, u32[]{:S(2)}, u32[]{:S(2)}) collective-permute-start(f32[1,2048]{1,0:T(1,128)S(1)} %get-tuple-element.28), channel_id=1, source_target_pairs={{0,2},{1,3},{2,0},{3,1},{4,6},{5,7},{6,4},{7,5},{8,10},{9,11},{10,... | collective-permute-start | bytes 24584 | tf_op jit(solution)/shard_map/ppermute | solution.py:68
  83.9 0.3 collective-permute-start.11
  84.2 1.2 %collective-permute-done.13 = f32[1,2048]{1,0:T(1,128)S(1)} collective-permute-done((f32[1,2048]{1,0:T(1,128)S(1)}, f32[1,2048]{1,0:T(1,128)S(1)}, u32[]{:S(2)}, u32[]{:S(2)}) %collective-permute-start.13) | collective-permute-done | bytes 8224 | tf_op jit(solution)/shard_map/ppermute | solution.py:68
  85.4 0.6 collective-permute-done.12
  86.1 0.1 broadcast_in_dim.27
  86.3 12.2 %all_to_all.22.last_ref = f32[8,1,8192]{2,1,0:T(1,128)S(1)} all-to-all(f32[8,1,8192]{2,1,0:T(1,128)S(1)} %broadcast_in_dim.27), channel_id=1, replica_groups=mesh['batch'=8,'proto'=4] {'batch'}, dimensions={0} | all-to-all | bytes 524288 | tf_op jit(solution)/shard_map/all_to_all | solution.py:83
  98.4 11.2 %embed_part.1 = f32[256,256]{1,0:T(8,128)S(1)} custom-call(s32[3]{0:T(128)S(1)} %pad_add_fusion.me_ref, f32[8,1,8192]{2,1,0:T(1,128)S(1)} %all_to_all.22.last_ref, f32[1,2048]{1,0:T(1,128)S(1)} %get-tuple-element.32.f_ref, f32[1,2048]{1,0:T(1,128)S(1)} %get-tuple-element.27.r_ref, f32[1,2048]{1,0:T(1,128)S(1)} %get-tuple-element.33.v_ref, ...), custom_call_target="tpu_custom_call" | custom-call | flops 4294967296 | bytes 8388608 | tf_op jit(solution)/shard_map/embed_part/pallas_call | solution.py:541
  109.6 0.1 collective-permute-start.16
  109.7 0.6 collective-permute-start.15
  110.3 1.2 collective-permute-start.14
  111.5 7.2 %proto_part.1 = f32[2048,256]{1,0:T(8,128)} custom-call(f32[8,1,8192]{2,1,0:T(1,128)S(1)} %all_to_all.22.last_ref, f32[1,2048]{1,0:T(1,128)S(1)} %get-tuple-element.27.r_ref, f32[1,2048]{1,0:T(1,128)S(1)} %get-tuple-element.33.v_ref, f32[2048,128]{1,0:T(8,128)S(1)} %get-tuple-element.24.refs_6_.a_ref, f32[2048,128]{1,0:T(8,128)S(1)} %get-tuple-element.34.h_ref, ...), custom_call_target="tpu_custom_call" | custom-call | flops 2147483648 | bytes 16777216 | tf_op jit(solution)/shard_map/proto_part/pallas_call | solution.py:610
  118.8 0.0 collective-permute-done.16
  118.8 3.4 %collective-permute-done.15 = f32[256,256]{1,0:T(8,128)S(1)} collective-permute-done((f32[256,256]{1,0:T(8,128)S(1)}, f32[256,256]{1,0:T(8,128)S(1)}, u32[]{:S(2)}, u32[]{:S(2)}) %collective-permute-start.15) | collective-permute-done | bytes 262176 | tf_op jit(solution)/shard_map/ppermute | solution.py:68
  122.2 0.8 add_add_fusion
  (15 shorter events, 0.1 us)
Async XLA Ops:
  0.7 0.9 copy-start
  3.0 21.7 %all-to-all-start = ((bf16[8,128,256]{2,1,0:T(8,128)(2,1)}), bf16[8,128,256]{2,1,0:T(8,128)(2,1)S(1)}, u32[]{:S(2)}, u32[]{:S(2)}) async-start(bf16[8,128,256]{2,1,0:T(8,128)(2,1)} %half_copies.1), calls=%async_computation | async-start | bytes 1048576 | tf_op jit(solution)/shard_map/all_to_all | solution.py:83
  10.2 0.9 copy-start.1
  11.2 49.6 %copy-start.3 = (f32[256]{0:T(256)S(1)}, f32[256]{0:T(256)}, u32[]{:S(2)}) copy-start(f32[256]{0:T(256)} %param.6) | copy-start | bytes 3076
  24.7 10.8 %collective-permute-start = (bf16[8,128,256]{2,1,0:T(8,128)(2,1)S(1)}, bf16[8,128,256]{2,1,0:T(8,128)(2,1)S(1)}, u32[]{:S(2)}, u32[]{:S(2)}) collective-permute-start(bf16[8,128,256]{2,1,0:T(8,128)(2,1)S(1)} %all-to-all-done.mine_ref), channel_id=1, source_target_pairs={{0,1},{1,0},{2,3},{3,2},{4,5},{5,4},{6,7},{7,6},{8,9},{9,8},{10,11... | collective-permute-start | bytes 1572872 | tf_op jit(solution)/shard_map/ppermute | solution.py:632
  46.9 3.1 %collective-permute-start.3 = (f32[1,2048]{1,0:T(1,128)S(1)}, f32[1,2048]{1,0:T(1,128)S(1)}, u32[]{:S(2)}, u32[]{:S(2)}) collective-permute-start(f32[1,2048]{1,0:T(1,128)S(1)} %get-tuple-element.22), channel_id=1, source_target_pairs={{0,3},{1,2},{2,1},{3,0},{4,7},{5,6},{6,5},{7,4},{8,11},{9,10},{10,... | collective-permute-start | bytes 24584 | tf_op jit(solution)/shard_map/ppermute | solution.py:68
  47.2 3.7 %collective-permute-start.2 = (f32[1,2048]{1,0:T(1,128)S(1)}, f32[1,2048]{1,0:T(1,128)S(1)}, u32[]{:S(2)}, u32[]{:S(2)}) collective-permute-start(f32[1,2048]{1,0:T(1,128)S(1)} %get-tuple-element.22), channel_id=1, source_target_pairs={{0,2},{1,3},{2,0},{3,1},{4,6},{5,7},{6,4},{7,5},{8,10},{9,11},{10,... | collective-permute-start | bytes 24584 | tf_op jit(solution)/shard_map/ppermute | solution.py:68
  48.8 2.1 %collective-permute-start.1 = (f32[1,2048]{1,0:T(1,128)S(1)}, f32[1,2048]{1,0:T(1,128)S(1)}, u32[]{:S(2)}, u32[]{:S(2)}) collective-permute-start(f32[1,2048]{1,0:T(1,128)S(1)} %get-tuple-element.22), channel_id=1, source_target_pairs={{0,1},{1,0},{2,3},{3,2},{4,5},{5,4},{6,7},{7,6},{8,9},{9,8},{10,11... | collective-permute-start | bytes 24584 | tf_op jit(solution)/shard_map/ppermute | solution.py:68
  50.9 3.7 %collective-permute-start.4 = (f32[1,2048]{1,0:T(1,128)S(1)}, f32[1,2048]{1,0:T(1,128)S(1)}, u32[]{:S(2)}, u32[]{:S(2)}) collective-permute-start(f32[1,2048]{1,0:T(1,128)S(1)} %add_add_fusion.3), channel_id=1, source_target_pairs={{0,4},{4,0},{8,12},{12,8},{16,20},{20,16},{24,28},{28,24},{1,5},{5... | collective-permute-start | bytes 24584 | tf_op jit(solution)/shard_map/ppermute | solution.py:68
  54.6 5.5 %collective-permute-start.7 = (f32[1,2048]{1,0:T(1,128)S(1)}, f32[1,2048]{1,0:T(1,128)S(1)}, u32[]{:S(2)}, u32[]{:S(2)}) collective-permute-start(f32[1,2048]{1,0:T(1,128)S(1)} %add.47.refs_0_), channel_id=1, source_target_pairs={{0,24},{4,28},{8,16},{12,20},{16,8},{20,12},{24,0},{28,4},{1,25},{... | collective-permute-start | bytes 24584 | tf_op jit(solution)/shard_map/ppermute | solution.py:68
  55.3 4.8 %collective-permute-start.6 = (f32[1,2048]{1,0:T(1,128)S(1)}, f32[1,2048]{1,0:T(1,128)S(1)}, u32[]{:S(2)}, u32[]{:S(2)}) collective-permute-start(f32[1,2048]{1,0:T(1,128)S(1)} %add.47.refs_0_), channel_id=1, source_target_pairs={{0,16},{4,20},{8,24},{12,28},{16,0},{20,4},{24,8},{28,12},{1,17},{... | collective-permute-start | bytes 24584 | tf_op jit(solution)/shard_map/ppermute | solution.py:68
  56.8 4.0 %collective-permute-start.5 = (f32[1,2048]{1,0:T(1,128)S(1)}, f32[1,2048]{1,0:T(1,128)S(1)}, u32[]{:S(2)}, u32[]{:S(2)}) collective-permute-start(f32[1,2048]{1,0:T(1,128)S(1)} %add.47.refs_0_), channel_id=1, source_target_pairs={{0,8},{4,12},{8,0},{12,4},{16,24},{20,28},{24,16},{28,20},{1,9},{5... | collective-permute-start | bytes 24584 | tf_op jit(solution)/shard_map/ppermute | solution.py:68
  64.7 3.1 %collective-permute-start.10 = (f32[1,2048]{1,0:T(1,128)S(1)}, f32[1,2048]{1,0:T(1,128)S(1)}, u32[]{:S(2)}, u32[]{:S(2)}) collective-permute-start(f32[1,2048]{1,0:T(1,128)S(1)} %get-tuple-element.26), channel_id=1, source_target_pairs={{0,3},{1,2},{2,1},{3,0},{4,7},{5,6},{6,5},{7,4},{8,11},{9,10},{10,... | collective-permute-start | bytes 24584 | tf_op jit(solution)/shard_map/ppermute | solution.py:68
  64.8 3.7 %collective-permute-start.9 = (f32[1,2048]{1,0:T(1,128)S(1)}, f32[1,2048]{1,0:T(1,128)S(1)}, u32[]{:S(2)}, u32[]{:S(2)}) collective-permute-start(f32[1,2048]{1,0:T(1,128)S(1)} %get-tuple-element.26), channel_id=1, source_target_pairs={{0,2},{1,3},{2,0},{3,1},{4,6},{5,7},{6,4},{7,5},{8,10},{9,11},{10,... | collective-permute-start | bytes 24584 | tf_op jit(solution)/shard_map/ppermute | solution.py:68
  66.4 2.1 %collective-permute-start.8 = (f32[1,2048]{1,0:T(1,128)S(1)}, f32[1,2048]{1,0:T(1,128)S(1)}, u32[]{:S(2)}, u32[]{:S(2)}) collective-permute-start(f32[1,2048]{1,0:T(1,128)S(1)} %get-tuple-element.26), channel_id=1, source_target_pairs={{0,1},{1,0},{2,3},{3,2},{4,5},{5,4},{6,7},{7,6},{8,9},{9,8},{10,11... | collective-permute-start | bytes 24584 | tf_op jit(solution)/shard_map/ppermute | solution.py:68
  79.0 19.4 %copy-start.2 = (bf16[256,256]{1,0:T(8,128)(2,1)S(1)}, bf16[256,256]{1,0:T(8,128)(2,1)}, u32[]{:S(2)}) copy-start(bf16[256,256]{1,0:T(8,128)(2,1)} %e_ref.5) | copy-start | bytes 393220
  82.2 3.2 %collective-permute-start.13 = (f32[1,2048]{1,0:T(1,128)S(1)}, f32[1,2048]{1,0:T(1,128)S(1)}, u32[]{:S(2)}, u32[]{:S(2)}) collective-permute-start(f32[1,2048]{1,0:T(1,128)S(1)} %get-tuple-element.28), channel_id=1, source_target_pairs={{0,3},{1,2},{2,1},{3,0},{4,7},{5,6},{6,5},{7,4},{8,11},{9,10},{10,... | collective-permute-start | bytes 24584 | tf_op jit(solution)/shard_map/ppermute | solution.py:68
  82.3 3.7 %collective-permute-start.12 = (f32[1,2048]{1,0:T(1,128)S(1)}, f32[1,2048]{1,0:T(1,128)S(1)}, u32[]{:S(2)}, u32[]{:S(2)}) collective-permute-start(f32[1,2048]{1,0:T(1,128)S(1)} %get-tuple-element.28), channel_id=1, source_target_pairs={{0,2},{1,3},{2,0},{3,1},{4,6},{5,7},{6,4},{7,5},{8,10},{9,11},{10,... | collective-permute-start | bytes 24584 | tf_op jit(solution)/shard_map/ppermute | solution.py:68
  83.9 2.2 %collective-permute-start.11 = (f32[1,2048]{1,0:T(1,128)S(1)}, f32[1,2048]{1,0:T(1,128)S(1)}, u32[]{:S(2)}, u32[]{:S(2)}) collective-permute-start(f32[1,2048]{1,0:T(1,128)S(1)} %get-tuple-element.28), channel_id=1, source_target_pairs={{0,1},{1,0},{2,3},{3,2},{4,5},{5,4},{6,7},{7,6},{8,9},{9,8},{10,11... | collective-permute-start | bytes 24584 | tf_op jit(solution)/shard_map/ppermute | solution.py:68
  109.6 9.1 %collective-permute-start.16 = (f32[256,256]{1,0:T(8,128)S(1)}, f32[256,256]{1,0:T(8,128)S(1)}, u32[]{:S(2)}, u32[]{:S(2)}) collective-permute-start(f32[256,256]{1,0:T(8,128)S(1)} %embed_part.1), channel_id=1, source_target_pairs={{0,3},{1,2},{2,1},{3,0},{4,7},{5,6},{6,5},{7,4},{8,11},{9,10},{10,... | collective-permute-start | bytes 786440 | tf_op jit(solution)/shard_map/ppermute | solution.py:68
  109.7 12.5 %collective-permute-start.15 = (f32[256,256]{1,0:T(8,128)S(1)}, f32[256,256]{1,0:T(8,128)S(1)}, u32[]{:S(2)}, u32[]{:S(2)}) collective-permute-start(f32[256,256]{1,0:T(8,128)S(1)} %embed_part.1), channel_id=1, source_target_pairs={{0,2},{1,3},{2,0},{3,1},{4,6},{5,7},{6,4},{7,5},{8,10},{9,11},{10,... | collective-permute-start | bytes 786440 | tf_op jit(solution)/shard_map/ppermute | solution.py:68
  110.3 11.9 %collective-permute-start.14 = (f32[256,256]{1,0:T(8,128)S(1)}, f32[256,256]{1,0:T(8,128)S(1)}, u32[]{:S(2)}, u32[]{:S(2)}) collective-permute-start(f32[256,256]{1,0:T(8,128)S(1)} %embed_part.1), channel_id=1, source_target_pairs={{0,1},{1,0},{2,3},{3,2},{4,5},{5,4},{6,7},{7,6},{8,9},{9,8},{10,11... | collective-permute-start | bytes 786440 | tf_op jit(solution)/shard_map/ppermute | solution.py:68

commit v3 on v2

--- a/solution.py
+++ b/solution.py
@@ -9,7 +9,6 @@
 from jax.sharding import PartitionSpec as P
 
 score_scale = 4.0
-to_base2 = score_scale * math.log2(math.e)
 lanes = 128
 sublanes = 8
 both = ("batch", "proto")
@@ -204,23 +203,27 @@
     return values + [single] * 2
 
 
-def half_copies_kernel(me_ref, e_ref, copies_ref):
+def half_copies_kernel(me_ref, e_ref, copies_ref, sem):
     copies, half, _ = copies_ref.shape
-    value = e_ref[pl.ds(pl.multiple_of(me_ref[1] * half, half), half), :]
-    for d in range(copies):
-        copies_ref[d] = value
+    source = e_ref.at[pl.ds(pl.multiple_of(me_ref[1] * half, half), half), :]
+    moves = [pltpu.make_async_copy(source, copies_ref.at[d], sem.at[d]) for d in range(copies)]
+    for move in moves:
+        move.start()
+    for move in moves:
+        move.wait()
 
 
 def half_copies(me, embeddings, copies):
     rows, depth = embeddings.shape
     return pl.pallas_call(
         half_copies_kernel,
-        in_specs=[in_smem, whole],
-        out_specs=whole,
+        in_specs=[in_smem, anywhere],
+        out_specs=anywhere,
         out_shape=jax.ShapeDtypeStruct((copies, rows // 2, depth), bf16),
+        scratch_shapes=[pltpu.SemaphoreType.DMA((copies,))],
         compiler_params=beside_plan,
         name="half_copies",
-    )(me, embeddings)
+    )(me, in_hbm(embeddings))
 
 
 def row_lse_kernel(e_ref, p_ref, copies_ref, turned_ref, top_ref, mass_ref):
@@ -230,16 +233,16 @@
 
     @pl.when(step == 0)
     def _():
-        turned_ref[...] = e_ref[...].T
+        turned_ref[...] = (e_ref[...] * score_scale).T
         top_ref[...] = jnp.full_like(top_ref, -1e30)
         mass_ref[...] = jnp.zeros_like(mass_ref)
 
     top, mass = top_ref[...], mass_ref[...]
-    for at in chunks(width, width // 2):
-        t = dot_nn(p_ref[at, :], turned_ref[...]) * to_base2
+    for at in chunks(width, 2 * lanes):
+        t = dot_nn(p_ref[at, :], turned_ref[...])
         t = t.reshape(t.shape[0] // sublanes, sublanes, rows)
         new = jnp.maximum(top, jnp.max(t, axis=0))
-        mass = mass * jnp.exp2(top - new) + jnp.sum(jnp.exp2(t - new[None]), axis=0)
+        mass = mass * jnp.exp(top - new) + jnp.sum(jnp.exp(t - new[None]), axis=0)
         top = new
     top_ref[...] = top
     mass_ref[...] = mass
@@ -247,8 +250,8 @@
     @pl.when(step == pl.num_programs(0) - 1)
     def _():
         peak = jnp.max(top, axis=0, keepdims=True)
-        total = jnp.sum(mass * jnp.exp2(top - peak), axis=0, keepdims=True)
-        lse = peak + jnp.log2(total)
+        total = jnp.sum(mass * jnp.exp(top - peak), axis=0, keepdims=True)
+        lse = peak + jnp.log(total)
         for d in range(copies_ref.shape[0]):
             copies_ref[d] = lse
 
@@ -276,7 +279,7 @@
             flops=2 * rows * count * depth, bytes_accessed=count * depth * 2, transcendentals=rows * count
         ),
         name="row_lse",
-    )(embeddings, in_hbm(prototypes))
+    )(in_hbm(embeddings), in_hbm(prototypes))
 
 
 def col_softmax_kernel(
@@ -319,14 +322,14 @@
     for d in range(members):
         pieces = [lse_ref[d * proto + k] for k in range(proto)]
         top = tree(jnp.maximum, pieces)
-        mass = tree(add, [jnp.exp2(piece - top) for piece in pieces])
-        f_ref[:, d * held : (d + 1) * held] = -math.log2(rows) - (top + jnp.log2(mass))
+        mass = tree(add, [jnp.exp(piece - top) for piece in pieces])
+        f_ref[:, d * held : (d + 1) * held] = -math.log(rows) - (top + jnp.log(mass))
     for move in moves:
         move.wait()
     lanes_to_rows(cot_ref[...], cot_tall_ref)
     for d in range(members):
         at = slice(d * held, (d + 1) * held)
-        turned_ref[:, at] = all_ref[at, :].T
+        turned_ref[:, at] = (all_ref[at, :] * score_scale).T
 
     height = t_ref.shape[1]
     blocks = count // height
@@ -335,7 +338,7 @@
         p = p_ref[pl.ds(pl.multiple_of(block * height, height), height), :]
         part = None
         for c in chunks(rows, 2 * lanes):
-            t = dot_nn(p, turned_ref[:, c]) * to_base2 + f_ref[:, c]
+            t = dot_nn(p, turned_ref[:, c]) + f_ref[:, c]
             t_ref[slot, :, c] = t
             here = jnp.maximum(t[:, :lanes], t[:, lanes:])
             part = here if part is None else jnp.maximum(part, here)
@@ -348,7 +351,7 @@
             top = a_ref[at, :]
             mass = jnp.zeros((sublanes, lanes), f32)
             for c in chunks(rows):
-                e = jnp.exp2(t_ref[slot, inner, c] - top)
+                e = jnp.exp(t_ref[slot, inner, c] - top)
                 e_ref[at, c] = e
                 mass = mass + e
             part_ref[at, :] = mass
@@ -368,9 +371,9 @@
 
         lax.fori_loop(0, blocks // 2, pair, 0)
     top = a_ref[...]
-    h_ref[...] = jnp.exp2(top + math.log2(rows))
+    h_ref[...] = jnp.exp(top + math.log(rows))
     mass = lane_total(part_ref[...], jnp.sum)
-    part_ref[...] = top + jnp.log2(mass)
+    part_ref[...] = top + jnp.log(mass)
     a_ref[...] = 1.0 / mass
     rows_to_lanes(part_ref, col_lse_ref)
     accumulate(e_ref, a_ref, acc_ref)
@@ -383,7 +386,7 @@
     rows = 2 * members * half
     count = prototypes.shape[0] // members
     devices = lse.shape[0]
-    height = min(count, 4 * lanes) if few(rows) else lanes
+    height = min(count, 2 * lanes) if few(rows) else lanes
     halves = whole if few(rows) else anywhere
     return pl.pallas_call(
         functools.partial(col_softmax_kernel, devices // members),
@@ -512,10 +515,10 @@
         left_ref[...] = stack_lanes(left_factors([-r, -x, one], -v))
 
     y, lse, a = (last_ref[step, :, total + k * width : total + (k + 1) * width] for k in range(3))
-    w = jnp.exp2(lse + math.log2(total))
+    w = jnp.exp(lse + math.log(total))
     rows_of = stack_sublanes(right_factors([a, w, y], jnp.ones_like(a)), width)
     right_ref[0 : rows_of.shape[0], :] = rows_of
-    e = e_ref[...]
+    e = e_ref[...] * score_scale
     left = left_ref[...]
     f = tall_ref[0]
     sub = min(2 * lanes, width)
@@ -523,8 +526,8 @@
     for c in chunks(width, sub):
         s = dot_nt(e, p_ref[c, :])
         bracket = dot_nn(left, right_ref[:, c])
-        t = s * to_base2 - lse[:, c]
-        plan = jnp.concatenate([jnp.exp2(t[:, at] + f) for at in chunks(sub)], axis=1)
+        t = s - lse[:, c]
+        plan = jnp.concatenate([jnp.exp(t[:, at] + f) for at in chunks(sub)], axis=1)
         b_ref[:, c] = (plan * bracket).astype(bf16)
         if c.stop % group == 0:
             done = slice(c.stop - group, c.stop)
@@ -565,7 +568,7 @@
             flops=4 * rows * count * depth, bytes_accessed=count * depth * 2, transcendentals=rows * count
         ),
         name="embed_part",
-    )(me, last, f, r, v, embeddings, in_hbm(prototypes))
+    )(me, last, f, r, v, in_hbm(embeddings), in_hbm(prototypes))
 
 
 def proto_kernel(last_ref, r_ref, v_ref, a_ref, h_ref, z_ref, ay_ref, all_ref, e_ref, out_ref, right_ref, b_ref):

time: 124 us -> 139 us (1.12)
  Pallas kernels: 47.7 us -> 63.3 us
  local copies, waits for them, and re-layouts: 1.99 us -> 0.18 us
  waiting for transfers between devices: 18.1 us -> 19.7 us
    pallas_call x1, Pallas kernels: 1.37 us -> 17.6 us  [half_copies(): pl.pallas_call(half_copies_kernel, in_specs=[in_smem, anywhere], out_spec...]
    unnamed x8 -> x2, local copies, waits for them, and re-layouts: 1.81 us -> 0.01 us
    all_to_all x1, waiting for transfers between devices: 4.24 us -> 5.86 us  [swap_copies(): return lax.all_to_all(copies, axis, split_axis=0, concat_axis=0, tiled=True)]
  transfers between devices with their start and end apart: 18 -> 18, of which waited for: 11 -> 11; matrix products, arithmetic and copies ran while one was open for 0% -> 0% of each run, Pallas kernels for 13% -> 11%
where the time goes in v3:
time: 139 us; the launch traced here: 138 us
  Pallas kernels  63.3 us (46%)
  blocking collectives  33.4 us (24%)
  starting transfers between devices  20.1 us (14%)
  waiting for transfers between devices  19.7 us (14%)
    all_to_all x3, blocking collectives, swap_copies(): return lax.all_to_all(copies, axis, split_axis=0, concat_axis=0, tiled=True)  33.4 us
    pallas_call x1, Pallas kernels, half_copies(): pl.pallas_call(half_copies_kernel, in_specs=[in_smem, anywhere], out_spec...  17.6 us
    ppermute x16, waiting for transfers between devices, partners(): lax.ppermute(x, axis, [(i, i ^ d * stride) for i in range(total)])  13.8 us
    ppermute x16, starting transfers between devices, partners(): lax.ppermute(x, axis, [(i, i ^ d * stride) for i in range(total)])  12.9 us
    pallas_call x1, Pallas kernels, col_softmax(): pl.pallas_call(functools.partial(col_softmax_kernel, devices // members),...  11.4 us
    pallas_call x1, Pallas kernels, embed_part(): pl.pallas_call(functools.partial(embed_kernel, total), grid_spec=pltpu.Pr...  11.2 us
    pallas_call x1, Pallas kernels, row_lse(): pl.pallas_call(row_lse_kernel, grid=(count // width,), in_specs=[pl.Block...  8.61 us
    all_to_all x1, starting transfers between devices, swap_copies(): return lax.all_to_all(copies, axis, split_axis=0, concat_axis=0, tiled=True)  7.26 us
  transfers between devices with their start and end apart: 18, of which 11 were waited for; matrix products, arithmetic and copies ran while one was open for 0% of the time, Pallas kernels for 11%

profile of v3, /device:TPU:0, one launch (start us, length us, event | category | flops | bytes accessed | tf_op | source)
XLA Modules:
  0.0 138.3 jit_solution(10534031371315010176)
XLA Ops:
  0.6 0.1 pad_add_fusion.me_ref
  0.7 17.6 %half_copies.1 = bf16[8,128,256]{2,1,0:T(8,128)(2,1)} custom-call(s32[3]{0:T(128)S(1)} %pad_add_fusion.me_ref, bf16[256,256]{1,0:T(8,128)(2,1)} %e_ref.5), custom_call_target="tpu_custom_call" | custom-call | tf_op jit(solution)/shard_map/half_copies/pallas_call | solution.py:218
  18.3 7.3 %all-to-all-start = ((bf16[8,128,256]{2,1,0:T(8,128)(2,1)}), bf16[8,128,256]{2,1,0:T(8,128)(2,1)S(1)}, u32[]{:S(2)}, u32[]{:S(2)}) async-start(bf16[8,128,256]{2,1,0:T(8,128)(2,1)} %half_copies.1), calls=%async_computation | async-start | bytes 1048576 | tf_op jit(solution)/shard_map/all_to_all | solution.py:82
  25.6 8.6 %row_lse.1 = f32[32,1,256]{2,1,0:T(1,128)S(1)} custom-call(bf16[256,256]{1,0:T(8,128)(2,1)} %e_ref.5, bf16[16384,256]{1,0:T(8,128)(2,1)} %p_ref.3), custom_call_target="tpu_custom_call" | custom-call | flops 2147483648 | bytes 8388608 | tf_op jit(solution)/shard_map/row_lse/pallas_call | solution.py:263
  34.2 5.9 %all-to-all-done.mine_ref = bf16[8,128,256]{2,1,0:T(8,128)(2,1)S(1)} async-done(((bf16[8,128,256]{2,1,0:T(8,128)(2,1)}), bf16[8,128,256]{2,1,0:T(8,128)(2,1)S(1)}, u32[]{:S(2)}, u32[]{:S(2)}) %all-to-all-start) | async-done | bytes 524320 | tf_op jit(solution)/shard_map/all_to_all | solution.py:82
  40.1 0.0 collective-permute-start
  40.1 10.8 %all_to_all.20.lse_ref = f32[32,1,256]{2,1,0:T(1,128)S(1)} all-to-all(f32[32,1,256]{2,1,0:T(1,128)S(1)} %row_lse.1), channel_id=1, replica_groups=mesh['batch'=8,'proto'=4] {'batch','proto'}, dimensions={0} | all-to-all | bytes 65536 | tf_op jit(solution)/shard_map/all_to_all | solution.py:82
  50.9 0.0 collective-permute-done.other_ref
  50.9 11.4 %col_softmax.1 = (f32[2048,2048]{1,0:T(8,128)S(1)}, f32[1,2048]{1,0:T(1,128)S(1)}, f32[1,2048]{1,0:T(1,128)S(1)}, f32[1,2048]{1,0:T(1,128)S(1)}, bf16[2048,256]{...) custom-call(s32[3]{0:T(128)S(1)} %pad_add_fusion.me_ref, ...), custom_call_target="tpu_custom_call" | custom-call | flops 2147483648 | bytes 16777216 | tf_op jit(solution)/shard_map/col_softmax/pallas_call | solution.py:391
  62.3 0.3 collective-permute-start.3
  62.6 1.5 %collective-permute-start.2 = (f32[1,2048]{1,0:T(1,128)S(1)}, f32[1,2048]{1,0:T(1,128)S(1)}, u32[]{:S(2)}, u32[]{:S(2)}) collective-permute-start(f32[1,2048]{1,0:T(1,128)S(1)} %get-tuple-element.22), channel_id=1, source_target_pairs={{0,2},{1,3},{2,0},{3,1},{4,6},{5,7},{6,4},{7,5},{8,10},{9,11},{10,... | collective-permute-start | bytes 24584 | tf_op jit(solution)/shard_map/ppermute | solution.py:67
  64.1 0.1 collective-permute-start.1
  64.3 1.2 collective-permute-done.3
  65.4 0.8 collective-permute-done.2
  66.2 0.0 collective-permute-done.1
  66.3 0.7 collective-permute-start.4
  66.9 3.0 %collective-permute-done.4 = f32[1,2048]{1,0:T(1,128)S(1)} collective-permute-done((f32[1,2048]{1,0:T(1,128)S(1)}, f32[1,2048]{1,0:T(1,128)S(1)}, u32[]{:S(2)}, u32[]{:S(2)}) %collective-permute-start.4) | collective-permute-done | bytes 8224 | tf_op jit(solution)/shard_map/ppermute | solution.py:67
  70.0 0.7 collective-permute-start.7
  70.7 1.4 %collective-permute-start.6 = (f32[1,2048]{1,0:T(1,128)S(1)}, f32[1,2048]{1,0:T(1,128)S(1)}, u32[]{:S(2)}, u32[]{:S(2)}) collective-permute-start(f32[1,2048]{1,0:T(1,128)S(1)} %add.47.refs_0_), channel_id=1, source_target_pairs={{0,16},{4,20},{8,24},{12,28},{16,0},{20,4},{24,8},{28,12},{1,17},{... | collective-permute-start | bytes 24584 | tf_op jit(solution)/shard_map/ppermute | solution.py:67
  72.1 2.3 %collective-permute-start.5 = (f32[1,2048]{1,0:T(1,128)S(1)}, f32[1,2048]{1,0:T(1,128)S(1)}, u32[]{:S(2)}, u32[]{:S(2)}) collective-permute-start(f32[1,2048]{1,0:T(1,128)S(1)} %add.47.refs_0_), channel_id=1, source_target_pairs={{0,8},{4,12},{8,0},{12,4},{16,24},{20,28},{24,16},{28,20},{1,9},{5... | collective-permute-start | bytes 24584 | tf_op jit(solution)/shard_map/ppermute | solution.py:67
  74.4 1.1 collective-permute-done.7.refs_3_
  75.5 0.0 collective-permute-done.6.refs_2_
  75.5 0.6 collective-permute-done.5.refs_1_
  76.1 4.0 %second_pair.1 = (f32[1,2048]{1,0:T(1,128)S(1)}, f32[1,2048]{1,0:T(1,128)S(1)}, f32[1,2048]{1,0:T(1,128)S(1)}, f32[2048,128]{1,0:T(8,128)S(1)}) custom-call(s32[3]{0:T(128)S(1)} %pad_add_fusion.me_ref, f32[1,2048]{1,0:T(1,128)S(1)} %add.47.refs_0_, f32[1,2048]{1,0:T(1,128)S(1)} %collective-permute-done.5.refs_1_, ...), custom_call_target="tpu_custom_call" | custom-call | flops 16777216 | bytes 16777216 | tf_op jit(solution)/shard_map/second_pair/pallas_call | solution.py:440
  80.1 0.1 collective-permute-start.10
  80.2 1.6 %collective-permute-start.9 = (f32[1,2048]{1,0:T(1,128)S(1)}, f32[1,2048]{1,0:T(1,128)S(1)}, u32[]{:S(2)}, u32[]{:S(2)}) collective-permute-start(f32[1,2048]{1,0:T(1,128)S(1)} %get-tuple-element.26), channel_id=1, source_target_pairs={{0,2},{1,3},{2,0},{3,1},{4,6},{5,7},{6,4},{7,5},{8,10},{9,11},{10,... | collective-permute-start | bytes 24584 | tf_op jit(solution)/shard_map/ppermute | solution.py:67
  81.7 0.3 collective-permute-start.8
  82.0 1.2 collective-permute-done.10
  83.2 0.6 collective-permute-done.9
  83.9 10.4 %all_to_all.21.bar_ref = f32[8,1,2048]{2,1,0:T(1,128)S(1)} all-to-all(f32[8,1,2048]{2,1,0:T(1,128)S(1)} %broadcast_in_dim.25), channel_id=1, replica_groups=mesh['batch'=8,'proto'=4] {'batch'}, dimensions={0} | all-to-all | bytes 131072 | tf_op jit(solution)/shard_map/all_to_all | solution.py:82
  94.3 3.3 %first_pair.1 = (f32[1,2048]{1,0:T(1,128)S(1)}, f32[1,2048]{1,0:T(1,128)S(1)}, f32[1,2048]{1,0:T(1,128)S(1)}, f32[2048,128]{1,0:T(8,128)S(1)}) custom-call(f32[8,1,2048]{2,1,0:T(1,128)S(1)} %all_to_all.21.bar_ref, f32[1,2048]{1,0:T(1,128)S(1)} %get-tuple-element.27.r_ref, f32[2048,128]{1,0:T(8,128)S(1)} %get-tuple-element.24.refs_6_.a_ref, ...), custom_call_target="tpu_custom_call" | custom-call | flops 16777216 | bytes 16777216 | tf_op jit(solution)/shard_map/first_pair/pallas_call | solution.py:476
  97.6 0.1 collective-permute-start.13
  97.7 1.5 %collective-permute-start.12 = (f32[1,2048]{1,0:T(1,128)S(1)}, f32[1,2048]{1,0:T(1,128)S(1)}, u32[]{:S(2)}, u32[]{:S(2)}) collective-permute-start(f32[1,2048]{1,0:T(1,128)S(1)} %get-tuple-element.28), channel_id=1, source_target_pairs={{0,2},{1,3},{2,0},{3,1},{4,6},{5,7},{6,4},{7,5},{8,10},{9,11},{10,... | collective-permute-start | bytes 24584 | tf_op jit(solution)/shard_map/ppermute | solution.py:67
  99.2 0.3 collective-permute-start.11
  99.5 1.3 collective-permute-done.13
  100.8 0.6 collective-permute-done.12
  101.4 0.0 collective-permute-done.11
  101.5 0.1 broadcast_in_dim.27
  101.6 12.1 %all_to_all.22.last_ref = f32[8,1,8192]{2,1,0:T(1,128)S(1)} all-to-all(f32[8,1,8192]{2,1,0:T(1,128)S(1)} %broadcast_in_dim.27), channel_id=1, replica_groups=mesh['batch'=8,'proto'=4] {'batch'}, dimensions={0} | all-to-all | bytes 524288 | tf_op jit(solution)/shard_map/all_to_all | solution.py:82
  113.7 11.2 %embed_part.1 = f32[256,256]{1,0:T(8,128)S(1)} custom-call(s32[3]{0:T(128)S(1)} %pad_add_fusion.me_ref, f32[8,1,8192]{2,1,0:T(1,128)S(1)} %all_to_all.22.last_ref, f32[1,2048]{1,0:T(1,128)S(1)} %get-tuple-element.32.f_ref, f32[1,2048]{1,0:T(1,128)S(1)} %get-tuple-element.27.r_ref, f32[1,2048]{1,0:T(1,128)S(1)} %get-tuple-element.33.v_ref, ...), custom_call_target="tpu_custom_call" | custom-call | flops 4294967296 | bytes 8388608 | tf_op jit(solution)/shard_map/embed_part/pallas_call | solution.py:544
  125.0 0.1 collective-permute-start.16
  125.1 0.6 collective-permute-start.15
  125.7 1.2 collective-permute-start.14
  126.9 7.2 %proto_part.1 = f32[2048,256]{1,0:T(8,128)} custom-call(f32[8,1,8192]{2,1,0:T(1,128)S(1)} %all_to_all.22.last_ref, f32[1,2048]{1,0:T(1,128)S(1)} %get-tuple-element.27.r_ref, f32[1,2048]{1,0:T(1,128)S(1)} %get-tuple-element.33.v_ref, f32[2048,128]{1,0:T(8,128)S(1)} %get-tuple-element.24.refs_6_.a_ref, f32[2048,128]{1,0:T(8,128)S(1)} %get-tuple-element.34.h_ref, ...), custom_call_target="tpu_custom_call" | custom-call | flops 2147483648 | bytes 16777216 | tf_op jit(solution)/shard_map/proto_part/pallas_call | solution.py:613
  134.1 0.0 collective-permute-done.16
  134.1 3.4 %collective-permute-done.15 = f32[256,256]{1,0:T(8,128)S(1)} collective-permute-done((f32[256,256]{1,0:T(8,128)S(1)}, f32[256,256]{1,0:T(8,128)S(1)}, u32[]{:S(2)}, u32[]{:S(2)}) %collective-permute-start.15) | collective-permute-done | bytes 262176 | tf_op jit(solution)/shard_map/ppermute | solution.py:67
  137.6 0.0 collective-permute-done.14
  137.6 0.8 add_add_fusion
  (9 shorter events, 0.1 us)
Async XLA Ops:
  18.3 21.8 %all-to-all-start = ((bf16[8,128,256]{2,1,0:T(8,128)(2,1)}), bf16[8,128,256]{2,1,0:T(8,128)(2,1)S(1)}, u32[]{:S(2)}, u32[]{:S(2)}) async-start(bf16[8,128,256]{2,1,0:T(8,128)(2,1)} %half_copies.1), calls=%async_computation | async-start | bytes 1048576 | tf_op jit(solution)/shard_map/all_to_all | solution.py:82
  25.6 50.5 %copy-start = (f32[256]{0:T(256)S(1)}, f32[256]{0:T(256)}, u32[]{:S(2)}) copy-start(f32[256]{0:T(256)} %param.6) | copy-start | bytes 3076
  40.1 10.8 %collective-permute-start = (bf16[8,128,256]{2,1,0:T(8,128)(2,1)S(1)}, bf16[8,128,256]{2,1,0:T(8,128)(2,1)S(1)}, u32[]{:S(2)}, u32[]{:S(2)}) collective-permute-start(bf16[8,128,256]{2,1,0:T(8,128)(2,1)S(1)} %all-to-all-done.mine_ref), channel_id=1, source_target_pairs={{0,1},{1,0},{2,3},{3,2},{4,5},{5,4},{6,7},{7,6},{8,9},{9,8},{10,11... | collective-permute-start | bytes 1572872 | tf_op jit(solution)/shard_map/ppermute | solution.py:635
  62.3 3.1 %collective-permute-start.3 = (f32[1,2048]{1,0:T(1,128)S(1)}, f32[1,2048]{1,0:T(1,128)S(1)}, u32[]{:S(2)}, u32[]{:S(2)}) collective-permute-start(f32[1,2048]{1,0:T(1,128)S(1)} %get-tuple-element.22), channel_id=1, source_target_pairs={{0,3},{1,2},{2,1},{3,0},{4,7},{5,6},{6,5},{7,4},{8,11},{9,10},{10,... | collective-permute-start | bytes 24584 | tf_op jit(solution)/shard_map/ppermute | solution.py:67
  62.6 3.7 %collective-permute-start.2 = (f32[1,2048]{1,0:T(1,128)S(1)}, f32[1,2048]{1,0:T(1,128)S(1)}, u32[]{:S(2)}, u32[]{:S(2)}) collective-permute-start(f32[1,2048]{1,0:T(1,128)S(1)} %get-tuple-element.22), channel_id=1, source_target_pairs={{0,2},{1,3},{2,0},{3,1},{4,6},{5,7},{6,4},{7,5},{8,10},{9,11},{10,... | collective-permute-start | bytes 24584 | tf_op jit(solution)/shard_map/ppermute | solution.py:67
  64.1 2.1 %collective-permute-start.1 = (f32[1,2048]{1,0:T(1,128)S(1)}, f32[1,2048]{1,0:T(1,128)S(1)}, u32[]{:S(2)}, u32[]{:S(2)}) collective-permute-start(f32[1,2048]{1,0:T(1,128)S(1)} %get-tuple-element.22), channel_id=1, source_target_pairs={{0,1},{1,0},{2,3},{3,2},{4,5},{5,4},{6,7},{7,6},{8,9},{9,8},{10,11... | collective-permute-start | bytes 24584 | tf_op jit(solution)/shard_map/ppermute | solution.py:67
  66.3 3.7 %collective-permute-start.4 = (f32[1,2048]{1,0:T(1,128)S(1)}, f32[1,2048]{1,0:T(1,128)S(1)}, u32[]{:S(2)}, u32[]{:S(2)}) collective-permute-start(f32[1,2048]{1,0:T(1,128)S(1)} %add_add_fusion.3), channel_id=1, source_target_pairs={{0,4},{4,0},{8,12},{12,8},{16,20},{20,16},{24,28},{28,24},{1,5},{5... | collective-permute-start | bytes 24584 | tf_op jit(solution)/shard_map/ppermute | solution.py:67
  70.0 5.5 %collective-permute-start.7 = (f32[1,2048]{1,0:T(1,128)S(1)}, f32[1,2048]{1,0:T(1,128)S(1)}, u32[]{:S(2)}, u32[]{:S(2)}) collective-permute-start(f32[1,2048]{1,0:T(1,128)S(1)} %add.47.refs_0_), channel_id=1, source_target_pairs={{0,24},{4,28},{8,16},{12,20},{16,8},{20,12},{24,0},{28,4},{1,25},{... | collective-permute-start | bytes 24584 | tf_op jit(solution)/shard_map/ppermute | solution.py:67
  70.7 4.8 %collective-permute-start.6 = (f32[1,2048]{1,0:T(1,128)S(1)}, f32[1,2048]{1,0:T(1,128)S(1)}, u32[]{:S(2)}, u32[]{:S(2)}) collective-permute-start(f32[1,2048]{1,0:T(1,128)S(1)} %add.47.refs_0_), channel_id=1, source_target_pairs={{0,16},{4,20},{8,24},{12,28},{16,0},{20,4},{24,8},{28,12},{1,17},{... | collective-permute-start | bytes 24584 | tf_op jit(solution)/shard_map/ppermute | solution.py:67
  72.1 4.0 %collective-permute-start.5 = (f32[1,2048]{1,0:T(1,128)S(1)}, f32[1,2048]{1,0:T(1,128)S(1)}, u32[]{:S(2)}, u32[]{:S(2)}) collective-permute-start(f32[1,2048]{1,0:T(1,128)S(1)} %add.47.refs_0_), channel_id=1, source_target_pairs={{0,8},{4,12},{8,0},{12,4},{16,24},{20,28},{24,16},{28,20},{1,9},{5... | collective-permute-start | bytes 24584 | tf_op jit(solution)/shard_map/ppermute | solution.py:67
  80.1 3.1 %collective-permute-start.10 = (f32[1,2048]{1,0:T(1,128)S(1)}, f32[1,2048]{1,0:T(1,128)S(1)}, u32[]{:S(2)}, u32[]{:S(2)}) collective-permute-start(f32[1,2048]{1,0:T(1,128)S(1)} %get-tuple-element.26), channel_id=1, source_target_pairs={{0,3},{1,2},{2,1},{3,0},{4,7},{5,6},{6,5},{7,4},{8,11},{9,10},{10,... | collective-permute-start | bytes 24584 | tf_op jit(solution)/shard_map/ppermute | solution.py:67
  80.2 3.7 %collective-permute-start.9 = (f32[1,2048]{1,0:T(1,128)S(1)}, f32[1,2048]{1,0:T(1,128)S(1)}, u32[]{:S(2)}, u32[]{:S(2)}) collective-permute-start(f32[1,2048]{1,0:T(1,128)S(1)} %get-tuple-element.26), channel_id=1, source_target_pairs={{0,2},{1,3},{2,0},{3,1},{4,6},{5,7},{6,4},{7,5},{8,10},{9,11},{10,... | collective-permute-start | bytes 24584 | tf_op jit(solution)/shard_map/ppermute | solution.py:67
  81.7 2.1 %collective-permute-start.8 = (f32[1,2048]{1,0:T(1,128)S(1)}, f32[1,2048]{1,0:T(1,128)S(1)}, u32[]{:S(2)}, u32[]{:S(2)}) collective-permute-start(f32[1,2048]{1,0:T(1,128)S(1)} %get-tuple-element.26), channel_id=1, source_target_pairs={{0,1},{1,0},{2,3},{3,2},{4,5},{5,4},{6,7},{7,6},{8,9},{9,8},{10,11... | collective-permute-start | bytes 24584 | tf_op jit(solution)/shard_map/ppermute | solution.py:67
  97.6 3.2 %collective-permute-start.13 = (f32[1,2048]{1,0:T(1,128)S(1)}, f32[1,2048]{1,0:T(1,128)S(1)}, u32[]{:S(2)}, u32[]{:S(2)}) collective-permute-start(f32[1,2048]{1,0:T(1,128)S(1)} %get-tuple-element.28), channel_id=1, source_target_pairs={{0,3},{1,2},{2,1},{3,0},{4,7},{5,6},{6,5},{7,4},{8,11},{9,10},{10,... | collective-permute-start | bytes 24584 | tf_op jit(solution)/shard_map/ppermute | solution.py:67
  97.7 3.7 %collective-permute-start.12 = (f32[1,2048]{1,0:T(1,128)S(1)}, f32[1,2048]{1,0:T(1,128)S(1)}, u32[]{:S(2)}, u32[]{:S(2)}) collective-permute-start(f32[1,2048]{1,0:T(1,128)S(1)} %get-tuple-element.28), channel_id=1, source_target_pairs={{0,2},{1,3},{2,0},{3,1},{4,6},{5,7},{6,4},{7,5},{8,10},{9,11},{10,... | collective-permute-start | bytes 24584 | tf_op jit(solution)/shard_map/ppermute | solution.py:67
  99.2 2.2 %collective-permute-start.11 = (f32[1,2048]{1,0:T(1,128)S(1)}, f32[1,2048]{1,0:T(1,128)S(1)}, u32[]{:S(2)}, u32[]{:S(2)}) collective-permute-start(f32[1,2048]{1,0:T(1,128)S(1)} %get-tuple-element.28), channel_id=1, source_target_pairs={{0,1},{1,0},{2,3},{3,2},{4,5},{5,4},{6,7},{7,6},{8,9},{9,8},{10,11... | collective-permute-start | bytes 24584 | tf_op jit(solution)/shard_map/ppermute | solution.py:67
  125.0 9.1 %collective-permute-start.16 = (f32[256,256]{1,0:T(8,128)S(1)}, f32[256,256]{1,0:T(8,128)S(1)}, u32[]{:S(2)}, u32[]{:S(2)}) collective-permute-start(f32[256,256]{1,0:T(8,128)S(1)} %embed_part.1), channel_id=1, source_target_pairs={{0,3},{1,2},{2,1},{3,0},{4,7},{5,6},{6,5},{7,4},{8,11},{9,10},{10,... | collective-permute-start | bytes 786440 | tf_op jit(solution)/shard_map/ppermute | solution.py:67
  125.1 12.5 %collective-permute-start.15 = (f32[256,256]{1,0:T(8,128)S(1)}, f32[256,256]{1,0:T(8,128)S(1)}, u32[]{:S(2)}, u32[]{:S(2)}) collective-permute-start(f32[256,256]{1,0:T(8,128)S(1)} %embed_part.1), channel_id=1, source_target_pairs={{0,2},{1,3},{2,0},{3,1},{4,6},{5,7},{6,4},{7,5},{8,10},{9,11},{10,... | collective-permute-start | bytes 786440 | tf_op jit(solution)/shard_map/ppermute | solution.py:67
  125.7 11.9 %collective-permute-start.14 = (f32[256,256]{1,0:T(8,128)S(1)}, f32[256,256]{1,0:T(8,128)S(1)}, u32[]{:S(2)}, u32[]{:S(2)}) collective-permute-start(f32[256,256]{1,0:T(8,128)S(1)} %embed_part.1), channel_id=1, source_target_pairs={{0,1},{1,0},{2,3},{3,2},{4,5},{5,4},{6,7},{7,6},{8,9},{9,8},{10,11... | collective-permute-start | bytes 786440 | tf_op jit(solution)/shard_map/ppermute | solution.py:67

commit v4 on v3

--- a/solution.py
+++ b/solution.py
@@ -17,7 +17,6 @@
 whole = pl.BlockSpec(memory_space=pltpu.VMEM)
 anywhere = pl.BlockSpec(memory_space=pl.ANY)
 in_smem = pl.BlockSpec(memory_space=pltpu.SMEM)
-kept_products = ((0, 0), (0, 1), (1, 0))
 
 
 def held(shape, dtype=f32, small=True):
@@ -162,68 +161,31 @@
         acc_ref[:, c] = total
 
 
-def split(value):
-    high = value.astype(bf16).astype(f32)
-    return high, value - high
-
-
-def stack_lanes(values):
-    which = lax.broadcasted_iota(jnp.int32, values[0].shape, 1)
-    result = jnp.zeros(values[0].shape, f32)
-    for k, value in enumerate(values):
-        result = jnp.where(which == k, value, result)
-    return result.astype(bf16)
-
-
-def stack_sublanes(values, width):
-    height = -(-len(values) // (2 * sublanes)) * 2 * sublanes
-    pieces = []
-    for start in range(0, height, sublanes):
-        which = lax.broadcasted_iota(jnp.int32, (sublanes, width), 0)
-        result = jnp.zeros((sublanes, width), f32)
-        for k, value in enumerate(values[start : start + sublanes]):
-            result = jnp.where(which == k, value, result)
-        pieces.append(result)
-    return jnp.concatenate(pieces, axis=0).astype(bf16)
-
-
-def left_factors(products, single):
-    values = []
-    for value in products:
-        parts = split(value)
-        values += [parts[a] for a, _ in kept_products]
-    return values + list(split(single))
-
-
-def right_factors(products, single):
-    values = []
-    for value in products:
-        parts = split(value)
-        values += [parts[b] for _, b in kept_products]
-    return values + [single] * 2
-
-
-def half_copies_kernel(me_ref, e_ref, copies_ref, sem):
+def repeated(vector):
+    return jnp.broadcast_to(vector, (sublanes, vector.shape[1]))
+
+
+def by_register(value):
+    return value.reshape(value.shape[0] // sublanes, sublanes, lanes)
+
+
+def half_copies_kernel(me_ref, e_ref, copies_ref):
     copies, half, _ = copies_ref.shape
-    source = e_ref.at[pl.ds(pl.multiple_of(me_ref[1] * half, half), half), :]
-    moves = [pltpu.make_async_copy(source, copies_ref.at[d], sem.at[d]) for d in range(copies)]
-    for move in moves:
-        move.start()
-    for move in moves:
-        move.wait()
+    value = e_ref[pl.ds(pl.multiple_of(me_ref[1] * half, half), half), :]
+    for d in range(copies):
+        copies_ref[d] = value
 
 
 def half_copies(me, embeddings, copies):
     rows, depth = embeddings.shape
     return pl.pallas_call(
         half_copies_kernel,
-        in_specs=[in_smem, anywhere],
-        out_specs=anywhere,
+        in_specs=[in_smem, whole],
+        out_specs=whole,
         out_shape=jax.ShapeDtypeStruct((copies, rows // 2, depth), bf16),
-        scratch_shapes=[pltpu.SemaphoreType.DMA((copies,))],
         compiler_params=beside_plan,
         name="half_copies",
-    )(me, in_hbm(embeddings))
+    )(me, embeddings)
 
 
 def row_lse_kernel(e_ref, p_ref, copies_ref, turned_ref, top_ref, mass_ref):
@@ -497,7 +459,7 @@
 
 
 def embed_kernel(
-    total, me_ref, last_ref, f_ref, r_ref, v_ref, e_ref, p_ref, out_ref, left_ref, right_ref, tall_ref, b_ref
+    total, me_ref, last_ref, f_ref, r_ref, v_ref, e_ref, p_ref, out_ref, tall_ref, cols_ref, s_ref, b_ref
 ):
     step = pl.program_id(0)
     rows, width = b_ref.shape
@@ -505,33 +467,29 @@
     @pl.when(step == 0)
     def _():
         out_ref[...] = jnp.zeros_like(out_ref)
-        right_ref[...] = jnp.zeros_like(right_ref)
         mine = pl.ds(pl.multiple_of(me_ref[0] * rows, rows), rows)
         x = tree(add, [last_ref[d, :, mine] for d in range(last_ref.shape[0])])
         for k, value in enumerate((f_ref[:, mine], r_ref[:, mine], v_ref[:, mine], x)):
             lanes_to_rows(value, tall_ref.at[k])
-        r, v, x = (tall_ref[k] for k in (1, 2, 3))
-        one = jnp.ones_like(r)
-        left_ref[...] = stack_lanes(left_factors([-r, -x, one], -v))
 
     y, lse, a = (last_ref[step, :, total + k * width : total + (k + 1) * width] for k in range(3))
     w = jnp.exp(lse + math.log(total))
-    rows_of = stack_sublanes(right_factors([a, w, y], jnp.ones_like(a)), width)
-    right_ref[0 : rows_of.shape[0], :] = rows_of
+    for k, value in enumerate((lse, a, y, w)):
+        cols_ref[k] = repeated(value)
     e = e_ref[...] * score_scale
-    left = left_ref[...]
-    f = tall_ref[0]
-    sub = min(2 * lanes, width)
-    group = min(4 * sub, width)
-    for c in chunks(width, sub):
-        s = dot_nt(e, p_ref[c, :])
-        bracket = dot_nn(left, right_ref[:, c])
-        t = s - lse[:, c]
-        plan = jnp.concatenate([jnp.exp(t[:, at] + f) for at in chunks(sub)], axis=1)
-        b_ref[:, c] = (plan * bracket).astype(bf16)
-        if c.stop % group == 0:
-            done = slice(c.stop - group, c.stop)
-            out_ref[...] += score_scale * dot_nn(b_ref[:, done], p_ref[done, :])
+    part = min(8 * lanes, width)
+    height = min(4 * sublanes, rows)
+    for span in chunks(width, part):
+        s_ref[:, span] = dot_nt(e, p_ref[span, :])
+        for at in chunks(rows, height):
+            f, r, v, x = (by_register(tall_ref[k, at, :]) for k in range(4))
+            for k in range(part // lanes):
+                c = slice(span.start + k * lanes, span.start + (k + 1) * lanes)
+                lse, a, y, w = (cols_ref[k, :, c] for k in range(4))
+                plan = jnp.exp(by_register(s_ref[at, c]) - lse + f)
+                value = plan * (y - (r * a + v + x * w))
+                b_ref[at, c] = value.reshape(height, lanes).astype(bf16)
+        out_ref[...] += score_scale * dot_nn(b_ref[:, span], p_ref[span, :])
 
 
 def embed_part(me, last, f, r, v, embeddings, prototypes):
@@ -556,9 +514,9 @@
             ],
             out_specs=full((rows, depth)),
             scratch_shapes=[
-                pltpu.VMEM((rows, lanes), bf16),
-                pltpu.VMEM((lanes, width), bf16),
                 pltpu.VMEM((4, rows, lanes), f32),
+                pltpu.VMEM((4, sublanes, width), f32),
+                pltpu.VMEM((rows, width), f32),
                 pltpu.VMEM((rows, width), bf16),
             ],
         ),
@@ -571,21 +529,22 @@
     )(me, last, f, r, v, in_hbm(embeddings), in_hbm(prototypes))
 
 
-def proto_kernel(last_ref, r_ref, v_ref, a_ref, h_ref, z_ref, ay_ref, all_ref, e_ref, out_ref, right_ref, b_ref):
+def proto_kernel(last_ref, r_ref, v_ref, a_ref, h_ref, z_ref, ay_ref, all_ref, e_ref, out_ref, rows_ref, b_ref):
     count, rows = e_ref.shape
     height = b_ref.shape[1]
+    blocks = count // height
     x = tree(add, [last_ref[d, :, 0:rows] for d in range(last_ref.shape[0])])
-    right_ref[...] = jnp.zeros_like(right_ref)
-    rows_of = stack_sublanes(right_factors([-r_ref[...], -v_ref[...], -x], jnp.ones_like(x)), rows)
-    right_ref[0 : rows_of.shape[0], :] = rows_of
-
-    blocks = count // height
+    for k, value in enumerate((r_ref[...], v_ref[...], x)):
+        rows_ref[k] = repeated(value)
 
     def bracket(block, slot):
-        at = pl.ds(pl.multiple_of(block * height, height), height)
-        left = stack_lanes(left_factors([z_ref[at, :], a_ref[at, :], h_ref[at, :]], ay_ref[at, :]))
-        for c in chunks(rows, 2 * lanes):
-            b_ref[slot, :, c] = (e_ref[at, c] * dot_nn(left, right_ref[:, c])).astype(bf16)
+        for inner in chunks(height, min(4 * sublanes, height)):
+            at = pl.ds(pl.multiple_of(block * height, height) + inner.start, inner.stop - inner.start)
+            z, a, h, ay = (by_register(ref[at, :]) for ref in (z_ref, a_ref, h_ref, ay_ref))
+            for c in chunks(rows):
+                r, v, x = (rows_ref[k, :, c] for k in range(3))
+                value = by_register(e_ref[at, c]) * (ay - (r * z + v * a + x * h))
+                b_ref[slot, inner, c] = value.reshape(-1, lanes).astype(bf16)
 
     def product(block, slot):
         at = pl.ds(pl.multiple_of(block * height, height), height)
@@ -609,13 +568,13 @@
 def proto_part(last, r, v, a, h, z, ay, all_rows, e):
     count, rows = e.shape
     depth = all_rows.shape[1]
-    height = min(count, 4 * lanes)
+    height = min(count, 2 * lanes if few(rows) else lanes)
     return pl.pallas_call(
         proto_kernel,
         in_specs=[whole] * 9,
         out_specs=whole,
         out_shape=jax.ShapeDtypeStruct((count, depth), f32),
-        scratch_shapes=[pltpu.VMEM((lanes, rows), bf16), pltpu.VMEM((2, height, rows), bf16)],
+        scratch_shapes=[pltpu.VMEM((3, sublanes, rows), f32), pltpu.VMEM((2, height, rows), bf16)],
         compiler_params=beside_plan,
         cost_estimate=pl.CostEstimate(
             flops=2 * rows * count * depth, bytes_accessed=count * rows * 4, transcendentals=0

time: 139 us -> 124 us (0.89)
  Pallas kernels: 63.3 us -> 48.9 us
  waiting for transfers between devices: 19.7 us -> 18.1 us
    pallas_call x1, Pallas kernels: 17.6 us -> 1.37 us  [half_copies(): pl.pallas_call(half_copies_kernel, in_specs=[in_smem, whole], out_specs=w...]
    pallas_call x1, Pallas kernels: 7.21 us -> 8.79 us  [proto_part(): pl.pallas_call(proto_kernel, in_specs=[whole] * 9, out_specs=whole, out_s...]
    ppermute x16, waiting for transfers between devices: 13.8 us -> 12.3 us  [partners(): lax.ppermute(x, axis, [(i, i ^ d * stride) for i in range(total)])]
  transfers between devices with their start and end apart: 18 -> 18, of which waited for: 11 -> 11; matrix products, arithmetic and copies ran while one was open for 0% -> 0% of each run, Pallas kernels for 11% -> 14%
where the time goes in v4:
time: 124 us; the launch traced here: 123 us
  Pallas kernels  48.9 us (39%)
  blocking collectives  33.4 us (27%)
  starting transfers between devices  20.1 us (16%)
  waiting for transfers between devices  18.1 us (15%)
    all_to_all x3, blocking collectives, swap_copies(): return lax.all_to_all(copies, axis, split_axis=0, concat_axis=0, tiled=True)  33.4 us
    ppermute x16, starting transfers between devices, partners(): lax.ppermute(x, axis, [(i, i ^ d * stride) for i in range(total)])  12.8 us
    ppermute x16, waiting for transfers between devices, partners(): lax.ppermute(x, axis, [(i, i ^ d * stride) for i in range(total)])  12.3 us
    pallas_call x1, Pallas kernels, embed_part(): pl.pallas_call(functools.partial(embed_kernel, total), grid_spec=pltpu.Pr...  11.5 us
    pallas_call x1, Pallas kernels, col_softmax(): pl.pallas_call(functools.partial(col_softmax_kernel, devices // members),...  11.4 us
    pallas_call x1, Pallas kernels, proto_part(): pl.pallas_call(proto_kernel, in_specs=[whole] * 9, out_specs=whole, out_s...  8.79 us
    pallas_call x1, Pallas kernels, row_lse(): pl.pallas_call(row_lse_kernel, grid=(count // width,), in_specs=[pl.Block...  8.61 us
    all_to_all x1, starting transfers between devices, swap_copies(): return lax.all_to_all(copies, axis, split_axis=0, concat_axis=0, tiled=True)  7.25 us
  transfers between devices with their start and end apart: 18, of which 11 were waited for; matrix products, arithmetic and copies ran while one was open for 0% of the time, Pallas kernels for 14%

profile of v4, /device:TPU:0, one launch (start us, length us, event | category | flops | bytes accessed | tf_op | source)
XLA Modules:
  0.0 123.3 jit_solution(12143316772620662116)
XLA Ops:
  0.6 0.1 pad_add_fusion.me_ref
  0.7 0.9 copy-done
  1.6 1.4 %half_copies.1 = bf16[8,128,256]{2,1,0:T(8,128)(2,1)} custom-call(s32[3]{0:T(128)S(1)} %pad_add_fusion.me_ref, bf16[256,256]{1,0:T(8,128)(2,1)S(1)} %copy-done), custom_call_target="tpu_custom_call" | custom-call | tf_op jit(solution)/shard_map/half_copies/pallas_call | solution.py:181
  3.0 7.3 %all-to-all-start = ((bf16[8,128,256]{2,1,0:T(8,128)(2,1)}), bf16[8,128,256]{2,1,0:T(8,128)(2,1)S(1)}, u32[]{:S(2)}, u32[]{:S(2)}) async-start(bf16[8,128,256]{2,1,0:T(8,128)(2,1)} %half_copies.1), calls=%async_computation | async-start | bytes 1048576 | tf_op jit(solution)/shard_map/all_to_all | solution.py:81
  10.3 8.6 %row_lse.1 = f32[32,1,256]{2,1,0:T(1,128)S(1)} custom-call(bf16[256,256]{1,0:T(8,128)(2,1)} %e_ref.5, bf16[16384,256]{1,0:T(8,128)(2,1)} %p_ref.3), custom_call_target="tpu_custom_call" | custom-call | flops 2147483648 | bytes 8388608 | tf_op jit(solution)/shard_map/row_lse/pallas_call | solution.py:225
  18.9 5.9 %all-to-all-done.mine_ref = bf16[8,128,256]{2,1,0:T(8,128)(2,1)S(1)} async-done(((bf16[8,128,256]{2,1,0:T(8,128)(2,1)}), bf16[8,128,256]{2,1,0:T(8,128)(2,1)S(1)}, u32[]{:S(2)}, u32[]{:S(2)}) %all-to-all-start) | async-done | bytes 524320 | tf_op jit(solution)/shard_map/all_to_all | solution.py:81
  24.7 0.0 collective-permute-start
  24.7 10.8 %all_to_all.20.lse_ref = f32[32,1,256]{2,1,0:T(1,128)S(1)} all-to-all(f32[32,1,256]{2,1,0:T(1,128)S(1)} %row_lse.1), channel_id=1, replica_groups=mesh['batch'=8,'proto'=4] {'batch','proto'}, dimensions={0} | all-to-all | bytes 65536 | tf_op jit(solution)/shard_map/all_to_all | solution.py:81
  35.6 0.0 collective-permute-done.other_ref
  35.6 11.4 %col_softmax.1 = (f32[2048,2048]{1,0:T(8,128)S(1)}, f32[1,2048]{1,0:T(1,128)S(1)}, f32[1,2048]{1,0:T(1,128)S(1)}, f32[1,2048]{1,0:T(1,128)S(1)}, bf16[2048,256]{...) custom-call(s32[3]{0:T(128)S(1)} %pad_add_fusion.me_ref, ...), custom_call_target="tpu_custom_call" | custom-call | flops 2147483648 | bytes 16777216 | tf_op jit(solution)/shard_map/col_softmax/pallas_call | solution.py:353
  47.0 0.3 collective-permute-start.3
  47.2 1.6 %collective-permute-start.2 = (f32[1,2048]{1,0:T(1,128)S(1)}, f32[1,2048]{1,0:T(1,128)S(1)}, u32[]{:S(2)}, u32[]{:S(2)}) collective-permute-start(f32[1,2048]{1,0:T(1,128)S(1)} %get-tuple-element.22), channel_id=1, source_target_pairs={{0,2},{1,3},{2,0},{3,1},{4,6},{5,7},{6,4},{7,5},{8,10},{9,11},{10,... | collective-permute-start | bytes 24584 | tf_op jit(solution)/shard_map/ppermute | solution.py:66
  48.8 0.1 collective-permute-start.1
  48.9 1.2 collective-permute-done.3
  50.1 0.8 collective-permute-done.2
  50.9 0.0 collective-permute-done.1
  50.9 0.7 collective-permute-start.4
  51.6 3.0 %collective-permute-done.4 = f32[1,2048]{1,0:T(1,128)S(1)} collective-permute-done((f32[1,2048]{1,0:T(1,128)S(1)}, f32[1,2048]{1,0:T(1,128)S(1)}, u32[]{:S(2)}, u32[]{:S(2)}) %collective-permute-start.4) | collective-permute-done | bytes 8224 | tf_op jit(solution)/shard_map/ppermute | solution.py:66
  54.6 0.7 collective-permute-start.7
  55.3 1.4 %collective-permute-start.6 = (f32[1,2048]{1,0:T(1,128)S(1)}, f32[1,2048]{1,0:T(1,128)S(1)}, u32[]{:S(2)}, u32[]{:S(2)}) collective-permute-start(f32[1,2048]{1,0:T(1,128)S(1)} %add.47.refs_0_), channel_id=1, source_target_pairs={{0,16},{4,20},{8,24},{12,28},{16,0},{20,4},{24,8},{28,12},{1,17},{... | collective-permute-start | bytes 24584 | tf_op jit(solution)/shard_map/ppermute | solution.py:66
  56.8 2.3 %collective-permute-start.5 = (f32[1,2048]{1,0:T(1,128)S(1)}, f32[1,2048]{1,0:T(1,128)S(1)}, u32[]{:S(2)}, u32[]{:S(2)}) collective-permute-start(f32[1,2048]{1,0:T(1,128)S(1)} %add.47.refs_0_), channel_id=1, source_target_pairs={{0,8},{4,12},{8,0},{12,4},{16,24},{20,28},{24,16},{28,20},{1,9},{5... | collective-permute-start | bytes 24584 | tf_op jit(solution)/shard_map/ppermute | solution.py:66
  59.1 1.1 collective-permute-done.7.refs_3_
  60.2 0.0 collective-permute-done.6.refs_2_
  60.2 0.6 collective-permute-done.5.refs_1_
  60.7 4.0 %second_pair.1 = (f32[1,2048]{1,0:T(1,128)S(1)}, f32[1,2048]{1,0:T(1,128)S(1)}, f32[1,2048]{1,0:T(1,128)S(1)}, f32[2048,128]{1,0:T(8,128)S(1)}) custom-call(s32[3]{0:T(128)S(1)} %pad_add_fusion.me_ref, f32[1,2048]{1,0:T(1,128)S(1)} %add.47.refs_0_, f32[1,2048]{1,0:T(1,128)S(1)} %collective-permute-done.5.refs_1_, ...), custom_call_target="tpu_custom_call" | custom-call | flops 16777216 | bytes 16777216 | tf_op jit(solution)/shard_map/second_pair/pallas_call | solution.py:402
  64.7 0.1 collective-permute-start.10
  64.8 1.6 %collective-permute-start.9 = (f32[1,2048]{1,0:T(1,128)S(1)}, f32[1,2048]{1,0:T(1,128)S(1)}, u32[]{:S(2)}, u32[]{:S(2)}) collective-permute-start(f32[1,2048]{1,0:T(1,128)S(1)} %get-tuple-element.26), channel_id=1, source_target_pairs={{0,2},{1,3},{2,0},{3,1},{4,6},{5,7},{6,4},{7,5},{8,10},{9,11},{10,... | collective-permute-start | bytes 24584 | tf_op jit(solution)/shard_map/ppermute | solution.py:66
  66.4 0.2 collective-permute-start.8
  66.7 1.2 collective-permute-done.10
  67.9 0.7 collective-permute-done.9
  68.5 0.0 collective-permute-done.8
  68.6 10.4 %all_to_all.21.bar_ref = f32[8,1,2048]{2,1,0:T(1,128)S(1)} all-to-all(f32[8,1,2048]{2,1,0:T(1,128)S(1)} %broadcast_in_dim.25), channel_id=1, replica_groups=mesh['batch'=8,'proto'=4] {'batch'}, dimensions={0} | all-to-all | bytes 131072 | tf_op jit(solution)/shard_map/all_to_all | solution.py:81
  79.0 3.3 %first_pair.1 = (f32[1,2048]{1,0:T(1,128)S(1)}, f32[1,2048]{1,0:T(1,128)S(1)}, f32[1,2048]{1,0:T(1,128)S(1)}, f32[2048,128]{1,0:T(8,128)S(1)}) custom-call(f32[8,1,2048]{2,1,0:T(1,128)S(1)} %all_to_all.21.bar_ref, f32[1,2048]{1,0:T(1,128)S(1)} %get-tuple-element.27.r_ref, f32[2048,128]{1,0:T(8,128)S(1)} %get-tuple-element.24.refs_6_.a_ref, ...), custom_call_target="tpu_custom_call" | custom-call | flops 16777216 | bytes 16777216 | tf_op jit(solution)/shard_map/first_pair/pallas_call | solution.py:438
  82.3 0.1 collective-permute-start.13
  82.3 1.6 %collective-permute-start.12 = (f32[1,2048]{1,0:T(1,128)S(1)}, f32[1,2048]{1,0:T(1,128)S(1)}, u32[]{:S(2)}, u32[]{:S(2)}) collective-permute-start(f32[1,2048]{1,0:T(1,128)S(1)} %get-tuple-element.28), channel_id=1, source_target_pairs={{0,2},{1,3},{2,0},{3,1},{4,6},{5,7},{6,4},{7,5},{8,10},{9,11},{10,... | collective-permute-start | bytes 24584 | tf_op jit(solution)/shard_map/ppermute | solution.py:66
  83.9 0.3 collective-permute-start.11
  84.2 1.2 %collective-permute-done.13 = f32[1,2048]{1,0:T(1,128)S(1)} collective-permute-done((f32[1,2048]{1,0:T(1,128)S(1)}, f32[1,2048]{1,0:T(1,128)S(1)}, u32[]{:S(2)}, u32[]{:S(2)}) %collective-permute-start.13) | collective-permute-done | bytes 8224 | tf_op jit(solution)/shard_map/ppermute | solution.py:66
  85.4 0.6 collective-permute-done.12
  86.1 0.1 broadcast_in_dim.27
  86.3 12.2 %all_to_all.22.last_ref = f32[8,1,8192]{2,1,0:T(1,128)S(1)} all-to-all(f32[8,1,8192]{2,1,0:T(1,128)S(1)} %broadcast_in_dim.27), channel_id=1, replica_groups=mesh['batch'=8,'proto'=4] {'batch'}, dimensions={0} | all-to-all | bytes 524288 | tf_op jit(solution)/shard_map/all_to_all | solution.py:81
  98.4 11.5 %embed_part.1 = f32[256,256]{1,0:T(8,128)S(1)} custom-call(s32[3]{0:T(128)S(1)} %pad_add_fusion.me_ref, f32[8,1,8192]{2,1,0:T(1,128)S(1)} %all_to_all.22.last_ref, f32[1,2048]{1,0:T(1,128)S(1)} %get-tuple-element.32.f_ref, f32[1,2048]{1,0:T(1,128)S(1)} %get-tuple-element.27.r_ref, f32[1,2048]{1,0:T(1,128)S(1)} %get-tuple-element.33.v_ref, ...), custom_call_target="tpu_custom_call" | custom-call | flops 4294967296 | bytes 8388608 | tf_op jit(solution)/shard_map/embed_part/pallas_call | solution.py:502
  110.0 0.1 collective-permute-start.16
  110.1 0.6 collective-permute-start.15
  110.7 1.2 collective-permute-start.14
  111.9 8.8 %proto_part.1 = f32[2048,256]{1,0:T(8,128)} custom-call(f32[8,1,8192]{2,1,0:T(1,128)S(1)} %all_to_all.22.last_ref, f32[1,2048]{1,0:T(1,128)S(1)} %get-tuple-element.27.r_ref, f32[1,2048]{1,0:T(1,128)S(1)} %get-tuple-element.33.v_ref, f32[2048,128]{1,0:T(8,128)S(1)} %get-tuple-element.24.refs_6_.a_ref, f32[2048,128]{1,0:T(8,128)S(1)} %get-tuple-element.34.h_ref, ...), custom_call_target="tpu_custom_call" | custom-call | flops 2147483648 | bytes 16777216 | tf_op jit(solution)/shard_map/proto_part/pallas_call | solution.py:572
  120.7 0.0 collective-permute-done.16
  120.7 1.8 %collective-permute-done.15 = f32[256,256]{1,0:T(8,128)S(1)} collective-permute-done((f32[256,256]{1,0:T(8,128)S(1)}, f32[256,256]{1,0:T(8,128)S(1)}, u32[]{:S(2)}, u32[]{:S(2)}) %collective-permute-start.15) | collective-permute-done | bytes 262176 | tf_op jit(solution)/shard_map/ppermute | solution.py:66
  122.5 0.8 add_add_fusion
  (11 shorter events, 0.1 us)
Async XLA Ops:
  0.7 0.9 copy-start
  3.0 21.7 %all-to-all-start = ((bf16[8,128,256]{2,1,0:T(8,128)(2,1)}), bf16[8,128,256]{2,1,0:T(8,128)(2,1)S(1)}, u32[]{:S(2)}, u32[]{:S(2)}) async-start(bf16[8,128,256]{2,1,0:T(8,128)(2,1)} %half_copies.1), calls=%async_computation | async-start | bytes 1048576 | tf_op jit(solution)/shard_map/all_to_all | solution.py:81
  10.2 50.5 %copy-start.1 = (f32[256]{0:T(256)S(1)}, f32[256]{0:T(256)}, u32[]{:S(2)}) copy-start(f32[256]{0:T(256)} %param.6) | copy-start | bytes 3076
  24.7 10.8 %collective-permute-start = (bf16[8,128,256]{2,1,0:T(8,128)(2,1)S(1)}, bf16[8,128,256]{2,1,0:T(8,128)(2,1)S(1)}, u32[]{:S(2)}, u32[]{:S(2)}) collective-permute-start(bf16[8,128,256]{2,1,0:T(8,128)(2,1)S(1)} %all-to-all-done.mine_ref), channel_id=1, source_target_pairs={{0,1},{1,0},{2,3},{3,2},{4,5},{5,4},{6,7},{7,6},{8,9},{9,8},{10,11... | collective-permute-start | bytes 1572872 | tf_op jit(solution)/shard_map/ppermute | solution.py:594
  47.0 3.1 %collective-permute-start.3 = (f32[1,2048]{1,0:T(1,128)S(1)}, f32[1,2048]{1,0:T(1,128)S(1)}, u32[]{:S(2)}, u32[]{:S(2)}) collective-permute-start(f32[1,2048]{1,0:T(1,128)S(1)} %get-tuple-element.22), channel_id=1, source_target_pairs={{0,3},{1,2},{2,1},{3,0},{4,7},{5,6},{6,5},{7,4},{8,11},{9,10},{10,... | collective-permute-start | bytes 24584 | tf_op jit(solution)/shard_map/ppermute | solution.py:66
  47.2 3.7 %collective-permute-start.2 = (f32[1,2048]{1,0:T(1,128)S(1)}, f32[1,2048]{1,0:T(1,128)S(1)}, u32[]{:S(2)}, u32[]{:S(2)}) collective-permute-start(f32[1,2048]{1,0:T(1,128)S(1)} %get-tuple-element.22), channel_id=1, source_target_pairs={{0,2},{1,3},{2,0},{3,1},{4,6},{5,7},{6,4},{7,5},{8,10},{9,11},{10,... | collective-permute-start | bytes 24584 | tf_op jit(solution)/shard_map/ppermute | solution.py:66
  48.8 2.1 %collective-permute-start.1 = (f32[1,2048]{1,0:T(1,128)S(1)}, f32[1,2048]{1,0:T(1,128)S(1)}, u32[]{:S(2)}, u32[]{:S(2)}) collective-permute-start(f32[1,2048]{1,0:T(1,128)S(1)} %get-tuple-element.22), channel_id=1, source_target_pairs={{0,1},{1,0},{2,3},{3,2},{4,5},{5,4},{6,7},{7,6},{8,9},{9,8},{10,11... | collective-permute-start | bytes 24584 | tf_op jit(solution)/shard_map/ppermute | solution.py:66
  50.9 3.7 %collective-permute-start.4 = (f32[1,2048]{1,0:T(1,128)S(1)}, f32[1,2048]{1,0:T(1,128)S(1)}, u32[]{:S(2)}, u32[]{:S(2)}) collective-permute-start(f32[1,2048]{1,0:T(1,128)S(1)} %add_add_fusion.3), channel_id=1, source_target_pairs={{0,4},{4,0},{8,12},{12,8},{16,20},{20,16},{24,28},{28,24},{1,5},{5... | collective-permute-start | bytes 24584 | tf_op jit(solution)/shard_map/ppermute | solution.py:66
  54.6 5.5 %collective-permute-start.7 = (f32[1,2048]{1,0:T(1,128)S(1)}, f32[1,2048]{1,0:T(1,128)S(1)}, u32[]{:S(2)}, u32[]{:S(2)}) collective-permute-start(f32[1,2048]{1,0:T(1,128)S(1)} %add.47.refs_0_), channel_id=1, source_target_pairs={{0,24},{4,28},{8,16},{12,20},{16,8},{20,12},{24,0},{28,4},{1,25},{... | collective-permute-start | bytes 24584 | tf_op jit(solution)/shard_map/ppermute | solution.py:66
  55.3 4.8 %collective-permute-start.6 = (f32[1,2048]{1,0:T(1,128)S(1)}, f32[1,2048]{1,0:T(1,128)S(1)}, u32[]{:S(2)}, u32[]{:S(2)}) collective-permute-start(f32[1,2048]{1,0:T(1,128)S(1)} %add.47.refs_0_), channel_id=1, source_target_pairs={{0,16},{4,20},{8,24},{12,28},{16,0},{20,4},{24,8},{28,12},{1,17},{... | collective-permute-start | bytes 24584 | tf_op jit(solution)/shard_map/ppermute | solution.py:66
  56.8 4.0 %collective-permute-start.5 = (f32[1,2048]{1,0:T(1,128)S(1)}, f32[1,2048]{1,0:T(1,128)S(1)}, u32[]{:S(2)}, u32[]{:S(2)}) collective-permute-start(f32[1,2048]{1,0:T(1,128)S(1)} %add.47.refs_0_), channel_id=1, source_target_pairs={{0,8},{4,12},{8,0},{12,4},{16,24},{20,28},{24,16},{28,20},{1,9},{5... | collective-permute-start | bytes 24584 | tf_op jit(solution)/shard_map/ppermute | solution.py:66
  64.7 3.1 %collective-permute-start.10 = (f32[1,2048]{1,0:T(1,128)S(1)}, f32[1,2048]{1,0:T(1,128)S(1)}, u32[]{:S(2)}, u32[]{:S(2)}) collective-permute-start(f32[1,2048]{1,0:T(1,128)S(1)} %get-tuple-element.26), channel_id=1, source_target_pairs={{0,3},{1,2},{2,1},{3,0},{4,7},{5,6},{6,5},{7,4},{8,11},{9,10},{10,... | collective-permute-start | bytes 24584 | tf_op jit(solution)/shard_map/ppermute | solution.py:66
  64.8 3.7 %collective-permute-start.9 = (f32[1,2048]{1,0:T(1,128)S(1)}, f32[1,2048]{1,0:T(1,128)S(1)}, u32[]{:S(2)}, u32[]{:S(2)}) collective-permute-start(f32[1,2048]{1,0:T(1,128)S(1)} %get-tuple-element.26), channel_id=1, source_target_pairs={{0,2},{1,3},{2,0},{3,1},{4,6},{5,7},{6,4},{7,5},{8,10},{9,11},{10,... | collective-permute-start | bytes 24584 | tf_op jit(solution)/shard_map/ppermute | solution.py:66
  66.4 2.1 %collective-permute-start.8 = (f32[1,2048]{1,0:T(1,128)S(1)}, f32[1,2048]{1,0:T(1,128)S(1)}, u32[]{:S(2)}, u32[]{:S(2)}) collective-permute-start(f32[1,2048]{1,0:T(1,128)S(1)} %get-tuple-element.26), channel_id=1, source_target_pairs={{0,1},{1,0},{2,3},{3,2},{4,5},{5,4},{6,7},{7,6},{8,9},{9,8},{10,11... | collective-permute-start | bytes 24584 | tf_op jit(solution)/shard_map/ppermute | solution.py:66
  82.3 3.2 %collective-permute-start.13 = (f32[1,2048]{1,0:T(1,128)S(1)}, f32[1,2048]{1,0:T(1,128)S(1)}, u32[]{:S(2)}, u32[]{:S(2)}) collective-permute-start(f32[1,2048]{1,0:T(1,128)S(1)} %get-tuple-element.28), channel_id=1, source_target_pairs={{0,3},{1,2},{2,1},{3,0},{4,7},{5,6},{6,5},{7,4},{8,11},{9,10},{10,... | collective-permute-start | bytes 24584 | tf_op jit(solution)/shard_map/ppermute | solution.py:66
  82.3 3.7 %collective-permute-start.12 = (f32[1,2048]{1,0:T(1,128)S(1)}, f32[1,2048]{1,0:T(1,128)S(1)}, u32[]{:S(2)}, u32[]{:S(2)}) collective-permute-start(f32[1,2048]{1,0:T(1,128)S(1)} %get-tuple-element.28), channel_id=1, source_target_pairs={{0,2},{1,3},{2,0},{3,1},{4,6},{5,7},{6,4},{7,5},{8,10},{9,11},{10,... | collective-permute-start | bytes 24584 | tf_op jit(solution)/shard_map/ppermute | solution.py:66
  83.9 2.1 %collective-permute-start.11 = (f32[1,2048]{1,0:T(1,128)S(1)}, f32[1,2048]{1,0:T(1,128)S(1)}, u32[]{:S(2)}, u32[]{:S(2)}) collective-permute-start(f32[1,2048]{1,0:T(1,128)S(1)} %get-tuple-element.28), channel_id=1, source_target_pairs={{0,1},{1,0},{2,3},{3,2},{4,5},{5,4},{6,7},{7,6},{8,9},{9,8},{10,11... | collective-permute-start | bytes 24584 | tf_op jit(solution)/shard_map/ppermute | solution.py:66
  110.0 10.7 %collective-permute-start.16 = (f32[256,256]{1,0:T(8,128)S(1)}, f32[256,256]{1,0:T(8,128)S(1)}, u32[]{:S(2)}, u32[]{:S(2)}) collective-permute-start(f32[256,256]{1,0:T(8,128)S(1)} %embed_part.1), channel_id=1, source_target_pairs={{0,3},{1,2},{2,1},{3,0},{4,7},{5,6},{6,5},{7,4},{8,11},{9,10},{10,... | collective-permute-start | bytes 786440 | tf_op jit(solution)/shard_map/ppermute | solution.py:66
  110.1 12.5 %collective-permute-start.15 = (f32[256,256]{1,0:T(8,128)S(1)}, f32[256,256]{1,0:T(8,128)S(1)}, u32[]{:S(2)}, u32[]{:S(2)}) collective-permute-start(f32[256,256]{1,0:T(8,128)S(1)} %embed_part.1), channel_id=1, source_target_pairs={{0,2},{1,3},{2,0},{3,1},{4,6},{5,7},{6,4},{7,5},{8,10},{9,11},{10,... | collective-permute-start | bytes 786440 | tf_op jit(solution)/shard_map/ppermute | solution.py:66
  110.7 11.9 %collective-permute-start.14 = (f32[256,256]{1,0:T(8,128)S(1)}, f32[256,256]{1,0:T(8,128)S(1)}, u32[]{:S(2)}, u32[]{:S(2)}) collective-permute-start(f32[256,256]{1,0:T(8,128)S(1)} %embed_part.1), channel_id=1, source_target_pairs={{0,1},{1,0},{2,3},{3,2},{4,5},{5,4},{6,7},{7,6},{8,9},{9,8},{10,11... | collective-permute-start | bytes 786440 | tf_op jit(solution)/shard_map/ppermute | solution.py:66

commit v5 on v3

--- a/solution.py
+++ b/solution.py
@@ -203,10 +203,13 @@
     return values + [single] * 2
 
 
-def half_copies_kernel(me_ref, e_ref, copies_ref, sem):
+def half_copies_kernel(me_ref, e_ref, copies_ref, half_ref, sem):
     copies, half, _ = copies_ref.shape
     source = e_ref.at[pl.ds(pl.multiple_of(me_ref[1] * half, half), half), :]
-    moves = [pltpu.make_async_copy(source, copies_ref.at[d], sem.at[d]) for d in range(copies)]
+    fetch = pltpu.make_async_copy(source, half_ref, sem.at[copies])
+    fetch.start()
+    fetch.wait()
+    moves = [pltpu.make_async_copy(half_ref, copies_ref.at[d], sem.at[d]) for d in range(copies)]
     for move in moves:
         move.start()
     for move in moves:
@@ -220,46 +223,51 @@
         in_specs=[in_smem, anywhere],
         out_specs=anywhere,
         out_shape=jax.ShapeDtypeStruct((copies, rows // 2, depth), bf16),
-        scratch_shapes=[pltpu.SemaphoreType.DMA((copies,))],
+        scratch_shapes=[pltpu.VMEM((rows // 2, depth), bf16), pltpu.SemaphoreType.DMA((copies + 1,))],
         compiler_params=beside_plan,
         name="half_copies",
     )(me, in_hbm(embeddings))
 
 
-def row_lse_kernel(e_ref, p_ref, copies_ref, turned_ref, top_ref, mass_ref):
+def row_lse_kernel(e_ref, p_ref, copies_ref, s_ref, top_ref, mass_ref):
     step = pl.program_id(0)
-    width = p_ref.shape[0]
-    _, rows = top_ref.shape
+    rows, width = s_ref.shape
 
     @pl.when(step == 0)
     def _():
-        turned_ref[...] = (e_ref[...] * score_scale).T
-        top_ref[...] = jnp.full_like(top_ref, -1e30)
+        top_ref[...] = jnp.full_like(top_ref, -jnp.inf)
         mass_ref[...] = jnp.zeros_like(mass_ref)
 
-    top, mass = top_ref[...], mass_ref[...]
+    top = top_ref[...]
+    e = e_ref[...] * score_scale
     for at in chunks(width, 2 * lanes):
-        t = dot_nn(p_ref[at, :], turned_ref[...])
-        t = t.reshape(t.shape[0] // sublanes, sublanes, rows)
-        new = jnp.maximum(top, jnp.max(t, axis=0))
-        mass = mass * jnp.exp(top - new) + jnp.sum(jnp.exp(t - new[None]), axis=0)
-        top = new
+        s = dot_nt(e, p_ref[at, :])
+        s_ref[:, at] = s
+        top = jnp.maximum(top, jnp.maximum(s[:, :lanes], s[:, lanes:]))
+    mass_ref[...] = mass_ref[...] * jnp.exp(top_ref[...] - top)
     top_ref[...] = top
-    mass_ref[...] = mass
+
+    for g in range(rows // sublanes):
+        at = slice(g * sublanes, (g + 1) * sublanes)
+        new = top_ref[at, :]
+        mass = mass_ref[at, :]
+        for c in chunks(width):
+            mass = mass + jnp.exp(s_ref[at, c] - new)
+        mass_ref[at, :] = mass
 
     @pl.when(step == pl.num_programs(0) - 1)
     def _():
-        peak = jnp.max(top, axis=0, keepdims=True)
-        total = jnp.sum(mass * jnp.exp(top - peak), axis=0, keepdims=True)
-        lse = peak + jnp.log(total)
-        for d in range(copies_ref.shape[0]):
-            copies_ref[d] = lse
-
-
-def row_lse(embeddings, prototypes, copies):
+        peak = lane_total(top_ref[...], jnp.max)
+        mass = lane_total(mass_ref[...] * jnp.exp(top_ref[...] - peak), jnp.sum)
+        top_ref[...] = peak + jnp.log(mass)
+        rows_to_lanes(top_ref, copies_ref.at[0])
+        for d in range(1, copies_ref.shape[0]):
+            copies_ref[d] = copies_ref[0]
+
+
+def row_lse(embeddings, prototypes, copies, width):
     rows, depth = embeddings.shape
     count = prototypes.shape[0]
-    width = min(2048, count)
     return pl.pallas_call(
         row_lse_kernel,
         grid=(count // width,),
@@ -267,12 +275,17 @@
             pl.BlockSpec((rows, depth), lambda s: (0, 0)),
             pl.BlockSpec((width, depth), lambda s: (s, 0)),
         ],
-        out_specs=pl.BlockSpec((copies, 1, rows), lambda s: (0, 0, 0)),
-        out_shape=jax.ShapeDtypeStruct((copies, 1, rows), f32),
+        out_specs=[
+            pl.BlockSpec((copies, 1, rows), lambda s: (0, 0, 0)),
+            pl.BlockSpec((rows, width), lambda s: (0, s)),
+        ],
+        out_shape=[
+            jax.ShapeDtypeStruct((copies, 1, rows), f32),
+            pltpu.HBM((rows, count), f32),
+        ],
         scratch_shapes=[
-            pltpu.VMEM((depth, rows), bf16),
-            pltpu.VMEM((sublanes, rows), f32),
-            pltpu.VMEM((sublanes, rows), f32),
+            pltpu.VMEM((rows, lanes), f32),
+            pltpu.VMEM((rows, lanes), f32),
         ],
         compiler_params=beside_plan,
         cost_estimate=pl.CostEstimate(
@@ -497,7 +510,7 @@
 
 
 def embed_kernel(
-    total, me_ref, last_ref, f_ref, r_ref, v_ref, e_ref, p_ref, out_ref, left_ref, right_ref, tall_ref, b_ref
+    total, me_ref, last_ref, f_ref, r_ref, v_ref, s_ref, p_ref, out_ref, left_ref, right_ref, tall_ref, b_ref
 ):
     step = pl.program_id(0)
     rows, width = b_ref.shape
@@ -518,15 +531,13 @@
     w = jnp.exp(lse + math.log(total))
     rows_of = stack_sublanes(right_factors([a, w, y], jnp.ones_like(a)), width)
     right_ref[0 : rows_of.shape[0], :] = rows_of
-    e = e_ref[...] * score_scale
     left = left_ref[...]
     f = tall_ref[0]
     sub = min(2 * lanes, width)
     group = min(4 * sub, width)
     for c in chunks(width, sub):
-        s = dot_nt(e, p_ref[c, :])
         bracket = dot_nn(left, right_ref[:, c])
-        t = s - lse[:, c]
+        t = s_ref[:, c] - lse[:, c]
         plan = jnp.concatenate([jnp.exp(t[:, at] + f) for at in chunks(sub)], axis=1)
         b_ref[:, c] = (plan * bracket).astype(bf16)
         if c.stop % group == 0:
@@ -534,8 +545,8 @@
             out_ref[...] += score_scale * dot_nn(b_ref[:, done], p_ref[done, :])
 
 
-def embed_part(me, last, f, r, v, embeddings, prototypes):
-    rows, depth = embeddings.shape
+def embed_part(me, last, f, r, v, scores, prototypes):
+    rows, depth = scores.shape[0], prototypes.shape[1]
     members = last.shape[0]
     total = f.shape[1]
     count = prototypes.shape[0]
@@ -551,7 +562,7 @@
                 full(f.shape),
                 full(f.shape),
                 full(f.shape),
-                full((rows, depth)),
+                pl.BlockSpec((rows, width), lambda s, me: (0, s)),
                 pl.BlockSpec((width, depth), lambda s, me: (s, 0)),
             ],
             out_specs=full((rows, depth)),
@@ -568,7 +579,7 @@
             flops=4 * rows * count * depth, bytes_accessed=count * depth * 2, transcendentals=rows * count
         ),
         name="embed_part",
-    )(me, last, f, r, v, in_hbm(embeddings), in_hbm(prototypes))
+    )(me, last, f, r, v, in_hbm(scores), in_hbm(prototypes))
 
 
 def proto_kernel(last_ref, r_ref, v_ref, a_ref, h_ref, z_ref, ay_ref, all_ref, e_ref, out_ref, right_ref, b_ref):
@@ -630,7 +641,7 @@
     me = jnp.stack([member, holder % 2, holder]).astype(jnp.int32)
 
     mine = swap_copies(half_copies(me, embeddings, batch), "batch")
-    lse = row_lse(embeddings, prototypes, batch * proto)
+    lse, scores = row_lse(embeddings, prototypes, batch * proto, prototypes.shape[0] // batch)
     mine, lse = lax.optimization_barrier((mine, lse))
     other = lax.ppermute(mine, "proto", [(i, i ^ 1) for i in range(proto)])
     lse = swap_copies(lse, both)
@@ -640,7 +651,7 @@
     x, v, y, ay = first_pair(bar, r, a, e)
     x = tree(add, partners(x, "proto"))
     last = share(jnp.concatenate([x, y, col_lse, ratio], axis=1), "batch")
-    embed = embed_part(me, last, f, r, v, embeddings, prototypes)
+    embed = embed_part(me, last, f, r, v, scores, prototypes)
     embed_grad = tree(add, partners(embed, "proto"))
     proto_grad = proto_part(last, r, v, a, h, z, ay, all_rows, e)
     return (embed_grad, proto_grad)

time: 139 us -> 127 us (0.914)
  Pallas kernels: 63.3 us -> 54.2 us
  waiting for transfers between devices: 19.7 us -> 13.2 us
    pallas_call x1, Pallas kernels: 17.6 us -> 2.24 us  [half_copies(): pl.pallas_call(half_copies_kernel, in_specs=[in_smem, anywhere], out_spec...]
    pallas_call x1, Pallas kernels: 8.61 us -> 12.9 us  [row_lse(): pl.pallas_call(row_lse_kernel, grid=(count // width,), in_specs=[pl.Block...]
    all_to_all x1, waiting for transfers between devices: 5.86 us -> 1.56 us  [swap_copies(): return lax.all_to_all(copies, axis, split_axis=0, concat_axis=0, tiled=True)]
    ppermute x16, waiting for transfers between devices: 13.8 us -> 11.7 us  [partners(): lax.ppermute(x, axis, [(i, i ^ d * stride) for i in range(total)])]
    pallas_call x1, Pallas kernels: 11.2 us -> 13.2 us  [embed_part(): pl.pallas_call(functools.partial(embed_kernel, total), grid_spec=pltpu.Pr...]
  transfers between devices with their start and end apart: 18 -> 18, of which waited for: 11 -> 10; matrix products, arithmetic and copies ran while one was open for 0% -> 0% of each run, Pallas kernels for 11% -> 16%
where the time goes in v5:
time: 127 us; the launch traced here: 125 us
  Pallas kernels  54.2 us (43%)
  blocking collectives  34.7 us (27%)
  starting transfers between devices  21.3 us (17%)
  waiting for transfers between devices  13.2 us (10%)
    all_to_all x3, blocking collectives, swap_copies(): return lax.all_to_all(copies, axis, split_axis=0, concat_axis=0, tiled=True)  34.7 us
    ppermute x16, starting transfers between devices, partners(): lax.ppermute(x, axis, [(i, i ^ d * stride) for i in range(total)])  14 us
    pallas_call x1, Pallas kernels, embed_part(): pl.pallas_call(functools.partial(embed_kernel, total), grid_spec=pltpu.Pr...  13.2 us
    pallas_call x1, Pallas kernels, row_lse(): pl.pallas_call(row_lse_kernel, grid=(count // width,), in_specs=[pl.Block...  12.9 us
    ppermute x16, waiting for transfers between devices, partners(): lax.ppermute(x, axis, [(i, i ^ d * stride) for i in range(total)])  11.7 us
    pallas_call x1, Pallas kernels, col_softmax(): pl.pallas_call(functools.partial(col_softmax_kernel, devices // members),...  11.4 us
    all_to_all x1, starting transfers between devices, swap_copies(): return lax.all_to_all(copies, axis, split_axis=0, concat_axis=0, tiled=True)  7.26 us
    pallas_call x1, Pallas kernels, proto_part(): pl.pallas_call(proto_kernel, in_specs=[whole] * 9, out_specs=whole, out_s...  7.21 us
  transfers between devices with their start and end apart: 18, of which 10 were waited for; matrix products, arithmetic and copies ran while one was open for 0% of the time, Pallas kernels for 16%

profile of v5, /device:TPU:0, one launch (start us, length us, event | category | flops | bytes accessed | tf_op | source)
XLA Modules:
  0.0 125.3 jit_solution(10826505289454824260)
XLA Ops:
  0.7 0.1 pad_add_fusion.me_ref
  0.7 2.2 %half_copies.1 = bf16[8,128,256]{2,1,0:T(8,128)(2,1)} custom-call(s32[3]{0:T(128)S(1)} %pad_add_fusion.me_ref, bf16[256,256]{1,0:T(8,128)(2,1)} %e_ref.3), custom_call_target="tpu_custom_call" | custom-call | tf_op jit(solution)/shard_map/half_copies/pallas_call | solution.py:221
  3.0 7.3 %all-to-all-start = ((bf16[8,128,256]{2,1,0:T(8,128)(2,1)}), bf16[8,128,256]{2,1,0:T(8,128)(2,1)S(1)}, u32[]{:S(2)}, u32[]{:S(2)}) async-start(bf16[8,128,256]{2,1,0:T(8,128)(2,1)} %half_copies.1), calls=%async_computation | async-start | bytes 1048576 | tf_op jit(solution)/shard_map/all_to_all | solution.py:82
  10.2 12.9 %row_lse.1 = (f32[32,1,256]{2,1,0:T(1,128)S(1)}, f32[256,16384]{1,0:T(8,128)}) custom-call(bf16[256,256]{1,0:T(8,128)(2,1)} %e_ref.3, bf16[16384,256]{1,0:T(8,128)(2,1)} %p_ref.3), custom_call_target="tpu_custom_call" | custom-call | flops 2147483648 | bytes 8388608 | tf_op jit(solution)/shard_map/row_lse/pallas_call | solution.py:271
  23.2 1.6 %all-to-all-done.mine_ref = bf16[8,128,256]{2,1,0:T(8,128)(2,1)S(1)} async-done(((bf16[8,128,256]{2,1,0:T(8,128)(2,1)}), bf16[8,128,256]{2,1,0:T(8,128)(2,1)S(1)}, u32[]{:S(2)}, u32[]{:S(2)}) %all-to-all-start) | async-done | bytes 524320 | tf_op jit(solution)/shard_map/all_to_all | solution.py:82
  24.7 0.0 collective-permute-start
  24.7 11.6 %all_to_all.20.lse_ref = f32[32,1,256]{2,1,0:T(1,128)S(1)} all-to-all(f32[32,1,256]{2,1,0:T(1,128)S(1)} %get-tuple-element.23), channel_id=1, replica_groups=mesh['batch'=8,'proto'=4] {'batch','proto'}, dimensions={0} | all-to-all | bytes 65536 | tf_op jit(solution)/shard_map/all_to_all | solution.py:82
  36.4 0.0 collective-permute-done.other_ref
  36.4 11.4 %col_softmax.1 = (f32[2048,2048]{1,0:T(8,128)S(1)}, f32[1,2048]{1,0:T(1,128)S(1)}, f32[1,2048]{1,0:T(1,128)S(1)}, f32[1,2048]{1,0:T(1,128)S(1)}, bf16[2048,256]{...) custom-call(s32[3]{0:T(128)S(1)} %pad_add_fusion.me_ref, ...), custom_call_target="tpu_custom_call" | custom-call | flops 2147483648 | bytes 16777216 | tf_op jit(solution)/shard_map/col_softmax/pallas_call | solution.py:404
  47.7 0.6 collective-permute-start.2
  48.3 1.0 collective-permute-start.3
  49.3 0.7 collective-permute-start.1
  50.0 1.5 %collective-permute-done.2 = f32[1,2048]{1,0:T(1,128)S(1)} collective-permute-done((f32[1,2048]{1,0:T(1,128)S(1)}, f32[1,2048]{1,0:T(1,128)S(1)}, u32[]{:S(2)}, u32[]{:S(2)}) %collective-permute-start.2) | collective-permute-done | bytes 8224 | tf_op jit(solution)/shard_map/ppermute | solution.py:67
  51.5 0.0 collective-permute-done.3
  51.5 0.0 collective-permute-done.1
  51.5 0.8 collective-permute-start.4
  52.3 3.0 %collective-permute-done.4 = f32[1,2048]{1,0:T(1,128)S(1)} collective-permute-done((f32[1,2048]{1,0:T(1,128)S(1)}, f32[1,2048]{1,0:T(1,128)S(1)}, u32[]{:S(2)}, u32[]{:S(2)}) %collective-permute-start.4) | collective-permute-done | bytes 8224 | tf_op jit(solution)/shard_map/ppermute | solution.py:67
  55.2 0.7 collective-permute-start.5
  55.9 0.6 collective-permute-start.6
  56.5 3.2 %collective-permute-start.7 = (f32[1,2048]{1,0:T(1,128)S(1)}, f32[1,2048]{1,0:T(1,128)S(1)}, u32[]{:S(2)}, u32[]{:S(2)}) collective-permute-start(f32[1,2048]{1,0:T(1,128)S(1)} %add.47.refs_0_), channel_id=1, source_target_pairs={{0,24},{4,28},{8,16},{12,20},{16,8},{20,12},{24,0},{28,4},{1,25},{... | collective-permute-start | bytes 24584 | tf_op jit(solution)/shard_map/ppermute | solution.py:67
  59.7 0.0 collective-permute-done.5.refs_1_
  59.7 0.7 collective-permute-done.6.refs_2_
  60.4 1.5 %collective-permute-done.7.refs_3_ = f32[1,2048]{1,0:T(1,128)S(1)} collective-permute-done((f32[1,2048]{1,0:T(1,128)S(1)}, f32[1,2048]{1,0:T(1,128)S(1)}, u32[]{:S(2)}, u32[]{:S(2)}) %collective-permute-start.7) | collective-permute-done | bytes 8224 | tf_op jit(solution)/shard_map/ppermute | solution.py:67
  61.9 4.0 %second_pair.1 = (f32[1,2048]{1,0:T(1,128)S(1)}, f32[1,2048]{1,0:T(1,128)S(1)}, f32[1,2048]{1,0:T(1,128)S(1)}, f32[2048,128]{1,0:T(8,128)S(1)}) custom-call(s32[3]{0:T(128)S(1)} %pad_add_fusion.me_ref, f32[1,2048]{1,0:T(1,128)S(1)} %add.47.refs_0_, f32[1,2048]{1,0:T(1,128)S(1)} %collective-permute-done.5.refs_1_, ...), custom_call_target="tpu_custom_call" | custom-call | flops 16777216 | bytes 16777216 | tf_op jit(solution)/shard_map/second_pair/pallas_call | solution.py:453
  65.9 1.5 %collective-permute-start.9 = (f32[1,2048]{1,0:T(1,128)S(1)}, f32[1,2048]{1,0:T(1,128)S(1)}, u32[]{:S(2)}, u32[]{:S(2)}) collective-permute-start(f32[1,2048]{1,0:T(1,128)S(1)} %get-tuple-element.29), channel_id=1, source_target_pairs={{0,2},{1,3},{2,0},{3,1},{4,6},{5,7},{6,4},{7,5},{8,10},{9,11},{10,... | collective-permute-start | bytes 24584 | tf_op jit(solution)/shard_map/ppermute | solution.py:67
  67.4 0.0 collective-permute-start.10
  67.5 0.7 collective-permute-start.8
  68.1 1.5 %collective-permute-done.9 = f32[1,2048]{1,0:T(1,128)S(1)} collective-permute-done((f32[1,2048]{1,0:T(1,128)S(1)}, f32[1,2048]{1,0:T(1,128)S(1)}, u32[]{:S(2)}, u32[]{:S(2)}) %collective-permute-start.9) | collective-permute-done | bytes 8224 | tf_op jit(solution)/shard_map/ppermute | solution.py:67
  69.6 0.9 collective-permute-done.10
  70.5 0.0 collective-permute-done.8
  70.6 11.3 %all_to_all.21.bar_ref = f32[8,1,2048]{2,1,0:T(1,128)S(1)} all-to-all(f32[8,1,2048]{2,1,0:T(1,128)S(1)} %broadcast_in_dim.25), channel_id=1, replica_groups=mesh['batch'=8,'proto'=4] {'batch'}, dimensions={0} | all-to-all | bytes 131072 | tf_op jit(solution)/shard_map/all_to_all | solution.py:82
  81.9 3.3 %first_pair.1 = (f32[1,2048]{1,0:T(1,128)S(1)}, f32[1,2048]{1,0:T(1,128)S(1)}, f32[1,2048]{1,0:T(1,128)S(1)}, f32[2048,128]{1,0:T(8,128)S(1)}) custom-call(f32[8,1,2048]{2,1,0:T(1,128)S(1)} %all_to_all.21.bar_ref, f32[1,2048]{1,0:T(1,128)S(1)} %get-tuple-element.30.r_ref, f32[2048,128]{1,0:T(8,128)S(1)} %get-tuple-element.27.refs_6_.a_ref, ...), custom_call_target="tpu_custom_call" | custom-call | flops 16777216 | bytes 16777216 | tf_op jit(solution)/shard_map/first_pair/pallas_call | solution.py:489
  85.1 0.8 collective-permute-start.12
  85.9 0.0 collective-permute-start.13
  85.9 1.4 %collective-permute-start.11 = (f32[1,2048]{1,0:T(1,128)S(1)}, f32[1,2048]{1,0:T(1,128)S(1)}, u32[]{:S(2)}, u32[]{:S(2)}) collective-permute-start(f32[1,2048]{1,0:T(1,128)S(1)} %get-tuple-element.31), channel_id=1, source_target_pairs={{0,1},{1,0},{2,3},{3,2},{4,5},{5,4},{6,7},{7,6},{8,9},{9,8},{10,11... | collective-permute-start | bytes 24584 | tf_op jit(solution)/shard_map/ppermute | solution.py:67
  87.3 1.5 %collective-permute-done.12 = f32[1,2048]{1,0:T(1,128)S(1)} collective-permute-done((f32[1,2048]{1,0:T(1,128)S(1)}, f32[1,2048]{1,0:T(1,128)S(1)}, u32[]{:S(2)}, u32[]{:S(2)}) %collective-permute-start.12) | collective-permute-done | bytes 8224 | tf_op jit(solution)/shard_map/ppermute | solution.py:67
  88.8 0.2 collective-permute-done.13
  89.0 0.0 collective-permute-done.11
  89.1 0.1 broadcast_in_dim.27
  89.2 11.8 %all_to_all.22.last_ref = f32[8,1,8192]{2,1,0:T(1,128)S(1)} all-to-all(f32[8,1,8192]{2,1,0:T(1,128)S(1)} %broadcast_in_dim.27), channel_id=1, replica_groups=mesh['batch'=8,'proto'=4] {'batch'}, dimensions={0} | all-to-all | bytes 524288 | tf_op jit(solution)/shard_map/all_to_all | solution.py:82
  101.0 13.2 %embed_part.1 = f32[256,256]{1,0:T(8,128)S(1)} custom-call(s32[3]{0:T(128)S(1)} %pad_add_fusion.me_ref, f32[8,1,8192]{2,1,0:T(1,128)S(1)} %all_to_all.22.last_ref, f32[1,2048]{1,0:T(1,128)S(1)} %get-tuple-element.35.f_ref, f32[1,2048]{1,0:T(1,128)S(1)} %get-tuple-element.30.r_ref, f32[1,2048]{1,0:T(1,128)S(1)} %get-tuple-element.36.v_ref, ...), custom_call_target="tpu_custom_call" | custom-call | flops 4294967296 | bytes 8388608 | tf_op jit(solution)/shard_map/embed_part/pallas_call | solution.py:555
  114.3 0.7 collective-permute-start.15
  114.9 0.0 collective-permute-start.16
  114.9 1.5 %collective-permute-start.14 = (f32[256,256]{1,0:T(8,128)S(1)}, f32[256,256]{1,0:T(8,128)S(1)}, u32[]{:S(2)}, u32[]{:S(2)}) collective-permute-start(f32[256,256]{1,0:T(8,128)S(1)} %embed_part.1), channel_id=1, source_target_pairs={{0,1},{1,0},{2,3},{3,2},{4,5},{5,4},{6,7},{7,6},{8,9},{9,8},{10,11... | collective-permute-start | bytes 786440 | tf_op jit(solution)/shard_map/ppermute | solution.py:67
  116.5 7.2 %proto_part.1 = f32[2048,256]{1,0:T(8,128)} custom-call(f32[8,1,8192]{2,1,0:T(1,128)S(1)} %all_to_all.22.last_ref, f32[1,2048]{1,0:T(1,128)S(1)} %get-tuple-element.30.r_ref, f32[1,2048]{1,0:T(1,128)S(1)} %get-tuple-element.36.v_ref, f32[2048,128]{1,0:T(8,128)S(1)} %get-tuple-element.27.refs_6_.a_ref, f32[2048,128]{1,0:T(8,128)S(1)} %get-tuple-element.38.h_ref, ...), custom_call_target="tpu_custom_call" | custom-call | flops 2147483648 | bytes 16777216 | tf_op jit(solution)/shard_map/proto_part/pallas_call | solution.py:624
  123.7 0.0 collective-permute-done.15
  123.7 0.9 collective-permute-done.16
  124.6 0.8 add_add_fusion
  (9 shorter events, 0.1 us)
Async XLA Ops:
  0.6 61.3 %copy-start = (f32[256]{0:T(256)S(1)}, f32[256]{0:T(256)}, u32[]{:S(2)}) copy-start(f32[256]{0:T(256)} %param.6) | copy-start | bytes 3076
  3.0 21.8 %all-to-all-start = ((bf16[8,128,256]{2,1,0:T(8,128)(2,1)}), bf16[8,128,256]{2,1,0:T(8,128)(2,1)S(1)}, u32[]{:S(2)}, u32[]{:S(2)}) async-start(bf16[8,128,256]{2,1,0:T(8,128)(2,1)} %half_copies.1), calls=%async_computation | async-start | bytes 1048576 | tf_op jit(solution)/shard_map/all_to_all | solution.py:82
  24.7 11.6 %collective-permute-start = (bf16[8,128,256]{2,1,0:T(8,128)(2,1)S(1)}, bf16[8,128,256]{2,1,0:T(8,128)(2,1)S(1)}, u32[]{:S(2)}, u32[]{:S(2)}) collective-permute-start(bf16[8,128,256]{2,1,0:T(8,128)(2,1)S(1)} %all-to-all-done.mine_ref), channel_id=1, source_target_pairs={{0,1},{1,0},{2,3},{3,2},{4,5},{5,4},{6,7},{7,6},{8,9},{9,8},{10,11... | collective-permute-start | bytes 1572872 | tf_op jit(solution)/shard_map/ppermute | solution.py:646
  47.7 3.7 %collective-permute-start.2 = (f32[1,2048]{1,0:T(1,128)S(1)}, f32[1,2048]{1,0:T(1,128)S(1)}, u32[]{:S(2)}, u32[]{:S(2)}) collective-permute-start(f32[1,2048]{1,0:T(1,128)S(1)} %get-tuple-element.25), channel_id=1, source_target_pairs={{0,2},{1,3},{2,0},{3,1},{4,6},{5,7},{6,4},{7,5},{8,10},{9,11},{10,... | collective-permute-start | bytes 24584 | tf_op jit(solution)/shard_map/ppermute | solution.py:67
  48.3 3.2 %collective-permute-start.3 = (f32[1,2048]{1,0:T(1,128)S(1)}, f32[1,2048]{1,0:T(1,128)S(1)}, u32[]{:S(2)}, u32[]{:S(2)}) collective-permute-start(f32[1,2048]{1,0:T(1,128)S(1)} %get-tuple-element.25), channel_id=1, source_target_pairs={{0,3},{1,2},{2,1},{3,0},{4,7},{5,6},{6,5},{7,4},{8,11},{9,10},{10,... | collective-permute-start | bytes 24584 | tf_op jit(solution)/shard_map/ppermute | solution.py:67
  49.3 2.2 %collective-permute-start.1 = (f32[1,2048]{1,0:T(1,128)S(1)}, f32[1,2048]{1,0:T(1,128)S(1)}, u32[]{:S(2)}, u32[]{:S(2)}) collective-permute-start(f32[1,2048]{1,0:T(1,128)S(1)} %get-tuple-element.25), channel_id=1, source_target_pairs={{0,1},{1,0},{2,3},{3,2},{4,5},{5,4},{6,7},{7,6},{8,9},{9,8},{10,11... | collective-permute-start | bytes 24584 | tf_op jit(solution)/shard_map/ppermute | solution.py:67
  51.5 3.7 %collective-permute-start.4 = (f32[1,2048]{1,0:T(1,128)S(1)}, f32[1,2048]{1,0:T(1,128)S(1)}, u32[]{:S(2)}, u32[]{:S(2)}) collective-permute-start(f32[1,2048]{1,0:T(1,128)S(1)} %add_add_fusion.3), channel_id=1, source_target_pairs={{0,4},{4,0},{8,12},{12,8},{16,20},{20,16},{24,28},{28,24},{1,5},{5... | collective-permute-start | bytes 24584 | tf_op jit(solution)/shard_map/ppermute | solution.py:67
  55.2 4.5 %collective-permute-start.5 = (f32[1,2048]{1,0:T(1,128)S(1)}, f32[1,2048]{1,0:T(1,128)S(1)}, u32[]{:S(2)}, u32[]{:S(2)}) collective-permute-start(f32[1,2048]{1,0:T(1,128)S(1)} %add.47.refs_0_), channel_id=1, source_target_pairs={{0,8},{4,12},{8,0},{12,4},{16,24},{20,28},{24,16},{28,20},{1,9},{5... | collective-permute-start | bytes 24584 | tf_op jit(solution)/shard_map/ppermute | solution.py:67
  55.9 4.5 %collective-permute-start.6 = (f32[1,2048]{1,0:T(1,128)S(1)}, f32[1,2048]{1,0:T(1,128)S(1)}, u32[]{:S(2)}, u32[]{:S(2)}) collective-permute-start(f32[1,2048]{1,0:T(1,128)S(1)} %add.47.refs_0_), channel_id=1, source_target_pairs={{0,16},{4,20},{8,24},{12,28},{16,0},{20,4},{24,8},{28,12},{1,17},{... | collective-permute-start | bytes 24584 | tf_op jit(solution)/shard_map/ppermute | solution.py:67
  56.5 5.4 %collective-permute-start.7 = (f32[1,2048]{1,0:T(1,128)S(1)}, f32[1,2048]{1,0:T(1,128)S(1)}, u32[]{:S(2)}, u32[]{:S(2)}) collective-permute-start(f32[1,2048]{1,0:T(1,128)S(1)} %add.47.refs_0_), channel_id=1, source_target_pairs={{0,24},{4,28},{8,16},{12,20},{16,8},{20,12},{24,0},{28,4},{1,25},{... | collective-permute-start | bytes 24584 | tf_op jit(solution)/shard_map/ppermute | solution.py:67
  65.9 3.7 %collective-permute-start.9 = (f32[1,2048]{1,0:T(1,128)S(1)}, f32[1,2048]{1,0:T(1,128)S(1)}, u32[]{:S(2)}, u32[]{:S(2)}) collective-permute-start(f32[1,2048]{1,0:T(1,128)S(1)} %get-tuple-element.29), channel_id=1, source_target_pairs={{0,2},{1,3},{2,0},{3,1},{4,6},{5,7},{6,4},{7,5},{8,10},{9,11},{10,... | collective-permute-start | bytes 24584 | tf_op jit(solution)/shard_map/ppermute | solution.py:67
  67.4 3.1 %collective-permute-start.10 = (f32[1,2048]{1,0:T(1,128)S(1)}, f32[1,2048]{1,0:T(1,128)S(1)}, u32[]{:S(2)}, u32[]{:S(2)}) collective-permute-start(f32[1,2048]{1,0:T(1,128)S(1)} %get-tuple-element.29), channel_id=1, source_target_pairs={{0,3},{1,2},{2,1},{3,0},{4,7},{5,6},{6,5},{7,4},{8,11},{9,10},{10,... | collective-permute-start | bytes 24584 | tf_op jit(solution)/shard_map/ppermute | solution.py:67
  67.5 3.1 %collective-permute-start.8 = (f32[1,2048]{1,0:T(1,128)S(1)}, f32[1,2048]{1,0:T(1,128)S(1)}, u32[]{:S(2)}, u32[]{:S(2)}) collective-permute-start(f32[1,2048]{1,0:T(1,128)S(1)} %get-tuple-element.29), channel_id=1, source_target_pairs={{0,1},{1,0},{2,3},{3,2},{4,5},{5,4},{6,7},{7,6},{8,9},{9,8},{10,11... | collective-permute-start | bytes 24584 | tf_op jit(solution)/shard_map/ppermute | solution.py:67
  85.1 3.7 %collective-permute-start.12 = (f32[1,2048]{1,0:T(1,128)S(1)}, f32[1,2048]{1,0:T(1,128)S(1)}, u32[]{:S(2)}, u32[]{:S(2)}) collective-permute-start(f32[1,2048]{1,0:T(1,128)S(1)} %get-tuple-element.31), channel_id=1, source_target_pairs={{0,2},{1,3},{2,0},{3,1},{4,6},{5,7},{6,4},{7,5},{8,10},{9,11},{10,... | collective-permute-start | bytes 24584 | tf_op jit(solution)/shard_map/ppermute | solution.py:67
  85.9 3.1 %collective-permute-start.13 = (f32[1,2048]{1,0:T(1,128)S(1)}, f32[1,2048]{1,0:T(1,128)S(1)}, u32[]{:S(2)}, u32[]{:S(2)}) collective-permute-start(f32[1,2048]{1,0:T(1,128)S(1)} %get-tuple-element.31), channel_id=1, source_target_pairs={{0,3},{1,2},{2,1},{3,0},{4,7},{5,6},{6,5},{7,4},{8,11},{9,10},{10,... | collective-permute-start | bytes 24584 | tf_op jit(solution)/shard_map/ppermute | solution.py:67
  85.9 3.1 %collective-permute-start.11 = (f32[1,2048]{1,0:T(1,128)S(1)}, f32[1,2048]{1,0:T(1,128)S(1)}, u32[]{:S(2)}, u32[]{:S(2)}) collective-permute-start(f32[1,2048]{1,0:T(1,128)S(1)} %get-tuple-element.31), channel_id=1, source_target_pairs={{0,1},{1,0},{2,3},{3,2},{4,5},{5,4},{6,7},{7,6},{8,9},{9,8},{10,11... | collective-permute-start | bytes 24584 | tf_op jit(solution)/shard_map/ppermute | solution.py:67
  114.3 9.4 %collective-permute-start.15 = (f32[256,256]{1,0:T(8,128)S(1)}, f32[256,256]{1,0:T(8,128)S(1)}, u32[]{:S(2)}, u32[]{:S(2)}) collective-permute-start(f32[256,256]{1,0:T(8,128)S(1)} %embed_part.1), channel_id=1, source_target_pairs={{0,2},{1,3},{2,0},{3,1},{4,6},{5,7},{6,4},{7,5},{8,10},{9,11},{10,... | collective-permute-start | bytes 786440 | tf_op jit(solution)/shard_map/ppermute | solution.py:67
  114.9 9.6 %collective-permute-start.16 = (f32[256,256]{1,0:T(8,128)S(1)}, f32[256,256]{1,0:T(8,128)S(1)}, u32[]{:S(2)}, u32[]{:S(2)}) collective-permute-start(f32[256,256]{1,0:T(8,128)S(1)} %embed_part.1), channel_id=1, source_target_pairs={{0,3},{1,2},{2,1},{3,0},{4,7},{5,6},{6,5},{7,4},{8,11},{9,10},{10,... | collective-permute-start | bytes 786440 | tf_op jit(solution)/shard_map/ppermute | solution.py:67
  114.9 9.6 %collective-permute-start.14 = (f32[256,256]{1,0:T(8,128)S(1)}, f32[256,256]{1,0:T(8,128)S(1)}, u32[]{:S(2)}, u32[]{:S(2)}) collective-permute-start(f32[256,256]{1,0:T(8,128)S(1)} %embed_part.1), channel_id=1, source_target_pairs={{0,1},{1,0},{2,3},{3,2},{4,5},{5,4},{6,7},{7,6},{8,9},{9,8},{10,11... | collective-permute-start | bytes 786440 | tf_op jit(solution)/shard_map/ppermute | solution.py:67

commit v6 on v3

--- a/solution.py
+++ b/solution.py
@@ -126,6 +126,22 @@
     return lax.fori_loop(0, count // height, tile, carry)
 
 
+def in_two_slots(blocks, work):
+    work((0, 0), None)
+    if blocks == 1:
+        work(None, (0, 0))
+        return
+
+    def pair(index, carry):
+        work((2 * index + 1, 1), (2 * index, 0))
+        work((2 * index + 2, 0), (2 * index + 1, 1))
+        return carry
+
+    lax.fori_loop(0, blocks // 2 - 1, pair, 0)
+    work((blocks - 1, 1), (blocks - 2, 0))
+    work(None, (blocks - 1, 1))
+
+
 def sum_rows(ref):
     return tree(add, [ref[d] for d in range(ref.shape[0])])
 
@@ -201,29 +217,6 @@
         parts = split(value)
         values += [parts[b] for _, b in kept_products]
     return values + [single] * 2
-
-
-def half_copies_kernel(me_ref, e_ref, copies_ref, sem):
-    copies, half, _ = copies_ref.shape
-    source = e_ref.at[pl.ds(pl.multiple_of(me_ref[1] * half, half), half), :]
-    moves = [pltpu.make_async_copy(source, copies_ref.at[d], sem.at[d]) for d in range(copies)]
-    for move in moves:
-        move.start()
-    for move in moves:
-        move.wait()
-
-
-def half_copies(me, embeddings, copies):
-    rows, depth = embeddings.shape
-    return pl.pallas_call(
-        half_copies_kernel,
-        in_specs=[in_smem, anywhere],
-        out_specs=anywhere,
-        out_shape=jax.ShapeDtypeStruct((copies, rows // 2, depth), bf16),
-        scratch_shapes=[pltpu.SemaphoreType.DMA((copies,))],
-        compiler_params=beside_plan,
-        name="half_copies",
-    )(me, in_hbm(embeddings))
 
 
 def row_lse_kernel(e_ref, p_ref, copies_ref, turned_ref, top_ref, mass_ref):
@@ -334,42 +327,38 @@
     height = t_ref.shape[1]
     blocks = count // height
 
-    def scores(block, slot):
-        p = p_ref[pl.ds(pl.multiple_of(block * height, height), height), :]
+    def rows_of(block):
+        return pl.ds(pl.multiple_of(block * height, height), height)
+
+    def work(ahead, block):
+        spans = chunks(rows, 2 * lanes)
+        total = height // sublanes
         part = None
-        for c in chunks(rows, 2 * lanes):
-            t = dot_nn(p, turned_ref[:, c]) + f_ref[:, c]
-            t_ref[slot, :, c] = t
-            here = jnp.maximum(t[:, :lanes], t[:, lanes:])
-            part = here if part is None else jnp.maximum(part, here)
-        a_ref[pl.ds(pl.multiple_of(block * height, height), height), :] = lane_total(part, jnp.max)
-
-    def exponent(block, slot):
-        for g in range(height // sublanes):
-            at = pl.ds(pl.multiple_of(block * height, height) + g * sublanes, sublanes)
-            inner = slice(g * sublanes, (g + 1) * sublanes)
-            top = a_ref[at, :]
-            mass = jnp.zeros((sublanes, lanes), f32)
-            for c in chunks(rows):
-                e = jnp.exp(t_ref[slot, inner, c] - top)
-                e_ref[at, c] = e
-                mass = mass + e
-            part_ref[at, :] = mass
-
-    if blocks == 1:
-        scores(0, 0)
-        exponent(0, 0)
-    else:
-        scores(0, 0)
-
-        def pair(index, carry):
-            scores(2 * index + 1, 1)
-            exponent(2 * index, 0)
-            scores(jnp.minimum(2 * index + 2, blocks - 1), 0)
-            exponent(2 * index + 1, 1)
-            return carry
-
-        lax.fori_loop(0, blocks // 2, pair, 0)
+        for k, c in enumerate(spans):
+            if ahead is not None:
+                number, slot = ahead
+                t = dot_nn(p_ref[rows_of(number), :], turned_ref[:, c]) + f_ref[:, c]
+                t_ref[slot, :, c] = t
+                here = jnp.maximum(t[:, :lanes], t[:, lanes:])
+                part = here if part is None else jnp.maximum(part, here)
+            if block is not None:
+                for g in range(k * total // len(spans), (k + 1) * total // len(spans)):
+                    exponent(*block, g)
+        if ahead is not None:
+            a_ref[rows_of(ahead[0]), :] = lane_total(part, jnp.max)
+
+    def exponent(number, slot, g):
+        at = pl.ds(pl.multiple_of(number * height, height) + g * sublanes, sublanes)
+        inner = slice(g * sublanes, (g + 1) * sublanes)
+        top = a_ref[at, :]
+        mass = jnp.zeros((sublanes, lanes), f32)
+        for c in chunks(rows):
+            e = jnp.exp(t_ref[slot, inner, c] - top)
+            e_ref[at, c] = e
+            mass = mass + e
+        part_ref[at, :] = mass
+
+    in_two_slots(blocks, work)
     top = a_ref[...]
     h_ref[...] = jnp.exp(top + math.log(rows))
     mass = lane_total(part_ref[...], jnp.sum)
@@ -523,9 +512,16 @@
     f = tall_ref[0]
     sub = min(2 * lanes, width)
     group = min(4 * sub, width)
-    for c in chunks(width, sub):
-        s = dot_nt(e, p_ref[c, :])
-        bracket = dot_nn(left, right_ref[:, c])
+    spans = chunks(width, sub)
+
+    def dots(c):
+        return dot_nt(e, p_ref[c, :]), dot_nn(left, right_ref[:, c])
+
+    ahead = dots(spans[0])
+    for k, c in enumerate(spans):
+        s, bracket = ahead
+        if k + 1 < len(spans):
+            ahead = dots(spans[k + 1])
         t = s - lse[:, c]
         plan = jnp.concatenate([jnp.exp(t[:, at] + f) for at in chunks(sub)], axis=1)
         b_ref[:, c] = (plan * bracket).astype(bf16)
@@ -581,35 +577,31 @@
 
     blocks = count // height
 
-    def bracket(block, slot):
-        at = pl.ds(pl.multiple_of(block * height, height), height)
-        left = stack_lanes(left_factors([z_ref[at, :], a_ref[at, :], h_ref[at, :]], ay_ref[at, :]))
-        for c in chunks(rows, 2 * lanes):
-            b_ref[slot, :, c] = (e_ref[at, c] * dot_nn(left, right_ref[:, c])).astype(bf16)
-
-    def product(block, slot):
-        at = pl.ds(pl.multiple_of(block * height, height), height)
-        out_ref[at, :] = score_scale * dot_nn(b_ref[slot], all_ref[...])
-
-    bracket(0, 0)
-    if blocks == 1:
-        product(0, 0)
-    else:
-
-        def pair(index, carry):
-            bracket(2 * index + 1, 1)
-            product(2 * index, 0)
-            bracket(jnp.minimum(2 * index + 2, blocks - 1), 0)
-            product(2 * index + 1, 1)
-            return carry
-
-        lax.fori_loop(0, blocks // 2, pair, 0)
+    def rows_of(block):
+        return pl.ds(pl.multiple_of(block * height, height), height)
+
+    def work(ahead, block):
+        spans = chunks(rows, 2 * lanes)
+        if ahead is not None:
+            at = rows_of(ahead[0])
+            left = stack_lanes(left_factors([z_ref[at, :], a_ref[at, :], h_ref[at, :]], ay_ref[at, :]))
+        parts = chunks(height, height // 2)
+        for k, c in enumerate(spans):
+            if ahead is not None:
+                b_ref[ahead[1], :, c] = (e_ref[at, c] * dot_nn(left, right_ref[:, c])).astype(bf16)
+            if block is not None and (k + 1) % (len(spans) // 2) == 0:
+                part = parts[(k + 1) // (len(spans) // 2) - 1]
+                number, slot = block
+                here = pl.ds(pl.multiple_of(number * height, height) + part.start, height // 2)
+                out_ref[here, :] = score_scale * dot_nn(b_ref[slot, part, :], all_ref[...])
+
+    in_two_slots(blocks, work)
 
 
 def proto_part(last, r, v, a, h, z, ay, all_rows, e):
     count, rows = e.shape
     depth = all_rows.shape[1]
-    height = min(count, 4 * lanes)
+    height = min(count, 2 * lanes)
     return pl.pallas_call(
         proto_kernel,
         in_specs=[whole] * 9,
@@ -629,9 +621,11 @@
     member, holder = lax.axis_index("batch"), lax.axis_index("proto")
     me = jnp.stack([member, holder % 2, holder]).astype(jnp.int32)
 
-    mine = swap_copies(half_copies(me, embeddings, batch), "batch")
+    short = embeddings.shape[0] // 2
+    half = lax.dynamic_slice_in_dim(embeddings, (holder % 2) * short, short, axis=0)
+    mine = share(half, "batch")
     lse = row_lse(embeddings, prototypes, batch * proto)
-    mine, lse = lax.optimization_barrier((mine, lse))
+    mine, lse, me = lax.optimization_barrier((mine, lse, me))
     other = lax.ppermute(mine, "proto", [(i, i ^ 1) for i in range(proto)])
     lse = swap_copies(lse, both)
     e, rho, col_lse, f, all_rows, a, h, cot = col_softmax(me, lse, mine, other, prototypes, col_cot[None, :])

time: 139 us -> 123 us (0.88)
  Pallas kernels: 63.3 us -> 45.2 us
  local copies, waits for them, and re-layouts: 0.18 us -> 1.85 us
    pallas_call x1 -> x0, Pallas kernels: 17.6 us -> none  [half_copies(): pl.pallas_call(half_copies_kernel, in_specs=[in_smem, anywhere], out_spec...]
  transfers between devices with their start and end apart: 18 -> 18, of which waited for: 11 -> 11; matrix products, arithmetic and copies ran while one was open for 0% -> 0% of each run, Pallas kernels for 11% -> 13%
where the time goes in v6:
time: 123 us; the launch traced here: 122 us
  Pallas kernels  45.2 us (37%)
  blocking collectives  33.4 us (27%)
  starting transfers between devices  20.1 us (16%)
  waiting for transfers between devices  19.8 us (16%)
  local copies, waits for them, and re-layouts  1.85 us (2%)
    all_to_all x3, blocking collectives, swap_copies(): return lax.all_to_all(copies, axis, split_axis=0, concat_axis=0, tiled=True)  33.4 us
    ppermute x16, waiting for transfers between devices, partners(): lax.ppermute(x, axis, [(i, i ^ d * stride) for i in range(total)])  14 us
    ppermute x16, starting transfers between devices, partners(): lax.ppermute(x, axis, [(i, i ^ d * stride) for i in range(total)])  12.9 us
    pallas_call x1, Pallas kernels, embed_part(): pl.pallas_call(functools.partial(embed_kernel, total), grid_spec=pltpu.Pr...  11.3 us
    pallas_call x1, Pallas kernels, col_softmax(): pl.pallas_call(functools.partial(col_softmax_kernel, devices // members),...  11 us
    pallas_call x1, Pallas kernels, row_lse(): pl.pallas_call(row_lse_kernel, grid=(count // width,), in_specs=[pl.Block...  8.61 us
    all_to_all x1, starting transfers between devices, swap_copies(): return lax.all_to_all(copies, axis, split_axis=0, concat_axis=0, tiled=True)  7.25 us
    pallas_call x1, Pallas kernels, proto_part(): pl.pallas_call(proto_kernel, in_specs=[whole] * 9, out_specs=whole, out_s...  7.03 us
  transfers between devices with their start and end apart: 18, of which 11 were waited for; matrix products, arithmetic and copies ran while one was open for 0% of the time, Pallas kernels for 13%

profile of v6, /device:TPU:0, one launch (start us, length us, event | category | flops | bytes accessed | tf_op | source)
XLA Modules:
  0.0 122.0 jit_solution(2040373033229441352)
XLA Ops:
  0.6 0.8 constant_dynamic-slice_fusion
  1.5 0.8 broadcast_in_dim.28
  2.3 7.3 %all-to-all-start = ((bf16[8,128,256]{2,1,0:T(8,128)(2,1)}), bf16[8,128,256]{2,1,0:T(8,128)(2,1)S(1)}, u32[]{:S(2)}, u32[]{:S(2)}) async-start(bf16[8,128,256]{2,1,0:T(8,128)(2,1)} %broadcast_in_dim.28), calls=%async_computation | async-start | bytes 1048576 | tf_op jit(solution)/shard_map/all_to_all | solution.py:82
  9.6 0.1 pad_add_fusion.me_ref
  9.7 8.6 %row_lse.1 = f32[32,1,256]{2,1,0:T(1,128)S(1)} custom-call(bf16[256,256]{1,0:T(8,128)(2,1)} %e_ref.3, bf16[16384,256]{1,0:T(8,128)(2,1)} %p_ref.3), custom_call_target="tpu_custom_call" | custom-call | flops 2147483648 | bytes 8388608 | tf_op jit(solution)/shard_map/row_lse/pallas_call | solution.py:256
  18.3 5.8 %all-to-all-done.mine_ref = bf16[8,128,256]{2,1,0:T(8,128)(2,1)S(1)} async-done(((bf16[8,128,256]{2,1,0:T(8,128)(2,1)}), bf16[8,128,256]{2,1,0:T(8,128)(2,1)S(1)}, u32[]{:S(2)}, u32[]{:S(2)}) %all-to-all-start) | async-done | bytes 524320 | tf_op jit(solution)/shard_map/all_to_all | solution.py:82
  24.1 0.0 collective-permute-start
  24.1 10.8 %all_to_all.20.lse_ref = f32[32,1,256]{2,1,0:T(1,128)S(1)} all-to-all(f32[32,1,256]{2,1,0:T(1,128)S(1)} %row_lse.1), channel_id=1, replica_groups=mesh['batch'=8,'proto'=4] {'batch','proto'}, dimensions={0} | all-to-all | bytes 65536 | tf_op jit(solution)/shard_map/all_to_all | solution.py:82
  34.9 0.0 collective-permute-done.other_ref
  34.9 11.0 %col_softmax.1 = (f32[2048,2048]{1,0:T(8,128)S(1)}, f32[1,2048]{1,0:T(1,128)S(1)}, f32[1,2048]{1,0:T(1,128)S(1)}, f32[1,2048]{1,0:T(1,128)S(1)}, bf16[2048,256]{...) custom-call(s32[3]{0:T(128)S(1)} %pad_add_fusion.me_ref, ...), custom_call_target="tpu_custom_call" | custom-call | flops 2147483648 | bytes 16777216 | tf_op jit(solution)/shard_map/col_softmax/pallas_call | solution.py:380
  45.9 0.3 collective-permute-start.3
  46.2 1.5 %collective-permute-start.2 = (f32[1,2048]{1,0:T(1,128)S(1)}, f32[1,2048]{1,0:T(1,128)S(1)}, u32[]{:S(2)}, u32[]{:S(2)}) collective-permute-start(f32[1,2048]{1,0:T(1,128)S(1)} %get-tuple-element.24), channel_id=1, source_target_pairs={{0,2},{1,3},{2,0},{3,1},{4,6},{5,7},{6,4},{7,5},{8,10},{9,11},{10,... | collective-permute-start | bytes 24584 | tf_op jit(solution)/shard_map/ppermute | solution.py:67
  47.7 0.1 collective-permute-start.1
  47.9 1.2 collective-permute-done.3
  49.1 0.8 collective-permute-done.2
  49.9 0.0 collective-permute-done.1
  49.9 0.7 collective-permute-start.4
  50.6 3.0 %collective-permute-done.4 = f32[1,2048]{1,0:T(1,128)S(1)} collective-permute-done((f32[1,2048]{1,0:T(1,128)S(1)}, f32[1,2048]{1,0:T(1,128)S(1)}, u32[]{:S(2)}, u32[]{:S(2)}) %collective-permute-start.4) | collective-permute-done | bytes 8224 | tf_op jit(solution)/shard_map/ppermute | solution.py:67
  53.6 0.7 collective-permute-start.7
  54.3 1.4 %collective-permute-start.6 = (f32[1,2048]{1,0:T(1,128)S(1)}, f32[1,2048]{1,0:T(1,128)S(1)}, u32[]{:S(2)}, u32[]{:S(2)}) collective-permute-start(f32[1,2048]{1,0:T(1,128)S(1)} %add.52.refs_0_), channel_id=1, source_target_pairs={{0,16},{4,20},{8,24},{12,28},{16,0},{20,4},{24,8},{28,12},{1,17},{... | collective-permute-start | bytes 24584 | tf_op jit(solution)/shard_map/ppermute | solution.py:67
  55.7 2.3 %collective-permute-start.5 = (f32[1,2048]{1,0:T(1,128)S(1)}, f32[1,2048]{1,0:T(1,128)S(1)}, u32[]{:S(2)}, u32[]{:S(2)}) collective-permute-start(f32[1,2048]{1,0:T(1,128)S(1)} %add.52.refs_0_), channel_id=1, source_target_pairs={{0,8},{4,12},{8,0},{12,4},{16,24},{20,28},{24,16},{28,20},{1,9},{5... | collective-permute-start | bytes 24584 | tf_op jit(solution)/shard_map/ppermute | solution.py:67
  58.1 1.1 collective-permute-done.7.refs_3_
  59.1 0.0 collective-permute-done.6.refs_2_
  59.1 0.6 collective-permute-done.5.refs_1_
  59.7 4.0 %second_pair.1 = (f32[1,2048]{1,0:T(1,128)S(1)}, f32[1,2048]{1,0:T(1,128)S(1)}, f32[1,2048]{1,0:T(1,128)S(1)}, f32[2048,128]{1,0:T(8,128)S(1)}) custom-call(s32[3]{0:T(128)S(1)} %pad_add_fusion.me_ref, f32[1,2048]{1,0:T(1,128)S(1)} %add.52.refs_0_, f32[1,2048]{1,0:T(1,128)S(1)} %collective-permute-done.5.refs_1_, ...), custom_call_target="tpu_custom_call" | custom-call | flops 16777216 | bytes 16777216 | tf_op jit(solution)/shard_map/second_pair/pallas_call | solution.py:429
  63.7 0.1 collective-permute-start.10
  63.8 1.6 %collective-permute-start.9 = (f32[1,2048]{1,0:T(1,128)S(1)}, f32[1,2048]{1,0:T(1,128)S(1)}, u32[]{:S(2)}, u32[]{:S(2)}) collective-permute-start(f32[1,2048]{1,0:T(1,128)S(1)} %get-tuple-element.28), channel_id=1, source_target_pairs={{0,2},{1,3},{2,0},{3,1},{4,6},{5,7},{6,4},{7,5},{8,10},{9,11},{10,... | collective-permute-start | bytes 24584 | tf_op jit(solution)/shard_map/ppermute | solution.py:67
  65.4 0.3 collective-permute-start.8
  65.6 1.2 collective-permute-done.10
  66.9 0.6 collective-permute-done.9
  67.5 0.0 collective-permute-done.8
  67.6 10.4 %all_to_all.21.bar_ref = f32[8,1,2048]{2,1,0:T(1,128)S(1)} all-to-all(f32[8,1,2048]{2,1,0:T(1,128)S(1)} %broadcast_in_dim.32), channel_id=1, replica_groups=mesh['batch'=8,'proto'=4] {'batch'}, dimensions={0} | all-to-all | bytes 131072 | tf_op jit(solution)/shard_map/all_to_all | solution.py:82
  78.0 3.3 %first_pair.1 = (f32[1,2048]{1,0:T(1,128)S(1)}, f32[1,2048]{1,0:T(1,128)S(1)}, f32[1,2048]{1,0:T(1,128)S(1)}, f32[2048,128]{1,0:T(8,128)S(1)}) custom-call(f32[8,1,2048]{2,1,0:T(1,128)S(1)} %all_to_all.21.bar_ref, f32[1,2048]{1,0:T(1,128)S(1)} %get-tuple-element.29.r_ref, f32[2048,128]{1,0:T(8,128)S(1)} %get-tuple-element.26.refs_6_.a_ref, ...), custom_call_target="tpu_custom_call" | custom-call | flops 16777216 | bytes 16777216 | tf_op jit(solution)/shard_map/first_pair/pallas_call | solution.py:465
  81.2 0.1 collective-permute-start.13
  81.3 1.5 %collective-permute-start.12 = (f32[1,2048]{1,0:T(1,128)S(1)}, f32[1,2048]{1,0:T(1,128)S(1)}, u32[]{:S(2)}, u32[]{:S(2)}) collective-permute-start(f32[1,2048]{1,0:T(1,128)S(1)} %get-tuple-element.30), channel_id=1, source_target_pairs={{0,2},{1,3},{2,0},{3,1},{4,6},{5,7},{6,4},{7,5},{8,10},{9,11},{10,... | collective-permute-start | bytes 24584 | tf_op jit(solution)/shard_map/ppermute | solution.py:67
  82.8 0.3 collective-permute-start.11
  83.2 1.3 %collective-permute-done.13 = f32[1,2048]{1,0:T(1,128)S(1)} collective-permute-done((f32[1,2048]{1,0:T(1,128)S(1)}, f32[1,2048]{1,0:T(1,128)S(1)}, u32[]{:S(2)}, u32[]{:S(2)}) %collective-permute-start.13) | collective-permute-done | bytes 8224 | tf_op jit(solution)/shard_map/ppermute | solution.py:67
  84.4 0.6 collective-permute-done.12
  85.1 0.1 broadcast_in_dim.34
  85.2 12.1 %all_to_all.22.last_ref = f32[8,1,8192]{2,1,0:T(1,128)S(1)} all-to-all(f32[8,1,8192]{2,1,0:T(1,128)S(1)} %broadcast_in_dim.34), channel_id=1, replica_groups=mesh['batch'=8,'proto'=4] {'batch'}, dimensions={0} | all-to-all | bytes 524288 | tf_op jit(solution)/shard_map/all_to_all | solution.py:82
  97.4 11.3 %embed_part.1 = f32[256,256]{1,0:T(8,128)S(1)} custom-call(s32[3]{0:T(128)S(1)} %pad_add_fusion.me_ref, f32[8,1,8192]{2,1,0:T(1,128)S(1)} %all_to_all.22.last_ref, f32[1,2048]{1,0:T(1,128)S(1)} %get-tuple-element.34.f_ref, f32[1,2048]{1,0:T(1,128)S(1)} %get-tuple-element.29.r_ref, f32[1,2048]{1,0:T(1,128)S(1)} %get-tuple-element.35.v_ref, ...), custom_call_target="tpu_custom_call" | custom-call | flops 4294967296 | bytes 8388608 | tf_op jit(solution)/shard_map/embed_part/pallas_call | solution.py:540
  108.6 0.1 collective-permute-start.16
  108.7 0.6 collective-permute-start.15
  109.3 1.2 collective-permute-start.14
  110.6 7.0 %proto_part.1 = f32[2048,256]{1,0:T(8,128)} custom-call(f32[8,1,8192]{2,1,0:T(1,128)S(1)} %all_to_all.22.last_ref, f32[1,2048]{1,0:T(1,128)S(1)} %get-tuple-element.29.r_ref, f32[1,2048]{1,0:T(1,128)S(1)} %get-tuple-element.35.v_ref, f32[2048,128]{1,0:T(8,128)S(1)} %get-tuple-element.26.refs_6_.a_ref, f32[2048,128]{1,0:T(8,128)S(1)} %get-tuple-element.36.h_ref, ...), custom_call_target="tpu_custom_call" | custom-call | flops 2147483648 | bytes 16777216 | tf_op jit(solution)/shard_map/proto_part/pallas_call | solution.py:605
  117.6 3.6 %collective-permute-done.15 = f32[256,256]{1,0:T(8,128)S(1)} collective-permute-done((f32[256,256]{1,0:T(8,128)S(1)}, f32[256,256]{1,0:T(8,128)S(1)}, u32[]{:S(2)}, u32[]{:S(2)}) %collective-permute-start.15) | collective-permute-done | bytes 262176 | tf_op jit(solution)/shard_map/ppermute | solution.py:67
  121.2 0.0 collective-permute-done.14
  121.2 0.8 add_add_fusion
  (10 shorter events, 0.1 us)
Async XLA Ops:
  2.3 21.7 %all-to-all-start = ((bf16[8,128,256]{2,1,0:T(8,128)(2,1)}), bf16[8,128,256]{2,1,0:T(8,128)(2,1)S(1)}, u32[]{:S(2)}, u32[]{:S(2)}) async-start(bf16[8,128,256]{2,1,0:T(8,128)(2,1)} %broadcast_in_dim.28), calls=%async_computation | async-start | bytes 1048576 | tf_op jit(solution)/shard_map/all_to_all | solution.py:82
  9.7 50.0 %copy-start = (f32[256]{0:T(256)S(1)}, f32[256]{0:T(256)}, u32[]{:S(2)}) copy-start(f32[256]{0:T(256)} %param.6) | copy-start | bytes 3076
  24.1 10.8 %collective-permute-start = (bf16[8,128,256]{2,1,0:T(8,128)(2,1)S(1)}, bf16[8,128,256]{2,1,0:T(8,128)(2,1)S(1)}, u32[]{:S(2)}, u32[]{:S(2)}) collective-permute-start(bf16[8,128,256]{2,1,0:T(8,128)(2,1)S(1)} %all-to-all-done.mine_ref), channel_id=1, source_target_pairs={{0,1},{1,0},{2,3},{3,2},{4,5},{5,4},{6,7},{7,6},{8,9},{9,8},{10,11... | collective-permute-start | bytes 1572872 | tf_op jit(solution)/shard_map/ppermute | solution.py:629
  45.9 3.1 %collective-permute-start.3 = (f32[1,2048]{1,0:T(1,128)S(1)}, f32[1,2048]{1,0:T(1,128)S(1)}, u32[]{:S(2)}, u32[]{:S(2)}) collective-permute-start(f32[1,2048]{1,0:T(1,128)S(1)} %get-tuple-element.24), channel_id=1, source_target_pairs={{0,3},{1,2},{2,1},{3,0},{4,7},{5,6},{6,5},{7,4},{8,11},{9,10},{10,... | collective-permute-start | bytes 24584 | tf_op jit(solution)/shard_map/ppermute | solution.py:67
  46.2 3.7 %collective-permute-start.2 = (f32[1,2048]{1,0:T(1,128)S(1)}, f32[1,2048]{1,0:T(1,128)S(1)}, u32[]{:S(2)}, u32[]{:S(2)}) collective-permute-start(f32[1,2048]{1,0:T(1,128)S(1)} %get-tuple-element.24), channel_id=1, source_target_pairs={{0,2},{1,3},{2,0},{3,1},{4,6},{5,7},{6,4},{7,5},{8,10},{9,11},{10,... | collective-permute-start | bytes 24584 | tf_op jit(solution)/shard_map/ppermute | solution.py:67
  47.7 2.1 %collective-permute-start.1 = (f32[1,2048]{1,0:T(1,128)S(1)}, f32[1,2048]{1,0:T(1,128)S(1)}, u32[]{:S(2)}, u32[]{:S(2)}) collective-permute-start(f32[1,2048]{1,0:T(1,128)S(1)} %get-tuple-element.24), channel_id=1, source_target_pairs={{0,1},{1,0},{2,3},{3,2},{4,5},{5,4},{6,7},{7,6},{8,9},{9,8},{10,11... | collective-permute-start | bytes 24584 | tf_op jit(solution)/shard_map/ppermute | solution.py:67
  49.9 3.7 %collective-permute-start.4 = (f32[1,2048]{1,0:T(1,128)S(1)}, f32[1,2048]{1,0:T(1,128)S(1)}, u32[]{:S(2)}, u32[]{:S(2)}) collective-permute-start(f32[1,2048]{1,0:T(1,128)S(1)} %add_add_fusion.3), channel_id=1, source_target_pairs={{0,4},{4,0},{8,12},{12,8},{16,20},{20,16},{24,28},{28,24},{1,5},{5... | collective-permute-start | bytes 24584 | tf_op jit(solution)/shard_map/ppermute | solution.py:67
  53.6 5.5 %collective-permute-start.7 = (f32[1,2048]{1,0:T(1,128)S(1)}, f32[1,2048]{1,0:T(1,128)S(1)}, u32[]{:S(2)}, u32[]{:S(2)}) collective-permute-start(f32[1,2048]{1,0:T(1,128)S(1)} %add.52.refs_0_), channel_id=1, source_target_pairs={{0,24},{4,28},{8,16},{12,20},{16,8},{20,12},{24,0},{28,4},{1,25},{... | collective-permute-start | bytes 24584 | tf_op jit(solution)/shard_map/ppermute | solution.py:67
  54.3 4.8 %collective-permute-start.6 = (f32[1,2048]{1,0:T(1,128)S(1)}, f32[1,2048]{1,0:T(1,128)S(1)}, u32[]{:S(2)}, u32[]{:S(2)}) collective-permute-start(f32[1,2048]{1,0:T(1,128)S(1)} %add.52.refs_0_), channel_id=1, source_target_pairs={{0,16},{4,20},{8,24},{12,28},{16,0},{20,4},{24,8},{28,12},{1,17},{... | collective-permute-start | bytes 24584 | tf_op jit(solution)/shard_map/ppermute | solution.py:67
  55.7 4.0 %collective-permute-start.5 = (f32[1,2048]{1,0:T(1,128)S(1)}, f32[1,2048]{1,0:T(1,128)S(1)}, u32[]{:S(2)}, u32[]{:S(2)}) collective-permute-start(f32[1,2048]{1,0:T(1,128)S(1)} %add.52.refs_0_), channel_id=1, source_target_pairs={{0,8},{4,12},{8,0},{12,4},{16,24},{20,28},{24,16},{28,20},{1,9},{5... | collective-permute-start | bytes 24584 | tf_op jit(solution)/shard_map/ppermute | solution.py:67
  63.7 3.1 %collective-permute-start.10 = (f32[1,2048]{1,0:T(1,128)S(1)}, f32[1,2048]{1,0:T(1,128)S(1)}, u32[]{:S(2)}, u32[]{:S(2)}) collective-permute-start(f32[1,2048]{1,0:T(1,128)S(1)} %get-tuple-element.28), channel_id=1, source_target_pairs={{0,3},{1,2},{2,1},{3,0},{4,7},{5,6},{6,5},{7,4},{8,11},{9,10},{10,... | collective-permute-start | bytes 24584 | tf_op jit(solution)/shard_map/ppermute | solution.py:67
  63.8 3.7 %collective-permute-start.9 = (f32[1,2048]{1,0:T(1,128)S(1)}, f32[1,2048]{1,0:T(1,128)S(1)}, u32[]{:S(2)}, u32[]{:S(2)}) collective-permute-start(f32[1,2048]{1,0:T(1,128)S(1)} %get-tuple-element.28), channel_id=1, source_target_pairs={{0,2},{1,3},{2,0},{3,1},{4,6},{5,7},{6,4},{7,5},{8,10},{9,11},{10,... | collective-permute-start | bytes 24584 | tf_op jit(solution)/shard_map/ppermute | solution.py:67
  65.4 2.1 %collective-permute-start.8 = (f32[1,2048]{1,0:T(1,128)S(1)}, f32[1,2048]{1,0:T(1,128)S(1)}, u32[]{:S(2)}, u32[]{:S(2)}) collective-permute-start(f32[1,2048]{1,0:T(1,128)S(1)} %get-tuple-element.28), channel_id=1, source_target_pairs={{0,1},{1,0},{2,3},{3,2},{4,5},{5,4},{6,7},{7,6},{8,9},{9,8},{10,11... | collective-permute-start | bytes 24584 | tf_op jit(solution)/shard_map/ppermute | solution.py:67
  81.2 3.2 %collective-permute-start.13 = (f32[1,2048]{1,0:T(1,128)S(1)}, f32[1,2048]{1,0:T(1,128)S(1)}, u32[]{:S(2)}, u32[]{:S(2)}) collective-permute-start(f32[1,2048]{1,0:T(1,128)S(1)} %get-tuple-element.30), channel_id=1, source_target_pairs={{0,3},{1,2},{2,1},{3,0},{4,7},{5,6},{6,5},{7,4},{8,11},{9,10},{10,... | collective-permute-start | bytes 24584 | tf_op jit(solution)/shard_map/ppermute | solution.py:67
  81.3 3.7 %collective-permute-start.12 = (f32[1,2048]{1,0:T(1,128)S(1)}, f32[1,2048]{1,0:T(1,128)S(1)}, u32[]{:S(2)}, u32[]{:S(2)}) collective-permute-start(f32[1,2048]{1,0:T(1,128)S(1)} %get-tuple-element.30), channel_id=1, source_target_pairs={{0,2},{1,3},{2,0},{3,1},{4,6},{5,7},{6,4},{7,5},{8,10},{9,11},{10,... | collective-permute-start | bytes 24584 | tf_op jit(solution)/shard_map/ppermute | solution.py:67
  82.8 2.2 %collective-permute-start.11 = (f32[1,2048]{1,0:T(1,128)S(1)}, f32[1,2048]{1,0:T(1,128)S(1)}, u32[]{:S(2)}, u32[]{:S(2)}) collective-permute-start(f32[1,2048]{1,0:T(1,128)S(1)} %get-tuple-element.30), channel_id=1, source_target_pairs={{0,1},{1,0},{2,3},{3,2},{4,5},{5,4},{6,7},{7,6},{8,9},{9,8},{10,11... | collective-permute-start | bytes 24584 | tf_op jit(solution)/shard_map/ppermute | solution.py:67
  108.6 9.0 %collective-permute-start.16 = (f32[256,256]{1,0:T(8,128)S(1)}, f32[256,256]{1,0:T(8,128)S(1)}, u32[]{:S(2)}, u32[]{:S(2)}) collective-permute-start(f32[256,256]{1,0:T(8,128)S(1)} %embed_part.1), channel_id=1, source_target_pairs={{0,3},{1,2},{2,1},{3,0},{4,7},{5,6},{6,5},{7,4},{8,11},{9,10},{10,... | collective-permute-start | bytes 786440 | tf_op jit(solution)/shard_map/ppermute | solution.py:67
  108.7 12.5 %collective-permute-start.15 = (f32[256,256]{1,0:T(8,128)S(1)}, f32[256,256]{1,0:T(8,128)S(1)}, u32[]{:S(2)}, u32[]{:S(2)}) collective-permute-start(f32[256,256]{1,0:T(8,128)S(1)} %embed_part.1), channel_id=1, source_target_pairs={{0,2},{1,3},{2,0},{3,1},{4,6},{5,7},{6,4},{7,5},{8,10},{9,11},{10,... | collective-permute-start | bytes 786440 | tf_op jit(solution)/shard_map/ppermute | solution.py:67
  109.3 11.8 %collective-permute-start.14 = (f32[256,256]{1,0:T(8,128)S(1)}, f32[256,256]{1,0:T(8,128)S(1)}, u32[]{:S(2)}, u32[]{:S(2)}) collective-permute-start(f32[256,256]{1,0:T(8,128)S(1)} %embed_part.1), channel_id=1, source_target_pairs={{0,1},{1,0},{2,3},{3,2},{4,5},{5,4},{6,7},{7,6},{8,9},{9,8},{10,11... | collective-permute-start | bytes 786440 | tf_op jit(solution)/shard_map/ppermute | solution.py:67

commit v7 on v6

--- a/solution.py
+++ b/solution.py
@@ -317,9 +317,10 @@
         top = tree(jnp.maximum, pieces)
         mass = tree(add, [jnp.exp(piece - top) for piece in pieces])
         f_ref[:, d * held : (d + 1) * held] = -math.log(rows) - (top + jnp.log(mass))
+    moves.pop().wait()
+    lanes_to_rows(cot_ref[...], cot_tall_ref)
     for move in moves:
         move.wait()
-    lanes_to_rows(cot_ref[...], cot_tall_ref)
     for d in range(members):
         at = slice(d * held, (d + 1) * held)
         turned_ref[:, at] = (all_ref[at, :] * score_scale).T
@@ -486,85 +487,75 @@
 
 
 def embed_kernel(
-    total, me_ref, last_ref, f_ref, r_ref, v_ref, e_ref, p_ref, out_ref, left_ref, right_ref, tall_ref, b_ref
+    me_ref, last_ref, f_ref, r_ref, v_ref, e_ref, p_ref, out_ref, left_ref, right_ref, tall_ref, b_ref
 ):
-    step = pl.program_id(0)
     rows, width = b_ref.shape
-
-    @pl.when(step == 0)
-    def _():
-        out_ref[...] = jnp.zeros_like(out_ref)
-        right_ref[...] = jnp.zeros_like(right_ref)
-        mine = pl.ds(pl.multiple_of(me_ref[0] * rows, rows), rows)
-        x = tree(add, [last_ref[d, :, mine] for d in range(last_ref.shape[0])])
-        for k, value in enumerate((f_ref[:, mine], r_ref[:, mine], v_ref[:, mine], x)):
-            lanes_to_rows(value, tall_ref.at[k])
-        r, v, x = (tall_ref[k] for k in (1, 2, 3))
-        one = jnp.ones_like(r)
-        left_ref[...] = stack_lanes(left_factors([-r, -x, one], -v))
-
-    y, lse, a = (last_ref[step, :, total + k * width : total + (k + 1) * width] for k in range(3))
-    w = jnp.exp(lse + math.log(total))
-    rows_of = stack_sublanes(right_factors([a, w, y], jnp.ones_like(a)), width)
-    right_ref[0 : rows_of.shape[0], :] = rows_of
-    e = e_ref[...] * score_scale
-    left = left_ref[...]
-    f = tall_ref[0]
+    total = f_ref.shape[1]
+    out_ref[...] = jnp.zeros_like(out_ref)
+    right_ref[...] = jnp.zeros_like(right_ref)
+    mine = pl.ds(pl.multiple_of(me_ref[0] * rows, rows), rows)
+    x = tree(add, [last_ref[d, :, mine] for d in range(last_ref.shape[0])])
+    for k, value in enumerate((f_ref[:, mine], r_ref[:, mine], v_ref[:, mine], x)):
+        lanes_to_rows(value, tall_ref.at[k])
+    r, v, x = (tall_ref[k] for k in (1, 2, 3))
+    left_ref[...] = stack_lanes(left_factors([-r, -x, jnp.ones_like(r)], -v))
     sub = min(2 * lanes, width)
     group = min(4 * sub, width)
     spans = chunks(width, sub)
 
-    def dots(c):
-        return dot_nt(e, p_ref[c, :]), dot_nn(left, right_ref[:, c])
-
-    ahead = dots(spans[0])
-    for k, c in enumerate(spans):
-        s, bracket = ahead
-        if k + 1 < len(spans):
-            ahead = dots(spans[k + 1])
-        t = s - lse[:, c]
-        plan = jnp.concatenate([jnp.exp(t[:, at] + f) for at in chunks(sub)], axis=1)
-        b_ref[:, c] = (plan * bracket).astype(bf16)
-        if c.stop % group == 0:
-            done = slice(c.stop - group, c.stop)
-            out_ref[...] += score_scale * dot_nn(b_ref[:, done], p_ref[done, :])
+    def member(step, carry):
+        y, lse, a = (last_ref[step, :, total + k * width : total + (k + 1) * width] for k in range(3))
+        w = jnp.exp(lse + math.log(total))
+        factors = stack_sublanes(right_factors([a, w, y], jnp.ones_like(a)), width)
+        right_ref[0 : factors.shape[0], :] = factors
+        e = e_ref[...] * score_scale
+        left = left_ref[...]
+        f = tall_ref[0]
+
+        def columns(span):
+            start = pl.multiple_of(step * width, width) + span.start
+            return p_ref[pl.ds(start, span.stop - span.start), :]
+
+        def dots(c):
+            return dot_nt(e, columns(c)), dot_nn(left, right_ref[:, c])
+
+        ahead = dots(spans[0])
+        for k, c in enumerate(spans):
+            s, bracket = ahead
+            if k + 1 < len(spans):
+                ahead = dots(spans[k + 1])
+            t = s - lse[:, c]
+            plan = jnp.concatenate([jnp.exp(t[:, at] + f) for at in chunks(sub)], axis=1)
+            b_ref[:, c] = (plan * bracket).astype(bf16)
+            if c.stop % group == 0:
+                done = slice(c.stop - group, c.stop)
+                out_ref[...] += score_scale * dot_nn(b_ref[:, done], columns(done))
+        return carry
+
+    lax.fori_loop(0, last_ref.shape[0], member, 0)
 
 
 def embed_part(me, last, f, r, v, embeddings, prototypes):
     rows, depth = embeddings.shape
-    members = last.shape[0]
-    total = f.shape[1]
     count = prototypes.shape[0]
-    width = count // members
-    full = lambda shape: pl.BlockSpec(shape, lambda s, me: (0,) * len(shape))
+    width = count // last.shape[0]
     return pl.pallas_call(
-        functools.partial(embed_kernel, total),
-        grid_spec=pltpu.PrefetchScalarGridSpec(
-            num_scalar_prefetch=1,
-            grid=(members,),
-            in_specs=[
-                full(last.shape),
-                full(f.shape),
-                full(f.shape),
-                full(f.shape),
-                full((rows, depth)),
-                pl.BlockSpec((width, depth), lambda s, me: (s, 0)),
-            ],
-            out_specs=full((rows, depth)),
-            scratch_shapes=[
-                pltpu.VMEM((rows, lanes), bf16),
-                pltpu.VMEM((lanes, width), bf16),
-                pltpu.VMEM((4, rows, lanes), f32),
-                pltpu.VMEM((rows, width), bf16),
-            ],
-        ),
+        embed_kernel,
+        in_specs=[in_smem] + [whole] * 6,
+        out_specs=whole,
         out_shape=jax.ShapeDtypeStruct((rows, depth), f32),
+        scratch_shapes=[
+            pltpu.VMEM((rows, lanes), bf16),
+            pltpu.VMEM((lanes, width), bf16),
+            pltpu.VMEM((4, rows, lanes), f32),
+            pltpu.VMEM((rows, width), bf16),
+        ],
         compiler_params=beside_plan,
         cost_estimate=pl.CostEstimate(
             flops=4 * rows * count * depth, bytes_accessed=count * depth * 2, transcendentals=rows * count
         ),
         name="embed_part",
-    )(me, last, f, r, v, in_hbm(embeddings), in_hbm(prototypes))
+    )(me, last, f, r, v, in_vmem(embeddings), in_vmem(prototypes))
 
 
 def proto_kernel(last_ref, r_ref, v_ref, a_ref, h_ref, z_ref, ay_ref, all_ref, e_ref, out_ref, right_ref, b_ref):
@@ -635,7 +626,12 @@
     x = tree(add, partners(x, "proto"))
     last = share(jnp.concatenate([x, y, col_lse, ratio], axis=1), "batch")
     embed = embed_part(me, last, f, r, v, embeddings, prototypes)
-    embed_grad = tree(add, partners(embed, "proto"))
+    stride = 1
+    while 2 * stride < proto:
+        embed = tree(add, partners(embed, "proto", stride, 2))
+        stride *= 2
+    embed, last = lax.optimization_barrier((embed, last))
+    embed_grad = tree(add, partners(embed, "proto", stride, 2))
     proto_grad = proto_part(last, r, v, a, h, z, ay, all_rows, e)
     return (embed_grad, proto_grad)
 

time: 123 us -> 119 us (0.967)
  Pallas kernels: 45.2 us -> 43.6 us
  starting transfers between devices: 20.1 us -> 18.8 us
  waiting for transfers between devices: 19.8 us -> 18.5 us
    pallas_call x1, Pallas kernels: 11.3 us -> 9.5 us  [embed_part(): pl.pallas_call(embed_kernel, in_specs=[in_smem] + [whole] * 6, out_specs=...]
    ppermute x16 -> x15, starting transfers between devices: 12.9 us -> 11.6 us  [partners(): lax.ppermute(x, axis, [(i, i ^ d * stride) for i in range(total)])]
    ppermute x16 -> x15, waiting for transfers between devices: 14 us -> 12.7 us  [partners(): lax.ppermute(x, axis, [(i, i ^ d * stride) for i in range(total)])]
  transfers between devices with their start and end apart: 18 -> 17, of which waited for: 11 -> 12; matrix products, arithmetic and copies ran while one was open for 0% -> 0% of each run, Pallas kernels for 13% -> 13%
where the time goes in v7:
time: 119 us; the launch traced here: 118 us
  Pallas kernels  43.6 us (37%)
  blocking collectives  33.7 us (28%)
  starting transfers between devices  18.8 us (16%)
  waiting for transfers between devices  18.5 us (16%)
  local copies, waits for them, and re-layouts  1.87 us (2%)
    all_to_all x3, blocking collectives, swap_copies(): return lax.all_to_all(copies, axis, split_axis=0, concat_axis=0, tiled=True)  33.7 us
    ppermute x15, waiting for transfers between devices, partners(): lax.ppermute(x, axis, [(i, i ^ d * stride) for i in range(total)])  12.7 us
    ppermute x15, starting transfers between devices, partners(): lax.ppermute(x, axis, [(i, i ^ d * stride) for i in range(total)])  11.6 us
    pallas_call x1, Pallas kernels, col_softmax(): pl.pallas_call(functools.partial(col_softmax_kernel, devices // members),...  11.1 us
    pallas_call x1, Pallas kernels, embed_part(): pl.pallas_call(embed_kernel, in_specs=[in_smem] + [whole] * 6, out_specs=...  9.5 us
    pallas_call x1, Pallas kernels, row_lse(): pl.pallas_call(row_lse_kernel, grid=(count // width,), in_specs=[pl.Block...  8.61 us
    all_to_all x1, starting transfers between devices, swap_copies(): return lax.all_to_all(copies, axis, split_axis=0, concat_axis=0, tiled=True)  7.25 us
    pallas_call x1, Pallas kernels, proto_part(): pl.pallas_call(proto_kernel, in_specs=[whole] * 9, out_specs=whole, out_s...  7.03 us
  transfers between devices with their start and end apart: 17, of which 12 were waited for; matrix products, arithmetic and copies ran while one was open for 0% of the time, Pallas kernels for 13%

profile of v7, /device:TPU:0, one launch (start us, length us, event | category | flops | bytes accessed | tf_op | source)
XLA Modules:
  0.0 118.2 jit_solution(842445926340510669)
XLA Ops:
  0.6 0.8 constant_dynamic-slice_fusion
  1.5 0.8 broadcast_in_dim.28
  2.3 7.3 %all-to-all-start = ((bf16[8,128,256]{2,1,0:T(8,128)(2,1)}), bf16[8,128,256]{2,1,0:T(8,128)(2,1)S(1)}, u32[]{:S(2)}, u32[]{:S(2)}) async-start(bf16[8,128,256]{2,1,0:T(8,128)(2,1)} %broadcast_in_dim.28), calls=%async_computation | async-start | bytes 1048576 | tf_op jit(solution)/shard_map/all_to_all | solution.py:82
  9.6 0.1 pad_add_fusion.me_ref
  9.7 8.6 %row_lse.1 = f32[32,1,256]{2,1,0:T(1,128)S(1)} custom-call(bf16[256,256]{1,0:T(8,128)(2,1)} %e_ref.3, bf16[16384,256]{1,0:T(8,128)(2,1)} %p_ref.3), custom_call_target="tpu_custom_call" | custom-call | flops 2147483648 | bytes 8388608 | tf_op jit(solution)/shard_map/row_lse/pallas_call | solution.py:256
  18.3 5.8 %all-to-all-done.mine_ref = bf16[8,128,256]{2,1,0:T(8,128)(2,1)S(1)} async-done(((bf16[8,128,256]{2,1,0:T(8,128)(2,1)}), bf16[8,128,256]{2,1,0:T(8,128)(2,1)S(1)}, u32[]{:S(2)}, u32[]{:S(2)}) %all-to-all-start) | async-done | bytes 524320 | tf_op jit(solution)/shard_map/all_to_all | solution.py:82
  24.1 0.0 collective-permute-start
  24.1 10.8 %all_to_all.20.lse_ref = f32[32,1,256]{2,1,0:T(1,128)S(1)} all-to-all(f32[32,1,256]{2,1,0:T(1,128)S(1)} %row_lse.1), channel_id=1, replica_groups=mesh['batch'=8,'proto'=4] {'batch','proto'}, dimensions={0} | all-to-all | bytes 65536 | tf_op jit(solution)/shard_map/all_to_all | solution.py:82
  34.9 0.0 collective-permute-done.other_ref
  34.9 11.1 %col_softmax.1 = (f32[2048,2048]{1,0:T(8,128)S(1)}, f32[1,2048]{1,0:T(1,128)S(1)}, f32[1,2048]{1,0:T(1,128)S(1)}, f32[1,2048]{1,0:T(1,128)S(1)}, bf16[2048,256]{...) custom-call(s32[3]{0:T(128)S(1)} %pad_add_fusion.me_ref, ...), custom_call_target="tpu_custom_call" | custom-call | flops 2147483648 | bytes 16777216 | tf_op jit(solution)/shard_map/col_softmax/pallas_call | solution.py:381
  46.0 0.3 collective-permute-start.3
  46.3 1.5 %collective-permute-start.2 = (f32[1,2048]{1,0:T(1,128)S(1)}, f32[1,2048]{1,0:T(1,128)S(1)}, u32[]{:S(2)}, u32[]{:S(2)}) collective-permute-start(f32[1,2048]{1,0:T(1,128)S(1)} %get-tuple-element.26), channel_id=1, source_target_pairs={{0,2},{1,3},{2,0},{3,1},{4,6},{5,7},{6,4},{7,5},{8,10},{9,11},{10,... | collective-permute-start | bytes 24584 | tf_op jit(solution)/shard_map/ppermute | solution.py:67
  47.8 0.1 collective-permute-start.1
  48.0 1.2 collective-permute-done.3
  49.1 0.8 collective-permute-done.2
  49.9 0.0 collective-permute-done.1
  50.0 0.6 collective-permute-start.4
  50.6 3.1 %collective-permute-done.4 = f32[1,2048]{1,0:T(1,128)S(1)} collective-permute-done((f32[1,2048]{1,0:T(1,128)S(1)}, f32[1,2048]{1,0:T(1,128)S(1)}, u32[]{:S(2)}, u32[]{:S(2)}) %collective-permute-start.4) | collective-permute-done | bytes 8224 | tf_op jit(solution)/shard_map/ppermute | solution.py:67
  53.7 0.6 collective-permute-start.7
  54.3 1.5 %collective-permute-start.6 = (f32[1,2048]{1,0:T(1,128)S(1)}, f32[1,2048]{1,0:T(1,128)S(1)}, u32[]{:S(2)}, u32[]{:S(2)}) collective-permute-start(f32[1,2048]{1,0:T(1,128)S(1)} %add.49.refs_0_), channel_id=1, source_target_pairs={{0,16},{4,20},{8,24},{12,28},{16,0},{20,4},{24,8},{28,12},{1,17},{... | collective-permute-start | bytes 24584 | tf_op jit(solution)/shard_map/ppermute | solution.py:67
  55.8 2.3 %collective-permute-start.5 = (f32[1,2048]{1,0:T(1,128)S(1)}, f32[1,2048]{1,0:T(1,128)S(1)}, u32[]{:S(2)}, u32[]{:S(2)}) collective-permute-start(f32[1,2048]{1,0:T(1,128)S(1)} %add.49.refs_0_), channel_id=1, source_target_pairs={{0,8},{4,12},{8,0},{12,4},{16,24},{20,28},{24,16},{28,20},{1,9},{5... | collective-permute-start | bytes 24584 | tf_op jit(solution)/shard_map/ppermute | solution.py:67
  58.1 1.1 collective-permute-done.7.refs_3_
  59.2 0.0 collective-permute-done.6.refs_2_
  59.2 0.6 collective-permute-done.5.refs_1_
  59.8 4.1 %second_pair.1 = (f32[1,2048]{1,0:T(1,128)S(1)}, f32[1,2048]{1,0:T(1,128)S(1)}, f32[1,2048]{1,0:T(1,128)S(1)}, f32[2048,128]{1,0:T(8,128)S(1)}) custom-call(s32[3]{0:T(128)S(1)} %pad_add_fusion.me_ref, f32[1,2048]{1,0:T(1,128)S(1)} %add.49.refs_0_, f32[1,2048]{1,0:T(1,128)S(1)} %collective-permute-done.5.refs_1_, ...), custom_call_target="tpu_custom_call" | custom-call | flops 16777216 | bytes 16777216 | tf_op jit(solution)/shard_map/second_pair/pallas_call | solution.py:430
  63.9 0.1 collective-permute-start.10
  63.9 1.6 %collective-permute-start.9 = (f32[1,2048]{1,0:T(1,128)S(1)}, f32[1,2048]{1,0:T(1,128)S(1)}, u32[]{:S(2)}, u32[]{:S(2)}) collective-permute-start(f32[1,2048]{1,0:T(1,128)S(1)} %get-tuple-element.30), channel_id=1, source_target_pairs={{0,2},{1,3},{2,0},{3,1},{4,6},{5,7},{6,4},{7,5},{8,10},{9,11},{10,... | collective-permute-start | bytes 24584 | tf_op jit(solution)/shard_map/ppermute | solution.py:67
  65.5 0.3 collective-permute-start.8
  65.8 1.2 %collective-permute-done.10 = f32[1,2048]{1,0:T(1,128)S(1)} collective-permute-done((f32[1,2048]{1,0:T(1,128)S(1)}, f32[1,2048]{1,0:T(1,128)S(1)}, u32[]{:S(2)}, u32[]{:S(2)}) %collective-permute-start.10) | collective-permute-done | bytes 8224 | tf_op jit(solution)/shard_map/ppermute | solution.py:67
  67.0 0.6 collective-permute-done.9
  67.7 0.0 collective-permute-done.8
  67.7 0.0 slice-start.1
  67.7 10.6 %all_to_all.21.bar_ref = f32[8,1,2048]{2,1,0:T(1,128)S(1)} all-to-all(f32[8,1,2048]{2,1,0:T(1,128)S(1)} %broadcast_in_dim.32), channel_id=1, replica_groups=mesh['batch'=8,'proto'=4] {'batch'}, dimensions={0} | all-to-all | bytes 131072 | tf_op jit(solution)/shard_map/all_to_all | solution.py:82
  78.4 3.3 %first_pair.1 = (f32[1,2048]{1,0:T(1,128)S(1)}, f32[1,2048]{1,0:T(1,128)S(1)}, f32[1,2048]{1,0:T(1,128)S(1)}, f32[2048,128]{1,0:T(8,128)S(1)}) custom-call(f32[8,1,2048]{2,1,0:T(1,128)S(1)} %all_to_all.21.bar_ref, f32[1,2048]{1,0:T(1,128)S(1)} %get-tuple-element.31.r_ref, f32[2048,128]{1,0:T(8,128)S(1)} %get-tuple-element.28.refs_6_.a_ref, ...), custom_call_target="tpu_custom_call" | custom-call | flops 16777216 | bytes 16777216 | tf_op jit(solution)/shard_map/first_pair/pallas_call | solution.py:466
  81.6 0.1 collective-permute-start.13
  81.7 1.6 %collective-permute-start.12 = (f32[1,2048]{1,0:T(1,128)S(1)}, f32[1,2048]{1,0:T(1,128)S(1)}, u32[]{:S(2)}, u32[]{:S(2)}) collective-permute-start(f32[1,2048]{1,0:T(1,128)S(1)} %get-tuple-element.32), channel_id=1, source_target_pairs={{0,2},{1,3},{2,0},{3,1},{4,6},{5,7},{6,4},{7,5},{8,10},{9,11},{10,... | collective-permute-start | bytes 24584 | tf_op jit(solution)/shard_map/ppermute | solution.py:67
  83.3 0.3 collective-permute-start.11
  83.6 1.2 %collective-permute-done.13 = f32[1,2048]{1,0:T(1,128)S(1)} collective-permute-done((f32[1,2048]{1,0:T(1,128)S(1)}, f32[1,2048]{1,0:T(1,128)S(1)}, u32[]{:S(2)}, u32[]{:S(2)}) %collective-permute-start.13) | collective-permute-done | bytes 8224 | tf_op jit(solution)/shard_map/ppermute | solution.py:67
  84.8 0.6 collective-permute-done.12
  85.5 0.1 broadcast_in_dim.34
  85.6 12.2 %all_to_all.22.last_ref = f32[8,1,8192]{2,1,0:T(1,128)S(1)} all-to-all(f32[8,1,8192]{2,1,0:T(1,128)S(1)} %broadcast_in_dim.34), channel_id=1, replica_groups=mesh['batch'=8,'proto'=4] {'batch'}, dimensions={0} | all-to-all | bytes 524288 | tf_op jit(solution)/shard_map/all_to_all | solution.py:82
  97.9 9.5 %embed_part.1 = f32[256,256]{1,0:T(8,128)S(1)} custom-call(s32[3]{0:T(128)S(1)} %pad_add_fusion.me_ref, f32[8,1,8192]{2,1,0:T(1,128)S(1)} %all_to_all.22.last_ref, f32[1,2048]{1,0:T(1,128)S(1)} %get-tuple-element.36.f_ref, f32[1,2048]{1,0:T(1,128)S(1)} %get-tuple-element.31.r_ref, f32[1,2048]{1,0:T(1,128)S(1)} %get-tuple-element.37.v_ref, ...), custom_call_target="tpu_custom_call" | custom-call | flops 4294967296 | bytes 8388608 | tf_op jit(solution)/shard_map/embed_part/pallas_call | solution.py:542
  107.4 0.1 collective-permute-start.14
  107.4 1.5 %collective-permute-done.14 = f32[256,256]{1,0:T(8,128)S(1)} collective-permute-done((f32[256,256]{1,0:T(8,128)S(1)}, f32[256,256]{1,0:T(8,128)S(1)}, u32[]{:S(2)}, u32[]{:S(2)}) %collective-permute-start.14) | collective-permute-done | bytes 262176 | tf_op jit(solution)/shard_map/ppermute | solution.py:67
  109.0 0.6 collective-permute-start.15
  109.6 7.0 %proto_part.1 = f32[2048,256]{1,0:T(8,128)} custom-call(f32[8,1,8192]{2,1,0:T(1,128)S(1)} %all_to_all.22.last_ref, f32[1,2048]{1,0:T(1,128)S(1)} %get-tuple-element.31.r_ref, f32[1,2048]{1,0:T(1,128)S(1)} %get-tuple-element.37.v_ref, f32[2048,128]{1,0:T(8,128)S(1)} %get-tuple-element.28.refs_6_.a_ref, f32[2048,128]{1,0:T(8,128)S(1)} %get-tuple-element.40.h_ref, ...), custom_call_target="tpu_custom_call" | custom-call | flops 2147483648 | bytes 16777216 | tf_op jit(solution)/shard_map/proto_part/pallas_call | solution.py:596
  116.6 0.8 collective-permute-done.15
  117.4 0.7 add.57
  (16 shorter events, 0.2 us)
Async XLA Ops:
  2.3 21.7 %all-to-all-start = ((bf16[8,128,256]{2,1,0:T(8,128)(2,1)}), bf16[8,128,256]{2,1,0:T(8,128)(2,1)S(1)}, u32[]{:S(2)}, u32[]{:S(2)}) async-start(bf16[8,128,256]{2,1,0:T(8,128)(2,1)} %broadcast_in_dim.28), calls=%async_computation | async-start | bytes 1048576 | tf_op jit(solution)/shard_map/all_to_all | solution.py:82
  9.7 50.1 %copy-start.1 = (f32[256]{0:T(256)S(1)}, f32[256]{0:T(256)}, u32[]{:S(2)}) copy-start(f32[256]{0:T(256)} %param.6) | copy-start | bytes 3076
  24.1 10.8 %collective-permute-start = (bf16[8,128,256]{2,1,0:T(8,128)(2,1)S(1)}, bf16[8,128,256]{2,1,0:T(8,128)(2,1)S(1)}, u32[]{:S(2)}, u32[]{:S(2)}) collective-permute-start(bf16[8,128,256]{2,1,0:T(8,128)(2,1)S(1)} %all-to-all-done.mine_ref), channel_id=1, source_target_pairs={{0,1},{1,0},{2,3},{3,2},{4,5},{5,4},{6,7},{7,6},{8,9},{9,8},{10,11... | collective-permute-start | bytes 1572872 | tf_op jit(solution)/shard_map/ppermute | solution.py:620
  46.0 3.1 %collective-permute-start.3 = (f32[1,2048]{1,0:T(1,128)S(1)}, f32[1,2048]{1,0:T(1,128)S(1)}, u32[]{:S(2)}, u32[]{:S(2)}) collective-permute-start(f32[1,2048]{1,0:T(1,128)S(1)} %get-tuple-element.26), channel_id=1, source_target_pairs={{0,3},{1,2},{2,1},{3,0},{4,7},{5,6},{6,5},{7,4},{8,11},{9,10},{10,... | collective-permute-start | bytes 24584 | tf_op jit(solution)/shard_map/ppermute | solution.py:67
  46.3 3.7 %collective-permute-start.2 = (f32[1,2048]{1,0:T(1,128)S(1)}, f32[1,2048]{1,0:T(1,128)S(1)}, u32[]{:S(2)}, u32[]{:S(2)}) collective-permute-start(f32[1,2048]{1,0:T(1,128)S(1)} %get-tuple-element.26), channel_id=1, source_target_pairs={{0,2},{1,3},{2,0},{3,1},{4,6},{5,7},{6,4},{7,5},{8,10},{9,11},{10,... | collective-permute-start | bytes 24584 | tf_op jit(solution)/shard_map/ppermute | solution.py:67
  47.8 2.1 %collective-permute-start.1 = (f32[1,2048]{1,0:T(1,128)S(1)}, f32[1,2048]{1,0:T(1,128)S(1)}, u32[]{:S(2)}, u32[]{:S(2)}) collective-permute-start(f32[1,2048]{1,0:T(1,128)S(1)} %get-tuple-element.26), channel_id=1, source_target_pairs={{0,1},{1,0},{2,3},{3,2},{4,5},{5,4},{6,7},{7,6},{8,9},{9,8},{10,11... | collective-permute-start | bytes 24584 | tf_op jit(solution)/shard_map/ppermute | solution.py:67
  50.0 3.7 %collective-permute-start.4 = (f32[1,2048]{1,0:T(1,128)S(1)}, f32[1,2048]{1,0:T(1,128)S(1)}, u32[]{:S(2)}, u32[]{:S(2)}) collective-permute-start(f32[1,2048]{1,0:T(1,128)S(1)} %add_add_fusion.2), channel_id=1, source_target_pairs={{0,4},{4,0},{8,12},{12,8},{16,20},{20,16},{24,28},{28,24},{1,5},{5... | collective-permute-start | bytes 24584 | tf_op jit(solution)/shard_map/ppermute | solution.py:67
  53.7 5.5 %collective-permute-start.7 = (f32[1,2048]{1,0:T(1,128)S(1)}, f32[1,2048]{1,0:T(1,128)S(1)}, u32[]{:S(2)}, u32[]{:S(2)}) collective-permute-start(f32[1,2048]{1,0:T(1,128)S(1)} %add.49.refs_0_), channel_id=1, source_target_pairs={{0,24},{4,28},{8,16},{12,20},{16,8},{20,12},{24,0},{28,4},{1,25},{... | collective-permute-start | bytes 24584 | tf_op jit(solution)/shard_map/ppermute | solution.py:67
  54.3 4.9 %collective-permute-start.6 = (f32[1,2048]{1,0:T(1,128)S(1)}, f32[1,2048]{1,0:T(1,128)S(1)}, u32[]{:S(2)}, u32[]{:S(2)}) collective-permute-start(f32[1,2048]{1,0:T(1,128)S(1)} %add.49.refs_0_), channel_id=1, source_target_pairs={{0,16},{4,20},{8,24},{12,28},{16,0},{20,4},{24,8},{28,12},{1,17},{... | collective-permute-start | bytes 24584 | tf_op jit(solution)/shard_map/ppermute | solution.py:67
  55.8 4.0 %collective-permute-start.5 = (f32[1,2048]{1,0:T(1,128)S(1)}, f32[1,2048]{1,0:T(1,128)S(1)}, u32[]{:S(2)}, u32[]{:S(2)}) collective-permute-start(f32[1,2048]{1,0:T(1,128)S(1)} %add.49.refs_0_), channel_id=1, source_target_pairs={{0,8},{4,12},{8,0},{12,4},{16,24},{20,28},{24,16},{28,20},{1,9},{5... | collective-permute-start | bytes 24584 | tf_op jit(solution)/shard_map/ppermute | solution.py:67
  59.8 38.1 %slice-start = ((s8[8388608]{0:T(1024)(128)(4,1)}), s8[4194304]{0:T(1024)(128)(4,1)S(1)}, s32[]{:S(2)}) async-start(s8[8388608]{0:T(1024)(128)(4,1)} %bitcast.7), calls=%async_computation.4 | async-start | bytes 8388608
  63.9 3.1 %collective-permute-start.10 = (f32[1,2048]{1,0:T(1,128)S(1)}, f32[1,2048]{1,0:T(1,128)S(1)}, u32[]{:S(2)}, u32[]{:S(2)}) collective-permute-start(f32[1,2048]{1,0:T(1,128)S(1)} %get-tuple-element.30), channel_id=1, source_target_pairs={{0,3},{1,2},{2,1},{3,0},{4,7},{5,6},{6,5},{7,4},{8,11},{9,10},{10,... | collective-permute-start | bytes 24584 | tf_op jit(solution)/shard_map/ppermute | solution.py:67
  63.9 3.7 %collective-permute-start.9 = (f32[1,2048]{1,0:T(1,128)S(1)}, f32[1,2048]{1,0:T(1,128)S(1)}, u32[]{:S(2)}, u32[]{:S(2)}) collective-permute-start(f32[1,2048]{1,0:T(1,128)S(1)} %get-tuple-element.30), channel_id=1, source_target_pairs={{0,2},{1,3},{2,0},{3,1},{4,6},{5,7},{6,4},{7,5},{8,10},{9,11},{10,... | collective-permute-start | bytes 24584 | tf_op jit(solution)/shard_map/ppermute | solution.py:67
  65.5 2.1 %collective-permute-start.8 = (f32[1,2048]{1,0:T(1,128)S(1)}, f32[1,2048]{1,0:T(1,128)S(1)}, u32[]{:S(2)}, u32[]{:S(2)}) collective-permute-start(f32[1,2048]{1,0:T(1,128)S(1)} %get-tuple-element.30), channel_id=1, source_target_pairs={{0,1},{1,0},{2,3},{3,2},{4,5},{5,4},{6,7},{7,6},{8,9},{9,8},{10,11... | collective-permute-start | bytes 24584 | tf_op jit(solution)/shard_map/ppermute | solution.py:67
  67.7 30.2 %slice-start.1 = ((s8[8388608]{0:T(1024)(128)(4,1)}), s8[4194304]{0:T(1024)(128)(4,1)S(1)}, s32[]{:S(2)}) async-start(s8[8388608]{0:T(1024)(128)(4,1)} %bitcast.7), calls=%async_computation.5 | async-start | bytes 8388608
  78.4 19.5 %copy-start = (bf16[256,256]{1,0:T(8,128)(2,1)S(1)}, bf16[256,256]{1,0:T(8,128)(2,1)}, u32[]{:S(2)}) copy-start(bf16[256,256]{1,0:T(8,128)(2,1)} %e_ref.3) | copy-start | bytes 393220
  81.6 3.2 %collective-permute-start.13 = (f32[1,2048]{1,0:T(1,128)S(1)}, f32[1,2048]{1,0:T(1,128)S(1)}, u32[]{:S(2)}, u32[]{:S(2)}) collective-permute-start(f32[1,2048]{1,0:T(1,128)S(1)} %get-tuple-element.32), channel_id=1, source_target_pairs={{0,3},{1,2},{2,1},{3,0},{4,7},{5,6},{6,5},{7,4},{8,11},{9,10},{10,... | collective-permute-start | bytes 24584 | tf_op jit(solution)/shard_map/ppermute | solution.py:67
  81.7 3.7 %collective-permute-start.12 = (f32[1,2048]{1,0:T(1,128)S(1)}, f32[1,2048]{1,0:T(1,128)S(1)}, u32[]{:S(2)}, u32[]{:S(2)}) collective-permute-start(f32[1,2048]{1,0:T(1,128)S(1)} %get-tuple-element.32), channel_id=1, source_target_pairs={{0,2},{1,3},{2,0},{3,1},{4,6},{5,7},{6,4},{7,5},{8,10},{9,11},{10,... | collective-permute-start | bytes 24584 | tf_op jit(solution)/shard_map/ppermute | solution.py:67
  83.3 2.1 %collective-permute-start.11 = (f32[1,2048]{1,0:T(1,128)S(1)}, f32[1,2048]{1,0:T(1,128)S(1)}, u32[]{:S(2)}, u32[]{:S(2)}) collective-permute-start(f32[1,2048]{1,0:T(1,128)S(1)} %get-tuple-element.32), channel_id=1, source_target_pairs={{0,1},{1,0},{2,3},{3,2},{4,5},{5,4},{6,7},{7,6},{8,9},{9,8},{10,11... | collective-permute-start | bytes 24584 | tf_op jit(solution)/shard_map/ppermute | solution.py:67
  107.4 1.6 %collective-permute-start.14 = (f32[256,256]{1,0:T(8,128)S(1)}, f32[256,256]{1,0:T(8,128)S(1)}, u32[]{:S(2)}, u32[]{:S(2)}) collective-permute-start(f32[256,256]{1,0:T(8,128)S(1)} %embed_part.1), channel_id=1, source_target_pairs={{0,1},{1,0},{2,3},{3,2},{4,5},{5,4},{6,7},{7,6},{8,9},{9,8},{10,11... | collective-permute-start | bytes 786440 | tf_op jit(solution)/shard_map/ppermute | solution.py:67
  109.0 8.4 %collective-permute-start.15 = (f32[256,256]{1,0:T(8,128)S(1)}, f32[256,256]{1,0:T(8,128)S(1)}, u32[]{:S(2)}, u32[]{:S(2)}) collective-permute-start(f32[256,256]{1,0:T(8,128)S(1)} %add.56), channel_id=1, source_target_pairs={{0,2},{1,3},{2,0},{3,1},{4,6},{5,7},{6,4},{7,5},{8,10},{9,11},{10,... | collective-permute-start | bytes 786440 | tf_op jit(solution)/shard_map/ppermute | solution.py:67

commit v8 on v7

--- a/solution.py
+++ b/solution.py
@@ -219,7 +219,7 @@
     return values + [single] * 2
 
 
-def row_lse_kernel(e_ref, p_ref, copies_ref, turned_ref, top_ref, mass_ref):
+def row_lse_kernel(me_ref, cot_ref, e_ref, p_ref, copies_ref, cot_tall_ref, turned_ref, top_ref, mass_ref):
     step = pl.program_id(0)
     width = p_ref.shape[0]
     _, rows = top_ref.shape
@@ -247,9 +247,12 @@
         lse = peak + jnp.log(total)
         for d in range(copies_ref.shape[0]):
             copies_ref[d] = lse
-
-
-def row_lse(embeddings, prototypes, copies):
+        count = cot_tall_ref.shape[0]
+        own = pl.ds(pl.multiple_of(me_ref[0] * count, count), count)
+        lanes_to_rows(cot_ref[:, own], cot_tall_ref)
+
+
+def row_lse(me, col_cot, embeddings, prototypes, copies, own):
     rows, depth = embeddings.shape
     count = prototypes.shape[0]
     width = min(2048, count)
@@ -257,11 +260,19 @@
         row_lse_kernel,
         grid=(count // width,),
         in_specs=[
+            in_smem,
+            pl.BlockSpec((1, count), lambda s: (0, 0)),
             pl.BlockSpec((rows, depth), lambda s: (0, 0)),
             pl.BlockSpec((width, depth), lambda s: (s, 0)),
         ],
-        out_specs=pl.BlockSpec((copies, 1, rows), lambda s: (0, 0, 0)),
-        out_shape=jax.ShapeDtypeStruct((copies, 1, rows), f32),
+        out_specs=[
+            pl.BlockSpec((copies, 1, rows), lambda s: (0, 0, 0)),
+            pl.BlockSpec((own, lanes), lambda s: (0, 0)),
+        ],
+        out_shape=[
+            jax.ShapeDtypeStruct((copies, 1, rows), f32),
+            pltpu.HBM((own, lanes), f32),
+        ],
         scratch_shapes=[
             pltpu.VMEM((depth, rows), bf16),
             pltpu.VMEM((sublanes, rows), f32),
@@ -272,7 +283,7 @@
             flops=2 * rows * count * depth, bytes_accessed=count * depth * 2, transcendentals=rows * count
         ),
         name="row_lse",
-    )(in_hbm(embeddings), in_hbm(prototypes))
+    )(me, col_cot, in_hbm(embeddings), in_hbm(prototypes))
 
 
 def col_softmax_kernel(
@@ -282,7 +293,6 @@
     mine_ref,
     other_ref,
     p_all_ref,
-    cot_all_ref,
     e_ref,
     copies_ref,
     col_lse_ref,
@@ -290,9 +300,7 @@
     all_ref,
     a_ref,
     h_ref,
-    cot_tall_ref,
     p_ref,
-    cot_ref,
     turned_ref,
     t_ref,
     acc_ref,
@@ -309,7 +317,6 @@
             moves.append(pltpu.make_async_copy(ref.at[d], all_ref.at[pl.ds(start, half), :], sem.at[len(moves)]))
     own = pl.ds(pl.multiple_of(me_ref[0] * count, count), count)
     moves.append(pltpu.make_async_copy(p_all_ref.at[own, :], p_ref, sem.at[len(moves)]))
-    moves.append(pltpu.make_async_copy(cot_all_ref.at[:, own], cot_ref, sem.at[len(moves)]))
     for move in moves:
         move.start()
     for d in range(members):
@@ -317,13 +324,13 @@
         top = tree(jnp.maximum, pieces)
         mass = tree(add, [jnp.exp(piece - top) for piece in pieces])
         f_ref[:, d * held : (d + 1) * held] = -math.log(rows) - (top + jnp.log(mass))
-    moves.pop().wait()
-    lanes_to_rows(cot_ref[...], cot_tall_ref)
+    fetch = moves.pop()
     for move in moves:
         move.wait()
     for d in range(members):
         at = slice(d * held, (d + 1) * held)
         turned_ref[:, at] = (all_ref[at, :] * score_scale).T
+    fetch.wait()
 
     height = t_ref.shape[1]
     blocks = count // height
@@ -335,10 +342,12 @@
         spans = chunks(rows, 2 * lanes)
         total = height // sublanes
         part = None
+        if ahead is not None:
+            number, slot = ahead
+            p = p_ref[rows_of(number), :]
         for k, c in enumerate(spans):
             if ahead is not None:
-                number, slot = ahead
-                t = dot_nn(p_ref[rows_of(number), :], turned_ref[:, c]) + f_ref[:, c]
+                t = dot_nn(p, turned_ref[:, c]) + f_ref[:, c]
                 t_ref[slot, :, c] = t
                 here = jnp.maximum(t[:, :lanes], t[:, lanes:])
                 part = here if part is None else jnp.maximum(part, here)
@@ -371,7 +380,7 @@
     copies_ref[...] = rho
 
 
-def col_softmax(me, lse, mine, other, prototypes, col_cot):
+def col_softmax(me, lse, mine, other, prototypes):
     members, half, depth = mine.shape
     rows = 2 * members * half
     count = prototypes.shape[0] // members
@@ -380,8 +389,8 @@
     halves = whole if few(rows) else anywhere
     return pl.pallas_call(
         functools.partial(col_softmax_kernel, devices // members),
-        in_specs=[in_smem, whole, halves, halves, anywhere, anywhere],
-        out_specs=[whole] * 8,
+        in_specs=[in_smem, whole, halves, halves, anywhere],
+        out_specs=[whole] * 7,
         out_shape=[
             held((count, rows)),
             jax.ShapeDtypeStruct((1, rows), f32),
@@ -390,23 +399,21 @@
             held((rows, depth), bf16, few(rows)),
             held((count, lanes)),
             held((count, lanes)),
-            held((count, lanes)),
         ],
         scratch_shapes=[
             pltpu.VMEM((count, depth), bf16),
-            pltpu.VMEM((1, count), f32),
             pltpu.VMEM((depth, rows), bf16),
             pltpu.VMEM((2, height, rows), f32),
             pltpu.VMEM((sublanes, rows), f32),
             pltpu.VMEM((count, lanes), f32),
-            pltpu.SemaphoreType.DMA((2 * members + 2,)),
+            pltpu.SemaphoreType.DMA((2 * members + 1,)),
         ],
         compiler_params=beside_plan if few(rows) else grant(36),
         cost_estimate=pl.CostEstimate(
             flops=2 * rows * count * depth, bytes_accessed=count * rows * 4, transcendentals=rows * count
         ),
         name="col_softmax",
-    )(me, lse, in_vmem(mine, few(rows)), in_vmem(other, few(rows)), in_hbm(prototypes), in_hbm(col_cot))
+    )(me, lse, in_vmem(mine, few(rows)), in_vmem(other, few(rows)), in_hbm(prototypes))
 
 
 def second_pair_kernel(pieces, me_ref, *refs):
@@ -613,13 +620,14 @@
     me = jnp.stack([member, holder % 2, holder]).astype(jnp.int32)
 
     short = embeddings.shape[0] // 2
-    half = lax.dynamic_slice_in_dim(embeddings, (holder % 2) * short, short, axis=0)
+    half = jnp.where(holder % 2 == 0, embeddings[:short], embeddings[short:])
     mine = share(half, "batch")
-    lse = row_lse(embeddings, prototypes, batch * proto)
+    own = prototypes.shape[0] // batch
+    lse, cot = row_lse(me, col_cot[None, :], embeddings, prototypes, batch * proto, own)
     mine, lse, me = lax.optimization_barrier((mine, lse, me))
     other = lax.ppermute(mine, "proto", [(i, i ^ 1) for i in range(proto)])
     lse = swap_copies(lse, both)
-    e, rho, col_lse, f, all_rows, a, h, cot = col_softmax(me, lse, mine, other, prototypes, col_cot[None, :])
+    e, rho, col_lse, f, all_rows, a, h = col_softmax(me, lse, mine, other, prototypes)
     bar, r, ratio, z = second_pair(me, total_pieces(rho), row_cot[None, :], cot, a, e)
     bar = share(tree(add, partners(bar, "proto")), "batch")
     x, v, y, ay = first_pair(bar, r, a, e)

time: 119 us -> 119 us (level)
  waiting for transfers between devices: 18.5 us -> 16.4 us
  Pallas kernels: 43.6 us -> 45 us
    all_to_all x1, waiting for transfers between devices: 5.79 us -> 3.62 us  [swap_copies(): return lax.all_to_all(copies, axis, split_axis=0, concat_axis=0, tiled=True)]
    pallas_call x1, Pallas kernels: 8.61 us -> 9.95 us  [row_lse(): pl.pallas_call(row_lse_kernel, grid=(count // width,), in_specs=[in_smem,...]
  transfers between devices with their start and end apart: 17 -> 17, of which waited for: 12 -> 12; matrix products, arithmetic and copies ran while one was open for 0% -> 0% of each run, Pallas kernels for 13% -> 14%
where the time goes in v8:
time: 119 us; the launch traced here: 118 us
  Pallas kernels  45 us (38%)
  blocking collectives  33.7 us (28%)
  starting transfers between devices  18.8 us (16%)
  waiting for transfers between devices  16.4 us (14%)
  local copies, waits for them, and re-layouts  1.88 us (2%)
  other arithmetic  1.83 us (2%)
    all_to_all x3, blocking collectives, swap_copies(): return lax.all_to_all(copies, axis, split_axis=0, concat_axis=0, tiled=True)  33.7 us
    ppermute x15, waiting for transfers between devices, partners(): lax.ppermute(x, axis, [(i, i ^ d * stride) for i in range(total)])  12.8 us
    ppermute x15, starting transfers between devices, partners(): lax.ppermute(x, axis, [(i, i ^ d * stride) for i in range(total)])  11.5 us
    pallas_call x1, Pallas kernels, col_softmax(): pl.pallas_call(functools.partial(col_softmax_kernel, devices // members),...  10.8 us
    pallas_call x1, Pallas kernels, row_lse(): pl.pallas_call(row_lse_kernel, grid=(count // width,), in_specs=[in_smem,...  9.95 us
    pallas_call x1, Pallas kernels, embed_part(): pl.pallas_call(embed_kernel, in_specs=[in_smem] + [whole] * 6, out_specs=...  9.85 us
    all_to_all x1, starting transfers between devices, swap_copies(): return lax.all_to_all(copies, axis, split_axis=0, concat_axis=0, tiled=True)  7.25 us
    pallas_call x1, Pallas kernels, proto_part(): pl.pallas_call(proto_kernel, in_specs=[whole] * 9, out_specs=whole, out_s...  7.03 us
  transfers between devices with their start and end apart: 17, of which 12 were waited for; matrix products, arithmetic and copies ran while one was open for 0% of the time, Pallas kernels for 14%

profile of v8, /device:TPU:0, one launch (start us, length us, event | category | flops | bytes accessed | tf_op | source)
XLA Modules:
  0.0 118.4 jit_solution(11869827156075490748)
XLA Ops:
  0.6 0.9 slice_select_fusion
  1.5 0.8 broadcast_in_dim.28
  2.4 7.3 %all-to-all-start = ((bf16[8,128,256]{2,1,0:T(8,128)(2,1)}), bf16[8,128,256]{2,1,0:T(8,128)(2,1)S(1)}, u32[]{:S(2)}, u32[]{:S(2)}) async-start(bf16[8,128,256]{2,1,0:T(8,128)(2,1)} %broadcast_in_dim.28), calls=%async_computation | async-start | bytes 1048576 | tf_op jit(solution)/shard_map/all_to_all | solution.py:82
  9.6 0.1 pad_add_fusion.me_ref
  9.7 0.8 copy-done.2
  10.5 10.0 %row_lse.1 = (f32[32,1,256]{2,1,0:T(1,128)S(1)}, f32[2048,128]{1,0:T(8,128)}) custom-call(s32[3]{0:T(128)S(1)} %pad_add_fusion.me_ref, f32[1,16384]{1,0:T(1,128)S(1)} %bitcast.9, bf16[256,256]{1,0:T(8,128)(2,1)} %e_ref.3, bf16[16384,256]{1,0:T(8,128)(2,1)} %p_ref.3), custom_call_target="tpu_custom_call" | custom-call | flops 2147483648 | bytes 8388608 | tf_op jit(solution)/shard_map/row_lse/pallas_call | solution.py:259
  20.5 3.6 %all-to-all-done.mine_ref = bf16[8,128,256]{2,1,0:T(8,128)(2,1)S(1)} async-done(((bf16[8,128,256]{2,1,0:T(8,128)(2,1)}), bf16[8,128,256]{2,1,0:T(8,128)(2,1)S(1)}, u32[]{:S(2)}, u32[]{:S(2)}) %all-to-all-start) | async-done | bytes 524320 | tf_op jit(solution)/shard_map/all_to_all | solution.py:82
  24.1 0.0 collective-permute-start
  24.1 10.8 %all_to_all.20.lse_ref = f32[32,1,256]{2,1,0:T(1,128)S(1)} all-to-all(f32[32,1,256]{2,1,0:T(1,128)S(1)} %get-tuple-element.26), channel_id=1, replica_groups=mesh['batch'=8,'proto'=4] {'batch','proto'}, dimensions={0} | all-to-all | bytes 65536 | tf_op jit(solution)/shard_map/all_to_all | solution.py:82
  35.0 0.0 collective-permute-done.other_ref
  35.0 10.8 %col_softmax.1 = (f32[2048,2048]{1,0:T(8,128)S(1)}, f32[1,2048]{1,0:T(1,128)S(1)}, f32[1,2048]{1,0:T(1,128)S(1)}, f32[1,2048]{1,0:T(1,128)S(1)}, bf16[2048,256]{...) custom-call(s32[3]{0:T(128)S(1)} %pad_add_fusion.me_ref, f32[32,1,256]{2,1,0:T(1,128)S(1)} %all_to_all.20.lse_ref, ...), custom_call_target="tpu_custom_call" | custom-call | flops 2147483648 | bytes 16777216 | tf_op jit(solution)/shard_map/col_softmax/pallas_call | solution.py:390
  45.8 0.3 collective-permute-start.3
  46.1 1.6 %collective-permute-start.2 = (f32[1,2048]{1,0:T(1,128)S(1)}, f32[1,2048]{1,0:T(1,128)S(1)}, u32[]{:S(2)}, u32[]{:S(2)}) collective-permute-start(f32[1,2048]{1,0:T(1,128)S(1)} %get-tuple-element.28), channel_id=1, source_target_pairs={{0,2},{1,3},{2,0},{3,1},{4,6},{5,7},{6,4},{7,5},{8,10},{9,11},{10,... | collective-permute-start | bytes 24584 | tf_op jit(solution)/shard_map/ppermute | solution.py:67
  47.6 0.1 collective-permute-start.1
  47.7 1.2 %collective-permute-done.3 = f32[1,2048]{1,0:T(1,128)S(1)} collective-permute-done((f32[1,2048]{1,0:T(1,128)S(1)}, f32[1,2048]{1,0:T(1,128)S(1)}, u32[]{:S(2)}, u32[]{:S(2)}) %collective-permute-start.3) | collective-permute-done | bytes 8224 | tf_op jit(solution)/shard_map/ppermute | solution.py:67
  48.9 0.8 collective-permute-done.2
  49.8 0.0 collective-permute-done.1
  49.8 0.7 collective-permute-start.4
  50.4 3.1 %collective-permute-done.4 = f32[1,2048]{1,0:T(1,128)S(1)} collective-permute-done((f32[1,2048]{1,0:T(1,128)S(1)}, f32[1,2048]{1,0:T(1,128)S(1)}, u32[]{:S(2)}, u32[]{:S(2)}) %collective-permute-start.4) | collective-permute-done | bytes 8224 | tf_op jit(solution)/shard_map/ppermute | solution.py:67
  53.5 0.6 collective-permute-start.7
  54.2 1.5 %collective-permute-start.6 = (f32[1,2048]{1,0:T(1,128)S(1)}, f32[1,2048]{1,0:T(1,128)S(1)}, u32[]{:S(2)}, u32[]{:S(2)}) collective-permute-start(f32[1,2048]{1,0:T(1,128)S(1)} %add.45.refs_0_), channel_id=1, source_target_pairs={{0,16},{4,20},{8,24},{12,28},{16,0},{20,4},{24,8},{28,12},{1,17},{... | collective-permute-start | bytes 24584 | tf_op jit(solution)/shard_map/ppermute | solution.py:67
  55.6 2.3 %collective-permute-start.5 = (f32[1,2048]{1,0:T(1,128)S(1)}, f32[1,2048]{1,0:T(1,128)S(1)}, u32[]{:S(2)}, u32[]{:S(2)}) collective-permute-start(f32[1,2048]{1,0:T(1,128)S(1)} %add.45.refs_0_), channel_id=1, source_target_pairs={{0,8},{4,12},{8,0},{12,4},{16,24},{20,28},{24,16},{28,20},{1,9},{5... | collective-permute-start | bytes 24584 | tf_op jit(solution)/shard_map/ppermute | solution.py:67
  58.0 1.1 collective-permute-done.7.refs_3_
  59.0 0.0 collective-permute-done.6.refs_2_
  59.0 0.6 collective-permute-done.5.refs_1_
  59.6 4.1 %second_pair.1 = (f32[1,2048]{1,0:T(1,128)S(1)}, f32[1,2048]{1,0:T(1,128)S(1)}, f32[1,2048]{1,0:T(1,128)S(1)}, f32[2048,128]{1,0:T(8,128)S(1)}) custom-call(s32[3]{0:T(128)S(1)} %pad_add_fusion.me_ref, f32[1,2048]{1,0:T(1,128)S(1)} %add.45.refs_0_, f32[1,2048]{1,0:T(1,128)S(1)} %collective-permute-done.5.refs_1_, ...), custom_call_target="tpu_custom_call" | custom-call | flops 16777216 | bytes 16777216 | tf_op jit(solution)/shard_map/second_pair/pallas_call | solution.py:437
  63.7 0.1 collective-permute-start.10
  63.8 1.6 %collective-permute-start.9 = (f32[1,2048]{1,0:T(1,128)S(1)}, f32[1,2048]{1,0:T(1,128)S(1)}, u32[]{:S(2)}, u32[]{:S(2)}) collective-permute-start(f32[1,2048]{1,0:T(1,128)S(1)} %get-tuple-element.32), channel_id=1, source_target_pairs={{0,2},{1,3},{2,0},{3,1},{4,6},{5,7},{6,4},{7,5},{8,10},{9,11},{10,... | collective-permute-start | bytes 24584 | tf_op jit(solution)/shard_map/ppermute | solution.py:67
  65.4 0.2 collective-permute-start.8
  65.6 1.2 %collective-permute-done.10 = f32[1,2048]{1,0:T(1,128)S(1)} collective-permute-done((f32[1,2048]{1,0:T(1,128)S(1)}, f32[1,2048]{1,0:T(1,128)S(1)}, u32[]{:S(2)}, u32[]{:S(2)}) %collective-permute-start.10) | collective-permute-done | bytes 8224 | tf_op jit(solution)/shard_map/ppermute | solution.py:67
  66.8 0.7 collective-permute-done.9
  67.5 0.0 slice-start.1
  67.6 10.6 %all_to_all.21.bar_ref = f32[8,1,2048]{2,1,0:T(1,128)S(1)} all-to-all(f32[8,1,2048]{2,1,0:T(1,128)S(1)} %broadcast_in_dim.32), channel_id=1, replica_groups=mesh['batch'=8,'proto'=4] {'batch'}, dimensions={0} | all-to-all | bytes 131072 | tf_op jit(solution)/shard_map/all_to_all | solution.py:82
  78.2 3.3 %first_pair.1 = (f32[1,2048]{1,0:T(1,128)S(1)}, f32[1,2048]{1,0:T(1,128)S(1)}, f32[1,2048]{1,0:T(1,128)S(1)}, f32[2048,128]{1,0:T(8,128)S(1)}) custom-call(f32[8,1,2048]{2,1,0:T(1,128)S(1)} %all_to_all.21.bar_ref, f32[1,2048]{1,0:T(1,128)S(1)} %get-tuple-element.33.r_ref, f32[2048,128]{1,0:T(8,128)S(1)} %get-tuple-element.30.refs_6_.a_ref, ...), custom_call_target="tpu_custom_call" | custom-call | flops 16777216 | bytes 16777216 | tf_op jit(solution)/shard_map/first_pair/pallas_call | solution.py:473
  81.5 0.1 collective-permute-start.13
  81.6 1.6 %collective-permute-start.12 = (f32[1,2048]{1,0:T(1,128)S(1)}, f32[1,2048]{1,0:T(1,128)S(1)}, u32[]{:S(2)}, u32[]{:S(2)}) collective-permute-start(f32[1,2048]{1,0:T(1,128)S(1)} %get-tuple-element.34), channel_id=1, source_target_pairs={{0,2},{1,3},{2,0},{3,1},{4,6},{5,7},{6,4},{7,5},{8,10},{9,11},{10,... | collective-permute-start | bytes 24584 | tf_op jit(solution)/shard_map/ppermute | solution.py:67
  83.1 0.3 collective-permute-start.11
  83.4 1.2 %collective-permute-done.13 = f32[1,2048]{1,0:T(1,128)S(1)} collective-permute-done((f32[1,2048]{1,0:T(1,128)S(1)}, f32[1,2048]{1,0:T(1,128)S(1)}, u32[]{:S(2)}, u32[]{:S(2)}) %collective-permute-start.13) | collective-permute-done | bytes 8224 | tf_op jit(solution)/shard_map/ppermute | solution.py:67
  84.6 0.6 collective-permute-done.12
  85.3 0.1 broadcast_in_dim.34
  85.5 12.2 %all_to_all.22.last_ref = f32[8,1,8192]{2,1,0:T(1,128)S(1)} all-to-all(f32[8,1,8192]{2,1,0:T(1,128)S(1)} %broadcast_in_dim.34), channel_id=1, replica_groups=mesh['batch'=8,'proto'=4] {'batch'}, dimensions={0} | all-to-all | bytes 524288 | tf_op jit(solution)/shard_map/all_to_all | solution.py:82
  97.7 9.8 %embed_part.1 = f32[256,256]{1,0:T(8,128)S(1)} custom-call(s32[3]{0:T(128)S(1)} %pad_add_fusion.me_ref, f32[8,1,8192]{2,1,0:T(1,128)S(1)} %all_to_all.22.last_ref, f32[1,2048]{1,0:T(1,128)S(1)} %get-tuple-element.38.f_ref, f32[1,2048]{1,0:T(1,128)S(1)} %get-tuple-element.33.r_ref, f32[1,2048]{1,0:T(1,128)S(1)} %get-tuple-element.39.v_ref, ...), custom_call_target="tpu_custom_call" | custom-call | flops 4294967296 | bytes 8388608 | tf_op jit(solution)/shard_map/embed_part/pallas_call | solution.py:549
  107.6 0.1 collective-permute-start.14
  107.6 1.5 %collective-permute-done.14 = f32[256,256]{1,0:T(8,128)S(1)} collective-permute-done((f32[256,256]{1,0:T(8,128)S(1)}, f32[256,256]{1,0:T(8,128)S(1)}, u32[]{:S(2)}, u32[]{:S(2)}) %collective-permute-start.14) | collective-permute-done | bytes 262176 | tf_op jit(solution)/shard_map/ppermute | solution.py:67
  109.2 0.6 collective-permute-start.15
  109.8 7.0 %proto_part.1 = f32[2048,256]{1,0:T(8,128)} custom-call(f32[8,1,8192]{2,1,0:T(1,128)S(1)} %all_to_all.22.last_ref, f32[1,2048]{1,0:T(1,128)S(1)} %get-tuple-element.33.r_ref, f32[1,2048]{1,0:T(1,128)S(1)} %get-tuple-element.39.v_ref, f32[2048,128]{1,0:T(8,128)S(1)} %get-tuple-element.30.refs_6_.a_ref, f32[2048,128]{1,0:T(8,128)S(1)} %get-tuple-element.42.h_ref, ...), custom_call_target="tpu_custom_call" | custom-call | flops 2147483648 | bytes 16777216 | tf_op jit(solution)/shard_map/proto_part/pallas_call | solution.py:603
  116.8 0.8 collective-permute-done.15
  117.6 0.7 add.53
  (20 shorter events, 0.2 us)
Async XLA Ops:
  2.4 21.7 %all-to-all-start = ((bf16[8,128,256]{2,1,0:T(8,128)(2,1)}), bf16[8,128,256]{2,1,0:T(8,128)(2,1)S(1)}, u32[]{:S(2)}, u32[]{:S(2)}) async-start(bf16[8,128,256]{2,1,0:T(8,128)(2,1)} %broadcast_in_dim.28), calls=%async_computation | async-start | bytes 1048576 | tf_op jit(solution)/shard_map/all_to_all | solution.py:82
  9.7 0.8 copy-start.2
  10.5 49.1 %copy-start.3 = (f32[256]{0:T(256)S(1)}, f32[256]{0:T(256)}, u32[]{:S(2)}) copy-start(f32[256]{0:T(256)} %param.6) | copy-start | bytes 3076
  24.1 35.5 %copy-start = (f32[2048,128]{1,0:T(8,128)S(1)}, f32[2048,128]{1,0:T(8,128)}, u32[]{:S(2)}) copy-start(f32[2048,128]{1,0:T(8,128)} %get-tuple-element.29.refs_5_) | copy-start | bytes 3145732
  24.1 10.8 %collective-permute-start = (bf16[8,128,256]{2,1,0:T(8,128)(2,1)S(1)}, bf16[8,128,256]{2,1,0:T(8,128)(2,1)S(1)}, u32[]{:S(2)}, u32[]{:S(2)}) collective-permute-start(bf16[8,128,256]{2,1,0:T(8,128)(2,1)S(1)} %all-to-all-done.mine_ref), channel_id=1, source_target_pairs={{0,1},{1,0},{2,3},{3,2},{4,5},{5,4},{6,7},{7,6},{8,9},{9,8},{10,11... | collective-permute-start | bytes 1572872 | tf_op jit(solution)/shard_map/ppermute | solution.py:628
  45.8 3.1 %collective-permute-start.3 = (f32[1,2048]{1,0:T(1,128)S(1)}, f32[1,2048]{1,0:T(1,128)S(1)}, u32[]{:S(2)}, u32[]{:S(2)}) collective-permute-start(f32[1,2048]{1,0:T(1,128)S(1)} %get-tuple-element.28), channel_id=1, source_target_pairs={{0,3},{1,2},{2,1},{3,0},{4,7},{5,6},{6,5},{7,4},{8,11},{9,10},{10,... | collective-permute-start | bytes 24584 | tf_op jit(solution)/shard_map/ppermute | solution.py:67
  46.1 3.7 %collective-permute-start.2 = (f32[1,2048]{1,0:T(1,128)S(1)}, f32[1,2048]{1,0:T(1,128)S(1)}, u32[]{:S(2)}, u32[]{:S(2)}) collective-permute-start(f32[1,2048]{1,0:T(1,128)S(1)} %get-tuple-element.28), channel_id=1, source_target_pairs={{0,2},{1,3},{2,0},{3,1},{4,6},{5,7},{6,4},{7,5},{8,10},{9,11},{10,... | collective-permute-start | bytes 24584 | tf_op jit(solution)/shard_map/ppermute | solution.py:67
  47.6 2.1 %collective-permute-start.1 = (f32[1,2048]{1,0:T(1,128)S(1)}, f32[1,2048]{1,0:T(1,128)S(1)}, u32[]{:S(2)}, u32[]{:S(2)}) collective-permute-start(f32[1,2048]{1,0:T(1,128)S(1)} %get-tuple-element.28), channel_id=1, source_target_pairs={{0,1},{1,0},{2,3},{3,2},{4,5},{5,4},{6,7},{7,6},{8,9},{9,8},{10,11... | collective-permute-start | bytes 24584 | tf_op jit(solution)/shard_map/ppermute | solution.py:67
  49.8 3.7 %collective-permute-start.4 = (f32[1,2048]{1,0:T(1,128)S(1)}, f32[1,2048]{1,0:T(1,128)S(1)}, u32[]{:S(2)}, u32[]{:S(2)}) collective-permute-start(f32[1,2048]{1,0:T(1,128)S(1)} %add_add_fusion.2), channel_id=1, source_target_pairs={{0,4},{4,0},{8,12},{12,8},{16,20},{20,16},{24,28},{28,24},{1,5},{5... | collective-permute-start | bytes 24584 | tf_op jit(solution)/shard_map/ppermute | solution.py:67
  53.5 5.5 %collective-permute-start.7 = (f32[1,2048]{1,0:T(1,128)S(1)}, f32[1,2048]{1,0:T(1,128)S(1)}, u32[]{:S(2)}, u32[]{:S(2)}) collective-permute-start(f32[1,2048]{1,0:T(1,128)S(1)} %add.45.refs_0_), channel_id=1, source_target_pairs={{0,24},{4,28},{8,16},{12,20},{16,8},{20,12},{24,0},{28,4},{1,25},{... | collective-permute-start | bytes 24584 | tf_op jit(solution)/shard_map/ppermute | solution.py:67
  54.2 4.9 %collective-permute-start.6 = (f32[1,2048]{1,0:T(1,128)S(1)}, f32[1,2048]{1,0:T(1,128)S(1)}, u32[]{:S(2)}, u32[]{:S(2)}) collective-permute-start(f32[1,2048]{1,0:T(1,128)S(1)} %add.45.refs_0_), channel_id=1, source_target_pairs={{0,16},{4,20},{8,24},{12,28},{16,0},{20,4},{24,8},{28,12},{1,17},{... | collective-permute-start | bytes 24584 | tf_op jit(solution)/shard_map/ppermute | solution.py:67
  55.6 4.0 %collective-permute-start.5 = (f32[1,2048]{1,0:T(1,128)S(1)}, f32[1,2048]{1,0:T(1,128)S(1)}, u32[]{:S(2)}, u32[]{:S(2)}) collective-permute-start(f32[1,2048]{1,0:T(1,128)S(1)} %add.45.refs_0_), channel_id=1, source_target_pairs={{0,8},{4,12},{8,0},{12,4},{16,24},{20,28},{24,16},{28,20},{1,9},{5... | collective-permute-start | bytes 24584 | tf_op jit(solution)/shard_map/ppermute | solution.py:67
  59.6 38.1 %slice-start = ((s8[8388608]{0:T(1024)(128)(4,1)}), s8[4194304]{0:T(1024)(128)(4,1)S(1)}, s32[]{:S(2)}) async-start(s8[8388608]{0:T(1024)(128)(4,1)} %bitcast.7), calls=%async_computation.4 | async-start | bytes 8388608
  63.7 3.1 %collective-permute-start.10 = (f32[1,2048]{1,0:T(1,128)S(1)}, f32[1,2048]{1,0:T(1,128)S(1)}, u32[]{:S(2)}, u32[]{:S(2)}) collective-permute-start(f32[1,2048]{1,0:T(1,128)S(1)} %get-tuple-element.32), channel_id=1, source_target_pairs={{0,3},{1,2},{2,1},{3,0},{4,7},{5,6},{6,5},{7,4},{8,11},{9,10},{10,... | collective-permute-start | bytes 24584 | tf_op jit(solution)/shard_map/ppermute | solution.py:67
  63.8 3.7 %collective-permute-start.9 = (f32[1,2048]{1,0:T(1,128)S(1)}, f32[1,2048]{1,0:T(1,128)S(1)}, u32[]{:S(2)}, u32[]{:S(2)}) collective-permute-start(f32[1,2048]{1,0:T(1,128)S(1)} %get-tuple-element.32), channel_id=1, source_target_pairs={{0,2},{1,3},{2,0},{3,1},{4,6},{5,7},{6,4},{7,5},{8,10},{9,11},{10,... | collective-permute-start | bytes 24584 | tf_op jit(solution)/shard_map/ppermute | solution.py:67
  65.4 2.1 %collective-permute-start.8 = (f32[1,2048]{1,0:T(1,128)S(1)}, f32[1,2048]{1,0:T(1,128)S(1)}, u32[]{:S(2)}, u32[]{:S(2)}) collective-permute-start(f32[1,2048]{1,0:T(1,128)S(1)} %get-tuple-element.32), channel_id=1, source_target_pairs={{0,1},{1,0},{2,3},{3,2},{4,5},{5,4},{6,7},{7,6},{8,9},{9,8},{10,11... | collective-permute-start | bytes 24584 | tf_op jit(solution)/shard_map/ppermute | solution.py:67
  67.5 30.2 %slice-start.1 = ((s8[8388608]{0:T(1024)(128)(4,1)}), s8[4194304]{0:T(1024)(128)(4,1)S(1)}, s32[]{:S(2)}) async-start(s8[8388608]{0:T(1024)(128)(4,1)} %bitcast.7), calls=%async_computation.5 | async-start | bytes 8388608
  78.2 19.5 %copy-start.1 = (bf16[256,256]{1,0:T(8,128)(2,1)S(1)}, bf16[256,256]{1,0:T(8,128)(2,1)}, u32[]{:S(2)}) copy-start(bf16[256,256]{1,0:T(8,128)(2,1)} %e_ref.3) | copy-start | bytes 393220
  81.5 3.2 %collective-permute-start.13 = (f32[1,2048]{1,0:T(1,128)S(1)}, f32[1,2048]{1,0:T(1,128)S(1)}, u32[]{:S(2)}, u32[]{:S(2)}) collective-permute-start(f32[1,2048]{1,0:T(1,128)S(1)} %get-tuple-element.34), channel_id=1, source_target_pairs={{0,3},{1,2},{2,1},{3,0},{4,7},{5,6},{6,5},{7,4},{8,11},{9,10},{10,... | collective-permute-start | bytes 24584 | tf_op jit(solution)/shard_map/ppermute | solution.py:67
  81.6 3.7 %collective-permute-start.12 = (f32[1,2048]{1,0:T(1,128)S(1)}, f32[1,2048]{1,0:T(1,128)S(1)}, u32[]{:S(2)}, u32[]{:S(2)}) collective-permute-start(f32[1,2048]{1,0:T(1,128)S(1)} %get-tuple-element.34), channel_id=1, source_target_pairs={{0,2},{1,3},{2,0},{3,1},{4,6},{5,7},{6,4},{7,5},{8,10},{9,11},{10,... | collective-permute-start | bytes 24584 | tf_op jit(solution)/shard_map/ppermute | solution.py:67
  83.1 2.1 %collective-permute-start.11 = (f32[1,2048]{1,0:T(1,128)S(1)}, f32[1,2048]{1,0:T(1,128)S(1)}, u32[]{:S(2)}, u32[]{:S(2)}) collective-permute-start(f32[1,2048]{1,0:T(1,128)S(1)} %get-tuple-element.34), channel_id=1, source_target_pairs={{0,1},{1,0},{2,3},{3,2},{4,5},{5,4},{6,7},{7,6},{8,9},{9,8},{10,11... | collective-permute-start | bytes 24584 | tf_op jit(solution)/shard_map/ppermute | solution.py:67
  107.6 1.6 %collective-permute-start.14 = (f32[256,256]{1,0:T(8,128)S(1)}, f32[256,256]{1,0:T(8,128)S(1)}, u32[]{:S(2)}, u32[]{:S(2)}) collective-permute-start(f32[256,256]{1,0:T(8,128)S(1)} %embed_part.1), channel_id=1, source_target_pairs={{0,1},{1,0},{2,3},{3,2},{4,5},{5,4},{6,7},{7,6},{8,9},{9,8},{10,11... | collective-permute-start | bytes 786440 | tf_op jit(solution)/shard_map/ppermute | solution.py:67
  109.2 8.4 %collective-permute-start.15 = (f32[256,256]{1,0:T(8,128)S(1)}, f32[256,256]{1,0:T(8,128)S(1)}, u32[]{:S(2)}, u32[]{:S(2)}) collective-permute-start(f32[256,256]{1,0:T(8,128)S(1)} %add.52), channel_id=1, source_target_pairs={{0,2},{1,3},{2,0},{3,1},{4,6},{5,7},{6,4},{7,5},{8,10},{9,11},{10,... | collective-permute-start | bytes 786440 | tf_op jit(solution)/shard_map/ppermute | solution.py:67

commit v9 on v7

--- a/solution.py
+++ b/solution.py
@@ -140,10 +140,6 @@
     lax.fori_loop(0, blocks // 2 - 1, pair, 0)
     work((blocks - 1, 1), (blocks - 2, 0))
     work(None, (blocks - 1, 1))
-
-
-def sum_rows(ref):
-    return tree(add, [ref[d] for d in range(ref.shape[0])])
 
 
 def weighted(e_ref, weight_ref, part_ref):
@@ -450,8 +446,10 @@
     )(me, *rho_pieces, row_cot, in_vmem(cot), in_vmem(a), in_vmem(e))
 
 
-def first_pair_kernel(bar_ref, r_ref, a_ref, e_ref, out_ref, v_ref, y_ref, ay_ref, weight_ref, acc_ref, part_ref):
-    v_ref[...] = r_ref[...] * sum_rows(bar_ref)
+def first_pair_kernel(pieces, *refs):
+    bar_refs = refs[:pieces]
+    r_ref, a_ref, e_ref, out_ref, v_ref, y_ref, ay_ref, weight_ref, acc_ref, part_ref = refs[pieces:]
+    v_ref[...] = r_ref[...] * tree(add, [ref[...] for ref in bar_refs])
     weight_ref[...] = jnp.broadcast_to(v_ref[...], weight_ref.shape)
     weighted(e_ref, weight_ref, part_ref)
     part_ref[...] = lane_total(part_ref[...], jnp.sum) * a_ref[...]
@@ -461,11 +459,11 @@
     out_ref[...] = jnp.sum(acc_ref[...], axis=0, keepdims=True)
 
 
-def first_pair(bar, r, a, e):
+def first_pair(bar_pieces, r, a, e):
     count, rows = e.shape
     return pl.pallas_call(
-        first_pair_kernel,
-        in_specs=[whole] * 4,
+        functools.partial(first_pair_kernel, len(bar_pieces)),
+        in_specs=[whole] * (len(bar_pieces) + 3),
         out_specs=[whole] * 4,
         out_shape=[
             jax.ShapeDtypeStruct((1, rows), f32),
@@ -483,7 +481,7 @@
             flops=4 * rows * count, bytes_accessed=count * rows * 4, transcendentals=0
         ),
         name="first_pair",
-    )(bar, r, in_vmem(a), in_vmem(e))
+    )(*bar_pieces, r, in_vmem(a), in_vmem(e))
 
 
 def embed_kernel(
@@ -558,7 +556,7 @@
     )(me, last, f, r, v, in_vmem(embeddings), in_vmem(prototypes))
 
 
-def proto_kernel(last_ref, r_ref, v_ref, a_ref, h_ref, z_ref, ay_ref, all_ref, e_ref, out_ref, right_ref, b_ref):
+def proto_kernel(last_ref, r_ref, v_ref, a_ref, h_ref, z_ref, ay_ref, all_ref, e_ref, out_ref, right_ref, b_ref, done_ref, sem):
     count, rows = e_ref.shape
     height = b_ref.shape[1]
     x = tree(add, [last_ref[d, :, 0:rows] for d in range(last_ref.shape[0])])
@@ -584,9 +582,16 @@
                 part = parts[(k + 1) // (len(spans) // 2) - 1]
                 number, slot = block
                 here = pl.ds(pl.multiple_of(number * height, height) + part.start, height // 2)
-                out_ref[here, :] = score_scale * dot_nn(b_ref[slot, part, :], all_ref[...])
+                done_ref[here, :] = score_scale * dot_nn(b_ref[slot, part, :], all_ref[...])
+        if block is not None:
+            move(block[0]).start()
+
+    def move(number):
+        return pltpu.make_async_copy(done_ref.at[rows_of(number), :], out_ref.at[rows_of(number), :], sem.at[number])
 
     in_two_slots(blocks, work)
+    for number in range(blocks):
+        move(number).wait()
 
 
 def proto_part(last, r, v, a, h, z, ay, all_rows, e):
@@ -596,9 +601,14 @@
     return pl.pallas_call(
         proto_kernel,
         in_specs=[whole] * 9,
-        out_specs=whole,
-        out_shape=jax.ShapeDtypeStruct((count, depth), f32),
-        scratch_shapes=[pltpu.VMEM((lanes, rows), bf16), pltpu.VMEM((2, height, rows), bf16)],
+        out_specs=anywhere,
+        out_shape=pltpu.HBM((count, depth), f32),
+        scratch_shapes=[
+            pltpu.VMEM((lanes, rows), bf16),
+            pltpu.VMEM((2, height, rows), bf16),
+            pltpu.VMEM((count, depth), f32),
+            pltpu.SemaphoreType.DMA((count // height,)),
+        ],
         compiler_params=beside_plan,
         cost_estimate=pl.CostEstimate(
             flops=2 * rows * count * depth, bytes_accessed=count * rows * 4, transcendentals=0
@@ -613,16 +623,16 @@
     me = jnp.stack([member, holder % 2, holder]).astype(jnp.int32)
 
     short = embeddings.shape[0] // 2
-    half = lax.dynamic_slice_in_dim(embeddings, (holder % 2) * short, short, axis=0)
-    mine = share(half, "batch")
+    shape = (batch, short, embeddings.shape[1])
+    halves = (jnp.broadcast_to(half[None], shape) for half in (embeddings[:short], embeddings[short:]))
+    mine = swap_copies(jnp.where(holder % 2 == 0, *halves), "batch")
     lse = row_lse(embeddings, prototypes, batch * proto)
     mine, lse, me = lax.optimization_barrier((mine, lse, me))
     other = lax.ppermute(mine, "proto", [(i, i ^ 1) for i in range(proto)])
     lse = swap_copies(lse, both)
     e, rho, col_lse, f, all_rows, a, h, cot = col_softmax(me, lse, mine, other, prototypes, col_cot[None, :])
     bar, r, ratio, z = second_pair(me, total_pieces(rho), row_cot[None, :], cot, a, e)
-    bar = share(tree(add, partners(bar, "proto")), "batch")
-    x, v, y, ay = first_pair(bar, r, a, e)
+    x, v, y, ay = first_pair(total_pieces(bar), r, a, e)
     x = tree(add, partners(x, "proto"))
     last = share(jnp.concatenate([x, y, col_lse, ratio], axis=1), "batch")
     embed = embed_part(me, last, f, r, v, embeddings, prototypes)

time: 119 us -> 119 us (level)
  blocking collectives: 33.7 us -> 23.2 us
  waiting for transfers between devices: 18.5 us -> 24.8 us
  starting transfers between devices: 18.8 us -> 23.9 us
    all_to_all x3 -> x2, blocking collectives: 33.7 us -> 23.2 us  [swap_copies(): return lax.all_to_all(copies, axis, split_axis=0, concat_axis=0, tiled=True)]
    ppermute x15 -> x19, waiting for transfers between devices: 12.7 us -> 19 us  [partners(): lax.ppermute(x, axis, [(i, i ^ d * stride) for i in range(total)])]
    ppermute x15 -> x19, starting transfers between devices: 11.6 us -> 16.7 us  [partners(): lax.ppermute(x, axis, [(i, i ^ d * stride) for i in range(total)])]
  transfers between devices with their start and end apart: 17 -> 21, of which waited for: 12 -> 16; matrix products, arithmetic and copies ran while one was open for 0% -> 0% of each run, Pallas kernels for 13% -> 13%
where the time goes in v9:
time: 119 us
  Pallas kernels  43.1 us (36%)
  waiting for transfers between devices  24.8 us (21%)
  starting transfers between devices  23.9 us (20%)
  blocking collectives  23.2 us (19%)
  other arithmetic  1.84 us (2%)
    all_to_all x2, blocking collectives, swap_copies(): return lax.all_to_all(copies, axis, split_axis=0, concat_axis=0, tiled=True)  23.2 us
    ppermute x19, waiting for transfers between devices, partners(): lax.ppermute(x, axis, [(i, i ^ d * stride) for i in range(total)])  19 us
    ppermute x19, starting transfers between devices, partners(): lax.ppermute(x, axis, [(i, i ^ d * stride) for i in range(total)])  16.7 us
    pallas_call x1, Pallas kernels, col_softmax(): pl.pallas_call(functools.partial(col_softmax_kernel, devices // members),...  11.1 us
    pallas_call x1, Pallas kernels, embed_part(): pl.pallas_call(embed_kernel, in_specs=[in_smem] + [whole] * 6, out_specs=...  9.57 us
    pallas_call x1, Pallas kernels, row_lse(): pl.pallas_call(row_lse_kernel, grid=(count // width,), in_specs=[pl.Block...  8.61 us
    all_to_all x1, starting transfers between devices, swap_copies(): return lax.all_to_all(copies, axis, split_axis=0, concat_axis=0, tiled=True)  7.25 us
    pallas_call x1, Pallas kernels, proto_part(): pl.pallas_call(proto_kernel, in_specs=[whole] * 9, out_specs=anywhere, ou...  6.51 us
  transfers between devices with their start and end apart: 21, of which 16 were waited for; matrix products, arithmetic and copies ran while one was open for 0% of the time, Pallas kernels for 13%

profile of v9, /device:TPU:0, one launch (start us, length us, event | category | flops | bytes accessed | tf_op | source)
XLA Modules:
  0.0 118.7 jit_solution(5766351855940026615)
XLA Ops:
  0.6 0.9 slice_select_fusion
  1.5 0.8 broadcast_in_dim.10
  2.4 7.3 %all-to-all-start = ((bf16[8,128,256]{2,1,0:T(8,128)(2,1)}), bf16[8,128,256]{2,1,0:T(8,128)(2,1)S(1)}, u32[]{:S(2)}, u32[]{:S(2)}) async-start(bf16[8,128,256]{2,1,0:T(8,128)(2,1)} %broadcast_in_dim.10), calls=%async_computation | async-start | bytes 1048576 | tf_op jit(solution)/shard_map/all_to_all | solution.py:82
  9.6 0.1 pad_add_fusion.me_ref
  9.7 8.6 %row_lse.1 = f32[32,1,256]{2,1,0:T(1,128)S(1)} custom-call(bf16[256,256]{1,0:T(8,128)(2,1)} %e_ref.3, bf16[16384,256]{1,0:T(8,128)(2,1)} %p_ref.3), custom_call_target="tpu_custom_call" | custom-call | flops 2147483648 | bytes 8388608 | tf_op jit(solution)/shard_map/row_lse/pallas_call | solution.py:252
  18.3 5.8 %all-to-all-done.mine_ref = bf16[8,128,256]{2,1,0:T(8,128)(2,1)S(1)} async-done(((bf16[8,128,256]{2,1,0:T(8,128)(2,1)}), bf16[8,128,256]{2,1,0:T(8,128)(2,1)S(1)}, u32[]{:S(2)}, u32[]{:S(2)}) %all-to-all-start) | async-done | bytes 524320 | tf_op jit(solution)/shard_map/all_to_all | solution.py:82
  24.1 10.8 %all_to_all.15.lse_ref = f32[32,1,256]{2,1,0:T(1,128)S(1)} all-to-all(f32[32,1,256]{2,1,0:T(1,128)S(1)} %row_lse.1), channel_id=1, replica_groups=mesh['batch'=8,'proto'=4] {'batch','proto'}, dimensions={0} | all-to-all | bytes 65536 | tf_op jit(solution)/shard_map/all_to_all | solution.py:82
  34.9 11.1 %col_softmax.1 = (f32[2048,2048]{1,0:T(8,128)S(1)}, f32[1,2048]{1,0:T(1,128)S(1)}, f32[1,2048]{1,0:T(1,128)S(1)}, f32[1,2048]{1,0:T(1,128)S(1)}, bf16[2048,256]{...) custom-call(s32[3]{0:T(128)S(1)} %pad_add_fusion.me_ref, ...), custom_call_target="tpu_custom_call" | custom-call | flops 2147483648 | bytes 16777216 | tf_op jit(solution)/shard_map/col_softmax/pallas_call | solution.py:377
  46.0 0.3 collective-permute-start.3
  46.3 1.5 %collective-permute-start.2 = (f32[1,2048]{1,0:T(1,128)S(1)}, f32[1,2048]{1,0:T(1,128)S(1)}, u32[]{:S(2)}, u32[]{:S(2)}) collective-permute-start(f32[1,2048]{1,0:T(1,128)S(1)} %get-tuple-element.26), channel_id=1, source_target_pairs={{0,2},{1,3},{2,0},{3,1},{4,6},{5,7},{6,4},{7,5},{8,10},{9,11},{10,... | collective-permute-start | bytes 24584 | tf_op jit(solution)/shard_map/ppermute | solution.py:67
  47.9 0.1 collective-permute-start.1
  48.0 1.2 collective-permute-done.3
  49.2 0.8 collective-permute-done.2
  50.0 0.6 collective-permute-start.4
  50.6 3.1 %collective-permute-done.4 = f32[1,2048]{1,0:T(1,128)S(1)} collective-permute-done((f32[1,2048]{1,0:T(1,128)S(1)}, f32[1,2048]{1,0:T(1,128)S(1)}, u32[]{:S(2)}, u32[]{:S(2)}) %collective-permute-start.4) | collective-permute-done | bytes 8224 | tf_op jit(solution)/shard_map/ppermute | solution.py:67
  53.7 0.6 collective-permute-start.7
  54.3 1.5 %collective-permute-start.6 = (f32[1,2048]{1,0:T(1,128)S(1)}, f32[1,2048]{1,0:T(1,128)S(1)}, u32[]{:S(2)}, u32[]{:S(2)}) collective-permute-start(f32[1,2048]{1,0:T(1,128)S(1)} %add.48.refs_0_), channel_id=1, source_target_pairs={{0,16},{4,20},{8,24},{12,28},{16,0},{20,4},{24,8},{28,12},{1,17},{... | collective-permute-start | bytes 24584 | tf_op jit(solution)/shard_map/ppermute | solution.py:67
  55.8 2.4 %collective-permute-start.5 = (f32[1,2048]{1,0:T(1,128)S(1)}, f32[1,2048]{1,0:T(1,128)S(1)}, u32[]{:S(2)}, u32[]{:S(2)}) collective-permute-start(f32[1,2048]{1,0:T(1,128)S(1)} %add.48.refs_0_), channel_id=1, source_target_pairs={{0,8},{4,12},{8,0},{12,4},{16,24},{20,28},{24,16},{28,20},{1,9},{5... | collective-permute-start | bytes 24584 | tf_op jit(solution)/shard_map/ppermute | solution.py:67
  58.2 1.1 collective-permute-done.7.refs_3_
  59.2 0.6 collective-permute-done.5.refs_1_
  59.8 4.1 %second_pair.1 = (f32[1,2048]{1,0:T(1,128)S(1)}, f32[1,2048]{1,0:T(1,128)S(1)}, f32[1,2048]{1,0:T(1,128)S(1)}, f32[2048,128]{1,0:T(8,128)S(1)}) custom-call(s32[3]{0:T(128)S(1)} %pad_add_fusion.me_ref, f32[1,2048]{1,0:T(1,128)S(1)} %add.48.refs_0_, f32[1,2048]{1,0:T(1,128)S(1)} %collective-permute-done.5.refs_1_, ...), custom_call_target="tpu_custom_call" | custom-call | flops 16777216 | bytes 16777216 | tf_op jit(solution)/shard_map/second_pair/pallas_call | solution.py:426
  64.0 1.6 %collective-permute-start.9 = (f32[1,2048]{1,0:T(1,128)S(1)}, f32[1,2048]{1,0:T(1,128)S(1)}, u32[]{:S(2)}, u32[]{:S(2)}) collective-permute-start(f32[1,2048]{1,0:T(1,128)S(1)} %get-tuple-element.30), channel_id=1, source_target_pairs={{0,2},{1,3},{2,0},{3,1},{4,6},{5,7},{6,4},{7,5},{8,10},{9,11},{10,... | collective-permute-start | bytes 24584 | tf_op jit(solution)/shard_map/ppermute | solution.py:67
  65.6 0.3 collective-permute-start.8
  65.8 1.2 %collective-permute-done.10 = f32[1,2048]{1,0:T(1,128)S(1)} collective-permute-done((f32[1,2048]{1,0:T(1,128)S(1)}, f32[1,2048]{1,0:T(1,128)S(1)}, u32[]{:S(2)}, u32[]{:S(2)}) %collective-permute-start.10) | collective-permute-done | bytes 8224 | tf_op jit(solution)/shard_map/ppermute | solution.py:67
  67.0 0.6 collective-permute-done.9
  67.7 0.6 collective-permute-start.11
  68.4 3.1 %collective-permute-done.11 = f32[1,2048]{1,0:T(1,128)S(1)} collective-permute-done((f32[1,2048]{1,0:T(1,128)S(1)}, f32[1,2048]{1,0:T(1,128)S(1)}, u32[]{:S(2)}, u32[]{:S(2)}) %collective-permute-start.11) | collective-permute-done | bytes 8224 | tf_op jit(solution)/shard_map/ppermute | solution.py:67
  71.4 2.4 %collective-permute-start.14 = (f32[1,2048]{1,0:T(1,128)S(1)}, f32[1,2048]{1,0:T(1,128)S(1)}, u32[]{:S(2)}, u32[]{:S(2)}) collective-permute-start(f32[1,2048]{1,0:T(1,128)S(1)} %add.52.refs_0_), channel_id=1, source_target_pairs={{0,24},{4,28},{8,16},{12,20},{16,8},{20,12},{24,0},{28,4},{1,25},{... | collective-permute-start | bytes 24584 | tf_op jit(solution)/shard_map/ppermute | solution.py:67
  73.9 1.1 collective-permute-start.13
  75.0 0.9 collective-permute-start.12
  75.9 1.1 collective-permute-done.14.refs_3_
  77.0 1.5 %collective-permute-done.13.refs_2_ = f32[1,2048]{1,0:T(1,128)S(1)} collective-permute-done((f32[1,2048]{1,0:T(1,128)S(1)}, f32[1,2048]{1,0:T(1,128)S(1)}, u32[]{:S(2)}, u32[]{:S(2)}) %collective-permute-start.13) | collective-permute-done | bytes 8224 | tf_op jit(solution)/shard_map/ppermute | solution.py:67
  78.4 0.2 collective-permute-done.12.refs_1_
  78.6 3.3 %first_pair.1 = (f32[1,2048]{1,0:T(1,128)S(1)}, f32[1,2048]{1,0:T(1,128)S(1)}, f32[1,2048]{1,0:T(1,128)S(1)}, f32[2048,128]{1,0:T(8,128)S(1)}) custom-call(f32[1,2048]{1,0:T(1,128)S(1)} %add.52.refs_0_, f32[1,2048]{1,0:T(1,128)S(1)} %collective-permute-done.12.refs_1_, f32[1,2048]{1,0:T(1,128)S(1)} %collective-permute-done.13.refs_2_, ...), custom_call_target="tpu_custom_call" | custom-call | flops 16777216 | bytes 16777216 | tf_op jit(solution)/shard_map/first_pair/pallas_call | solution.py:464
  81.9 0.1 collective-permute-start.17
  82.0 1.6 %collective-permute-start.16 = (f32[1,2048]{1,0:T(1,128)S(1)}, f32[1,2048]{1,0:T(1,128)S(1)}, u32[]{:S(2)}, u32[]{:S(2)}) collective-permute-start(f32[1,2048]{1,0:T(1,128)S(1)} %get-tuple-element.32), channel_id=1, source_target_pairs={{0,2},{1,3},{2,0},{3,1},{4,6},{5,7},{6,4},{7,5},{8,10},{9,11},{10,... | collective-permute-start | bytes 24584 | tf_op jit(solution)/shard_map/ppermute | solution.py:67
  83.6 0.3 collective-permute-start.15
  83.8 1.2 %collective-permute-done.17 = f32[1,2048]{1,0:T(1,128)S(1)} collective-permute-done((f32[1,2048]{1,0:T(1,128)S(1)}, f32[1,2048]{1,0:T(1,128)S(1)}, u32[]{:S(2)}, u32[]{:S(2)}) %collective-permute-start.17) | collective-permute-done | bytes 8224 | tf_op jit(solution)/shard_map/ppermute | solution.py:67
  85.1 0.6 collective-permute-done.16
  85.8 0.1 broadcast_in_dim.28
  85.9 12.4 %all_to_all.16.last_ref = f32[8,1,8192]{2,1,0:T(1,128)S(1)} all-to-all(f32[8,1,8192]{2,1,0:T(1,128)S(1)} %broadcast_in_dim.28), channel_id=1, replica_groups=mesh['batch'=8,'proto'=4] {'batch'}, dimensions={0} | all-to-all | bytes 524288 | tf_op jit(solution)/shard_map/all_to_all | solution.py:82
  98.3 9.6 %embed_part.1 = f32[256,256]{1,0:T(8,128)S(1)} custom-call(s32[3]{0:T(128)S(1)} %pad_add_fusion.me_ref, f32[8,1,8192]{2,1,0:T(1,128)S(1)} %all_to_all.16.last_ref, f32[1,2048]{1,0:T(1,128)S(1)} %get-tuple-element.36.f_ref, f32[1,2048]{1,0:T(1,128)S(1)} %get-tuple-element.31.refs_4_.r_ref, f32[1,2048]{1,0:T(1,128)S(1)} %get-tuple-element.37.v_ref, ...), custom_call_target="tpu_custom_call" | custom-call | flops 4294967296 | bytes 8388608 | tf_op jit(solution)/shard_map/embed_part/pallas_call | solution.py:540
  107.9 0.1 collective-permute-start.18
  108.0 1.5 %collective-permute-done.18 = f32[256,256]{1,0:T(8,128)S(1)} collective-permute-done((f32[256,256]{1,0:T(8,128)S(1)}, f32[256,256]{1,0:T(8,128)S(1)}, u32[]{:S(2)}, u32[]{:S(2)}) %collective-permute-start.18) | collective-permute-done | bytes 262176 | tf_op jit(solution)/shard_map/ppermute | solution.py:67
  109.5 0.6 collective-permute-start.19
  110.2 6.5 %proto_part.1 = f32[2048,256]{1,0:T(8,128)} custom-call(f32[8,1,8192]{2,1,0:T(1,128)S(1)} %all_to_all.16.last_ref, f32[1,2048]{1,0:T(1,128)S(1)} %get-tuple-element.31.refs_4_.r_ref, f32[1,2048]{1,0:T(1,128)S(1)} %get-tuple-element.37.v_ref, f32[2048,128]{1,0:T(8,128)S(1)} %get-tuple-element.28.refs_6_.refs_5_.a_ref, ...), custom_call_target="tpu_custom_call" | custom-call | flops 2147483648 | bytes 16777216 | tf_op jit(solution)/shard_map/proto_part/pallas_call | solution.py:601
  116.7 1.3 %collective-permute-done.19 = f32[256,256]{1,0:T(8,128)S(1)} collective-permute-done((f32[256,256]{1,0:T(8,128)S(1)}, f32[256,256]{1,0:T(8,128)S(1)}, u32[]{:S(2)}, u32[]{:S(2)}) %collective-permute-start.19) | collective-permute-done | bytes 262176 | tf_op jit(solution)/shard_map/ppermute | solution.py:67
  118.0 0.7 add.57
  (23 shorter events, 0.2 us)
Async XLA Ops:
  2.4 21.7 %all-to-all-start = ((bf16[8,128,256]{2,1,0:T(8,128)(2,1)}), bf16[8,128,256]{2,1,0:T(8,128)(2,1)S(1)}, u32[]{:S(2)}, u32[]{:S(2)}) async-start(bf16[8,128,256]{2,1,0:T(8,128)(2,1)} %broadcast_in_dim.10), calls=%async_computation | async-start | bytes 1048576 | tf_op jit(solution)/shard_map/all_to_all | solution.py:82
  9.7 50.1 %copy-start.1 = (f32[256]{0:T(256)S(1)}, f32[256]{0:T(256)}, u32[]{:S(2)}) copy-start(f32[256]{0:T(256)} %param.6) | copy-start | bytes 3076
  24.1 10.8 %collective-permute-start = (bf16[8,128,256]{2,1,0:T(8,128)(2,1)S(1)}, bf16[8,128,256]{2,1,0:T(8,128)(2,1)S(1)}, u32[]{:S(2)}, u32[]{:S(2)}) collective-permute-start(bf16[8,128,256]{2,1,0:T(8,128)(2,1)S(1)} %all-to-all-done.mine_ref), channel_id=1, source_target_pairs={{0,1},{1,0},{2,3},{3,2},{4,5},{5,4},{6,7},{7,6},{8,9},{9,8},{10,11... | collective-permute-start | bytes 1572872 | tf_op jit(solution)/shard_map/ppermute | solution.py:631
  34.9 63.4 %slice-start = ((s8[8388608]{0:T(1024)(128)(4,1)}), s8[4194304]{0:T(1024)(128)(4,1)S(1)}, s32[]{:S(2)}) async-start(s8[8388608]{0:T(1024)(128)(4,1)} %bitcast.6), calls=%async_computation.3 | async-start | bytes 8388608
  46.0 3.1 %collective-permute-start.3 = (f32[1,2048]{1,0:T(1,128)S(1)}, f32[1,2048]{1,0:T(1,128)S(1)}, u32[]{:S(2)}, u32[]{:S(2)}) collective-permute-start(f32[1,2048]{1,0:T(1,128)S(1)} %get-tuple-element.26), channel_id=1, source_target_pairs={{0,3},{1,2},{2,1},{3,0},{4,7},{5,6},{6,5},{7,4},{8,11},{9,10},{10,... | collective-permute-start | bytes 24584 | tf_op jit(solution)/shard_map/ppermute | solution.py:67
  46.3 3.7 %collective-permute-start.2 = (f32[1,2048]{1,0:T(1,128)S(1)}, f32[1,2048]{1,0:T(1,128)S(1)}, u32[]{:S(2)}, u32[]{:S(2)}) collective-permute-start(f32[1,2048]{1,0:T(1,128)S(1)} %get-tuple-element.26), channel_id=1, source_target_pairs={{0,2},{1,3},{2,0},{3,1},{4,6},{5,7},{6,4},{7,5},{8,10},{9,11},{10,... | collective-permute-start | bytes 24584 | tf_op jit(solution)/shard_map/ppermute | solution.py:67
  47.9 2.1 %collective-permute-start.1 = (f32[1,2048]{1,0:T(1,128)S(1)}, f32[1,2048]{1,0:T(1,128)S(1)}, u32[]{:S(2)}, u32[]{:S(2)}) collective-permute-start(f32[1,2048]{1,0:T(1,128)S(1)} %get-tuple-element.26), channel_id=1, source_target_pairs={{0,1},{1,0},{2,3},{3,2},{4,5},{5,4},{6,7},{7,6},{8,9},{9,8},{10,11... | collective-permute-start | bytes 24584 | tf_op jit(solution)/shard_map/ppermute | solution.py:67
  50.0 3.7 %collective-permute-start.4 = (f32[1,2048]{1,0:T(1,128)S(1)}, f32[1,2048]{1,0:T(1,128)S(1)}, u32[]{:S(2)}, u32[]{:S(2)}) collective-permute-start(f32[1,2048]{1,0:T(1,128)S(1)} %add_add_fusion.2), channel_id=1, source_target_pairs={{0,4},{4,0},{8,12},{12,8},{16,20},{20,16},{24,28},{28,24},{1,5},{5... | collective-permute-start | bytes 24584 | tf_op jit(solution)/shard_map/ppermute | solution.py:67
  53.7 5.5 %collective-permute-start.7 = (f32[1,2048]{1,0:T(1,128)S(1)}, f32[1,2048]{1,0:T(1,128)S(1)}, u32[]{:S(2)}, u32[]{:S(2)}) collective-permute-start(f32[1,2048]{1,0:T(1,128)S(1)} %add.48.refs_0_), channel_id=1, source_target_pairs={{0,24},{4,28},{8,16},{12,20},{16,8},{20,12},{24,0},{28,4},{1,25},{... | collective-permute-start | bytes 24584 | tf_op jit(solution)/shard_map/ppermute | solution.py:67
  54.3 4.9 %collective-permute-start.6 = (f32[1,2048]{1,0:T(1,128)S(1)}, f32[1,2048]{1,0:T(1,128)S(1)}, u32[]{:S(2)}, u32[]{:S(2)}) collective-permute-start(f32[1,2048]{1,0:T(1,128)S(1)} %add.48.refs_0_), channel_id=1, source_target_pairs={{0,16},{4,20},{8,24},{12,28},{16,0},{20,4},{24,8},{28,12},{1,17},{... | collective-permute-start | bytes 24584 | tf_op jit(solution)/shard_map/ppermute | solution.py:67
  55.8 4.0 %collective-permute-start.5 = (f32[1,2048]{1,0:T(1,128)S(1)}, f32[1,2048]{1,0:T(1,128)S(1)}, u32[]{:S(2)}, u32[]{:S(2)}) collective-permute-start(f32[1,2048]{1,0:T(1,128)S(1)} %add.48.refs_0_), channel_id=1, source_target_pairs={{0,8},{4,12},{8,0},{12,4},{16,24},{20,28},{24,16},{28,20},{1,9},{5... | collective-permute-start | bytes 24584 | tf_op jit(solution)/shard_map/ppermute | solution.py:67
  59.8 38.5 %slice-start.1 = ((s8[8388608]{0:T(1024)(128)(4,1)}), s8[4194304]{0:T(1024)(128)(4,1)S(1)}, s32[]{:S(2)}) async-start(s8[8388608]{0:T(1024)(128)(4,1)} %bitcast.6), calls=%async_computation.4 | async-start | bytes 8388608
  63.9 3.1 %collective-permute-start.10 = (f32[1,2048]{1,0:T(1,128)S(1)}, f32[1,2048]{1,0:T(1,128)S(1)}, u32[]{:S(2)}, u32[]{:S(2)}) collective-permute-start(f32[1,2048]{1,0:T(1,128)S(1)} %get-tuple-element.30), channel_id=1, source_target_pairs={{0,3},{1,2},{2,1},{3,0},{4,7},{5,6},{6,5},{7,4},{8,11},{9,10},{10,... | collective-permute-start | bytes 24584 | tf_op jit(solution)/shard_map/ppermute | solution.py:67
  64.0 3.7 %collective-permute-start.9 = (f32[1,2048]{1,0:T(1,128)S(1)}, f32[1,2048]{1,0:T(1,128)S(1)}, u32[]{:S(2)}, u32[]{:S(2)}) collective-permute-start(f32[1,2048]{1,0:T(1,128)S(1)} %get-tuple-element.30), channel_id=1, source_target_pairs={{0,2},{1,3},{2,0},{3,1},{4,6},{5,7},{6,4},{7,5},{8,10},{9,11},{10,... | collective-permute-start | bytes 24584 | tf_op jit(solution)/shard_map/ppermute | solution.py:67
  65.6 2.1 %collective-permute-start.8 = (f32[1,2048]{1,0:T(1,128)S(1)}, f32[1,2048]{1,0:T(1,128)S(1)}, u32[]{:S(2)}, u32[]{:S(2)}) collective-permute-start(f32[1,2048]{1,0:T(1,128)S(1)} %get-tuple-element.30), channel_id=1, source_target_pairs={{0,1},{1,0},{2,3},{3,2},{4,5},{5,4},{6,7},{7,6},{8,9},{9,8},{10,11... | collective-permute-start | bytes 24584 | tf_op jit(solution)/shard_map/ppermute | solution.py:67
  67.7 3.7 %collective-permute-start.11 = (f32[1,2048]{1,0:T(1,128)S(1)}, f32[1,2048]{1,0:T(1,128)S(1)}, u32[]{:S(2)}, u32[]{:S(2)}) collective-permute-start(f32[1,2048]{1,0:T(1,128)S(1)} %add_add_fusion.1), channel_id=1, source_target_pairs={{0,4},{4,0},{8,12},{12,8},{16,20},{20,16},{24,28},{28,24},{1,5},{5... | collective-permute-start | bytes 24584 | tf_op jit(solution)/shard_map/ppermute | solution.py:67
  71.4 5.5 %collective-permute-start.14 = (f32[1,2048]{1,0:T(1,128)S(1)}, f32[1,2048]{1,0:T(1,128)S(1)}, u32[]{:S(2)}, u32[]{:S(2)}) collective-permute-start(f32[1,2048]{1,0:T(1,128)S(1)} %add.52.refs_0_), channel_id=1, source_target_pairs={{0,24},{4,28},{8,16},{12,20},{16,8},{20,12},{24,0},{28,4},{1,25},{... | collective-permute-start | bytes 24584 | tf_op jit(solution)/shard_map/ppermute | solution.py:67
  73.9 4.5 %collective-permute-start.13 = (f32[1,2048]{1,0:T(1,128)S(1)}, f32[1,2048]{1,0:T(1,128)S(1)}, u32[]{:S(2)}, u32[]{:S(2)}) collective-permute-start(f32[1,2048]{1,0:T(1,128)S(1)} %add.52.refs_0_), channel_id=1, source_target_pairs={{0,16},{4,20},{8,24},{12,28},{16,0},{20,4},{24,8},{28,12},{1,17},{... | collective-permute-start | bytes 24584 | tf_op jit(solution)/shard_map/ppermute | solution.py:67
  75.0 3.7 %collective-permute-start.12 = (f32[1,2048]{1,0:T(1,128)S(1)}, f32[1,2048]{1,0:T(1,128)S(1)}, u32[]{:S(2)}, u32[]{:S(2)}) collective-permute-start(f32[1,2048]{1,0:T(1,128)S(1)} %add.52.refs_0_), channel_id=1, source_target_pairs={{0,8},{4,12},{8,0},{12,4},{16,24},{20,28},{24,16},{28,20},{1,9},{5... | collective-permute-start | bytes 24584 | tf_op jit(solution)/shard_map/ppermute | solution.py:67
  78.6 19.7 %copy-start = (bf16[256,256]{1,0:T(8,128)(2,1)S(1)}, bf16[256,256]{1,0:T(8,128)(2,1)}, u32[]{:S(2)}) copy-start(bf16[256,256]{1,0:T(8,128)(2,1)} %e_ref.3) | copy-start | bytes 393220
  81.9 3.1 %collective-permute-start.17 = (f32[1,2048]{1,0:T(1,128)S(1)}, f32[1,2048]{1,0:T(1,128)S(1)}, u32[]{:S(2)}, u32[]{:S(2)}) collective-permute-start(f32[1,2048]{1,0:T(1,128)S(1)} %get-tuple-element.32), channel_id=1, source_target_pairs={{0,3},{1,2},{2,1},{3,0},{4,7},{5,6},{6,5},{7,4},{8,11},{9,10},{10,... | collective-permute-start | bytes 24584 | tf_op jit(solution)/shard_map/ppermute | solution.py:67
  82.0 3.7 %collective-permute-start.16 = (f32[1,2048]{1,0:T(1,128)S(1)}, f32[1,2048]{1,0:T(1,128)S(1)}, u32[]{:S(2)}, u32[]{:S(2)}) collective-permute-start(f32[1,2048]{1,0:T(1,128)S(1)} %get-tuple-element.32), channel_id=1, source_target_pairs={{0,2},{1,3},{2,0},{3,1},{4,6},{5,7},{6,4},{7,5},{8,10},{9,11},{10,... | collective-permute-start | bytes 24584 | tf_op jit(solution)/shard_map/ppermute | solution.py:67
  83.6 2.1 %collective-permute-start.15 = (f32[1,2048]{1,0:T(1,128)S(1)}, f32[1,2048]{1,0:T(1,128)S(1)}, u32[]{:S(2)}, u32[]{:S(2)}) collective-permute-start(f32[1,2048]{1,0:T(1,128)S(1)} %get-tuple-element.32), channel_id=1, source_target_pairs={{0,1},{1,0},{2,3},{3,2},{4,5},{5,4},{6,7},{7,6},{8,9},{9,8},{10,11... | collective-permute-start | bytes 24584 | tf_op jit(solution)/shard_map/ppermute | solution.py:67
  107.9 1.6 %collective-permute-start.18 = (f32[256,256]{1,0:T(8,128)S(1)}, f32[256,256]{1,0:T(8,128)S(1)}, u32[]{:S(2)}, u32[]{:S(2)}) collective-permute-start(f32[256,256]{1,0:T(8,128)S(1)} %embed_part.1), channel_id=1, source_target_pairs={{0,1},{1,0},{2,3},{3,2},{4,5},{5,4},{6,7},{7,6},{8,9},{9,8},{10,11... | collective-permute-start | bytes 786440 | tf_op jit(solution)/shard_map/ppermute | solution.py:67
  109.5 8.4 %collective-permute-start.19 = (f32[256,256]{1,0:T(8,128)S(1)}, f32[256,256]{1,0:T(8,128)S(1)}, u32[]{:S(2)}, u32[]{:S(2)}) collective-permute-start(f32[256,256]{1,0:T(8,128)S(1)} %add.56), channel_id=1, source_target_pairs={{0,2},{1,3},{2,0},{3,1},{4,6},{5,7},{6,4},{7,5},{8,10},{9,11},{10,... | collective-permute-start | bytes 786440 | tf_op jit(solution)/shard_map/ppermute | solution.py:67

commit v10 on v7

--- a/solution.py
+++ b/solution.py
@@ -66,16 +66,6 @@
     return [x] + [
         lax.ppermute(x, axis, [(i, i ^ (d * stride)) for i in range(total)]) for d in range(1, size or total)
     ]
-
-
-def total_pieces(x):
-    pieces = partners(x, "proto")
-    total, stride = lax.axis_size("batch"), 1
-    while stride < total:
-        size = min(4, total // stride) if stride > 1 else 2
-        pieces = partners(tree(add, pieces), "batch", stride, size)
-        stride *= size
-    return pieces
 
 
 def swap_copies(copies, axis):
@@ -409,11 +399,11 @@
     )(me, lse, in_vmem(mine, few(rows)), in_vmem(other, few(rows)), in_hbm(prototypes), in_hbm(col_cot))
 
 
-def second_pair_kernel(pieces, me_ref, *refs):
-    rho_refs = refs[:pieces]
-    row_cot_ref, cot_ref, a_ref, e_ref, out_ref, r_ref, ratio_ref, z_ref, weight_ref, acc_ref, part_ref = refs[pieces:]
+def second_pair_kernel(
+    me_ref, rho_ref, row_cot_ref, cot_ref, a_ref, e_ref, out_ref, r_ref, ratio_ref, z_ref, weight_ref, acc_ref, part_ref
+):
     own = row_cot_ref.shape[1]
-    r_ref[...] = 1.0 / tree(add, [ref[...] for ref in rho_refs])
+    r_ref[...] = 1.0 / sum_rows(rho_ref)
     weight_ref[...] = jnp.broadcast_to(r_ref[...], weight_ref.shape)
     weighted(e_ref, weight_ref, part_ref)
     z_ref[...] = cot_ref[...] / lane_total(part_ref[...], jnp.sum)
@@ -425,11 +415,11 @@
     out_ref[:, mine] += jnp.where(me_ref[2] == 0, row_cot_ref[...], 0.0)
 
 
-def second_pair(me, rho_pieces, row_cot, cot, a, e):
+def second_pair(me, rho, row_cot, cot, a, e):
     count, rows = e.shape
     return pl.pallas_call(
-        functools.partial(second_pair_kernel, len(rho_pieces)),
-        in_specs=[in_smem] + [whole] * (len(rho_pieces) + 4),
+        second_pair_kernel,
+        in_specs=[in_smem] + [whole] * 5,
         out_specs=[whole] * 4,
         out_shape=[
             jax.ShapeDtypeStruct((1, rows), f32),
@@ -447,7 +437,7 @@
             flops=4 * rows * count, bytes_accessed=count * rows * 4, transcendentals=0
         ),
         name="second_pair",
-    )(me, *rho_pieces, row_cot, in_vmem(cot), in_vmem(a), in_vmem(e))
+    )(me, rho, row_cot, in_vmem(cot), in_vmem(a), in_vmem(e))
 
 
 def first_pair_kernel(bar_ref, r_ref, a_ref, e_ref, out_ref, v_ref, y_ref, ay_ref, weight_ref, acc_ref, part_ref):
@@ -558,7 +548,7 @@
     )(me, last, f, r, v, in_vmem(embeddings), in_vmem(prototypes))
 
 
-def proto_kernel(last_ref, r_ref, v_ref, a_ref, h_ref, z_ref, ay_ref, all_ref, e_ref, out_ref, right_ref, b_ref):
+def proto_kernel(last_ref, r_ref, v_ref, a_ref, h_ref, z_ref, ay_ref, all_ref, e_ref, out_ref, right_ref, b_ref, done_ref, sem):
     count, rows = e_ref.shape
     height = b_ref.shape[1]
     x = tree(add, [last_ref[d, :, 0:rows] for d in range(last_ref.shape[0])])
@@ -584,9 +574,16 @@
                 part = parts[(k + 1) // (len(spans) // 2) - 1]
                 number, slot = block
                 here = pl.ds(pl.multiple_of(number * height, height) + part.start, height // 2)
-                out_ref[here, :] = score_scale * dot_nn(b_ref[slot, part, :], all_ref[...])
+                done_ref[here, :] = score_scale * dot_nn(b_ref[slot, part, :], all_ref[...])
+        if block is not None:
+            move(block[0]).start()
+
+    def move(number):
+        return pltpu.make_async_copy(done_ref.at[rows_of(number), :], out_ref.at[rows_of(number), :], sem.at[number])
 
     in_two_slots(blocks, work)
+    for number in range(blocks):
+        move(number).wait()
 
 
 def proto_part(last, r, v, a, h, z, ay, all_rows, e):
@@ -596,9 +593,14 @@
     return pl.pallas_call(
         proto_kernel,
         in_specs=[whole] * 9,
-        out_specs=whole,
-        out_shape=jax.ShapeDtypeStruct((count, depth), f32),
-        scratch_shapes=[pltpu.VMEM((lanes, rows), bf16), pltpu.VMEM((2, height, rows), bf16)],
+        out_specs=anywhere,
+        out_shape=pltpu.HBM((count, depth), f32),
+        scratch_shapes=[
+            pltpu.VMEM((lanes, rows), bf16),
+            pltpu.VMEM((2, height, rows), bf16),
+            pltpu.VMEM((count, depth), f32),
+            pltpu.SemaphoreType.DMA((count // height,)),
+        ],
         compiler_params=beside_plan,
         cost_estimate=pl.CostEstimate(
             flops=2 * rows * count * depth, bytes_accessed=count * rows * 4, transcendentals=0
@@ -620,7 +622,8 @@
     other = lax.ppermute(mine, "proto", [(i, i ^ 1) for i in range(proto)])
     lse = swap_copies(lse, both)
     e, rho, col_lse, f, all_rows, a, h, cot = col_softmax(me, lse, mine, other, prototypes, col_cot[None, :])
-    bar, r, ratio, z = second_pair(me, total_pieces(rho), row_cot[None, :], cot, a, e)
+    rho = share(tree(add, partners(rho, "proto")), "batch")
+    bar, r, ratio, z = second_pair(me, rho, row_cot[None, :], cot, a, e)
     bar = share(tree(add, partners(bar, "proto")), "batch")
     x, v, y, ay = first_pair(bar, r, a, e)
     x = tree(add, partners(x, "proto"))

time: 119 us -> 117 us (0.983)
  blocking collectives: 33.7 us -> 41.9 us
  starting transfers between devices: 18.8 us -> 13.8 us
  waiting for transfers between devices: 18.5 us -> 14.3 us
    all_to_all x3 -> x4, blocking collectives: 33.7 us -> 41.9 us  [swap_copies(): return lax.all_to_all(copies, axis, split_axis=0, concat_axis=0, tiled=True)]
    ppermute x15 -> x11, starting transfers between devices: 11.6 us -> 6.5 us  [partners(): lax.ppermute(x, axis, [(i, i ^ d * stride) for i in range(total)])]
    ppermute x15 -> x11, waiting for transfers between devices: 12.7 us -> 8.5 us  [partners(): lax.ppermute(x, axis, [(i, i ^ d * stride) for i in range(total)])]
  transfers between devices with their start and end apart: 17 -> 13, of which waited for: 12 -> 9; matrix products, arithmetic and copies ran while one was open for 0% -> 0% of each run, Pallas kernels for 13% -> 13%
where the time goes in v10:
time: 117 us
  Pallas kernels  43 us (37%)
  blocking collectives  41.9 us (36%)
  waiting for transfers between devices  14.3 us (12%)
  starting transfers between devices  13.8 us (12%)
  local copies, waits for them, and re-layouts  1.9 us (2%)
    all_to_all x4, blocking collectives, swap_copies(): return lax.all_to_all(copies, axis, split_axis=0, concat_axis=0, tiled=True)  41.9 us
    pallas_call x1, Pallas kernels, col_softmax(): pl.pallas_call(functools.partial(col_softmax_kernel, devices // members),...  11.1 us
    pallas_call x1, Pallas kernels, embed_part(): pl.pallas_call(embed_kernel, in_specs=[in_smem] + [whole] * 6, out_specs=...  9.5 us
    pallas_call x1, Pallas kernels, row_lse(): pl.pallas_call(row_lse_kernel, grid=(count // width,), in_specs=[pl.Block...  8.61 us
    ppermute x11, waiting for transfers between devices, partners(): lax.ppermute(x, axis, [(i, i ^ d * stride) for i in range(total)])  8.5 us
    all_to_all x1, starting transfers between devices, swap_copies(): return lax.all_to_all(copies, axis, split_axis=0, concat_axis=0, tiled=True)  7.25 us
    pallas_call x1, Pallas kernels, proto_part(): pl.pallas_call(proto_kernel, in_specs=[whole] * 9, out_specs=anywhere, ou...  6.51 us
    ppermute x11, starting transfers between devices, partners(): lax.ppermute(x, axis, [(i, i ^ d * stride) for i in range(total)])  6.5 us
  transfers between devices with their start and end apart: 13, of which 9 were waited for; matrix products, arithmetic and copies ran while one was open for 0% of the time, Pallas kernels for 13%

profile of v10, /device:TPU:0, one launch (start us, length us, event | category | flops | bytes accessed | tf_op | source)
XLA Modules:
  0.0 116.6 jit_solution(2891201529324167733)
XLA Ops:
  0.6 0.8 constant_dynamic-slice_fusion
  1.5 0.8 broadcast_in_dim.36
  2.3 7.3 %all-to-all-start = ((bf16[8,128,256]{2,1,0:T(8,128)(2,1)}), bf16[8,128,256]{2,1,0:T(8,128)(2,1)S(1)}, u32[]{:S(2)}, u32[]{:S(2)}) async-start(bf16[8,128,256]{2,1,0:T(8,128)(2,1)} %broadcast_in_dim.36), calls=%async_computation | async-start | bytes 1048576 | tf_op jit(solution)/shard_map/all_to_all | solution.py:72
  9.6 0.1 pad_add_fusion.me_ref
  9.7 0.0 copy-start.1
  9.7 8.6 %row_lse.1 = f32[32,1,256]{2,1,0:T(1,128)S(1)} custom-call(bf16[256,256]{1,0:T(8,128)(2,1)} %e_ref.3, bf16[16384,256]{1,0:T(8,128)(2,1)} %p_ref.3), custom_call_target="tpu_custom_call" | custom-call | flops 2147483648 | bytes 8388608 | tf_op jit(solution)/shard_map/row_lse/pallas_call | solution.py:246
  18.3 5.8 %all-to-all-done.mine_ref = bf16[8,128,256]{2,1,0:T(8,128)(2,1)S(1)} async-done(((bf16[8,128,256]{2,1,0:T(8,128)(2,1)}), bf16[8,128,256]{2,1,0:T(8,128)(2,1)S(1)}, u32[]{:S(2)}, u32[]{:S(2)}) %all-to-all-start) | async-done | bytes 524320 | tf_op jit(solution)/shard_map/all_to_all | solution.py:72
  24.1 0.0 collective-permute-start
  24.1 10.8 %all_to_all.25.lse_ref = f32[32,1,256]{2,1,0:T(1,128)S(1)} all-to-all(f32[32,1,256]{2,1,0:T(1,128)S(1)} %row_lse.1), channel_id=1, replica_groups=mesh['batch'=8,'proto'=4] {'batch','proto'}, dimensions={0} | all-to-all | bytes 65536 | tf_op jit(solution)/shard_map/all_to_all | solution.py:72
  34.9 0.0 collective-permute-done.other_ref
  34.9 11.1 %col_softmax.1 = (f32[2048,2048]{1,0:T(8,128)S(1)}, f32[1,2048]{1,0:T(1,128)S(1)}, f32[1,2048]{1,0:T(1,128)S(1)}, f32[1,2048]{1,0:T(1,128)S(1)}, bf16[2048,256]{...) custom-call(s32[3]{0:T(128)S(1)} %pad_add_fusion.me_ref, ...), custom_call_target="tpu_custom_call" | custom-call | flops 2147483648 | bytes 16777216 | tf_op jit(solution)/shard_map/col_softmax/pallas_call | solution.py:371
  46.0 0.3 collective-permute-start.3
  46.3 1.5 %collective-permute-start.2 = (f32[1,2048]{1,0:T(1,128)S(1)}, f32[1,2048]{1,0:T(1,128)S(1)}, u32[]{:S(2)}, u32[]{:S(2)}) collective-permute-start(f32[1,2048]{1,0:T(1,128)S(1)} %get-tuple-element.26), channel_id=1, source_target_pairs={{0,2},{1,3},{2,0},{3,1},{4,6},{5,7},{6,4},{7,5},{8,10},{9,11},{10,... | collective-permute-start | bytes 24584 | tf_op jit(solution)/shard_map/ppermute | solution.py:67
  47.8 0.1 collective-permute-start.1
  48.0 1.2 %collective-permute-done.3 = f32[1,2048]{1,0:T(1,128)S(1)} collective-permute-done((f32[1,2048]{1,0:T(1,128)S(1)}, f32[1,2048]{1,0:T(1,128)S(1)}, u32[]{:S(2)}, u32[]{:S(2)}) %collective-permute-start.3) | collective-permute-done | bytes 8224 | tf_op jit(solution)/shard_map/ppermute | solution.py:67
  49.1 0.8 collective-permute-done.2
  49.9 0.0 collective-permute-done.1
  50.0 9.3 %all_to_all.26.rho_ref = f32[8,1,2048]{2,1,0:T(1,128)S(1)} all-to-all(f32[8,1,2048]{2,1,0:T(1,128)S(1)} %broadcast_in_dim.39), channel_id=1, replica_groups=mesh['batch'=8,'proto'=4] {'batch'}, dimensions={0} | all-to-all | bytes 131072 | tf_op jit(solution)/shard_map/all_to_all | solution.py:72
  59.3 0.0 copy-done.1
  59.3 0.0 slice-start
  59.3 4.1 %second_pair.1 = (f32[1,2048]{1,0:T(1,128)S(1)}, f32[1,2048]{1,0:T(1,128)S(1)}, f32[1,2048]{1,0:T(1,128)S(1)}, f32[2048,128]{1,0:T(8,128)S(1)}) custom-call(s32[3]{0:T(128)S(1)} %pad_add_fusion.me_ref, f32[8,1,2048]{2,1,0:T(1,128)S(1)} %all_to_all.26.rho_ref, f32[1,256]{1,0:T(1,128)S(1)} %bitcast.10, f32[2048,128]{1,0:T(8,128)S(1)} %get-tuple-element.27.cot_ref, ...), custom_call_target="tpu_custom_call" | custom-call | flops 16777216 | bytes 16777216 | tf_op jit(solution)/shard_map/second_pair/pallas_call | solution.py:420
  63.4 0.1 collective-permute-start.6
  63.5 1.6 %collective-permute-start.5 = (f32[1,2048]{1,0:T(1,128)S(1)}, f32[1,2048]{1,0:T(1,128)S(1)}, u32[]{:S(2)}, u32[]{:S(2)}) collective-permute-start(f32[1,2048]{1,0:T(1,128)S(1)} %get-tuple-element.30), channel_id=1, source_target_pairs={{0,2},{1,3},{2,0},{3,1},{4,6},{5,7},{6,4},{7,5},{8,10},{9,11},{10,... | collective-permute-start | bytes 24584 | tf_op jit(solution)/shard_map/ppermute | solution.py:67
  65.0 0.3 collective-permute-start.4
  65.3 1.2 %collective-permute-done.6 = f32[1,2048]{1,0:T(1,128)S(1)} collective-permute-done((f32[1,2048]{1,0:T(1,128)S(1)}, f32[1,2048]{1,0:T(1,128)S(1)}, u32[]{:S(2)}, u32[]{:S(2)}) %collective-permute-start.6) | collective-permute-done | bytes 8224 | tf_op jit(solution)/shard_map/ppermute | solution.py:67
  66.5 0.6 collective-permute-done.5
  67.2 0.0 collective-permute-done.4
  67.2 0.0 slice-start.1
  67.3 9.6 %all_to_all.27.bar_ref = f32[8,1,2048]{2,1,0:T(1,128)S(1)} all-to-all(f32[8,1,2048]{2,1,0:T(1,128)S(1)} %broadcast_in_dim.42), channel_id=1, replica_groups=mesh['batch'=8,'proto'=4] {'batch'}, dimensions={0} | all-to-all | bytes 131072 | tf_op jit(solution)/shard_map/all_to_all | solution.py:72
  76.8 3.3 %first_pair.1 = (f32[1,2048]{1,0:T(1,128)S(1)}, f32[1,2048]{1,0:T(1,128)S(1)}, f32[1,2048]{1,0:T(1,128)S(1)}, f32[2048,128]{1,0:T(8,128)S(1)}) custom-call(f32[8,1,2048]{2,1,0:T(1,128)S(1)} %all_to_all.27.bar_ref, f32[1,2048]{1,0:T(1,128)S(1)} %get-tuple-element.31.r_ref, f32[2048,128]{1,0:T(8,128)S(1)} %get-tuple-element.28.a_ref, ...), custom_call_target="tpu_custom_call" | custom-call | flops 16777216 | bytes 16777216 | tf_op jit(solution)/shard_map/first_pair/pallas_call | solution.py:456
  80.1 0.1 collective-permute-start.9
  80.2 1.6 %collective-permute-start.8 = (f32[1,2048]{1,0:T(1,128)S(1)}, f32[1,2048]{1,0:T(1,128)S(1)}, u32[]{:S(2)}, u32[]{:S(2)}) collective-permute-start(f32[1,2048]{1,0:T(1,128)S(1)} %get-tuple-element.32), channel_id=1, source_target_pairs={{0,2},{1,3},{2,0},{3,1},{4,6},{5,7},{6,4},{7,5},{8,10},{9,11},{10,... | collective-permute-start | bytes 24584 | tf_op jit(solution)/shard_map/ppermute | solution.py:67
  81.7 0.3 collective-permute-start.7
  82.0 1.2 %collective-permute-done.9 = f32[1,2048]{1,0:T(1,128)S(1)} collective-permute-done((f32[1,2048]{1,0:T(1,128)S(1)}, f32[1,2048]{1,0:T(1,128)S(1)}, u32[]{:S(2)}, u32[]{:S(2)}) %collective-permute-start.9) | collective-permute-done | bytes 8224 | tf_op jit(solution)/shard_map/ppermute | solution.py:67
  83.2 0.6 collective-permute-done.8
  83.9 0.0 collective-permute-done.7
  83.9 0.1 broadcast_in_dim.44
  84.1 12.2 %all_to_all.28.last_ref = f32[8,1,8192]{2,1,0:T(1,128)S(1)} all-to-all(f32[8,1,8192]{2,1,0:T(1,128)S(1)} %broadcast_in_dim.44), channel_id=1, replica_groups=mesh['batch'=8,'proto'=4] {'batch'}, dimensions={0} | all-to-all | bytes 524288 | tf_op jit(solution)/shard_map/all_to_all | solution.py:72
  96.3 0.0 slice-done
  96.3 0.0 slice-done.1
  96.3 0.0 copy-done
  96.3 9.5 %embed_part.1 = f32[256,256]{1,0:T(8,128)S(1)} custom-call(s32[3]{0:T(128)S(1)} %pad_add_fusion.me_ref, f32[8,1,8192]{2,1,0:T(1,128)S(1)} %all_to_all.28.last_ref, f32[1,2048]{1,0:T(1,128)S(1)} %get-tuple-element.36.f_ref, f32[1,2048]{1,0:T(1,128)S(1)} %get-tuple-element.31.r_ref, f32[1,2048]{1,0:T(1,128)S(1)} %get-tuple-element.37.v_ref, ...), custom_call_target="tpu_custom_call" | custom-call | flops 4294967296 | bytes 8388608 | tf_op jit(solution)/shard_map/embed_part/pallas_call | solution.py:532
  105.8 0.1 collective-permute-start.10
  105.9 1.5 %collective-permute-done.10 = f32[256,256]{1,0:T(8,128)S(1)} collective-permute-done((f32[256,256]{1,0:T(8,128)S(1)}, f32[256,256]{1,0:T(8,128)S(1)}, u32[]{:S(2)}, u32[]{:S(2)}) %collective-permute-start.10) | collective-permute-done | bytes 262176 | tf_op jit(solution)/shard_map/ppermute | solution.py:67
  107.4 0.6 collective-permute-start.11
  108.1 6.5 %proto_part.1 = f32[2048,256]{1,0:T(8,128)} custom-call(f32[8,1,8192]{2,1,0:T(1,128)S(1)} %all_to_all.28.last_ref, f32[1,2048]{1,0:T(1,128)S(1)} %get-tuple-element.31.r_ref, f32[1,2048]{1,0:T(1,128)S(1)} %get-tuple-element.37.v_ref, f32[2048,128]{1,0:T(8,128)S(1)} %get-tuple-element.28.a_ref, f32[2048,128]{1,0:T(8,128)S(1)} %get-tuple-element.40.h_ref, ...), custom_call_target="tpu_custom_call" | custom-call | flops 2147483648 | bytes 16777216 | tf_op jit(solution)/shard_map/proto_part/pallas_call | solution.py:593
  114.6 1.3 %collective-permute-done.11 = f32[256,256]{1,0:T(8,128)S(1)} collective-permute-done((f32[256,256]{1,0:T(8,128)S(1)}, f32[256,256]{1,0:T(8,128)S(1)}, u32[]{:S(2)}, u32[]{:S(2)}) %collective-permute-start.11) | collective-permute-done | bytes 262176 | tf_op jit(solution)/shard_map/ppermute | solution.py:67
  115.9 0.7 add.53
  (9 shorter events, 0.2 us)
Async XLA Ops:
  2.3 21.7 %all-to-all-start = ((bf16[8,128,256]{2,1,0:T(8,128)(2,1)}), bf16[8,128,256]{2,1,0:T(8,128)(2,1)S(1)}, u32[]{:S(2)}, u32[]{:S(2)}) async-start(bf16[8,128,256]{2,1,0:T(8,128)(2,1)} %broadcast_in_dim.36), calls=%async_computation | async-start | bytes 1048576 | tf_op jit(solution)/shard_map/all_to_all | solution.py:72
  9.7 49.6 %copy-start.1 = (f32[256]{0:T(256)S(1)}, f32[256]{0:T(256)}, u32[]{:S(2)}) copy-start(f32[256]{0:T(256)} %param.6) | copy-start | bytes 3076
  24.1 10.8 %collective-permute-start = (bf16[8,128,256]{2,1,0:T(8,128)(2,1)S(1)}, bf16[8,128,256]{2,1,0:T(8,128)(2,1)S(1)}, u32[]{:S(2)}, u32[]{:S(2)}) collective-permute-start(bf16[8,128,256]{2,1,0:T(8,128)(2,1)S(1)} %all-to-all-done.mine_ref), channel_id=1, source_target_pairs={{0,1},{1,0},{2,3},{3,2},{4,5},{5,4},{6,7},{7,6},{8,9},{9,8},{10,11... | collective-permute-start | bytes 1572872 | tf_op jit(solution)/shard_map/ppermute | solution.py:622
  46.0 3.1 %collective-permute-start.3 = (f32[1,2048]{1,0:T(1,128)S(1)}, f32[1,2048]{1,0:T(1,128)S(1)}, u32[]{:S(2)}, u32[]{:S(2)}) collective-permute-start(f32[1,2048]{1,0:T(1,128)S(1)} %get-tuple-element.26), channel_id=1, source_target_pairs={{0,3},{1,2},{2,1},{3,0},{4,7},{5,6},{6,5},{7,4},{8,11},{9,10},{10,... | collective-permute-start | bytes 24584 | tf_op jit(solution)/shard_map/ppermute | solution.py:67
  46.3 3.7 %collective-permute-start.2 = (f32[1,2048]{1,0:T(1,128)S(1)}, f32[1,2048]{1,0:T(1,128)S(1)}, u32[]{:S(2)}, u32[]{:S(2)}) collective-permute-start(f32[1,2048]{1,0:T(1,128)S(1)} %get-tuple-element.26), channel_id=1, source_target_pairs={{0,2},{1,3},{2,0},{3,1},{4,6},{5,7},{6,4},{7,5},{8,10},{9,11},{10,... | collective-permute-start | bytes 24584 | tf_op jit(solution)/shard_map/ppermute | solution.py:67
  47.8 2.1 %collective-permute-start.1 = (f32[1,2048]{1,0:T(1,128)S(1)}, f32[1,2048]{1,0:T(1,128)S(1)}, u32[]{:S(2)}, u32[]{:S(2)}) collective-permute-start(f32[1,2048]{1,0:T(1,128)S(1)} %get-tuple-element.26), channel_id=1, source_target_pairs={{0,1},{1,0},{2,3},{3,2},{4,5},{5,4},{6,7},{7,6},{8,9},{9,8},{10,11... | collective-permute-start | bytes 24584 | tf_op jit(solution)/shard_map/ppermute | solution.py:67
  59.3 37.0 %slice-start = ((s8[8388608]{0:T(1024)(128)(4,1)}), s8[4194304]{0:T(1024)(128)(4,1)S(1)}, s32[]{:S(2)}) async-start(s8[8388608]{0:T(1024)(128)(4,1)} %bitcast.8), calls=%async_computation.5 | async-start | bytes 8388608
  63.4 3.1 %collective-permute-start.6 = (f32[1,2048]{1,0:T(1,128)S(1)}, f32[1,2048]{1,0:T(1,128)S(1)}, u32[]{:S(2)}, u32[]{:S(2)}) collective-permute-start(f32[1,2048]{1,0:T(1,128)S(1)} %get-tuple-element.30), channel_id=1, source_target_pairs={{0,3},{1,2},{2,1},{3,0},{4,7},{5,6},{6,5},{7,4},{8,11},{9,10},{10,... | collective-permute-start | bytes 24584 | tf_op jit(solution)/shard_map/ppermute | solution.py:67
  63.5 3.7 %collective-permute-start.5 = (f32[1,2048]{1,0:T(1,128)S(1)}, f32[1,2048]{1,0:T(1,128)S(1)}, u32[]{:S(2)}, u32[]{:S(2)}) collective-permute-start(f32[1,2048]{1,0:T(1,128)S(1)} %get-tuple-element.30), channel_id=1, source_target_pairs={{0,2},{1,3},{2,0},{3,1},{4,6},{5,7},{6,4},{7,5},{8,10},{9,11},{10,... | collective-permute-start | bytes 24584 | tf_op jit(solution)/shard_map/ppermute | solution.py:67
  65.0 2.1 %collective-permute-start.4 = (f32[1,2048]{1,0:T(1,128)S(1)}, f32[1,2048]{1,0:T(1,128)S(1)}, u32[]{:S(2)}, u32[]{:S(2)}) collective-permute-start(f32[1,2048]{1,0:T(1,128)S(1)} %get-tuple-element.30), channel_id=1, source_target_pairs={{0,1},{1,0},{2,3},{3,2},{4,5},{5,4},{6,7},{7,6},{8,9},{9,8},{10,11... | collective-permute-start | bytes 24584 | tf_op jit(solution)/shard_map/ppermute | solution.py:67
  67.2 29.1 %slice-start.1 = ((s8[8388608]{0:T(1024)(128)(4,1)}), s8[4194304]{0:T(1024)(128)(4,1)S(1)}, s32[]{:S(2)}) async-start(s8[8388608]{0:T(1024)(128)(4,1)} %bitcast.8), calls=%async_computation.6 | async-start | bytes 8388608
  76.8 19.5 %copy-start = (bf16[256,256]{1,0:T(8,128)(2,1)S(1)}, bf16[256,256]{1,0:T(8,128)(2,1)}, u32[]{:S(2)}) copy-start(bf16[256,256]{1,0:T(8,128)(2,1)} %e_ref.3) | copy-start | bytes 393220
  80.1 3.1 %collective-permute-start.9 = (f32[1,2048]{1,0:T(1,128)S(1)}, f32[1,2048]{1,0:T(1,128)S(1)}, u32[]{:S(2)}, u32[]{:S(2)}) collective-permute-start(f32[1,2048]{1,0:T(1,128)S(1)} %get-tuple-element.32), channel_id=1, source_target_pairs={{0,3},{1,2},{2,1},{3,0},{4,7},{5,6},{6,5},{7,4},{8,11},{9,10},{10,... | collective-permute-start | bytes 24584 | tf_op jit(solution)/shard_map/ppermute | solution.py:67
  80.2 3.7 %collective-permute-start.8 = (f32[1,2048]{1,0:T(1,128)S(1)}, f32[1,2048]{1,0:T(1,128)S(1)}, u32[]{:S(2)}, u32[]{:S(2)}) collective-permute-start(f32[1,2048]{1,0:T(1,128)S(1)} %get-tuple-element.32), channel_id=1, source_target_pairs={{0,2},{1,3},{2,0},{3,1},{4,6},{5,7},{6,4},{7,5},{8,10},{9,11},{10,... | collective-permute-start | bytes 24584 | tf_op jit(solution)/shard_map/ppermute | solution.py:67
  81.7 2.1 %collective-permute-start.7 = (f32[1,2048]{1,0:T(1,128)S(1)}, f32[1,2048]{1,0:T(1,128)S(1)}, u32[]{:S(2)}, u32[]{:S(2)}) collective-permute-start(f32[1,2048]{1,0:T(1,128)S(1)} %get-tuple-element.32), channel_id=1, source_target_pairs={{0,1},{1,0},{2,3},{3,2},{4,5},{5,4},{6,7},{7,6},{8,9},{9,8},{10,11... | collective-permute-start | bytes 24584 | tf_op jit(solution)/shard_map/ppermute | solution.py:67
  105.8 1.6 %collective-permute-start.10 = (f32[256,256]{1,0:T(8,128)S(1)}, f32[256,256]{1,0:T(8,128)S(1)}, u32[]{:S(2)}, u32[]{:S(2)}) collective-permute-start(f32[256,256]{1,0:T(8,128)S(1)} %embed_part.1), channel_id=1, source_target_pairs={{0,1},{1,0},{2,3},{3,2},{4,5},{5,4},{6,7},{7,6},{8,9},{9,8},{10,11... | collective-permute-start | bytes 786440 | tf_op jit(solution)/shard_map/ppermute | solution.py:67
  107.4 8.4 %collective-permute-start.11 = (f32[256,256]{1,0:T(8,128)S(1)}, f32[256,256]{1,0:T(8,128)S(1)}, u32[]{:S(2)}, u32[]{:S(2)}) collective-permute-start(f32[256,256]{1,0:T(8,128)S(1)} %add.52), channel_id=1, source_target_pairs={{0,2},{1,3},{2,0},{3,1},{4,6},{5,7},{6,4},{7,5},{8,10},{9,11},{10,... | collective-permute-start | bytes 786440 | tf_op jit(solution)/shard_map/ppermute | solution.py:67

commit v11 on v10

--- a/solution.py
+++ b/solution.py
@@ -609,6 +609,11 @@
     )(last, r, v, *map(in_vmem, (a, h, z, ay)), in_vmem(all_rows, few(rows)), in_vmem(e))
 
 
+def log_sum(values):
+    top = tree(jnp.maximum, values)
+    return top + jnp.log(tree(add, [jnp.exp(value - top) for value in values]))
+
+
 def shards(embeddings, prototypes, row_cot, col_cot):
     batch, proto = lax.axis_size("batch"), lax.axis_size("proto")
     member, holder = lax.axis_index("batch"), lax.axis_index("proto")
@@ -617,10 +622,10 @@
     short = embeddings.shape[0] // 2
     half = lax.dynamic_slice_in_dim(embeddings, (holder % 2) * short, short, axis=0)
     mine = share(half, "batch")
-    lse = row_lse(embeddings, prototypes, batch * proto)
+    lse = log_sum(partners(row_lse(embeddings, prototypes, 1)[0], "proto"))
     mine, lse, me = lax.optimization_barrier((mine, lse, me))
     other = lax.ppermute(mine, "proto", [(i, i ^ 1) for i in range(proto)])
-    lse = swap_copies(lse, both)
+    lse = share(lse, "batch")
     e, rho, col_lse, f, all_rows, a, h, cot = col_softmax(me, lse, mine, other, prototypes, col_cot[None, :])
     rho = share(tree(add, partners(rho, "proto")), "batch")
     bar, r, ratio, z = second_pair(me, rho, row_cot[None, :], cot, a, e)

time: 117 us -> 116 us (level)
  waiting for transfers between devices: 14.3 us -> 11.2 us
  starting transfers between devices: 13.8 us -> 16.7 us
    all_to_all x1, waiting for transfers between devices: 5.79 us -> 1.28 us  [swap_copies(): return lax.all_to_all(copies, axis, split_axis=0, concat_axis=0, tiled=True)]
    ppermute x11 -> x14, starting transfers between devices: 6.5 us -> 9.41 us  [partners(): lax.ppermute(x, axis, [(i, i ^ d * stride) for i in range(total)])]
    ppermute x11 -> x14, waiting for transfers between devices: 8.5 us -> 9.95 us  [partners(): lax.ppermute(x, axis, [(i, i ^ d * stride) for i in range(total)])]
  transfers between devices with their start and end apart: 13 -> 16, of which waited for: 9 -> 11; matrix products, arithmetic and copies ran while one was open for 0% -> 0% of each run, Pallas kernels for 13% -> 13%
where the time goes in v11:
time: 116 us
  Pallas kernels  43 us (37%)
  blocking collectives  41.3 us (36%)
  starting transfers between devices  16.7 us (14%)
  waiting for transfers between devices  11.2 us (10%)
  local copies, waits for them, and re-layouts  1.91 us (2%)
    all_to_all x4, blocking collectives, swap_copies(): return lax.all_to_all(copies, axis, split_axis=0, concat_axis=0, tiled=True)  41.3 us
    pallas_call x1, Pallas kernels, col_softmax(): pl.pallas_call(functools.partial(col_softmax_kernel, devices // members),...  11.1 us
    ppermute x14, waiting for transfers between devices, partners(): lax.ppermute(x, axis, [(i, i ^ d * stride) for i in range(total)])  9.95 us
    pallas_call x1, Pallas kernels, embed_part(): pl.pallas_call(embed_kernel, in_specs=[in_smem] + [whole] * 6, out_specs=...  9.57 us
    ppermute x14, starting transfers between devices, partners(): lax.ppermute(x, axis, [(i, i ^ d * stride) for i in range(total)])  9.41 us
    pallas_call x1, Pallas kernels, row_lse(): pl.pallas_call(row_lse_kernel, grid=(count // width,), in_specs=[pl.Block...  8.59 us
    all_to_all x1, starting transfers between devices, swap_copies(): return lax.all_to_all(copies, axis, split_axis=0, concat_axis=0, tiled=True)  7.25 us
    pallas_call x1, Pallas kernels, proto_part(): pl.pallas_call(proto_kernel, in_specs=[whole] * 9, out_specs=anywhere, ou...  6.51 us
  transfers between devices with their start and end apart: 16, of which 11 were waited for; matrix products, arithmetic and copies ran while one was open for 0% of the time, Pallas kernels for 13%

profile of v11, /device:TPU:0, one launch (start us, length us, event | category | flops | bytes accessed | tf_op | source)
XLA Modules:
  0.0 115.9 jit_solution(588712753938474185)
XLA Ops:
  0.6 0.8 constant_dynamic-slice_fusion
  1.5 0.8 broadcast_in_dim.44
  2.3 7.3 %all-to-all-start = ((bf16[8,128,256]{2,1,0:T(8,128)(2,1)}), bf16[8,128,256]{2,1,0:T(8,128)(2,1)S(1)}, u32[]{:S(2)}, u32[]{:S(2)}) async-start(bf16[8,128,256]{2,1,0:T(8,128)(2,1)} %broadcast_in_dim.44), calls=%async_computation | async-start | bytes 1048576 | tf_op jit(solution)/shard_map/all_to_all | solution.py:72
  9.6 8.6 %row_lse.1 = f32[1,1,256]{2,1,0:T(1,128)S(1)} custom-call(bf16[256,256]{1,0:T(8,128)(2,1)} %e_ref.3, bf16[16384,256]{1,0:T(8,128)(2,1)} %p_ref.3), custom_call_target="tpu_custom_call" | custom-call | flops 2147483648 | bytes 8388608 | tf_op jit(solution)/shard_map/row_lse/pallas_call | solution.py:246
  18.2 1.6 %collective-permute-start.1 = (f32[1,256]{1,0:T(1,128)S(1)}, f32[1,256]{1,0:T(1,128)S(1)}, u32[]{:S(2)}, u32[]{:S(2)}) collective-permute-start(f32[1,256]{1,0:T(1,128)S(1)} %bitcast.13), channel_id=1, source_target_pairs={{0,2},{1,3},{2,0},{3,1},{4,6},{5,7},{6,4},{7,5},{8,10},{9,11},{10,... | collective-permute-start | bytes 3080 | tf_op jit(solution)/shard_map/ppermute | solution.py:67
  19.8 0.0 collective-permute-start.2
  19.8 0.6 collective-permute-start
  20.4 0.1 pad_add_fusion.me_ref
  20.5 1.4 %collective-permute-done.1 = f32[1,256]{1,0:T(1,128)S(1)} collective-permute-done((f32[1,256]{1,0:T(1,128)S(1)}, f32[1,256]{1,0:T(1,128)S(1)}, u32[]{:S(2)}, u32[]{:S(2)}) %collective-permute-start.1) | collective-permute-done | bytes 1056 | tf_op jit(solution)/shard_map/ppermute | solution.py:67
  21.8 0.9 collective-permute-done.2
  22.8 0.0 collective-permute-done
  22.8 1.3 %all-to-all-done.mine_ref = bf16[8,128,256]{2,1,0:T(8,128)(2,1)S(1)} async-done(((bf16[8,128,256]{2,1,0:T(8,128)(2,1)}), bf16[8,128,256]{2,1,0:T(8,128)(2,1)S(1)}, u32[]{:S(2)}, u32[]{:S(2)}) %all-to-all-start) | async-done | bytes 524320 | tf_op jit(solution)/shard_map/all_to_all | solution.py:72
  24.1 0.0 collective-permute-start.3
  24.1 11.1 %all_to_all.25.lse_ref = f32[8,1,256]{2,1,0:T(1,128)S(1)} all-to-all(f32[8,1,256]{2,1,0:T(1,128)S(1)} %broadcast_in_dim.46), channel_id=1, replica_groups=mesh['batch'=8,'proto'=4] {'batch'}, dimensions={0} | all-to-all | bytes 16384 | tf_op jit(solution)/shard_map/all_to_all | solution.py:72
  35.2 0.0 collective-permute-done.3.other_ref
  35.2 11.1 %col_softmax.1 = (f32[2048,2048]{1,0:T(8,128)S(1)}, f32[1,2048]{1,0:T(1,128)S(1)}, f32[1,2048]{1,0:T(1,128)S(1)}, f32[1,2048]{1,0:T(1,128)S(1)}, bf16[2048,256]{...) custom-call(s32[3]{0:T(128)S(1)} %pad_add_fusion.me_ref, ...), custom_call_target="tpu_custom_call" | custom-call | flops 2147483648 | bytes 16777216 | tf_op jit(solution)/shard_map/col_softmax/pallas_call | solution.py:371
  46.3 0.1 collective-permute-start.6
  46.4 0.7 collective-permute-start.5
  47.1 1.1 collective-permute-start.4
  48.2 1.2 %collective-permute-done.6 = f32[1,2048]{1,0:T(1,128)S(1)} collective-permute-done((f32[1,2048]{1,0:T(1,128)S(1)}, f32[1,2048]{1,0:T(1,128)S(1)}, u32[]{:S(2)}, u32[]{:S(2)}) %collective-permute-start.6) | collective-permute-done | bytes 8224 | tf_op jit(solution)/shard_map/ppermute | solution.py:67
  49.4 0.7 collective-permute-done.5
  50.1 0.0 collective-permute-done.4
  50.2 9.3 %all_to_all.26.rho_ref = f32[8,1,2048]{2,1,0:T(1,128)S(1)} all-to-all(f32[8,1,2048]{2,1,0:T(1,128)S(1)} %broadcast_in_dim.49), channel_id=1, replica_groups=mesh['batch'=8,'proto'=4] {'batch'}, dimensions={0} | all-to-all | bytes 131072 | tf_op jit(solution)/shard_map/all_to_all | solution.py:72
  59.5 4.0 %second_pair.1 = (f32[1,2048]{1,0:T(1,128)S(1)}, f32[1,2048]{1,0:T(1,128)S(1)}, f32[1,2048]{1,0:T(1,128)S(1)}, f32[2048,128]{1,0:T(8,128)S(1)}) custom-call(s32[3]{0:T(128)S(1)} %pad_add_fusion.me_ref, f32[8,1,2048]{2,1,0:T(1,128)S(1)} %all_to_all.26.rho_ref, f32[1,256]{1,0:T(1,128)S(1)} %bitcast.16, f32[2048,128]{1,0:T(8,128)S(1)} %get-tuple-element.27.cot_ref, ...), custom_call_target="tpu_custom_call" | custom-call | flops 16777216 | bytes 16777216 | tf_op jit(solution)/shard_map/second_pair/pallas_call | solution.py:420
  63.5 0.1 collective-permute-start.9
  63.6 0.7 collective-permute-start.8
  64.3 1.1 collective-permute-start.7
  65.4 1.2 %collective-permute-done.9 = f32[1,2048]{1,0:T(1,128)S(1)} collective-permute-done((f32[1,2048]{1,0:T(1,128)S(1)}, f32[1,2048]{1,0:T(1,128)S(1)}, u32[]{:S(2)}, u32[]{:S(2)}) %collective-permute-start.9) | collective-permute-done | bytes 8224 | tf_op jit(solution)/shard_map/ppermute | solution.py:67
  66.6 0.7 collective-permute-done.8
  67.3 0.0 collective-permute-done.7
  67.3 0.0 slice-start.1
  67.4 9.6 %all_to_all.27.bar_ref = f32[8,1,2048]{2,1,0:T(1,128)S(1)} all-to-all(f32[8,1,2048]{2,1,0:T(1,128)S(1)} %broadcast_in_dim.52), channel_id=1, replica_groups=mesh['batch'=8,'proto'=4] {'batch'}, dimensions={0} | all-to-all | bytes 131072 | tf_op jit(solution)/shard_map/all_to_all | solution.py:72
  76.9 3.3 %first_pair.1 = (f32[1,2048]{1,0:T(1,128)S(1)}, f32[1,2048]{1,0:T(1,128)S(1)}, f32[1,2048]{1,0:T(1,128)S(1)}, f32[2048,128]{1,0:T(8,128)S(1)}) custom-call(f32[8,1,2048]{2,1,0:T(1,128)S(1)} %all_to_all.27.bar_ref, f32[1,2048]{1,0:T(1,128)S(1)} %get-tuple-element.31.r_ref, f32[2048,128]{1,0:T(8,128)S(1)} %get-tuple-element.28.a_ref, ...), custom_call_target="tpu_custom_call" | custom-call | flops 16777216 | bytes 16777216 | tf_op jit(solution)/shard_map/first_pair/pallas_call | solution.py:456
  80.2 0.1 collective-permute-start.12
  80.3 0.7 collective-permute-start.11
  81.0 1.1 collective-permute-start.10
  82.1 1.2 %collective-permute-done.12 = f32[1,2048]{1,0:T(1,128)S(1)} collective-permute-done((f32[1,2048]{1,0:T(1,128)S(1)}, f32[1,2048]{1,0:T(1,128)S(1)}, u32[]{:S(2)}, u32[]{:S(2)}) %collective-permute-start.12) | collective-permute-done | bytes 8224 | tf_op jit(solution)/shard_map/ppermute | solution.py:67
  83.3 0.7 collective-permute-done.11
  84.0 0.0 collective-permute-done.10
  84.0 0.1 broadcast_in_dim.54
  84.2 11.3 %all_to_all.28.last_ref = f32[8,1,8192]{2,1,0:T(1,128)S(1)} all-to-all(f32[8,1,8192]{2,1,0:T(1,128)S(1)} %broadcast_in_dim.54), channel_id=1, replica_groups=mesh['batch'=8,'proto'=4] {'batch'}, dimensions={0} | all-to-all | bytes 524288 | tf_op jit(solution)/shard_map/all_to_all | solution.py:72
  95.5 9.6 %embed_part.1 = f32[256,256]{1,0:T(8,128)S(1)} custom-call(s32[3]{0:T(128)S(1)} %pad_add_fusion.me_ref, f32[8,1,8192]{2,1,0:T(1,128)S(1)} %all_to_all.28.last_ref, f32[1,2048]{1,0:T(1,128)S(1)} %get-tuple-element.36.f_ref, f32[1,2048]{1,0:T(1,128)S(1)} %get-tuple-element.31.r_ref, f32[1,2048]{1,0:T(1,128)S(1)} %get-tuple-element.37.v_ref, ...), custom_call_target="tpu_custom_call" | custom-call | flops 4294967296 | bytes 8388608 | tf_op jit(solution)/shard_map/embed_part/pallas_call | solution.py:532
  105.1 0.1 collective-permute-start.13
  105.2 1.5 %collective-permute-done.13 = f32[256,256]{1,0:T(8,128)S(1)} collective-permute-done((f32[256,256]{1,0:T(8,128)S(1)}, f32[256,256]{1,0:T(8,128)S(1)}, u32[]{:S(2)}, u32[]{:S(2)}) %collective-permute-start.13) | collective-permute-done | bytes 262176 | tf_op jit(solution)/shard_map/ppermute | solution.py:67
  106.7 1.4 %collective-permute-start.14 = (f32[256,256]{1,0:T(8,128)S(1)}, f32[256,256]{1,0:T(8,128)S(1)}, u32[]{:S(2)}, u32[]{:S(2)}) collective-permute-start(f32[256,256]{1,0:T(8,128)S(1)} %add.68), channel_id=1, source_target_pairs={{0,2},{1,3},{2,0},{3,1},{4,6},{5,7},{6,4},{7,5},{8,10},{9,11},{10,... | collective-permute-start | bytes 786440 | tf_op jit(solution)/shard_map/ppermute | solution.py:67
  108.1 6.5 %proto_part.1 = f32[2048,256]{1,0:T(8,128)} custom-call(f32[8,1,8192]{2,1,0:T(1,128)S(1)} %all_to_all.28.last_ref, f32[1,2048]{1,0:T(1,128)S(1)} %get-tuple-element.31.r_ref, f32[1,2048]{1,0:T(1,128)S(1)} %get-tuple-element.37.v_ref, f32[2048,128]{1,0:T(8,128)S(1)} %get-tuple-element.28.a_ref, f32[2048,128]{1,0:T(8,128)S(1)} %get-tuple-element.40.h_ref, ...), custom_call_target="tpu_custom_call" | custom-call | flops 2147483648 | bytes 16777216 | tf_op jit(solution)/shard_map/proto_part/pallas_call | solution.py:593
  114.6 0.5 collective-permute-done.14
  115.2 0.7 add.69
  (17 shorter events, 0.2 us)
Async XLA Ops:
  2.3 21.7 %all-to-all-start = ((bf16[8,128,256]{2,1,0:T(8,128)(2,1)}), bf16[8,128,256]{2,1,0:T(8,128)(2,1)S(1)}, u32[]{:S(2)}, u32[]{:S(2)}) async-start(bf16[8,128,256]{2,1,0:T(8,128)(2,1)} %broadcast_in_dim.44), calls=%async_computation | async-start | bytes 1048576 | tf_op jit(solution)/shard_map/all_to_all | solution.py:72
  9.6 49.9 %copy-start.1 = (f32[256]{0:T(256)S(1)}, f32[256]{0:T(256)}, u32[]{:S(2)}) copy-start(f32[256]{0:T(256)} %param.6) | copy-start | bytes 3076
  18.2 3.6 %collective-permute-start.1 = (f32[1,256]{1,0:T(1,128)S(1)}, f32[1,256]{1,0:T(1,128)S(1)}, u32[]{:S(2)}, u32[]{:S(2)}) collective-permute-start(f32[1,256]{1,0:T(1,128)S(1)} %bitcast.13), channel_id=1, source_target_pairs={{0,2},{1,3},{2,0},{3,1},{4,6},{5,7},{6,4},{7,5},{8,10},{9,11},{10,... | collective-permute-start | bytes 3080 | tf_op jit(solution)/shard_map/ppermute | solution.py:67
  19.8 3.0 %collective-permute-start.2 = (f32[1,256]{1,0:T(1,128)S(1)}, f32[1,256]{1,0:T(1,128)S(1)}, u32[]{:S(2)}, u32[]{:S(2)}) collective-permute-start(f32[1,256]{1,0:T(1,128)S(1)} %bitcast.14), channel_id=1, source_target_pairs={{0,3},{1,2},{2,1},{3,0},{4,7},{5,6},{6,5},{7,4},{8,11},{9,10},{10,... | collective-permute-start | bytes 3080 | tf_op jit(solution)/shard_map/ppermute | solution.py:67
  19.8 3.0 %collective-permute-start = (f32[1,256]{1,0:T(1,128)S(1)}, f32[1,256]{1,0:T(1,128)S(1)}, u32[]{:S(2)}, u32[]{:S(2)}) collective-permute-start(f32[1,256]{1,0:T(1,128)S(1)} %bitcast.15), channel_id=1, source_target_pairs={{0,1},{1,0},{2,3},{3,2},{4,5},{5,4},{6,7},{7,6},{8,9},{9,8},{10,11... | collective-permute-start | bytes 3080 | tf_op jit(solution)/shard_map/ppermute | solution.py:67
  24.1 11.1 %collective-permute-start.3 = (bf16[8,128,256]{2,1,0:T(8,128)(2,1)S(1)}, bf16[8,128,256]{2,1,0:T(8,128)(2,1)S(1)}, u32[]{:S(2)}, u32[]{:S(2)}) collective-permute-start(bf16[8,128,256]{2,1,0:T(8,128)(2,1)S(1)} %all-to-all-done.mine_ref), channel_id=1, source_target_pairs={{0,1},{1,0},{2,3},{3,2},{4,5},{5,4},{6,7},{7,6},{8,9},{9,8},{10,11... | collective-permute-start | bytes 1572872 | tf_op jit(solution)/shard_map/ppermute | solution.py:627
  46.3 3.1 %collective-permute-start.6 = (f32[1,2048]{1,0:T(1,128)S(1)}, f32[1,2048]{1,0:T(1,128)S(1)}, u32[]{:S(2)}, u32[]{:S(2)}) collective-permute-start(f32[1,2048]{1,0:T(1,128)S(1)} %get-tuple-element.26), channel_id=1, source_target_pairs={{0,3},{1,2},{2,1},{3,0},{4,7},{5,6},{6,5},{7,4},{8,11},{9,10},{10,... | collective-permute-start | bytes 24584 | tf_op jit(solution)/shard_map/ppermute | solution.py:67
  46.4 3.7 %collective-permute-start.5 = (f32[1,2048]{1,0:T(1,128)S(1)}, f32[1,2048]{1,0:T(1,128)S(1)}, u32[]{:S(2)}, u32[]{:S(2)}) collective-permute-start(f32[1,2048]{1,0:T(1,128)S(1)} %get-tuple-element.26), channel_id=1, source_target_pairs={{0,2},{1,3},{2,0},{3,1},{4,6},{5,7},{6,4},{7,5},{8,10},{9,11},{10,... | collective-permute-start | bytes 24584 | tf_op jit(solution)/shard_map/ppermute | solution.py:67
  47.1 3.0 %collective-permute-start.4 = (f32[1,2048]{1,0:T(1,128)S(1)}, f32[1,2048]{1,0:T(1,128)S(1)}, u32[]{:S(2)}, u32[]{:S(2)}) collective-permute-start(f32[1,2048]{1,0:T(1,128)S(1)} %get-tuple-element.26), channel_id=1, source_target_pairs={{0,1},{1,0},{2,3},{3,2},{4,5},{5,4},{6,7},{7,6},{8,9},{9,8},{10,11... | collective-permute-start | bytes 24584 | tf_op jit(solution)/shard_map/ppermute | solution.py:67
  59.5 36.1 %slice-start = ((s8[8388608]{0:T(1024)(128)(4,1)}), s8[4194304]{0:T(1024)(128)(4,1)S(1)}, s32[]{:S(2)}) async-start(s8[8388608]{0:T(1024)(128)(4,1)} %bitcast.11), calls=%async_computation.5 | async-start | bytes 8388608
  63.5 3.1 %collective-permute-start.9 = (f32[1,2048]{1,0:T(1,128)S(1)}, f32[1,2048]{1,0:T(1,128)S(1)}, u32[]{:S(2)}, u32[]{:S(2)}) collective-permute-start(f32[1,2048]{1,0:T(1,128)S(1)} %get-tuple-element.30), channel_id=1, source_target_pairs={{0,3},{1,2},{2,1},{3,0},{4,7},{5,6},{6,5},{7,4},{8,11},{9,10},{10,... | collective-permute-start | bytes 24584 | tf_op jit(solution)/shard_map/ppermute | solution.py:67
  63.6 3.7 %collective-permute-start.8 = (f32[1,2048]{1,0:T(1,128)S(1)}, f32[1,2048]{1,0:T(1,128)S(1)}, u32[]{:S(2)}, u32[]{:S(2)}) collective-permute-start(f32[1,2048]{1,0:T(1,128)S(1)} %get-tuple-element.30), channel_id=1, source_target_pairs={{0,2},{1,3},{2,0},{3,1},{4,6},{5,7},{6,4},{7,5},{8,10},{9,11},{10,... | collective-permute-start | bytes 24584 | tf_op jit(solution)/shard_map/ppermute | solution.py:67
  64.3 3.0 %collective-permute-start.7 = (f32[1,2048]{1,0:T(1,128)S(1)}, f32[1,2048]{1,0:T(1,128)S(1)}, u32[]{:S(2)}, u32[]{:S(2)}) collective-permute-start(f32[1,2048]{1,0:T(1,128)S(1)} %get-tuple-element.30), channel_id=1, source_target_pairs={{0,1},{1,0},{2,3},{3,2},{4,5},{5,4},{6,7},{7,6},{8,9},{9,8},{10,11... | collective-permute-start | bytes 24584 | tf_op jit(solution)/shard_map/ppermute | solution.py:67
  67.3 28.2 %slice-start.1 = ((s8[8388608]{0:T(1024)(128)(4,1)}), s8[4194304]{0:T(1024)(128)(4,1)S(1)}, s32[]{:S(2)}) async-start(s8[8388608]{0:T(1024)(128)(4,1)} %bitcast.11), calls=%async_computation.6 | async-start | bytes 8388608
  76.9 18.6 %copy-start = (bf16[256,256]{1,0:T(8,128)(2,1)S(1)}, bf16[256,256]{1,0:T(8,128)(2,1)}, u32[]{:S(2)}) copy-start(bf16[256,256]{1,0:T(8,128)(2,1)} %e_ref.3) | copy-start | bytes 393220
  80.2 3.1 %collective-permute-start.12 = (f32[1,2048]{1,0:T(1,128)S(1)}, f32[1,2048]{1,0:T(1,128)S(1)}, u32[]{:S(2)}, u32[]{:S(2)}) collective-permute-start(f32[1,2048]{1,0:T(1,128)S(1)} %get-tuple-element.32), channel_id=1, source_target_pairs={{0,3},{1,2},{2,1},{3,0},{4,7},{5,6},{6,5},{7,4},{8,11},{9,10},{10,... | collective-permute-start | bytes 24584 | tf_op jit(solution)/shard_map/ppermute | solution.py:67
  80.3 3.7 %collective-permute-start.11 = (f32[1,2048]{1,0:T(1,128)S(1)}, f32[1,2048]{1,0:T(1,128)S(1)}, u32[]{:S(2)}, u32[]{:S(2)}) collective-permute-start(f32[1,2048]{1,0:T(1,128)S(1)} %get-tuple-element.32), channel_id=1, source_target_pairs={{0,2},{1,3},{2,0},{3,1},{4,6},{5,7},{6,4},{7,5},{8,10},{9,11},{10,... | collective-permute-start | bytes 24584 | tf_op jit(solution)/shard_map/ppermute | solution.py:67
  81.0 3.0 %collective-permute-start.10 = (f32[1,2048]{1,0:T(1,128)S(1)}, f32[1,2048]{1,0:T(1,128)S(1)}, u32[]{:S(2)}, u32[]{:S(2)}) collective-permute-start(f32[1,2048]{1,0:T(1,128)S(1)} %get-tuple-element.32), channel_id=1, source_target_pairs={{0,1},{1,0},{2,3},{3,2},{4,5},{5,4},{6,7},{7,6},{8,9},{9,8},{10,11... | collective-permute-start | bytes 24584 | tf_op jit(solution)/shard_map/ppermute | solution.py:67
  105.1 1.6 %collective-permute-start.13 = (f32[256,256]{1,0:T(8,128)S(1)}, f32[256,256]{1,0:T(8,128)S(1)}, u32[]{:S(2)}, u32[]{:S(2)}) collective-permute-start(f32[256,256]{1,0:T(8,128)S(1)} %embed_part.1), channel_id=1, source_target_pairs={{0,1},{1,0},{2,3},{3,2},{4,5},{5,4},{6,7},{7,6},{8,9},{9,8},{10,11... | collective-permute-start | bytes 786440 | tf_op jit(solution)/shard_map/ppermute | solution.py:67
  106.7 8.4 %collective-permute-start.14 = (f32[256,256]{1,0:T(8,128)S(1)}, f32[256,256]{1,0:T(8,128)S(1)}, u32[]{:S(2)}, u32[]{:S(2)}) collective-permute-start(f32[256,256]{1,0:T(8,128)S(1)} %add.68), channel_id=1, source_target_pairs={{0,2},{1,3},{2,0},{3,1},{4,6},{5,7},{6,4},{7,5},{8,10},{9,11},{10,... | collective-permute-start | bytes 786440 | tf_op jit(solution)/shard_map/ppermute | solution.py:67
